TPU v7x, 32 devices: a whole 2x2x4 slice. The times are simulated.
32 devices in a mesh: grp: 2 (over x), gx: 8 (over z, y), gy: 2 (over core).
Axes of the slice: x: 2, y: 2, z: 4, core: 2. Of those that a mesh axis runs over, the one named last changes fastest.
Arguments:
- hidden_rows: bfloat16 [384, 8192], P(('grp', 'gy'), 'gx'), parts along dimension 0, may hold values from -40 to 40
- norm_gain: bfloat16 [8192], P('gx'), may hold values from 0.25 to 1.75
- w_query: bfloat16 [8192, 8192], P('gx', 'gy'), may hold values from -0.0625 to 0.0625
- key_weight: bfloat16 [8192, 1024], P('gx', 'gy'), may hold values from -0.0625 to 0.0625
- value_weight: bfloat16 [8192, 1024], P('gx', 'gy'), may hold values from -0.0625 to 0.0625
- query_bias: bfloat16 [8192], P('gy'), may hold values from -3 to 3
- key_bias_vector: bfloat16 [1024], P('gy'), may hold values from -3 to 3
- value_bias_vector: bfloat16 [1024], P('gy'), may hold values from -3 to 3
- rotated_key_cache: bfloat16 [384, 128, 1024], P(('grp', 'gx'), None, 'gy'), parts along dimension 0, may hold values from -2500 to 2500
- stored_value_cache: bfloat16 [384, 128, 1024], P(('grp', 'gx'), None, 'gy'), parts along dimension 0, may hold values from -6 to 6
- slot_valid_lengths: int32 [384], P('grp'), parts along dimension 0, may hold values from 2 to 128, as said below
- slot_of_row: int32 [384], P('grp'), parts along dimension 0, may hold values from 0 to 191, each once
- w_out: bfloat16 [8192, 8192], P('gy', 'gx'), may hold values from -0.0625 to 0.0625
Outputs:
- mixed: bfloat16 [384, 8192], P(('grp', 'gy'), 'gx'), parts along dimension 0
There are 2 independent parts, one for each index of `grp`. A program takes and returns all parts, laid end to end along the dimension named above; an argument that names none is the same for every part. Nothing has to cross between parts.
Inputs may be any that keep to these rules, and one draw needn't show every extreme that they name: `slot_valid_lengths`: every slot holds at least 2 valid positions; some slot holds all 128.
All inputs are finite; a program needn't handle non-finite values.
Results may differ from a plain program's by a relative error of at most 0.006.
Values may be sent and summed in bfloat16 or wider, within the bound.
No kernel may reach another device: no remote copies, remote signals or barrier semaphores. Data moves between devices by JAX's collectives and lax.ppermute only.
A program may use at most 128 MiB of HBM per device.

v0:
```python
import math

import jax
import jax.numpy as jnp
from jax import lax
from jax.sharding import PartitionSpec as P

MODEL_WIDTH = 8192
QUERY_HEADS = 64
KEY_VALUE_HEADS = 8
HEAD_SIZE = 128


EPSILON = 1e-06
ROPE_BASE = 1000000.0


def apply_rotary(values, positions, heads):
    total_row_count = values.shape[0]
    head_width = values.shape[1] // heads
    half_width = head_width // 2
    shaped = values.reshape(total_row_count, heads, head_width)
    frequency = ROPE_BASE ** (-(jnp.arange(half_width).astype(jnp.float32) * 2.0 / head_width))
    angles = positions.astype(jnp.float32)[:, None, None] * frequency[None, None, :]
    cosine = jnp.cos(angles)
    sine_part = jnp.sin(angles)
    first_half = shaped[:, :, :half_width]
    second_half = shaped[:, :, half_width:]
    turned = jnp.concatenate(
        [
            first_half * cosine - second_half * sine_part,
            second_half * cosine + first_half * sine_part,
        ],
        axis=2,
    )
    return turned.reshape(total_row_count, heads * head_width)


def attend(
    query_vectors, current_key, current_value, rotated_key_cache, stored_value_cache, lengths
):
    total_row_count = query_vectors.shape[0]
    positions = rotated_key_cache.shape[1]
    kv_heads = rotated_key_cache.shape[2] // HEAD_SIZE
    query_group_count = QUERY_HEADS // KEY_VALUE_HEADS
    grouped_queries = query_vectors.reshape(total_row_count, kv_heads, query_group_count, HEAD_SIZE)
    cached_key_rows = rotated_key_cache.reshape(total_row_count, positions, kv_heads, HEAD_SIZE)
    cached_value_rows = stored_value_cache.reshape(total_row_count, positions, kv_heads, HEAD_SIZE)
    appended_key = current_key.reshape(total_row_count, kv_heads, HEAD_SIZE)
    appended_value = current_value.reshape(total_row_count, kv_heads, HEAD_SIZE).astype(jnp.float32)
    score_scale = 1.0 / math.sqrt(HEAD_SIZE)
    cache_scores = (
        jnp.einsum(
            "rgqd,rpgd->rgqp", grouped_queries, cached_key_rows, preferred_element_type=jnp.float32
        )
        * score_scale
    )
    own_score = (
        jnp.einsum(
            "rgqd,rgd->rgq", grouped_queries, appended_key, preferred_element_type=jnp.float32
        )
        * score_scale
    )
    valid_mask = (jnp.arange(positions)[None, :] < lengths[:, None])[:, None, None, :]
    cache_scores = jnp.where(valid_mask, cache_scores, -1e30)
    row_max = jnp.maximum(jnp.max(cache_scores, axis=3), own_score)
    cache_exp = jnp.where(valid_mask, jnp.exp(cache_scores - row_max[..., None]), 0.0)
    own_exp = jnp.exp(own_score - row_max)
    denominator = jnp.sum(cache_exp, axis=3) + own_exp
    cache_weight = (cache_exp / denominator[..., None]).astype(jnp.bfloat16)
    own_weight = (own_exp / denominator).astype(jnp.bfloat16).astype(jnp.float32)
    combined = jnp.einsum(
        "rgqp,rpgd->rgqd", cache_weight, cached_value_rows, preferred_element_type=jnp.float32
    )
    combined = combined + own_weight[..., None] * appended_value[:, :, None, :]
    return combined.reshape(total_row_count, kv_heads * query_group_count * HEAD_SIZE).astype(
        jnp.bfloat16
    )


def on_device(
    hidden_rows,
    norm_gain,
    w_query,
    key_weight,
    value_weight,
    query_bias,
    key_bias_vector,
    value_bias_vector,
    rotated_key_cache,
    stored_value_cache,
    slot_valid_lengths,
    slot_of_row,
    w_out,
):
    widened = hidden_rows.astype(jnp.float32)
    local_squares = jnp.sum(widened * widened, axis=1)
    square_sum = lax.psum(local_squares, "gx")
    normed = (
        widened
        * lax.rsqrt(square_sum[:, None] / MODEL_WIDTH + EPSILON)
        * norm_gain.astype(jnp.float32)
    ).astype(jnp.bfloat16)
    rows_all = lax.all_gather(normed, "gy", axis=0, tiled=True)
    total_row_count = rows_all.shape[0]
    row_of_slot = (
        jnp.zeros((total_row_count,), jnp.int32)
        .at[slot_of_row]
        .set(jnp.arange(total_row_count, dtype=jnp.int32))
    )
    slotted = rows_all[row_of_slot]
    query_cols = w_query.shape[1]
    kv_cols = key_weight.shape[1]
    per_owner = rotated_key_cache.shape[0]
    joined = lax.psum_scatter(
        jnp.concatenate(
            [
                jnp.dot(slotted, w_query, preferred_element_type=jnp.float32),
                jnp.dot(slotted, key_weight, preferred_element_type=jnp.float32),
                jnp.dot(slotted, value_weight, preferred_element_type=jnp.float32),
            ],
            axis=1,
        ),
        "gx",
        scatter_dimension=0,
        tiled=True,
    )
    query_vectors = joined[:, :query_cols]
    current_key = joined[:, query_cols : query_cols + kv_cols]
    current_value = joined[:, query_cols + kv_cols :]
    slot_start = lax.axis_index("gx") * per_owner
    lengths = lax.dynamic_slice_in_dim(slot_valid_lengths, slot_start, per_owner, 0)
    query_vectors = apply_rotary(
        query_vectors + query_bias.astype(jnp.float32), lengths, query_cols // HEAD_SIZE
    ).astype(jnp.bfloat16)
    current_key = apply_rotary(
        current_key + key_bias_vector.astype(jnp.float32), lengths, kv_cols // HEAD_SIZE
    ).astype(jnp.bfloat16)
    current_value = (current_value + value_bias_vector.astype(jnp.float32)).astype(jnp.bfloat16)
    attended = attend(
        query_vectors, current_key, current_value, rotated_key_cache, stored_value_cache, lengths
    )
    slot_terms = jnp.dot(
        lax.all_gather(attended, "gx", axis=0, tiled=True),
        w_out,
        preferred_element_type=jnp.float32,
    )
    row_terms = slot_terms[slot_of_row]
    summed = lax.psum_scatter(row_terms, "gy", scatter_dimension=0, tiled=True)
    return (widened + summed).astype(jnp.bfloat16)


def solution(mesh):
    in_specs = (
        P(("grp", "gy"), "gx"),
        P("gx"),
        P("gx", "gy"),
        P("gx", "gy"),
        P("gx", "gy"),
        P("gy"),
        P("gy"),
        P("gy"),
        P(("grp", "gx"), None, "gy"),
        P(("grp", "gx"), None, "gy"),
        P("grp"),
        P("grp"),
        P("gy", "gx"),
    )
    out_specs = P(("grp", "gy"), "gx")
    return jax.shard_map(
        on_device, mesh=mesh, in_specs=in_specs, out_specs=out_specs, check_vma=False
    )
```

profile of v0, /device:TPU:0, one launch (start us, length us, event | category | flops | bytes accessed | tf_op | source)
XLA Modules:
  0.0 209.5 jit_solution(4801071053034756600)
XLA Ops:
  6.5 0.0 copy-start
  6.5 0.0 reduce-scatter.3.cloned.1.call-start
  6.5 0.8 compare_select_fusion.1
  7.4 1.2 scatter_custom_fusion
  8.6 0.7 convert_element_type.69
  9.3 1.1 fusion.18
  10.4 23.1 %psum.7 = f32[96]{0:T(128)S(1)} all-reduce(f32[96]{0:T(128)S(1)} %fusion.18), channel_id=1, replica_groups=mesh['grp'=2,'gx'=8,'gy'=2] {'gx'}, use_global_device_ids=true, to_apply=%region_1.0 | all-reduce | flops 96 | bytes 768 | tf_op jit(solution)/shard_map/psum | solution.py:98
  33.5 1.0 fusion.20
  34.5 2.1 all_gather.6
  36.6 1.8 gather_fusion
  38.4 5.4 %fusion.41 = f32[192,4096]{1,0:T(8,128)S(1)} fusion(bf16[192,1024]{1,0:T(8,128)(2,1)} %gather_fusion, bf16[1024,4096]{1,0:T(8,128)(2,1)} %param.15), kind=kOutput, calls=%fused_computation.64 | convolution fusion | flops 1610612736 | bytes 11927552 | tf_op jit(solution)/shard_map/dot_general | solution.py:118
  43.9 0.0 copy-done.1
  43.9 0.0 copy-done.3
  43.9 0.4 fusion.42
  44.3 0.4 fusion.43
  44.6 2.3 %pad_maximum_fusion = f32[192,5120]{1,0:T(8,128)} fusion(f32[192,512]{1,0:T(8,128)S(1)} %fusion.43, f32[192,512]{1,0:T(8,128)S(1)} %fusion.42, f32[192,4096]{1,0:T(8,128)S(1)} %fusion.41), kind=kLoop, calls=%fused_computation.3 | loop fusion | flops 1966080 | bytes 7864320 | tf_op jit(solution)/shard_map/concatenate | solution.py:116
  46.9 0.0 reduce-scatter.3.cloned.1.call-update
  46.9 0.0 all-gather.2.cloned.1.call-start
  47.0 0.6 copy-done.7
  47.6 0.0 copy-done.8
  47.6 0.0 copy-done.6
  47.6 0.0 copy-done.9
  47.6 0.1 fusion.39
  47.7 0.1 iota_compare_fusion
  47.8 0.1 multiply_cosine_fusion
  47.9 80.7 %reduce-scatter.3.cloned.1.call-done = f32[24,5120]{1,0:T(8,128)} async-done(((f32[192,5120]{1,0:T(8,128)}), f32[24,5120]{1,0:T(8,128)}) %reduce-scatter.3.cloned.1.call-update) | async-done | bytes 491536 | tf_op jit(solution)/shard_map/reduce_scatter | solution.py:115
  128.6 1.5 slice_add_fusion.2
  130.1 1.0 fusion.22
  131.1 0.1 copy.20
  131.2 0.1 subtract_convert_fusion.1
  131.3 0.2 subtract_convert_fusion
  131.5 0.1 maximum_bitcast_fusion.3
  131.6 0.3 fusion.29
  131.9 0.0 copy-done
  131.9 1.9 fusion.40
  133.8 0.4 fusion.23
  134.2 0.7 fusion.33
  134.9 1.4 reshape.121
  136.3 3.0 %fusion.15 = bf16[24,4,8,128]{3,2,1,0:T(8,128)(2,1)S(1)} fusion(f32[24,4,8,128]{3,2,1,0:T(8,128)S(1)} %get-tuple-element.18, f32[24,4,128]{2,1,0:T(4,128)} %reshape.121, f32[24,4,8]{2,1,0:T(4,128)} %get-tuple-element.12, f32[24,4,8]{2,1,0:T(4,128)} %get-tuple-element.11, f32[24,4,8]{2,1,0:T(4,128)} %copy-done.5, pred[24,128]{1,0:T(8,128)(4,1)S(1)} %iota_compare_fusion, ...), kind=kOutput, calls=%fused_computation.13 | convolution fusion | flops 25853952 | bytes 3796992 | tf_op jit(solution)/shard_map/rgqp,rpgd->rgqd/dot_general | solution.py:72
  139.3 0.8 copy.43
  140.1 0.0 all-gather.2.cloned.1.call-update
  140.1 0.0 reduce-scatter.5.cloned.1.call-start
  140.1 44.0 %all-gather.2.cloned.1.call-done = bf16[192,4096]{1,0:T(8,128)(2,1)} async-done(((bf16[24,4096]{1,0:T(8,128)(2,1)}), bf16[192,4096]{1,0:T(8,128)(2,1)}) %all-gather.2.cloned.1.call-update) | async-done | bytes 1572880 | tf_op jit(solution)/shard_map/all_gather | solution.py:144
  184.1 6.6 %fusion.44 = f32[192,1024]{1,0:T(8,128)} fusion(bf16[192,4096]{1,0:T(8,128)(2,1)} %all-gather.2.cloned.1.call-done, bf16[4096,1024]{1,0:T(8,128)(2,1)} %param.25), kind=kOutput, calls=%fused_computation.67 | convolution fusion | flops 1610612736 | bytes 10747904 | tf_op jit(solution)/shard_map/dot_general | solution.py:143
  190.7 3.3 %gather_fusion.1 = f32[192,1024]{1,0:T(8,128)} fusion(f32[192,1024]{1,0:T(8,128)} %fusion.44, s32[1024]{0:T(1024)S(1)} %pad_clamp_fusion), kind=kCustom, calls=%fused_computation.1 | custom fusion | bytes 1573632 | tf_op jit(solution)/shard_map/gather | solution.py:148
  194.0 0.0 reduce-scatter.5.cloned.1.call-update
  194.0 7.2 %reduce-scatter.5.cloned.1.call-done = f32[96,1024]{1,0:T(8,128)} async-done(((f32[192,1024]{1,0:T(8,128)}), f32[96,1024]{1,0:T(8,128)}) %reduce-scatter.5.cloned.1.call-update) | async-done | bytes 393232 | tf_op jit(solution)/shard_map/reduce_scatter | solution.py:149
  201.3 1.7 fusion.21
  (23 shorter events, 0.1 us)
Async XLA Ops:
  6.5 125.4 %copy-start = (bf16[24,128,512]{2,1,0:T(8,128)(2,1)S(1)}, bf16[24,128,512]{2,1,0:T(8,128)(2,1)}, u32[]{:S(2)}) copy-start(bf16[24,128,512]{2,1,0:T(8,128)(2,1)} %param.21) | copy-start | bytes 9437188
  6.5 122.1 %reduce-scatter.3.cloned.1.call-start = ((), (), s32[]{:S(2)}) async-start(), calls=%async_computation.2 | async-start | bytes 4423680 | tf_op jit(solution)/shard_map/reduce_scatter | solution.py:115
  38.4 5.5 %copy-start.1 = (bf16[192,1024]{1,0:T(8,128)(2,1)S(1)}, bf16[192,1024]{1,0:T(8,128)(2,1)}, u32[]{:S(2)}) copy-start(bf16[192,1024]{1,0:T(8,128)(2,1)} %gather_fusion) | copy-start | bytes 1179652
  38.4 5.5 %copy-start.3 = (bf16[1024,512]{1,0:T(8,128)(2,1)S(1)}, bf16[1024,512]{1,0:T(8,128)(2,1)}, u32[]{:S(2)}) copy-start(bf16[1024,512]{1,0:T(8,128)(2,1)} %param.16) | copy-start | bytes 3145732
  38.4 5.9 %copy-start.4 = (bf16[1024,512]{1,0:T(8,128)(2,1)S(1)}, bf16[1024,512]{1,0:T(8,128)(2,1)}, u32[]{:S(2)}) copy-start(bf16[1024,512]{1,0:T(8,128)(2,1)} %param.17) | copy-start | bytes 3145732
  46.9 0.7 copy-start.7
  46.9 0.7 copy-start.8
  46.9 0.7 copy-start.6
  46.9 0.7 copy-start.9
  46.9 137.2 %all-gather.2.cloned.1.call-start = ((), (), s32[]{:S(2)}) async-start(), calls=%async_computation.3 | async-start | bytes 1769472 | tf_op jit(solution)/shard_map/all_gather | solution.py:144
  133.8 1.1 copy-start.5
  140.1 61.2 %reduce-scatter.5.cloned.1.call-start = ((), (), s32[]{:S(2)}) async-start(), calls=%async_computation.4 | async-start | bytes 1179648 | tf_op jit(solution)/shard_map/reduce_scatter | solution.py:149
  190.7 10.6 %copy-start.2 = (bf16[96,1024]{1,0:T(8,128)(2,1)S(1)}, bf16[96,1024]{1,0:T(8,128)(2,1)}, u32[]{:S(2)}) copy-start(bf16[96,1024]{1,0:T(8,128)(2,1)} %param.13) | copy-start | bytes 589828
Sparse Core Ops, SparseCore 0:
  47.1 81.5 reduce-scatter.2
  140.2 43.8 all-gather.1
  194.2 7.0 reduce-scatter.4
where the time goes:
time: 210 us; the launch traced here: 209 us
  waiting for transfers between devices  132 us (63%)
  blocking collectives  25.2 us (12%)
  matrix products  17.9 us (9%)
  between operations  13.3 us (6%)
  other arithmetic  11.9 us (6%)
  local copies, waits for them, and re-layouts  9.26 us (4%)
    reduce_scatter x1, waiting for transfers between devices, on_device(): lax.psum_scatter(jnp.concatenate([jnp.dot(slotted, w_query, preferred_ele...  80.7 us
    all_gather x1, waiting for transfers between devices, on_device(): lax.all_gather(attended, 'gx', axis=0, tiled=True)  44 us
    psum x1, blocking collectives, on_device(): square_sum = lax.psum(local_squares, 'gx')  23.1 us
    reduce_scatter x1, waiting for transfers between devices, on_device(): summed = lax.psum_scatter(row_terms, 'gy', scatter_dimension=0, tiled=True)  7.21 us
    dot_general x1, matrix products, on_device(): jnp.dot(lax.all_gather(attended, 'gx', axis=0, tiled=True), w_out, prefer...  6.56 us
    dot_general x1, matrix products, on_device(): jnp.dot(slotted, w_query, preferred_element_type=jnp.float32)  5.44 us
  transfers between devices with their start and end apart: 3, of which 3 were waited for; matrix products, arithmetic and copies ran while one was open for 0% of the time, Pallas kernels for 0%

commit v1 on v0

v1 whole, which is shorter than its diff:
```python
import functools
import math

import jax
import jax.numpy as jnp
from jax import lax
from jax.experimental import pallas as pl
from jax.experimental.pallas import tpu as pltpu
from jax.sharding import PartitionSpec as P

MODEL_WIDTH = 8192
QUERY_HEADS = 64
KEY_VALUE_HEADS = 8
HEAD_SIZE = 128
QUERIES_PER_KV = QUERY_HEADS // KEY_VALUE_HEADS
TILES = QUERIES_PER_KV + 2
SQUARE_ROWS = 32

EPSILON = 1e-06
ROPE_BASE = 1000000.0
CHUNKS = 2
SLOTS_PER_STEP = 8
F32 = jnp.float32
BF16 = jnp.bfloat16


def peer(z, q, nz):
    return z ^ q


def peer_pairs(q, nz):
    pairs = []
    for z in range(nz):
        for y in range(2):
            pairs.append((z * 2 + y, peer(z, q, nz) * 2 + y))
    return pairs


def neighbour_pairs(nz):
    return [(z * 2 + y, z * 2 + 1 - y) for z in range(nz) for y in range(2)]


def slot_one_hot(place_ref, slot_of_row, nz, per):
    rows = slot_of_row.shape[1]
    place_z, place_y = place_ref[0], place_ref[1]
    base = lax.broadcasted_iota(jnp.int32, (per, rows), 0)
    blocks = []
    for h in range(2):
        for q in range(nz):
            owner = peer(place_z, q, nz) * 2 + (place_y ^ h)
            blocks.append(jnp.where(base + owner * per == slot_of_row, 1.0, 0.0).astype(F32))
    return jnp.concatenate(blocks, axis=0).astype(BF16)


def project_kernel(
    place_ref, own_ref, other_ref, gain_ref, sor_ref, wq_ref, wk_ref, wv_ref,
    keep_ref, send_ref, slotted_ref, acc, *, nz, per, first, heads,
):
    step = pl.program_id(0)
    half = nz * per

    if first:

        @pl.when(step == 0)
        def _():
            one_hot = slot_one_hot(place_ref, sor_ref[...], nz, per)
            rows = jnp.concatenate([own_ref[...], other_ref[...]], axis=0)
            hidden = jnp.dot(one_hot, rows, preferred_element_type=F32)
            slotted_ref[...] = (hidden * gain_ref[...].astype(F32)).astype(BF16)
            squares = jnp.sum(hidden * hidden, axis=1, keepdims=True)
            high = squares.astype(BF16).astype(F32)
            low = squares - high
            lane = lax.broadcasted_iota(jnp.int32, (per, HEAD_SIZE), 1)
            lane_high = place_ref[1] * 2
            for h, ref in enumerate((keep_ref, send_ref)):
                for q in range(nz):
                    at = h * half + q * per
                    packed = jnp.where(
                        lane == lane_high,
                        high[at : at + per],
                        jnp.where(lane == lane_high + 1, low[at : at + per], 0.0),
                    )
                    packed = jnp.concatenate(
                        [packed, jnp.zeros((SQUARE_ROWS - per, HEAD_SIZE), F32)], axis=0
                    )
                    ref[q, heads * TILES * per :, :] = packed.astype(BF16)

        source = slotted_ref
    else:
        source = own_ref

    columns = QUERIES_PER_KV * HEAD_SIZE
    acc[:, :columns] = jnp.dot(source[...], wq_ref[...], preferred_element_type=F32)
    acc[:, columns : columns + HEAD_SIZE] = jnp.dot(
        source[...], wk_ref[...], preferred_element_type=F32
    )
    acc[:, columns + HEAD_SIZE :] = jnp.dot(source[...], wv_ref[...], preferred_element_type=F32)
    start = pl.multiple_of(step * TILES * per, 16)
    for h, ref in enumerate((keep_ref, send_ref)):
        for q in range(nz):
            at = h * half + q * per
            block = jnp.concatenate(
                [
                    acc[at : at + per, c * HEAD_SIZE : (c + 1) * HEAD_SIZE]
                    for c in range(TILES)
                ],
                axis=0,
            )
            ref[q, pl.ds(start, TILES * per), :] = block.astype(BF16)


def project(place, own, other, gain, sor, wq, wk, wv, *, chunk, heads, nz, per):
    first = chunk == 0
    rows = 2 * nz * per
    depth = wq.shape[0]
    block_rows = heads * TILES * per + (SQUARE_ROWS if first else 0)
    out_block = jax.ShapeDtypeStruct((nz, block_rows, HEAD_SIZE), BF16)
    whole3 = pl.BlockSpec((nz, block_rows, HEAD_SIZE), lambda i, p: (0, 0, 0))
    column = lambda i, p: (0, chunk * heads + i)

    def whole2(array):
        return pl.BlockSpec(array.shape, lambda i, p: (0, 0))

    kernel = functools.partial(
        project_kernel, nz=nz, per=per, first=first, heads=heads
    )
    outs = pl.pallas_call(
        kernel,
        grid_spec=pltpu.PrefetchScalarGridSpec(
            num_scalar_prefetch=1,
            grid=(heads,),
            in_specs=[
                whole2(own),
                whole2(other),
                whole2(gain),
                whole2(sor),
                pl.BlockSpec((depth, QUERIES_PER_KV * HEAD_SIZE), column),
                pl.BlockSpec((depth, HEAD_SIZE), column),
                pl.BlockSpec((depth, HEAD_SIZE), column),
            ],
            out_specs=[whole3, whole3, pl.BlockSpec((rows, depth), lambda i, p: (0, 0))],
            scratch_shapes=[pltpu.VMEM((rows, TILES * HEAD_SIZE), F32)],
        ),
        out_shape=[out_block, out_block, jax.ShapeDtypeStruct((rows, depth), BF16)],
        compiler_params=pltpu.CompilerParams(vmem_limit_bytes=32 * 1024 * 1024),
        cost_estimate=pl.CostEstimate(
            flops=2 * rows * depth * heads * TILES * HEAD_SIZE,
            bytes_accessed=2 * depth * heads * TILES * HEAD_SIZE,
            transcendentals=0,
        ),
        name="project" + str(chunk),
    )(place, own, other, gain, sor, wq, wk, wv)
    return outs


def attend_kernel(
    *refs, parts, first, heads, per, group,
):
    lengths_ref = refs[0]
    part_refs = refs[1 : 1 + parts]
    if first:
        bias_ref, cos_ref, sin_ref, k_ref, v_ref, out_ref, scale_ref, fresh, result = refs[1 + parts :]
    else:
        (
            scale_in_ref, bias_ref, cos_ref, sin_ref, k_ref, v_ref, out_ref, fresh, result,
        ) = refs[1 + parts :]
    step = pl.program_id(0)
    body = heads * TILES * per
    head_rows = TILES * per

    @pl.when(step == 0)
    def _():
        if first:
            squares = part_refs[0][body : body + per, :].astype(F32) if per % 16 == 0 else (
                part_refs[0][body : body + SQUARE_ROWS, :].astype(F32)[:per]
            )
            for ref in part_refs[1:]:
                squares = squares + ref[body : body + SQUARE_ROWS, :].astype(F32)[:per]
            total = jnp.sum(squares, axis=1, keepdims=True)
            scale = jnp.broadcast_to(
                lax.rsqrt(total / MODEL_WIDTH + EPSILON), (per, HEAD_SIZE)
            )
            scale_ref[...] = scale
        else:
            scale = scale_in_ref[...]
        cos, sin = cos_ref[...], sin_ref[...]
        for g in range(heads):
            rows = pl.ds(g * head_rows, head_rows)
            summed = part_refs[0][rows, :].astype(F32)
            for ref in part_refs[1:]:
                summed = summed + ref[rows, :].astype(F32)
            for c in range(TILES):
                tile = summed[c * per : (c + 1) * per] * scale + bias_ref[
                    g * TILES + c : g * TILES + c + 1, :
                ].astype(F32)
                if c < TILES - 1:
                    tile = tile * cos + pltpu.roll(tile, HEAD_SIZE // 2, 1) * sin
                fresh[pl.ds(g * head_rows + c * per, per), :] = tile.astype(BF16).astype(F32)

    score_scale = 1.0 / math.sqrt(HEAD_SIZE)
    positions = k_ref.shape[1]
    qrows = heads * QUERIES_PER_KV
    scores, owns, masks = [], [], []
    position = lax.broadcasted_iota(jnp.int32, (qrows, positions), 1)
    zero = jnp.zeros((QUERIES_PER_KV, HEAD_SIZE), F32)
    for i in range(group):
        s = step * group + i
        query, own = [], []
        for g in range(heads):
            q = fresh[pl.ds(g * head_rows + s, QUERIES_PER_KV, stride=per), :]
            new_key = fresh[pl.ds(g * head_rows + QUERIES_PER_KV * per + s, 1), :]
            own.append(jnp.sum(q * new_key, axis=1, keepdims=True))
            query.append(jnp.concatenate([q if j == g else zero for j in range(heads)], axis=1))
        query = jnp.concatenate(query, axis=0).astype(BF16)
        score = lax.dot_general(
            query, k_ref[i], (((1,), (1,)), ((), ())), preferred_element_type=F32
        )
        valid = position < lengths_ref[s]
        masks.append(valid)
        scores.append(jnp.where(valid, score * score_scale, -1e30))
        owns.append(jnp.concatenate(own, axis=0) * score_scale)
    scores = jnp.concatenate(scores, axis=0)
    owns = jnp.concatenate(owns, axis=0)
    top = jnp.maximum(jnp.max(scores, axis=1, keepdims=True), owns)
    cache_exp = jnp.exp(scores - top)
    own_exp = jnp.exp(owns - top)
    cache_exp = jnp.concatenate(
        [
            jnp.where(masks[i], cache_exp[i * qrows : (i + 1) * qrows], 0.0)
            for i in range(group)
        ],
        axis=0,
    )
    denominator = jnp.sum(cache_exp, axis=1, keepdims=True) + own_exp
    weight = cache_exp / denominator
    own_weight = (own_exp / denominator).astype(BF16).astype(F32)
    for i in range(group):
        s = step * group + i
        mixed = jnp.dot(
            weight[i * qrows : (i + 1) * qrows].astype(BF16), v_ref[i], preferred_element_type=F32
        )
        for g in range(heads):
            lo, hi = g * QUERIES_PER_KV, (g + 1) * QUERIES_PER_KV
            new_value = fresh[pl.ds(g * head_rows + (QUERIES_PER_KV + 1) * per + s, 1), :]
            result[pl.ds(g * QUERIES_PER_KV * per + s, QUERIES_PER_KV, stride=per), :] = (
                mixed[lo:hi, g * HEAD_SIZE : (g + 1) * HEAD_SIZE]
                + own_weight[i * qrows + lo : i * qrows + hi] * new_value
            )

    @pl.when(step == pl.num_programs(0) - 1)
    def _():
        out_ref[...] = result[...].astype(BF16)


def attend(lengths, parts, scale, bias, cos, sin, keys, values, *, chunk, heads):
    first = chunk == 0
    per, positions = keys.shape[0], keys.shape[1]
    group = SLOTS_PER_STEP if per % SLOTS_PER_STEP == 0 else 1

    def whole2(array):
        return pl.BlockSpec(array.shape, lambda i, p: (0, 0))

    cache_spec = pl.BlockSpec(
        (group, positions, heads * HEAD_SIZE), lambda i, p: (i, 0, chunk)
    )
    ins = list(parts) + ([] if first else [scale]) + [bias, cos, sin]
    out_rows = heads * QUERIES_PER_KV * per
    out_shape = [jax.ShapeDtypeStruct((out_rows, HEAD_SIZE), BF16)]
    out_specs = [pl.BlockSpec((out_rows, HEAD_SIZE), lambda i, p: (0, 0))]
    if first:
        out_shape.append(jax.ShapeDtypeStruct((per, HEAD_SIZE), F32))
        out_specs.append(pl.BlockSpec((per, HEAD_SIZE), lambda i, p: (0, 0)))
    return pl.pallas_call(
        functools.partial(
            attend_kernel, parts=len(parts), first=first, heads=heads, per=per, group=group
        ),
        grid_spec=pltpu.PrefetchScalarGridSpec(
            num_scalar_prefetch=1,
            grid=(per // group,),
            in_specs=[whole2(a) for a in ins] + [cache_spec, cache_spec],
            out_specs=out_specs,
            scratch_shapes=[
                pltpu.VMEM((heads * TILES * per, HEAD_SIZE), F32),
                pltpu.VMEM((out_rows, HEAD_SIZE), F32),
            ],
        ),
        out_shape=out_shape,
        compiler_params=pltpu.CompilerParams(vmem_limit_bytes=32 * 1024 * 1024),
        cost_estimate=pl.CostEstimate(
            flops=4 * per * heads * QUERIES_PER_KV * positions * HEAD_SIZE,
            bytes_accessed=4 * per * positions * heads * HEAD_SIZE,
            transcendentals=per * heads * QUERIES_PER_KV * positions,
        ),
        name="attend" + str(chunk),
    )(lengths, *ins, keys, values)


def output_kernel(*refs, blocks, nz, per, first, last, steps):
    place_ref = refs[0]
    block_refs = refs[1 : 1 + blocks]
    rest = refs[1 + blocks :]
    sor_ref, w_ref = rest[0], rest[1]
    rest = rest[2:]
    if not first:
        acc_in_ref, rest = rest[0], rest[1:]
    if last:
        mine_ref, send_ref, permuted, total = rest
    else:
        acc_out_ref, permuted, total = rest
    step = pl.program_id(0)
    tiles = block_refs[0].shape[0] // per

    @pl.when(step == 0)
    def _():
        one_hot = slot_one_hot(place_ref, sor_ref[...], nz, per)
        wide = [ref[...].astype(F32) for ref in block_refs]
        for c in range(tiles):
            stacked = jnp.concatenate(
                [block[c * per : (c + 1) * per] for block in wide], axis=0
            ).astype(BF16)
            permuted[c // (tiles // steps), :, (c % (tiles // steps)) * HEAD_SIZE : (c % (tiles // steps) + 1) * HEAD_SIZE] = lax.dot_general(
                one_hot, stacked, (((0,), (0,)), ((), ())), preferred_element_type=F32
            ).astype(BF16)
        if first:
            total[...] = jnp.zeros_like(total)
        else:
            total[...] = acc_in_ref[...]

    total[...] += jnp.dot(permuted[step], w_ref[...], preferred_element_type=F32)

    @pl.when(step == steps - 1)
    def _():
        if last:
            half = total.shape[0] // 2
            mine_ref[...] = total[:half]
            send_ref[...] = total[half:].astype(BF16)
        else:
            acc_out_ref[...] = total[...]


def output(place, blocks, sor, w_out, acc, *, chunk, heads, chunks, nz, per):
    first, last = chunk == 0, chunk == chunks - 1
    rows = 2 * nz * per
    width = w_out.shape[1]
    depth = heads * QUERIES_PER_KV * HEAD_SIZE
    steps = 4
    step_depth = depth // steps

    def whole2(array):
        return pl.BlockSpec(array.shape, lambda i, p: (0, 0))

    half = jax.ShapeDtypeStruct((rows // 2, width), F32)
    half_sent = jax.ShapeDtypeStruct((rows // 2, width), BF16)
    full = jax.ShapeDtypeStruct((rows, width), F32)
    out_shape = [half, half_sent] if last else [full]
    ins = list(blocks) + [sor]
    in_specs = [whole2(a) for a in ins] + [
        pl.BlockSpec((step_depth, width), lambda i, p: (chunk * steps + i, 0))
    ]
    args = ins + [w_out]
    if not first:
        args.append(acc)
        in_specs.append(whole2(acc))
    return pl.pallas_call(
        functools.partial(
            output_kernel, blocks=len(blocks), nz=nz, per=per, first=first, last=last, steps=steps
        ),
        grid_spec=pltpu.PrefetchScalarGridSpec(
            num_scalar_prefetch=1,
            grid=(steps,),
            in_specs=in_specs,
            out_specs=[whole2(o) for o in out_shape],
            scratch_shapes=[
                pltpu.VMEM((steps, rows, step_depth), BF16),
                pltpu.VMEM((rows, width), F32),
            ],
        ),
        out_shape=out_shape,
        compiler_params=pltpu.CompilerParams(vmem_limit_bytes=40 * 1024 * 1024),
        cost_estimate=pl.CostEstimate(
            flops=2 * rows * depth * width, bytes_accessed=2 * depth * width, transcendentals=0
        ),
        name="output" + str(chunk),
    )(place, *args)


def on_device(
    hidden_rows,
    norm_gain,
    w_query,
    key_weight,
    value_weight,
    query_bias,
    key_bias_vector,
    value_bias_vector,
    rotated_key_cache,
    stored_value_cache,
    slot_valid_lengths,
    slot_of_row,
    w_out,
    *,
    size,
):
    nz = size // 2
    assert size % 2 == 0 and nz & (nz - 1) == 0
    per = rotated_key_cache.shape[0]
    kv_heads = key_weight.shape[1] // HEAD_SIZE
    heads = kv_heads // CHUNKS
    gx = lax.axis_index("gx")
    gy = lax.axis_index("gy")
    place = jnp.stack([gx // 2, gx % 2]).astype(jnp.int32)
    half = hidden_rows.shape[0]

    other = lax.ppermute(hidden_rows, "gy", [(0, 1), (1, 0)])
    sor = jnp.where(gy == 0, slot_of_row, jnp.roll(slot_of_row, half))[None, :]
    gain = norm_gain[None, :]

    lengths = lax.dynamic_slice_in_dim(slot_valid_lengths, gx * per, per, 0)
    half_width = HEAD_SIZE // 2
    frequency = ROPE_BASE ** (-(jnp.arange(half_width).astype(F32) * 2.0 / HEAD_SIZE))
    angles = lengths.astype(F32)[:, None] * frequency[None, :]
    cosine, sine = jnp.cos(angles), jnp.sin(angles)
    cos = jnp.concatenate([cosine, cosine], axis=1)
    sin = jnp.concatenate([-sine, sine], axis=1)
    bias = jnp.concatenate(
        [
            query_bias.reshape(kv_heads, QUERIES_PER_KV, HEAD_SIZE),
            key_bias_vector.reshape(kv_heads, 1, HEAD_SIZE),
            value_bias_vector.reshape(kv_heads, 1, HEAD_SIZE),
        ],
        axis=1,
    ).astype(F32).reshape(CHUNKS, heads * TILES, HEAD_SIZE)

    swapped, kept = [], []
    source, partner = hidden_rows, other
    for c in range(CHUNKS):
        keep, send, slotted = project(
            place, source, partner, gain, sor, w_query, key_weight, value_weight,
            chunk=c, heads=heads, nz=nz, per=per,
        )
        source = partner = slotted if c == 0 else source
        kept.append(keep)
        swapped.append(lax.ppermute(send, "gx", neighbour_pairs(nz)))
    parts = []
    for c in range(CHUNKS):
        blocks = []
        for q in range(nz):
            total = (kept[c][q].astype(F32) + swapped[c][q].astype(F32)).astype(BF16)
            blocks.append(total if q == 0 else lax.ppermute(total, "gx", peer_pairs(q, nz)))
        parts.append(blocks)

    scale = None
    gathered = []
    for c in range(CHUNKS):
        outs = attend(
            lengths, parts[c], scale, bias[c], cos, sin, rotated_key_cache, stored_value_cache,
            chunk=c, heads=heads,
        )
        if c == 0:
            attended, scale = outs
        else:
            (attended,) = outs
        blocks = [attended] + [
            lax.ppermute(attended, "gx", peer_pairs(q, nz)) for q in range(1, nz)
        ]
        blocks += [lax.ppermute(b, "gx", neighbour_pairs(nz)) for b in blocks]
        gathered.append(blocks)

    acc = None
    for c in range(CHUNKS):
        outs = output(
            place, gathered[c], sor, w_out, acc,
            chunk=c, heads=heads, chunks=CHUNKS, nz=nz, per=per,
        )
        if c < CHUNKS - 1:
            (acc,) = outs
    mine, send = outs
    received = lax.ppermute(send, "gy", [(0, 1), (1, 0)])
    return (hidden_rows.astype(F32) + mine + received.astype(F32)).astype(BF16)


def solution(mesh):
    in_specs = (
        P(("grp", "gy"), "gx"),
        P("gx"),
        P("gx", "gy"),
        P("gx", "gy"),
        P("gx", "gy"),
        P("gy"),
        P("gy"),
        P("gy"),
        P(("grp", "gx"), None, "gy"),
        P(("grp", "gx"), None, "gy"),
        P("grp"),
        P("grp"),
        P("gy", "gx"),
    )
    out_specs = P(("grp", "gy"), "gx")
    return jax.shard_map(
        functools.partial(on_device, size=mesh.shape["gx"]),
        mesh=mesh,
        in_specs=in_specs,
        out_specs=out_specs,
        check_vma=False,
    )
```

time: 210 us -> 110 us (0.52)
  waiting for transfers between devices: 132 us -> 23.6 us
  starting transfers between devices: 0.09 us -> 33.2 us
  blocking collectives: 25.2 us -> 0 us
  Pallas kernels: 0 us -> 20.8 us
  matrix products: 17.9 us -> 0 us
  local copies, waits for them, and re-layouts: 9.26 us -> 26.2 us
  between operations: 13.3 us -> 0.23 us
  other arithmetic: 11.9 us -> 5.51 us
    reduce_scatter x2 -> x0, waiting for transfers between devices: 87.9 us -> none  [the longest x1 80.7 us: on_device(): lax.psum_scatter(jnp.concatenate([jnp.dot(slotted, w_query, preferred_ele...]
    all_gather x1 -> x0, waiting for transfers between devices: 44 us -> none  [on_device(): lax.all_gather(attended, 'gx', axis=0, tiled=True)]
    ppermute x0 -> x24, starting transfers between devices: none -> 33.2 us  [the longest x6 13.1 us: on_device(): lax.ppermute(total, 'gx', peer_pairs(q, nz))]
    ppermute x0 -> x24, waiting for transfers between devices: none -> 23.6 us  [the longest x2 16 us: on_device(): swapped.append(lax.ppermute(send, 'gx', neighbour_pairs(nz)))]
    psum x1 -> x0, blocking collectives: 23.1 us -> none  [on_device(): square_sum = lax.psum(local_squares, 'gx')]
    unnamed x22 -> x52, local copies, waits for them, and re-layouts: 1.5 us -> 22.8 us
    pallas_call x0 -> x6, Pallas kernels: none -> 20.8 us  [the longest x2 8.54 us: attend(): pl.pallas_call(functools.partial(attend_kernel, parts=len(parts), first=f...]
    dot_general x7 -> x0, matrix products: 17.9 us -> none  [the longest x1 6.56 us: on_device(): jnp.dot(lax.all_gather(attended, 'gx', axis=0, tiled=True), w_out, prefer...]
  transfers between devices with their start and end apart: 3 -> 24, of which waited for: 3 -> 7; matrix products, arithmetic and copies ran while one was open for 0% -> 7% of each run, Pallas kernels for 0% -> 11%
where the time goes in v1:
time: 110 us
  starting transfers between devices  33.2 us (30%)
  local copies, waits for them, and re-layouts  26.2 us (24%)
  waiting for transfers between devices  23.6 us (21%)
  Pallas kernels  20.8 us (19%)
  other arithmetic  5.51 us (5%)
    unnamed x52, local copies, waits for them, and re-layouts  22.8 us
    ppermute x2, waiting for transfers between devices, on_device(): swapped.append(lax.ppermute(send, 'gx', neighbour_pairs(nz)))  16 us
    ppermute x6, starting transfers between devices, on_device(): lax.ppermute(total, 'gx', peer_pairs(q, nz))  13.1 us
    ppermute x6, starting transfers between devices, on_device(): lax.ppermute(attended, 'gx', peer_pairs(q, nz))  8.84 us
    pallas_call x2, Pallas kernels, attend(): pl.pallas_call(functools.partial(attend_kernel, parts=len(parts), first=f...  8.54 us
    ppermute x8, starting transfers between devices, on_device(): blocks += [lax.ppermute(b, 'gx', neighbour_pairs(nz)) for b in blocks]  8.07 us
    pallas_call x2, Pallas kernels, output(): pl.pallas_call(functools.partial(output_kernel, blocks=len(blocks), nz=nz...  6.62 us
    pallas_call x2, Pallas kernels, project(): pl.pallas_call(kernel, grid_spec=pltpu.PrefetchScalarGridSpec(num_scalar_...  5.66 us
  transfers between devices with their start and end apart: 24, of which 7 were waited for; matrix products, arithmetic and copies ran while one was open for 7% of the time, Pallas kernels for 11%

profile of v1, /device:TPU:0, one launch (start us, length us, event | category | flops | bytes accessed | tf_op | source)
XLA Modules:
  0.0 109.7 jit_solution(8194367585822487870)
XLA Ops:
  0.5 0.8 fusion.11
  1.3 0.7 broadcast_in_dim.8.gain_ref
  2.0 0.8 add_select_fusion
  2.8 3.4 %copy-done = bf16[1024,4096]{1,0:T(8,128)(2,1)S(1)} copy-done((bf16[1024,4096]{1,0:T(8,128)(2,1)S(1)}, bf16[1024,4096]{1,0:T(8,128)(2,1)}, u32[]{:S(2)}) %copy-start) | copy-done | bytes 8388632
  6.2 1.2 %copy-done.7 = bf16[1024,512]{1,0:T(8,128)(2,1)S(1)} copy-done((bf16[1024,512]{1,0:T(8,128)(2,1)S(1)}, bf16[1024,512]{1,0:T(8,128)(2,1)}, u32[]{:S(2)}) %copy-start.7) | copy-done | bytes 1048600
  7.4 1.2 %copy-done.9 = bf16[1024,512]{1,0:T(8,128)(2,1)S(1)} copy-done((bf16[1024,512]{1,0:T(8,128)(2,1)S(1)}, bf16[1024,512]{1,0:T(8,128)(2,1)}, u32[]{:S(2)}) %copy-start.9) | copy-done | bytes 1048600
  8.6 0.9 copy-done.11
  9.6 3.0 %project0.1 = (bf16[4,512,128]{2,1,0:T(8,128)(2,1)S(1)}, bf16[4,512,128]{2,1,0:T(8,128)(2,1)S(1)}, bf16[192,1024]{1,0:T(8,128)(2,1)S(1)}) custom-call(s32[2]{0:T(128)S(1)} %pad_add_fusion.place_ref.refs_0_, bf16[96,1024]{1,0:T(8,128)(2,1)S(1)} %copy-done.11, bf16[96,1024]{1,0:T(8,128)(2,1)S(1)} %collective-permute-done.other_ref, ...), custom_call_target="tpu_custom_call" | custom-call | flops 1006632960 | bytes 5242880 | tf_op jit(solution)/shard_map/project0/pallas_call | solution.py:127
  13.5 2.7 %project1.1 = (bf16[4,480,128]{2,1,0:T(8,128)(2,1)S(1)}, bf16[4,480,128]{2,1,0:T(8,128)(2,1)S(1)}, bf16[192,1024]{1,0:T(8,128)(2,1)}) custom-call(s32[2]{0:T(128)S(1)} %pad_add_fusion.place_ref.refs_0_, bf16[192,1024]{1,0:T(8,128)(2,1)S(1)} %get-tuple-element.14.own_ref.other_ref, bf16[192,1024]{1,0:T(8,128)(2,1)S(1)} %get-tuple-element.14.own_ref.other_ref, ...), custom_call_target="tpu_custom_call" | custom-call | flops 1006632960 | bytes 5242880 | tf_op jit(solution)/shard_map/project1/pallas_call | solution.py:127
  16.2 2.6 %collective-permute-start.1 = (bf16[4,480,128]{2,1,0:T(8,128)(2,1)S(1)}, bf16[4,480,128]{2,1,0:T(8,128)(2,1)S(1)}, u32[]{:S(2)}, u32[]{:S(2)}) collective-permute-start(bf16[4,480,128]{2,1,0:T(8,128)(2,1)S(1)} %get-tuple-element.16), channel_id=1, source_target_pairs={{0,2},{2,0},{4,6},{6,4},{8,10},{10,8},{12,14},{14,12},{1,3},{3,1},... | collective-permute-start | bytes 1474568 | tf_op jit(solution)/shard_map/ppermute | solution.py:443
  18.7 0.7 fusion.9
  19.6 0.6 fusion.10
  20.2 10.6 %collective-permute-done.1 = bf16[4,480,128]{2,1,0:T(8,128)(2,1)S(1)} collective-permute-done((bf16[4,480,128]{2,1,0:T(8,128)(2,1)S(1)}, bf16[4,480,128]{2,1,0:T(8,128)(2,1)S(1)}, u32[]{:S(2)}, u32[]{:S(2)}) %collective-permute-start.1) | collective-permute-done | bytes 491552 | tf_op jit(solution)/shard_map/ppermute | solution.py:443
  30.8 0.8 fusion.7
  31.6 4.1 %collective-permute-start.4 = (bf16[480,128]{1,0:T(8,128)(2,1)}, bf16[480,128]{1,0:T(8,128)(2,1)}, u32[]{:S(2)}, u32[]{:S(2)}) collective-permute-start(bf16[480,128]{1,0:T(8,128)(2,1)} %get-tuple-element.29), channel_id=1, source_target_pairs={{0,12},{2,14},{4,8},{6,10},{8,4},{10,6},{12,0},{14,2},{1,13},{3,15... | collective-permute-start | bytes 368648 | tf_op jit(solution)/shard_map/ppermute | solution.py:449
  35.8 5.4 %collective-permute-done.5 = bf16[4,512,128]{2,1,0:T(8,128)(2,1)S(1)} collective-permute-done((bf16[4,512,128]{2,1,0:T(8,128)(2,1)S(1)}, bf16[4,512,128]{2,1,0:T(8,128)(2,1)S(1)}, u32[]{:S(2)}, u32[]{:S(2)}) %collective-permute-start.5) | collective-permute-done | bytes 524320 | tf_op jit(solution)/shard_map/ppermute | solution.py:443
  41.2 0.8 fusion.3
  42.0 3.8 %collective-permute-start.8 = (bf16[512,128]{1,0:T(8,128)(2,1)}, bf16[512,128]{1,0:T(8,128)(2,1)S(1)}, u32[]{:S(2)}, u32[]{:S(2)}) collective-permute-start(bf16[512,128]{1,0:T(8,128)(2,1)} %get-tuple-element.25), channel_id=1, source_target_pairs={{0,12},{2,14},{4,8},{6,10},{8,4},{10,6},{12,0},{14,2},{1,13},{3,15... | collective-permute-start | bytes 393224 | tf_op jit(solution)/shard_map/ppermute | solution.py:449
  46.4 0.7 fusion.8
  47.8 2.7 %collective-permute-done.8.refs_4_ = bf16[512,128]{1,0:T(8,128)(2,1)S(1)} collective-permute-done((bf16[512,128]{1,0:T(8,128)(2,1)}, bf16[512,128]{1,0:T(8,128)(2,1)S(1)}, u32[]{:S(2)}, u32[]{:S(2)}) %collective-permute-start.8) | collective-permute-done | bytes 131104 | tf_op jit(solution)/shard_map/ppermute | solution.py:449
  50.5 4.6 %collective-permute-start.2 = (bf16[480,128]{1,0:T(8,128)(2,1)}, bf16[480,128]{1,0:T(8,128)(2,1)}, u32[]{:S(2)}, u32[]{:S(2)}) collective-permute-start(bf16[480,128]{1,0:T(8,128)(2,1)} %get-tuple-element.31), channel_id=1, source_target_pairs={{0,4},{2,6},{4,0},{6,2},{8,12},{10,14},{12,8},{14,10},{1,5},{3,7},... | collective-permute-start | bytes 368648 | tf_op jit(solution)/shard_map/ppermute | solution.py:449
  55.1 0.9 pad_maximum_fusion
  55.9 0.6 collective-permute-done.7.refs_3_
  56.6 1.9 %copy-done.5 = bf16[24,128,512]{2,1,0:T(8,128)(2,1)S(1)} copy-done((bf16[24,128,512]{2,1,0:T(8,128)(2,1)S(1)}, bf16[24,128,512]{2,1,0:T(8,128)(2,1)}, u32[]{:S(2)}) %copy-start.5) | copy-done | bytes 3145752
  58.4 0.7 copy-done.13
  59.2 0.7 copy-done.20
  59.8 4.6 %attend0.1 = (bf16[384,128]{1,0:T(8,128)(2,1)}, f32[24,128]{1,0:T(8,128)S(1)}) custom-call(s32[24]{0:T(128)S(1)} %copy-done.20, bf16[512,128]{1,0:T(8,128)(2,1)S(1)} %get-tuple-element.28.refs_1_, bf16[512,128]{1,0:T(8,128)(2,1)} %collective-permute-done.6.refs_2_, bf16[512,128]{1,0:T(8,128)(2,1)} %collective-permute-done.7.refs_3_, ...), custom_call_target="tpu_custom_call" | custom-call | flops 25165824 | bytes 3145728 | tf_op jit(solution)/shard_map/attend0/pallas_call | solution.py:273
  65.0 1.5 %collective-permute-start.19 = (bf16[384,128]{1,0:T(8,128)(2,1)}, bf16[384,128]{1,0:T(8,128)(2,1)S(1)}, u32[]{:S(2)}, u32[]{:S(2)}) collective-permute-start(bf16[384,128]{1,0:T(8,128)(2,1)} %get-tuple-element.20.refs_1_), channel_id=1, source_target_pairs={{0,2},{2,0},{4,6},{6,4},{8,10},{10,8},{12,14},{14,12},{1,3},{3,1},... | collective-permute-start | bytes 294920 | tf_op jit(solution)/shard_map/ppermute | solution.py:466
  66.5 2.4 %collective-permute-start.18 = (bf16[384,128]{1,0:T(8,128)(2,1)}, bf16[384,128]{1,0:T(8,128)(2,1)S(1)}, u32[]{:S(2)}, u32[]{:S(2)}) collective-permute-start(bf16[384,128]{1,0:T(8,128)(2,1)} %get-tuple-element.20.refs_1_), channel_id=1, source_target_pairs={{0,12},{2,14},{4,8},{6,10},{8,4},{10,6},{12,0},{14,2},{1,13},{3,15... | collective-permute-start | bytes 294920 | tf_op jit(solution)/shard_map/ppermute | solution.py:464
  68.9 2.0 %collective-permute-start.16 = (bf16[384,128]{1,0:T(8,128)(2,1)}, bf16[384,128]{1,0:T(8,128)(2,1)}, u32[]{:S(2)}, u32[]{:S(2)}) collective-permute-start(bf16[384,128]{1,0:T(8,128)(2,1)} %get-tuple-element.20.refs_1_), channel_id=1, source_target_pairs={{0,4},{2,6},{4,0},{6,2},{8,12},{10,14},{12,8},{14,10},{1,5},{3,7},... | collective-permute-start | bytes 294920 | tf_op jit(solution)/shard_map/ppermute | solution.py:464
  70.9 0.7 squeeze.5.refs_6_
  71.7 1.9 %copy-done.6 = bf16[24,128,512]{2,1,0:T(8,128)(2,1)S(1)} copy-done((bf16[24,128,512]{2,1,0:T(8,128)(2,1)S(1)}, bf16[24,128,512]{2,1,0:T(8,128)(2,1)}, u32[]{:S(2)}) %copy-start.6) | copy-done | bytes 3145752
  73.5 0.7 copy-done.17
  74.3 0.7 copy-done.21
  74.9 4.0 %attend1.1.refs_1_ = bf16[384,128]{1,0:T(8,128)(2,1)S(1)} custom-call(s32[24]{0:T(128)S(1)} %copy-done.21, bf16[480,128]{1,0:T(8,128)(2,1)S(1)} %get-tuple-element.32.refs_1_, bf16[480,128]{1,0:T(8,128)(2,1)} %collective-permute-done.2.refs_2_, bf16[480,128]{1,0:T(8,128)(2,1)} %collective-permute-done.3.refs_3_, ...), custom_call_target="tpu_custom_call" | custom-call | flops 25165824 | bytes 3145728 | tf_op jit(solution)/shard_map/attend1/pallas_call | solution.py:273
  78.9 2.4 %collective-permute-start.11 = (bf16[384,128]{1,0:T(8,128)(2,1)S(1)}, bf16[384,128]{1,0:T(8,128)(2,1)S(1)}, u32[]{:S(2)}, u32[]{:S(2)}) collective-permute-start(bf16[384,128]{1,0:T(8,128)(2,1)S(1)} %attend1.1.refs_1_), channel_id=1, source_target_pairs={{0,12},{2,14},{4,8},{6,10},{8,4},{10,6},{12,0},{14,2},{1,13},{3,15... | collective-permute-start | bytes 294920 | tf_op jit(solution)/shard_map/ppermute | solution.py:464
  81.3 2.0 %collective-permute-start.9 = (bf16[384,128]{1,0:T(8,128)(2,1)S(1)}, bf16[384,128]{1,0:T(8,128)(2,1)S(1)}, u32[]{:S(2)}, u32[]{:S(2)}) collective-permute-start(bf16[384,128]{1,0:T(8,128)(2,1)S(1)} %attend1.1.refs_1_), channel_id=1, source_target_pairs={{0,4},{2,6},{4,0},{6,2},{8,12},{10,14},{12,8},{14,10},{1,5},{3,7},... | collective-permute-start | bytes 294920 | tf_op jit(solution)/shard_map/ppermute | solution.py:464
  83.9 1.5 %collective-permute-start.21 = (bf16[384,128]{1,0:T(8,128)(2,1)}, bf16[384,128]{1,0:T(8,128)(2,1)S(1)}, u32[]{:S(2)}, u32[]{:S(2)}) collective-permute-start(bf16[384,128]{1,0:T(8,128)(2,1)} %collective-permute-done.17.refs_3_), channel_id=1, source_target_pairs={{0,2},{2,0},{4,6},{6,4},{8,10},{10,8},{12,14},{14,12},{1,3},{3,1},... | collective-permute-start | bytes 294920 | tf_op jit(solution)/shard_map/ppermute | solution.py:466
  86.2 2.4 %collective-permute-done.10.refs_3_ = bf16[384,128]{1,0:T(8,128)(2,1)S(1)} collective-permute-done((bf16[384,128]{1,0:T(8,128)(2,1)S(1)}, bf16[384,128]{1,0:T(8,128)(2,1)S(1)}, u32[]{:S(2)}, u32[]{:S(2)}) %collective-permute-start.10) | collective-permute-done | bytes 98336 | tf_op jit(solution)/shard_map/ppermute | solution.py:464
  89.1 1.5 %collective-permute-start.15 = (bf16[384,128]{1,0:T(8,128)(2,1)S(1)}, bf16[384,128]{1,0:T(8,128)(2,1)S(1)}, u32[]{:S(2)}, u32[]{:S(2)}) collective-permute-start(bf16[384,128]{1,0:T(8,128)(2,1)S(1)} %collective-permute-done.11.refs_4_), channel_id=1, source_target_pairs={{0,2},{2,0},{4,6},{6,4},{8,10},{10,8},{12,14},{14,12},{1,3},{3,1},... | collective-permute-start | bytes 294920 | tf_op jit(solution)/shard_map/ppermute | solution.py:466
  91.2 1.5 %collective-permute-start.13 = (bf16[384,128]{1,0:T(8,128)(2,1)S(1)}, bf16[384,128]{1,0:T(8,128)(2,1)S(1)}, u32[]{:S(2)}, u32[]{:S(2)}) collective-permute-start(bf16[384,128]{1,0:T(8,128)(2,1)S(1)} %collective-permute-done.9.refs_2_), channel_id=1, source_target_pairs={{0,2},{2,0},{4,6},{6,4},{8,10},{10,8},{12,14},{14,12},{1,3},{3,1},... | collective-permute-start | bytes 294920 | tf_op jit(solution)/shard_map/ppermute | solution.py:466
  92.7 3.4 %copy-done.2 = bf16[4096,1024]{1,0:T(8,128)(2,1)S(1)} copy-done((bf16[4096,1024]{1,0:T(8,128)(2,1)S(1)}, bf16[4096,1024]{1,0:T(8,128)(2,1)}, u32[]{:S(2)}) %copy-start.2) | copy-done | bytes 8388632
  96.1 0.7 copy-done.15
  97.3 3.8 %output0.1.refs_11_ = f32[192,1024]{1,0:T(8,128)S(1)} custom-call(s32[2]{0:T(128)S(1)} %copy-done.19, bf16[384,128]{1,0:T(8,128)(2,1)} %get-tuple-element.20.refs_1_, bf16[384,128]{1,0:T(8,128)(2,1)} %collective-permute-done.16.refs_2_, bf16[384,128]{1,0:T(8,128)(2,1)} %collective-permute-done.17.refs_3_, ...), custom_call_target="tpu_custom_call" | custom-call | flops 805306368 | bytes 4194304 | tf_op jit(solution)/shard_map/output0/pallas_call | solution.py:364
  101.2 3.4 %copy-done.3 = bf16[4096,1024]{1,0:T(8,128)(2,1)S(1)} copy-done((bf16[4096,1024]{1,0:T(8,128)(2,1)S(1)}, bf16[4096,1024]{1,0:T(8,128)(2,1)}, u32[]{:S(2)}) %copy-start.3) | copy-done | bytes 8388632
  104.6 2.8 %output1.1 = (f32[96,1024]{1,0:T(8,128)S(1)}, bf16[96,1024]{1,0:T(8,128)(2,1)S(1)}) custom-call(s32[2]{0:T(128)S(1)} %copy-done.19, bf16[384,128]{1,0:T(8,128)(2,1)S(1)} %attend1.1.refs_1_, bf16[384,128]{1,0:T(8,128)(2,1)S(1)} %collective-permute-done.9.refs_2_, bf16[384,128]{1,0:T(8,128)(2,1)S(1)} %collective-permute-done.10.refs_3_, ...), custom_call_target="tpu_custom_call" | custom-call | flops 805306368 | bytes 4194304 | tf_op jit(solution)/shard_map/output1/pallas_call | solution.py:364
  107.5 1.4 %collective-permute-done.23 = bf16[96,1024]{1,0:T(8,128)(2,1)S(1)} collective-permute-done((bf16[96,1024]{1,0:T(8,128)(2,1)S(1)}, bf16[96,1024]{1,0:T(8,128)(2,1)S(1)}, u32[]{:S(2)}, u32[]{:S(2)}) %collective-permute-start.23) | collective-permute-done | bytes 196640 | tf_op jit(solution)/shard_map/ppermute | solution.py:478
  108.9 0.7 add_convert_fusion
  (75 shorter events, 6.4 us)
Async XLA Ops:
  0.0 2.8 %collective-permute-start = (bf16[96,1024]{1,0:T(8,128)(2,1)}, bf16[96,1024]{1,0:T(8,128)(2,1)S(1)}, u32[]{:S(2)}, u32[]{:S(2)}) collective-permute-start(bf16[96,1024]{1,0:T(8,128)(2,1)} %own_ref.1), channel_id=1, source_target_pairs={{0,1},{1,0},{2,3},{3,2},{4,5},{5,4},{6,7},{7,6},{8,9},{9,8},{10,11... | collective-permute-start | bytes 589832 | tf_op jit(solution)/shard_map/ppermute | solution.py:414
  2.0 14.1 %copy-start.18 = (s32[2]{0:T(128)}, s32[2]{0:T(128)S(1)}, u32[]{:S(2)}) copy-start(s32[2]{0:T(128)S(1)} %pad_add_fusion.place_ref.refs_0_) | copy-start | bytes 28
  2.8 13.4 %copy-start.14 = (s32[192]{0:T(256)}, s32[192]{0:T(256)S(1)}, u32[]{:S(2)}) copy-start(s32[192]{0:T(256)S(1)} %add_select_fusion) | copy-start | bytes 2308
  2.8 3.4 %copy-start = (bf16[1024,4096]{1,0:T(8,128)(2,1)S(1)}, bf16[1024,4096]{1,0:T(8,128)(2,1)}, u32[]{:S(2)}) copy-start(bf16[1024,4096]{1,0:T(8,128)(2,1)} %wq_ref.3) | copy-start | bytes 25165828
  6.2 1.2 %copy-start.7 = (bf16[1024,512]{1,0:T(8,128)(2,1)S(1)}, bf16[1024,512]{1,0:T(8,128)(2,1)}, u32[]{:S(2)}) copy-start(bf16[1024,512]{1,0:T(8,128)(2,1)} %wk_ref.3) | copy-start | bytes 3145732
  7.4 1.2 %copy-start.9 = (bf16[1024,512]{1,0:T(8,128)(2,1)S(1)}, bf16[1024,512]{1,0:T(8,128)(2,1)}, u32[]{:S(2)}) copy-start(bf16[1024,512]{1,0:T(8,128)(2,1)} %wv_ref.3) | copy-start | bytes 3145732
  8.6 0.9 copy-start.11
  9.6 3.4 %copy-start.1 = (bf16[1024,4096]{1,0:T(8,128)(2,1)S(1)}, bf16[1024,4096]{1,0:T(8,128)(2,1)}, u32[]{:S(2)}) copy-start(bf16[1024,4096]{1,0:T(8,128)(2,1)} %wq_ref.3) | copy-start | bytes 25165828
  9.6 3.6 %copy-start.8 = (bf16[1024,512]{1,0:T(8,128)(2,1)S(1)}, bf16[1024,512]{1,0:T(8,128)(2,1)}, u32[]{:S(2)}) copy-start(bf16[1024,512]{1,0:T(8,128)(2,1)} %wk_ref.3) | copy-start | bytes 3145732
  9.6 3.9 %copy-start.10 = (bf16[1024,512]{1,0:T(8,128)(2,1)S(1)}, bf16[1024,512]{1,0:T(8,128)(2,1)}, u32[]{:S(2)}) copy-start(bf16[1024,512]{1,0:T(8,128)(2,1)} %wv_ref.3) | copy-start | bytes 3145732
  9.6 9.2 %copy-start.25 = (s32[192]{0:T(256)S(1)}, s32[192]{0:T(256)}, u32[]{:S(2)}) copy-start(s32[192]{0:T(256)} %param.23) | copy-start | bytes 2308
  9.6 9.8 %copy-start.23 = (bf16[512]{0:T(512)(128)(2,1)S(1)}, bf16[512]{0:T(512)(128)(2,1)}, u32[]{:S(2)}) copy-start(bf16[512]{0:T(512)(128)(2,1)} %param.19) | copy-start | bytes 3076
  9.6 9.8 %copy-start.24 = (bf16[512]{0:T(512)(128)(2,1)S(1)}, bf16[512]{0:T(512)(128)(2,1)}, u32[]{:S(2)}) copy-start(bf16[512]{0:T(512)(128)(2,1)} %param.20) | copy-start | bytes 3076
  9.6 9.8 %copy-start.22 = (bf16[4096]{0:T(1024)(128)(2,1)S(1)}, bf16[4096]{0:T(1024)(128)(2,1)}, u32[]{:S(2)}) copy-start(bf16[4096]{0:T(1024)(128)(2,1)} %param.18) | copy-start | bytes 24580
  12.6 43.9 %copy-start.4 = (bf16[24,128,512]{2,1,0:T(8,128)(2,1)S(1)}, bf16[24,128,512]{2,1,0:T(8,128)(2,1)}, u32[]{:S(2)}) copy-start(bf16[24,128,512]{2,1,0:T(8,128)(2,1)} %refs_9_.3) | copy-start | bytes 9437188
  16.2 14.6 %collective-permute-start.1 = (bf16[4,480,128]{2,1,0:T(8,128)(2,1)S(1)}, bf16[4,480,128]{2,1,0:T(8,128)(2,1)S(1)}, u32[]{:S(2)}, u32[]{:S(2)}) collective-permute-start(bf16[4,480,128]{2,1,0:T(8,128)(2,1)S(1)} %get-tuple-element.16), channel_id=1, source_target_pairs={{0,2},{2,0},{4,6},{6,4},{8,10},{10,8},{12,14},{14,12},{1,3},{3,1},... | collective-permute-start | bytes 1474568 | tf_op jit(solution)/shard_map/ppermute | solution.py:443
  19.5 21.7 %collective-permute-start.5 = (bf16[4,512,128]{2,1,0:T(8,128)(2,1)S(1)}, bf16[4,512,128]{2,1,0:T(8,128)(2,1)S(1)}, u32[]{:S(2)}, u32[]{:S(2)}) collective-permute-start(bf16[4,512,128]{2,1,0:T(8,128)(2,1)S(1)} %get-tuple-element.18), channel_id=1, source_target_pairs={{0,2},{2,0},{4,6},{6,4},{8,10},{10,8},{12,14},{14,12},{1,3},{3,1},... | collective-permute-start | bytes 1572872 | tf_op jit(solution)/shard_map/ppermute | solution.py:443
  31.6 37.3 %collective-permute-start.4 = (bf16[480,128]{1,0:T(8,128)(2,1)}, bf16[480,128]{1,0:T(8,128)(2,1)}, u32[]{:S(2)}, u32[]{:S(2)}) collective-permute-start(bf16[480,128]{1,0:T(8,128)(2,1)} %get-tuple-element.29), channel_id=1, source_target_pairs={{0,12},{2,14},{4,8},{6,10},{8,4},{10,6},{12,0},{14,2},{1,13},{3,15... | collective-permute-start | bytes 368648 | tf_op jit(solution)/shard_map/ppermute | solution.py:449
  35.8 33.1 %collective-permute-start.3 = (bf16[480,128]{1,0:T(8,128)(2,1)}, bf16[480,128]{1,0:T(8,128)(2,1)}, u32[]{:S(2)}, u32[]{:S(2)}) collective-permute-start(bf16[480,128]{1,0:T(8,128)(2,1)} %get-tuple-element.30), channel_id=1, source_target_pairs={{0,8},{2,10},{4,12},{6,14},{8,0},{10,2},{12,4},{14,6},{1,9},{3,11}... | collective-permute-start | bytes 368648 | tf_op jit(solution)/shard_map/ppermute | solution.py:449
  42.0 8.5 %collective-permute-start.8 = (bf16[512,128]{1,0:T(8,128)(2,1)}, bf16[512,128]{1,0:T(8,128)(2,1)S(1)}, u32[]{:S(2)}, u32[]{:S(2)}) collective-permute-start(bf16[512,128]{1,0:T(8,128)(2,1)} %get-tuple-element.25), channel_id=1, source_target_pairs={{0,12},{2,14},{4,8},{6,10},{8,4},{10,6},{12,0},{14,2},{1,13},{3,15... | collective-permute-start | bytes 393224 | tf_op jit(solution)/shard_map/ppermute | solution.py:449
  45.9 10.7 %collective-permute-start.7 = (bf16[512,128]{1,0:T(8,128)(2,1)}, bf16[512,128]{1,0:T(8,128)(2,1)}, u32[]{:S(2)}, u32[]{:S(2)}) collective-permute-start(bf16[512,128]{1,0:T(8,128)(2,1)} %get-tuple-element.26), channel_id=1, source_target_pairs={{0,8},{2,10},{4,12},{6,14},{8,0},{10,2},{12,4},{14,6},{1,9},{3,11}... | collective-permute-start | bytes 393224 | tf_op jit(solution)/shard_map/ppermute | solution.py:449
  45.9 10.7 %collective-permute-start.6 = (bf16[512,128]{1,0:T(8,128)(2,1)}, bf16[512,128]{1,0:T(8,128)(2,1)}, u32[]{:S(2)}, u32[]{:S(2)}) collective-permute-start(bf16[512,128]{1,0:T(8,128)(2,1)} %get-tuple-element.27), channel_id=1, source_target_pairs={{0,4},{2,6},{4,0},{6,2},{8,12},{10,14},{12,8},{14,10},{1,5},{3,7},... | collective-permute-start | bytes 393224 | tf_op jit(solution)/shard_map/ppermute | solution.py:449
  50.5 21.2 %collective-permute-start.2 = (bf16[480,128]{1,0:T(8,128)(2,1)}, bf16[480,128]{1,0:T(8,128)(2,1)}, u32[]{:S(2)}, u32[]{:S(2)}) collective-permute-start(bf16[480,128]{1,0:T(8,128)(2,1)} %get-tuple-element.31), channel_id=1, source_target_pairs={{0,4},{2,6},{4,0},{6,2},{8,12},{10,14},{12,8},{14,10},{1,5},{3,7},... | collective-permute-start | bytes 368648 | tf_op jit(solution)/shard_map/ppermute | solution.py:449
  56.5 1.9 %copy-start.5 = (bf16[24,128,512]{2,1,0:T(8,128)(2,1)S(1)}, bf16[24,128,512]{2,1,0:T(8,128)(2,1)}, u32[]{:S(2)}) copy-start(bf16[24,128,512]{2,1,0:T(8,128)(2,1)} %refs_10_.3) | copy-start | bytes 9437188
  58.4 0.7 copy-start.13
  59.1 0.7 copy-start.20
  65.0 16.3 %collective-permute-start.19 = (bf16[384,128]{1,0:T(8,128)(2,1)}, bf16[384,128]{1,0:T(8,128)(2,1)S(1)}, u32[]{:S(2)}, u32[]{:S(2)}) collective-permute-start(bf16[384,128]{1,0:T(8,128)(2,1)} %get-tuple-element.20.refs_1_), channel_id=1, source_target_pairs={{0,2},{2,0},{4,6},{6,4},{8,10},{10,8},{12,14},{14,12},{1,3},{3,1},... | collective-permute-start | bytes 294920 | tf_op jit(solution)/shard_map/ppermute | solution.py:466
  66.5 14.8 %collective-permute-start.18 = (bf16[384,128]{1,0:T(8,128)(2,1)}, bf16[384,128]{1,0:T(8,128)(2,1)S(1)}, u32[]{:S(2)}, u32[]{:S(2)}) collective-permute-start(bf16[384,128]{1,0:T(8,128)(2,1)} %get-tuple-element.20.refs_1_), channel_id=1, source_target_pairs={{0,12},{2,14},{4,8},{6,10},{8,4},{10,6},{12,0},{14,2},{1,13},{3,15... | collective-permute-start | bytes 294920 | tf_op jit(solution)/shard_map/ppermute | solution.py:464
  68.9 14.5 %collective-permute-start.17 = (bf16[384,128]{1,0:T(8,128)(2,1)}, bf16[384,128]{1,0:T(8,128)(2,1)}, u32[]{:S(2)}, u32[]{:S(2)}) collective-permute-start(bf16[384,128]{1,0:T(8,128)(2,1)} %get-tuple-element.20.refs_1_), channel_id=1, source_target_pairs={{0,8},{2,10},{4,12},{6,14},{8,0},{10,2},{12,4},{14,6},{1,9},{3,11}... | collective-permute-start | bytes 294920 | tf_op jit(solution)/shard_map/ppermute | solution.py:464
  68.9 14.9 %collective-permute-start.16 = (bf16[384,128]{1,0:T(8,128)(2,1)}, bf16[384,128]{1,0:T(8,128)(2,1)}, u32[]{:S(2)}, u32[]{:S(2)}) collective-permute-start(bf16[384,128]{1,0:T(8,128)(2,1)} %get-tuple-element.20.refs_1_), channel_id=1, source_target_pairs={{0,4},{2,6},{4,0},{6,2},{8,12},{10,14},{12,8},{14,10},{1,5},{3,7},... | collective-permute-start | bytes 294920 | tf_op jit(solution)/shard_map/ppermute | solution.py:464
  71.7 1.9 %copy-start.6 = (bf16[24,128,512]{2,1,0:T(8,128)(2,1)S(1)}, bf16[24,128,512]{2,1,0:T(8,128)(2,1)}, u32[]{:S(2)}) copy-start(bf16[24,128,512]{2,1,0:T(8,128)(2,1)} %refs_10_.3) | copy-start | bytes 9437188
  73.5 0.7 copy-start.17
  74.2 0.7 copy-start.21
  74.9 34.0 %copy-start.12 = (bf16[96,1024]{1,0:T(8,128)(2,1)S(1)}, bf16[96,1024]{1,0:T(8,128)(2,1)}, u32[]{:S(2)}) copy-start(bf16[96,1024]{1,0:T(8,128)(2,1)} %own_ref.1) | copy-start | bytes 589828
  78.9 6.8 %collective-permute-start.11 = (bf16[384,128]{1,0:T(8,128)(2,1)S(1)}, bf16[384,128]{1,0:T(8,128)(2,1)S(1)}, u32[]{:S(2)}, u32[]{:S(2)}) collective-permute-start(bf16[384,128]{1,0:T(8,128)(2,1)S(1)} %attend1.1.refs_1_), channel_id=1, source_target_pairs={{0,12},{2,14},{4,8},{6,10},{8,4},{10,6},{12,0},{14,2},{1,13},{3,15... | collective-permute-start | bytes 294920 | tf_op jit(solution)/shard_map/ppermute | solution.py:464
  81.3 7.3 %collective-permute-start.10 = (bf16[384,128]{1,0:T(8,128)(2,1)S(1)}, bf16[384,128]{1,0:T(8,128)(2,1)S(1)}, u32[]{:S(2)}, u32[]{:S(2)}) collective-permute-start(bf16[384,128]{1,0:T(8,128)(2,1)S(1)} %attend1.1.refs_1_), channel_id=1, source_target_pairs={{0,8},{2,10},{4,12},{6,14},{8,0},{10,2},{12,4},{14,6},{1,9},{3,11}... | collective-permute-start | bytes 294920 | tf_op jit(solution)/shard_map/ppermute | solution.py:464
  81.3 7.8 %collective-permute-start.9 = (bf16[384,128]{1,0:T(8,128)(2,1)S(1)}, bf16[384,128]{1,0:T(8,128)(2,1)S(1)}, u32[]{:S(2)}, u32[]{:S(2)}) collective-permute-start(bf16[384,128]{1,0:T(8,128)(2,1)S(1)} %attend1.1.refs_1_), channel_id=1, source_target_pairs={{0,4},{2,6},{4,0},{6,2},{8,12},{10,14},{12,8},{14,10},{1,5},{3,7},... | collective-permute-start | bytes 294920 | tf_op jit(solution)/shard_map/ppermute | solution.py:464
  83.4 7.3 %collective-permute-start.22 = (bf16[384,128]{1,0:T(8,128)(2,1)S(1)}, bf16[384,128]{1,0:T(8,128)(2,1)S(1)}, u32[]{:S(2)}, u32[]{:S(2)}) collective-permute-start(bf16[384,128]{1,0:T(8,128)(2,1)S(1)} %collective-permute-done.18.refs_4_), channel_id=1, source_target_pairs={{0,2},{2,0},{4,6},{6,4},{8,10},{10,8},{12,14},{14,12},{1,3},{3,1},... | collective-permute-start | bytes 294920 | tf_op jit(solution)/shard_map/ppermute | solution.py:466
  83.9 7.3 %collective-permute-start.21 = (bf16[384,128]{1,0:T(8,128)(2,1)}, bf16[384,128]{1,0:T(8,128)(2,1)S(1)}, u32[]{:S(2)}, u32[]{:S(2)}) collective-permute-start(bf16[384,128]{1,0:T(8,128)(2,1)} %collective-permute-done.17.refs_3_), channel_id=1, source_target_pairs={{0,2},{2,0},{4,6},{6,4},{8,10},{10,8},{12,14},{14,12},{1,3},{3,1},... | collective-permute-start | bytes 294920 | tf_op jit(solution)/shard_map/ppermute | solution.py:466
  85.7 7.0 %collective-permute-start.20 = (bf16[384,128]{1,0:T(8,128)(2,1)}, bf16[384,128]{1,0:T(8,128)(2,1)S(1)}, u32[]{:S(2)}, u32[]{:S(2)}) collective-permute-start(bf16[384,128]{1,0:T(8,128)(2,1)} %collective-permute-done.16.refs_2_), channel_id=1, source_target_pairs={{0,2},{2,0},{4,6},{6,4},{8,10},{10,8},{12,14},{14,12},{1,3},{3,1},... | collective-permute-start | bytes 294920 | tf_op jit(solution)/shard_map/ppermute | solution.py:466
  88.6 12.5 %collective-permute-start.12 = (bf16[384,128]{1,0:T(8,128)(2,1)S(1)}, bf16[384,128]{1,0:T(8,128)(2,1)S(1)}, u32[]{:S(2)}, u32[]{:S(2)}) collective-permute-start(bf16[384,128]{1,0:T(8,128)(2,1)S(1)} %attend1.1.refs_1_), channel_id=1, source_target_pairs={{0,2},{2,0},{4,6},{6,4},{8,10},{10,8},{12,14},{14,12},{1,3},{3,1},... | collective-permute-start | bytes 294920 | tf_op jit(solution)/shard_map/ppermute | solution.py:466
  89.1 12.0 %collective-permute-start.15 = (bf16[384,128]{1,0:T(8,128)(2,1)S(1)}, bf16[384,128]{1,0:T(8,128)(2,1)S(1)}, u32[]{:S(2)}, u32[]{:S(2)}) collective-permute-start(bf16[384,128]{1,0:T(8,128)(2,1)S(1)} %collective-permute-done.11.refs_4_), channel_id=1, source_target_pairs={{0,2},{2,0},{4,6},{6,4},{8,10},{10,8},{12,14},{14,12},{1,3},{3,1},... | collective-permute-start | bytes 294920 | tf_op jit(solution)/shard_map/ppermute | solution.py:466
  90.6 10.5 %collective-permute-start.14 = (bf16[384,128]{1,0:T(8,128)(2,1)S(1)}, bf16[384,128]{1,0:T(8,128)(2,1)S(1)}, u32[]{:S(2)}, u32[]{:S(2)}) collective-permute-start(bf16[384,128]{1,0:T(8,128)(2,1)S(1)} %collective-permute-done.10.refs_3_), channel_id=1, source_target_pairs={{0,2},{2,0},{4,6},{6,4},{8,10},{10,8},{12,14},{14,12},{1,3},{3,1},... | collective-permute-start | bytes 294920 | tf_op jit(solution)/shard_map/ppermute | solution.py:466
  91.2 10.0 %collective-permute-start.13 = (bf16[384,128]{1,0:T(8,128)(2,1)S(1)}, bf16[384,128]{1,0:T(8,128)(2,1)S(1)}, u32[]{:S(2)}, u32[]{:S(2)}) collective-permute-start(bf16[384,128]{1,0:T(8,128)(2,1)S(1)} %collective-permute-done.9.refs_2_), channel_id=1, source_target_pairs={{0,2},{2,0},{4,6},{6,4},{8,10},{10,8},{12,14},{14,12},{1,3},{3,1},... | collective-permute-start | bytes 294920 | tf_op jit(solution)/shard_map/ppermute | solution.py:466
  92.7 3.4 %copy-start.2 = (bf16[4096,1024]{1,0:T(8,128)(2,1)S(1)}, bf16[4096,1024]{1,0:T(8,128)(2,1)}, u32[]{:S(2)}) copy-start(bf16[4096,1024]{1,0:T(8,128)(2,1)} %refs_10_.5) | copy-start | bytes 25165828
  96.1 0.7 copy-start.15
  101.2 3.4 %copy-start.3 = (bf16[4096,1024]{1,0:T(8,128)(2,1)S(1)}, bf16[4096,1024]{1,0:T(8,128)(2,1)}, u32[]{:S(2)}) copy-start(bf16[4096,1024]{1,0:T(8,128)(2,1)} %refs_10_.5) | copy-start | bytes 25165828
  107.4 1.5 %collective-permute-start.23 = (bf16[96,1024]{1,0:T(8,128)(2,1)S(1)}, bf16[96,1024]{1,0:T(8,128)(2,1)S(1)}, u32[]{:S(2)}, u32[]{:S(2)}) collective-permute-start(bf16[96,1024]{1,0:T(8,128)(2,1)S(1)} %get-tuple-element.22), channel_id=1, source_target_pairs={{0,1},{1,0},{2,3},{3,2},{4,5},{5,4},{6,7},{7,6},{8,9},{9,8},{10,11... | collective-permute-start | bytes 589832 | tf_op jit(solution)/shard_map/ppermute | solution.py:478
  (2 other events, 1.2 us)

commit v2 on v1

v2 whole, which is shorter than its diff:
```python
import functools
import math

import jax
import jax.numpy as jnp
from jax import lax
from jax.experimental import pallas as pl
from jax.experimental.pallas import tpu as pltpu
from jax.sharding import PartitionSpec as P

MODEL_WIDTH = 8192
QUERY_HEADS = 64
KEY_VALUE_HEADS = 8
HEAD_SIZE = 128
QUERIES_PER_KV = QUERY_HEADS // KEY_VALUE_HEADS
TILES = QUERIES_PER_KV + 2
SQUARE_ROWS = 32

EPSILON = 1e-06
ROPE_BASE = 1000000.0
CHUNKS = 2
SLOTS_PER_STEP = 8
VMEM_LIMIT = 56 * 1024 * 1024
F32 = jnp.float32
BF16 = jnp.bfloat16


def peer(z, q, nz):
    return z ^ q


def peer_pairs(q, nz):
    pairs = []
    for z in range(nz):
        for y in range(2):
            pairs.append((z * 2 + y, peer(z, q, nz) * 2 + y))
    return pairs


def neighbour_pairs(nz):
    return [(z * 2 + y, z * 2 + 1 - y) for z in range(nz) for y in range(2)]


def slot_one_hot(place_ref, slot_of_row, nz, per):
    rows = slot_of_row.shape[1]
    place_z, place_y = place_ref[0], place_ref[1]
    base = lax.broadcasted_iota(jnp.int32, (per, rows), 0)
    blocks = []
    for h in range(2):
        for q in range(nz):
            owner = peer(place_z, q, nz) * 2 + (place_y ^ h)
            blocks.append(jnp.where(base + owner * per == slot_of_row, 1.0, 0.0).astype(F32))
    return jnp.concatenate(blocks, axis=0).astype(BF16)


def project_kernel(*refs, nz, per, first, heads):
    place_ref = refs[0]
    if first:
        (
            own_ref, other_ref, gain_ref, sor_ref, wq_ref, wk_ref, wv_ref,
            keep_ref, send_ref, slotted_ref, acc,
        ) = refs[1:]
    else:
        own_ref, wq_ref, wk_ref, wv_ref, keep_ref, send_ref, acc = refs[1:]
    step = pl.program_id(0)
    half = nz * per

    if first:

        @pl.when(step == 0)
        def _():
            one_hot = slot_one_hot(place_ref, sor_ref[...], nz, per)
            own, other = own_ref[...], other_ref[...]
            lower = place_ref[2] == 0
            rows = jnp.concatenate(
                [jnp.where(lower, own, other), jnp.where(lower, other, own)], axis=0
            )
            hidden = jnp.dot(one_hot, rows, preferred_element_type=F32)
            gain = gain_ref[...].astype(F32)
            gain = jnp.concatenate([gain[j : j + 1] for j in range(gain.shape[0])], axis=1)
            slotted_ref[...] = (hidden * gain).astype(BF16)
            squares = jnp.sum(hidden * hidden, axis=1, keepdims=True)
            high = squares.astype(BF16).astype(F32)
            low = squares - high
            lane = lax.broadcasted_iota(jnp.int32, (per, HEAD_SIZE), 1)
            lane_high = place_ref[1] * 2
            for h, ref in enumerate((keep_ref, send_ref)):
                for q in range(nz):
                    at = h * half + q * per
                    packed = jnp.where(
                        lane == lane_high,
                        high[at : at + per],
                        jnp.where(lane == lane_high + 1, low[at : at + per], 0.0),
                    )
                    packed = jnp.concatenate(
                        [packed, jnp.zeros((SQUARE_ROWS - per, HEAD_SIZE), F32)], axis=0
                    )
                    ref[q, heads * TILES * per :, :] = packed.astype(BF16)

        source = slotted_ref
    else:
        source = own_ref

    columns = QUERIES_PER_KV * HEAD_SIZE
    acc[:, :columns] = jnp.dot(source[...], wq_ref[...], preferred_element_type=F32)
    acc[:, columns : columns + HEAD_SIZE] = jnp.dot(
        source[...], wk_ref[...], preferred_element_type=F32
    )
    acc[:, columns + HEAD_SIZE :] = jnp.dot(source[...], wv_ref[...], preferred_element_type=F32)
    start = pl.multiple_of(step * TILES * per, 16)
    for h, ref in enumerate((keep_ref, send_ref)):
        for q in range(nz):
            at = h * half + q * per
            block = jnp.concatenate(
                [
                    acc[at : at + per, c * HEAD_SIZE : (c + 1) * HEAD_SIZE]
                    for c in range(TILES)
                ],
                axis=0,
            )
            ref[q, pl.ds(start, TILES * per), :] = block.astype(BF16)


def project(place, inputs, wq, wk, wv, *, chunk, heads, nz, per):
    first = chunk == 0
    rows = 2 * nz * per
    depth = wq.shape[0]
    block_rows = heads * TILES * per + (SQUARE_ROWS if first else 0)
    out_block = jax.ShapeDtypeStruct((nz, block_rows, HEAD_SIZE), BF16)
    whole3 = pl.BlockSpec((nz, block_rows, HEAD_SIZE), lambda i, p: (0, 0, 0))
    column = lambda i, p: (0, chunk * heads + i)

    def whole2(array):
        return pl.BlockSpec(array.shape, lambda i, p: (0, 0))

    slotted = jax.ShapeDtypeStruct((rows, depth), BF16)
    return pl.pallas_call(
        functools.partial(project_kernel, nz=nz, per=per, first=first, heads=heads),
        grid_spec=pltpu.PrefetchScalarGridSpec(
            num_scalar_prefetch=1,
            grid=(heads,),
            in_specs=[whole2(a) for a in inputs]
            + [
                pl.BlockSpec((depth, QUERIES_PER_KV * HEAD_SIZE), column),
                pl.BlockSpec((depth, HEAD_SIZE), column),
                pl.BlockSpec((depth, HEAD_SIZE), column),
            ],
            out_specs=[whole3, whole3] + ([whole2(slotted)] if first else []),
            scratch_shapes=[pltpu.VMEM((rows, TILES * HEAD_SIZE), F32)],
        ),
        out_shape=[out_block, out_block] + ([slotted] if first else []),
        compiler_params=pltpu.CompilerParams(vmem_limit_bytes=VMEM_LIMIT),
        cost_estimate=pl.CostEstimate(
            flops=20 * rows * depth * heads * TILES * HEAD_SIZE,
            bytes_accessed=20 * depth * heads * TILES * HEAD_SIZE,
            transcendentals=0,
        ),
        name="project" + str(chunk),
    )(place, *inputs, wq, wk, wv)


def attend_kernel(*refs, parts, first, heads, per, group, chunk):
    place_ref, lengths_ref = refs[:2]
    part_refs = refs[2 : 2 + parts]
    rest = refs[2 + parts :]
    if first:
        qb_ref, kb_ref, vb_ref, cos_ref, sin_ref, k_ref, v_ref, out_ref, scale_ref = rest[:9]
    else:
        scale_in_ref, qb_ref, kb_ref, vb_ref, cos_ref, sin_ref, k_ref, v_ref, out_ref = rest[:9]
    fresh, result = rest[9:]
    step = pl.program_id(0)
    body = heads * TILES * per
    head_rows = TILES * per

    @pl.when(step == 0)
    def _():
        if first:
            squares = part_refs[0][body:, :].astype(F32)
            for ref in part_refs[1:]:
                squares = squares + ref[body:, :].astype(F32)
            total = jnp.sum(squares[:per], axis=1, keepdims=True)
            scale = jnp.broadcast_to(
                lax.rsqrt(total / MODEL_WIDTH + EPSILON), (per, HEAD_SIZE)
            )
            scale_ref[...] = scale
        else:
            scale = scale_in_ref[...]
        cos, sin = cos_ref[...], sin_ref[...]
        query_bias = qb_ref[...].astype(F32)
        key_bias = kb_ref[...].astype(F32)
        value_bias = vb_ref[...].astype(F32)
        for g in range(heads):
            rows = pl.ds(g * head_rows, head_rows)
            summed = part_refs[0][rows, :].astype(F32)
            for ref in part_refs[1:]:
                summed = summed + ref[rows, :].astype(F32)
            head = chunk * heads + g
            for c in range(TILES):
                if c < QUERIES_PER_KV:
                    at = head * QUERIES_PER_KV + c
                    bias = query_bias[at : at + 1]
                else:
                    bias = (key_bias if c == QUERIES_PER_KV else value_bias)[head : head + 1]
                tile = summed[c * per : (c + 1) * per] * scale + bias
                if c < TILES - 1:
                    tile = tile * cos + pltpu.roll(tile, HEAD_SIZE // 2, 1) * sin
                fresh[pl.ds(g * head_rows + c * per, per), :] = tile.astype(BF16).astype(F32)

    positions = k_ref.shape[1]
    qrows = heads * QUERIES_PER_KV
    lanes = group * qrows
    extra = 16
    slots = [step * group + i for i in range(group)]
    queries = jnp.concatenate(
        [
            fresh[pl.ds(g * head_rows + s, QUERIES_PER_KV, stride=per), :]
            for s in slots
            for g in range(heads)
        ],
        axis=0,
    )
    turned = queries.T
    lane_block = lax.broadcasted_iota(jnp.int32, (HEAD_SIZE, lanes), 1) // QUERIES_PER_KV
    top_row = lax.broadcasted_iota(jnp.int32, (extra, HEAD_SIZE), 0) == 0
    scores = None
    for i, s in enumerate(slots):
        query, new_key = [], []
        for g in range(heads):
            query.append(jnp.where(lane_block == i * heads + g, turned, 0.0).astype(BF16))
            key = fresh[pl.ds(g * head_rows + QUERIES_PER_KV * per + s, 1), :]
            new_key.append(jnp.where(top_row, key, 0.0).astype(BF16))
        keys = jnp.concatenate([k_ref[i], jnp.concatenate(new_key, axis=1)], axis=0)
        term = jnp.dot(keys, jnp.concatenate(query, axis=0), preferred_element_type=F32)
        scores = term if scores is None else scores + term

    lane_slot = lax.broadcasted_iota(jnp.int32, (1, lanes), 1) // qrows
    lengths = jnp.zeros((1, lanes), jnp.int32)
    base = (place_ref[0] * 2 + place_ref[1]) * per
    for i, s in enumerate(slots):
        lengths = jnp.where(lane_slot == i, lengths_ref[base + s], lengths)
    row = lax.broadcasted_iota(jnp.int32, (positions + extra, lanes), 0)
    valid = (row < lengths) | (row == positions)
    scores = jnp.where(valid, scores * (1.0 / math.sqrt(HEAD_SIZE)), -1e30)
    top = jnp.max(scores, axis=0, keepdims=True)
    exps = jnp.where(valid, jnp.exp(scores - top), 0.0)
    weights = exps * (1.0 / jnp.sum(exps, axis=0, keepdims=True))
    cache_weights = weights[:positions].T.astype(BF16)
    own_weights = weights[positions : positions + 8].T[:, 0:1].astype(BF16).astype(F32)
    for i, s in enumerate(slots):
        mixed = jnp.dot(
            cache_weights[i * qrows : (i + 1) * qrows], v_ref[i], preferred_element_type=F32
        )
        for g in range(heads):
            lo, hi = g * QUERIES_PER_KV, (g + 1) * QUERIES_PER_KV
            new_value = fresh[pl.ds(g * head_rows + (QUERIES_PER_KV + 1) * per + s, 1), :]
            result[pl.ds(g * QUERIES_PER_KV * per + s, QUERIES_PER_KV, stride=per), :] = (
                mixed[lo:hi, g * HEAD_SIZE : (g + 1) * HEAD_SIZE]
                + own_weights[i * qrows + lo : i * qrows + hi] * new_value
            )

    @pl.when(step == pl.num_programs(0) - 1)
    def _():
        out_ref[...] = result[...].astype(BF16)


def attend(place, lengths, parts, scale, biases, cos, sin, keys, values, *, chunk, heads):
    first = chunk == 0
    per, positions = keys.shape[0], keys.shape[1]
    group = SLOTS_PER_STEP

    def whole2(array):
        return pl.BlockSpec(array.shape, lambda i, p, n: (0, 0))

    cache_spec = pl.BlockSpec(
        (group, positions, heads * HEAD_SIZE), lambda i, p, n: (i, 0, chunk)
    )
    ins = list(parts) + ([] if first else [scale]) + list(biases) + [cos, sin]
    out_rows = heads * QUERIES_PER_KV * per
    out_shape = [jax.ShapeDtypeStruct((out_rows, HEAD_SIZE), BF16)]
    if first:
        out_shape.append(jax.ShapeDtypeStruct((per, HEAD_SIZE), F32))
    return pl.pallas_call(
        functools.partial(
            attend_kernel,
            parts=len(parts),
            first=first,
            heads=heads,
            per=per,
            group=group,
            chunk=chunk,
        ),
        grid_spec=pltpu.PrefetchScalarGridSpec(
            num_scalar_prefetch=2,
            grid=(per // group,),
            in_specs=[whole2(a) for a in ins] + [cache_spec, cache_spec],
            out_specs=[whole2(o) for o in out_shape],
            scratch_shapes=[
                pltpu.VMEM((heads * TILES * per, HEAD_SIZE), F32),
                pltpu.VMEM((out_rows, HEAD_SIZE), F32),
            ],
        ),
        out_shape=out_shape,
        compiler_params=pltpu.CompilerParams(vmem_limit_bytes=VMEM_LIMIT),
        cost_estimate=pl.CostEstimate(
            flops=4 * per * heads * QUERIES_PER_KV * positions * HEAD_SIZE,
            bytes_accessed=4 * per * positions * heads * HEAD_SIZE,
            transcendentals=per * heads * QUERIES_PER_KV * positions,
        ),
        name="attend" + str(chunk),
    )(place, lengths, *ins, keys, values)


def output_kernel(*refs, blocks, nz, per, first, last):
    place_ref = refs[0]
    block_refs = refs[1 : 1 + blocks]
    rest = refs[1 + blocks :]
    sor_ref, w_ref = rest[:2]
    rest = rest[2:]
    if not first:
        acc_in_ref, rest = rest[0], rest[1:]
    if last:
        mine_ref, send_ref, stacked, permuted, total = rest
    else:
        acc_out_ref, stacked, permuted = rest
    tiles = block_refs[0].shape[0] // per

    @pl.when(pl.program_id(0) == 0)
    def _():
        one_hot = slot_one_hot(place_ref, sor_ref[...], nz, per)
        wide = [ref[...].astype(F32) for ref in block_refs]
        for c in range(tiles):
            stacked[:, c * HEAD_SIZE : (c + 1) * HEAD_SIZE] = jnp.concatenate(
                [block[c * per : (c + 1) * per] for block in wide], axis=0
            ).astype(BF16)
        permuted[...] = lax.dot_general(
            one_hot, stacked[...], (((0,), (0,)), ((), ())), preferred_element_type=F32
        ).astype(BF16)

    product = jnp.dot(permuted[...], w_ref[...], preferred_element_type=F32)
    if not first:
        product = product + acc_in_ref[...]
    if last:
        half = product.shape[0] // 2
        total[...] = product
        mine_ref[...] = total[pl.ds(pl.multiple_of(place_ref[2] * half, half), half), :]
        send_ref[...] = total[
            pl.ds(pl.multiple_of((1 - place_ref[2]) * half, half), half), :
        ].astype(BF16)
    else:
        acc_out_ref[...] = product


def output(place, blocks, sor, w_out, acc, *, chunk, heads, chunks, nz, per):
    first, last = chunk == 0, chunk == chunks - 1
    rows = 2 * nz * per
    width = w_out.shape[1]
    depth = heads * QUERIES_PER_KV * HEAD_SIZE
    columns = min(width, 256)

    def whole2(array):
        return pl.BlockSpec(array.shape, lambda i, p: (0, 0))

    def striped(count):
        return pl.BlockSpec((count, columns), lambda i, p: (0, i))

    if last:
        out_shape = [
            jax.ShapeDtypeStruct((rows // 2, width), F32),
            jax.ShapeDtypeStruct((rows // 2, width), BF16),
        ]
    else:
        out_shape = [jax.ShapeDtypeStruct((rows, width), F32)]
    ins = list(blocks) + [sor]
    in_specs = [whole2(a) for a in ins] + [
        pl.BlockSpec((depth, columns), lambda i, p: (chunk, i))
    ]
    args = ins + [w_out]
    if not first:
        args.append(acc)
        in_specs.append(striped(rows))
    return pl.pallas_call(
        functools.partial(
            output_kernel, blocks=len(blocks), nz=nz, per=per, first=first, last=last
        ),
        grid_spec=pltpu.PrefetchScalarGridSpec(
            num_scalar_prefetch=1,
            grid=(width // columns,),
            in_specs=in_specs,
            out_specs=[striped(o.shape[0]) for o in out_shape],
            scratch_shapes=[pltpu.VMEM((rows, depth), BF16), pltpu.VMEM((rows, depth), BF16)]
            + ([pltpu.VMEM((rows, columns), F32)] if last else []),
        ),
        out_shape=out_shape,
        compiler_params=pltpu.CompilerParams(vmem_limit_bytes=VMEM_LIMIT),
        cost_estimate=pl.CostEstimate(
            flops=2 * rows * depth * width, bytes_accessed=2 * depth * width, transcendentals=0
        ),
        name="output" + str(chunk),
    )(place, *args)


def on_device(
    hidden_rows,
    norm_gain,
    w_query,
    key_weight,
    value_weight,
    query_bias,
    key_bias_vector,
    value_bias_vector,
    rotated_key_cache,
    stored_value_cache,
    slot_valid_lengths,
    slot_of_row,
    w_out,
    *,
    size,
):
    nz = size // 2
    assert size % 2 == 0 and nz & (nz - 1) == 0
    per = rotated_key_cache.shape[0]
    kv_heads = key_weight.shape[1] // HEAD_SIZE
    heads = kv_heads // CHUNKS
    gx = lax.axis_index("gx")
    gy = lax.axis_index("gy")
    place = jnp.stack([gx // 2, gx % 2, gy]).astype(jnp.int32)

    other = lax.ppermute(hidden_rows, "gy", [(0, 1), (1, 0)])
    sor = slot_of_row[None, :]
    gain = norm_gain.reshape(-1, HEAD_SIZE)

    lengths = lax.dynamic_slice_in_dim(slot_valid_lengths, gx * per, per, 0)
    lane = jnp.arange(HEAD_SIZE)
    half_width = HEAD_SIZE // 2
    frequency = ROPE_BASE ** (-((lane % half_width).astype(F32) * 2.0 / HEAD_SIZE))
    angles = lengths.astype(F32)[:, None] * frequency[None, :]
    cos = jnp.cos(angles)
    sin = jnp.sin(angles) * jnp.where(lane < half_width, -1.0, 1.0)[None, :]
    biases = [b.reshape(-1, HEAD_SIZE) for b in (query_bias, key_bias_vector, value_bias_vector)]

    swapped, kept = [], []
    inputs = [hidden_rows, other, gain, sor]
    for c in range(CHUNKS):
        outs = project(
            place, inputs, w_query, key_weight, value_weight,
            chunk=c, heads=heads, nz=nz, per=per,
        )
        keep, send = outs[:2]
        if c == 0:
            inputs = [outs[2]]
        kept.append(keep)
        swapped.append(lax.ppermute(send, "gx", neighbour_pairs(nz)))
    parts = []
    for c in range(CHUNKS):
        blocks = []
        for q in range(nz):
            total = (kept[c][q].astype(F32) + swapped[c][q].astype(F32)).astype(BF16)
            blocks.append(total if q == 0 else lax.ppermute(total, "gx", peer_pairs(q, nz)))
        parts.append(blocks)

    scale = None
    gathered = []
    for c in range(CHUNKS):
        outs = attend(
            place, slot_valid_lengths, parts[c], scale, biases, cos, sin,
            rotated_key_cache, stored_value_cache, chunk=c, heads=heads,
        )
        if c == 0:
            attended, scale = outs
        else:
            (attended,) = outs
        blocks = [attended] + [
            lax.ppermute(attended, "gx", peer_pairs(q, nz)) for q in range(1, nz)
        ]
        blocks += [lax.ppermute(b, "gx", neighbour_pairs(nz)) for b in blocks]
        gathered.append(blocks)

    acc = None
    for c in range(CHUNKS):
        outs = output(
            place, gathered[c], sor, w_out, acc,
            chunk=c, heads=heads, chunks=CHUNKS, nz=nz, per=per,
        )
        if c < CHUNKS - 1:
            (acc,) = outs
    mine, send = outs
    received = lax.ppermute(send, "gy", [(0, 1), (1, 0)])
    return (hidden_rows.astype(F32) + mine + received.astype(F32)).astype(BF16)


def solution(mesh):
    in_specs = (
        P(("grp", "gy"), "gx"),
        P("gx"),
        P("gx", "gy"),
        P("gx", "gy"),
        P("gx", "gy"),
        P("gy"),
        P("gy"),
        P("gy"),
        P(("grp", "gx"), None, "gy"),
        P(("grp", "gx"), None, "gy"),
        P("grp"),
        P("grp"),
        P("gy", "gx"),
    )
    out_specs = P(("grp", "gy"), "gx")
    return jax.shard_map(
        functools.partial(on_device, size=mesh.shape["gx"]),
        mesh=mesh,
        in_specs=in_specs,
        out_specs=out_specs,
        check_vma=False,
    )
```

time: 110 us -> 106 us (0.964)
  local copies, waits for them, and re-layouts: 26.2 us -> 3.96 us
  Pallas kernels: 20.8 us -> 34.3 us
  waiting for transfers between devices: 23.6 us -> 27.7 us
    unnamed x52 -> x48, local copies, waits for them, and re-layouts: 22.8 us -> 3.96 us
    ppermute x6, waiting for transfers between devices: 3.36 us -> 9.8 us  [on_device(): lax.ppermute(total, 'gx', peer_pairs(q, nz))]
    pallas_call x2, Pallas kernels: 6.62 us -> 12.2 us  [output(): pl.pallas_call(functools.partial(output_kernel, blocks=len(blocks), nz=nz...]
    pallas_call x2, Pallas kernels: 5.66 us -> 10.9 us  [project(): pl.pallas_call(functools.partial(project_kernel, nz=nz, per=per, first=fi...]
    ppermute x2, waiting for transfers between devices: 16 us -> 12.6 us  [on_device(): swapped.append(lax.ppermute(send, 'gx', neighbour_pairs(nz)))]
    pallas_call x2, Pallas kernels: 8.54 us -> 11.2 us  [attend(): pl.pallas_call(functools.partial(attend_kernel, parts=len(parts), first=f...]
    slice x2 -> x0, local copies, waits for them, and re-layouts: 1.43 us -> none  [the longest x1 0.82 us: on_device(): sor = jnp.where(gy == 0, slot_of_row, jnp.roll(slot_of_row, half))[None, :]]
    squeeze x2 -> x0, local copies, waits for them, and re-layouts: 1.32 us -> none  [on_device(): bias[c]]
  transfers between devices with their start and end apart: 24 -> 24, of which waited for: 7 -> 7; matrix products, arithmetic and copies ran while one was open for 7% -> 4% of each run, Pallas kernels for 11% -> 21%
where the time goes in v2:
time: 106 us; the launch traced here: 105 us
  Pallas kernels  34.3 us (32%)
  starting transfers between devices  33.2 us (31%)
  waiting for transfers between devices  27.7 us (26%)
  other arithmetic  5.85 us (6%)
  local copies, waits for them, and re-layouts  3.96 us (4%)
    ppermute x6, starting transfers between devices, on_device(): lax.ppermute(total, 'gx', peer_pairs(q, nz))  12.9 us
    ppermute x2, waiting for transfers between devices, on_device(): swapped.append(lax.ppermute(send, 'gx', neighbour_pairs(nz)))  12.6 us
    pallas_call x2, Pallas kernels, output(): pl.pallas_call(functools.partial(output_kernel, blocks=len(blocks), nz=nz...  12.2 us
    pallas_call x2, Pallas kernels, attend(): pl.pallas_call(functools.partial(attend_kernel, parts=len(parts), first=f...  11.2 us
    pallas_call x2, Pallas kernels, project(): pl.pallas_call(functools.partial(project_kernel, nz=nz, per=per, first=fi...  10.9 us
    ppermute x6, waiting for transfers between devices, on_device(): lax.ppermute(total, 'gx', peer_pairs(q, nz))  9.8 us
    ppermute x6, starting transfers between devices, on_device(): lax.ppermute(attended, 'gx', peer_pairs(q, nz))  8.74 us
    ppermute x8, starting transfers between devices, on_device(): blocks += [lax.ppermute(b, 'gx', neighbour_pairs(nz)) for b in blocks]  8.13 us
  transfers between devices with their start and end apart: 24, of which 7 were waited for; matrix products, arithmetic and copies ran while one was open for 4% of the time, Pallas kernels for 21%

profile of v2, /device:TPU:0, one launch (start us, length us, event | category | flops | bytes accessed | tf_op | source)
XLA Modules:
  0.0 105.2 jit_solution(13219217539581272375)
XLA Ops:
  0.0 0.5 collective-permute-start
  0.5 0.7 pad_add_fusion.refs_0_
  1.1 0.6 collective-permute-done.refs_2_
  1.7 0.7 copy-done.23
  2.4 5.7 %project0.1 = (bf16[4,512,128]{2,1,0:T(8,128)(2,1)}, bf16[4,512,128]{2,1,0:T(8,128)(2,1)}, bf16[192,1024]{1,0:T(8,128)(2,1)}) custom-call(s32[3]{0:T(128)} %pad_add_fusion.refs_0_, bf16[96,1024]{1,0:T(8,128)(2,1)} %refs_1_.3, bf16[96,1024]{1,0:T(8,128)(2,1)} %copy-done.23, bf16[8,128]{1,0:T(8,128)(2,1)} %bitcast.33, s32[1,192]{1,0:T(1,128)} %bitcast.30, ...), custom_call_target="tpu_custom_call" | custom-call | flops 10066329600 | bytes 52428800 | tf_op jit(solution)/shard_map/project0/pallas_call | solution.py:137
  8.1 2.9 %collective-permute-start.5 = (bf16[4,512,128]{2,1,0:T(8,128)(2,1)}, bf16[4,512,128]{2,1,0:T(8,128)(2,1)S(1)}, u32[]{:S(2)}, u32[]{:S(2)}) collective-permute-start(bf16[4,512,128]{2,1,0:T(8,128)(2,1)} %get-tuple-element.18), channel_id=1, source_target_pairs={{0,2},{2,0},{4,6},{6,4},{8,10},{10,8},{12,14},{14,12},{1,3},{3,1},... | collective-permute-start | bytes 1572872 | tf_op jit(solution)/shard_map/ppermute | solution.py:452
  11.0 5.3 %project1.1 = (bf16[4,480,128]{2,1,0:T(8,128)(2,1)}, bf16[4,480,128]{2,1,0:T(8,128)(2,1)}) custom-call(s32[3]{0:T(128)} %pad_add_fusion.refs_0_, bf16[192,1024]{1,0:T(8,128)(2,1)} %get-tuple-element.14.refs_1_, bf16[1024,4096]{1,0:T(8,128)(2,1)} %refs_2_.1, bf16[1024,512]{1,0:T(8,128)(2,1)} %refs_3_.1, bf16[1024,512]{1,0:T(8,128)(2,1)} %refs_4_.1), custom_call_target="tpu_custom_call" | custom-call | flops 10066329600 | bytes 52428800 | tf_op jit(solution)/shard_map/project1/pallas_call | solution.py:137
  16.2 0.0 collective-permute-start.1
  16.3 0.1 dynamic-slice_convert_fusion
  16.4 7.5 %collective-permute-done.5 = bf16[4,512,128]{2,1,0:T(8,128)(2,1)S(1)} collective-permute-done((bf16[4,512,128]{2,1,0:T(8,128)(2,1)}, bf16[4,512,128]{2,1,0:T(8,128)(2,1)S(1)}, u32[]{:S(2)}, u32[]{:S(2)}) %collective-permute-start.5) | collective-permute-done | bytes 524320 | tf_op jit(solution)/shard_map/ppermute | solution.py:452
  23.9 0.8 fusion.3
  24.7 4.2 %collective-permute-start.8 = (bf16[512,128]{1,0:T(8,128)(2,1)S(1)}, bf16[512,128]{1,0:T(8,128)(2,1)S(1)}, u32[]{:S(2)}, u32[]{:S(2)}) collective-permute-start(bf16[512,128]{1,0:T(8,128)(2,1)S(1)} %get-tuple-element.23), channel_id=1, source_target_pairs={{0,12},{2,14},{4,8},{6,10},{8,4},{10,6},{12,0},{14,2},{1,13},{3,15... | collective-permute-start | bytes 393224 | tf_op jit(solution)/shard_map/ppermute | solution.py:458
  28.8 5.1 %collective-permute-done.1 = bf16[4,480,128]{2,1,0:T(8,128)(2,1)S(1)} collective-permute-done((bf16[4,480,128]{2,1,0:T(8,128)(2,1)}, bf16[4,480,128]{2,1,0:T(8,128)(2,1)S(1)}, u32[]{:S(2)}, u32[]{:S(2)}) %collective-permute-start.1) | collective-permute-done | bytes 491552 | tf_op jit(solution)/shard_map/ppermute | solution.py:452
  33.9 1.9 %fusion.7 = (bf16[480,128]{1,0:T(8,128)(2,1)S(1)}, bf16[480,128]{1,0:T(8,128)(2,1)S(1)}, bf16[480,128]{1,0:T(8,128)(2,1)S(1)}, bf16[480,128]{1,0:T(8,128)(2,1)}) fusion(bf16[4,480,128]{2,1,0:T(8,128)(2,1)S(1)} %collective-permute-done.1, bf16[4,480,128]{2,1,0:T(8,128)(2,1)} %get-tuple-element.15), kind=kLoop, calls=%fused_computation.16 | loop fusion | flops 983040 | bytes 1474560 | tf_op jit(solution)/shard_map/convert_element_type | solution.py:457
  35.8 3.8 %collective-permute-start.4 = (bf16[480,128]{1,0:T(8,128)(2,1)S(1)}, bf16[480,128]{1,0:T(8,128)(2,1)S(1)}, u32[]{:S(2)}, u32[]{:S(2)}) collective-permute-start(bf16[480,128]{1,0:T(8,128)(2,1)S(1)} %get-tuple-element.27), channel_id=1, source_target_pairs={{0,12},{2,14},{4,8},{6,10},{8,4},{10,6},{12,0},{14,2},{1,13},{3,15... | collective-permute-start | bytes 368648 | tf_op jit(solution)/shard_map/ppermute | solution.py:458
  39.6 0.6 collective-permute-start.2
  40.2 2.4 %collective-permute-start.7 = (bf16[512,128]{1,0:T(8,128)(2,1)S(1)}, bf16[512,128]{1,0:T(8,128)(2,1)S(1)}, u32[]{:S(2)}, u32[]{:S(2)}) collective-permute-start(bf16[512,128]{1,0:T(8,128)(2,1)S(1)} %get-tuple-element.24), channel_id=1, source_target_pairs={{0,8},{2,10},{4,12},{6,14},{8,0},{10,2},{12,4},{14,6},{1,9},{3,11}... | collective-permute-start | bytes 393224 | tf_op jit(solution)/shard_map/ppermute | solution.py:458
  42.6 2.0 %collective-permute-start.6 = (bf16[512,128]{1,0:T(8,128)(2,1)S(1)}, bf16[512,128]{1,0:T(8,128)(2,1)S(1)}, u32[]{:S(2)}, u32[]{:S(2)}) collective-permute-start(bf16[512,128]{1,0:T(8,128)(2,1)S(1)} %get-tuple-element.25), channel_id=1, source_target_pairs={{0,4},{2,6},{4,0},{6,2},{8,12},{10,14},{12,8},{14,10},{1,5},{3,7},... | collective-permute-start | bytes 393224 | tf_op jit(solution)/shard_map/ppermute | solution.py:458
  44.6 0.7 fusion.8
  45.3 9.8 %collective-permute-done.7.refs_4_ = bf16[512,128]{1,0:T(8,128)(2,1)S(1)} collective-permute-done((bf16[512,128]{1,0:T(8,128)(2,1)S(1)}, bf16[512,128]{1,0:T(8,128)(2,1)S(1)}, u32[]{:S(2)}, u32[]{:S(2)}) %collective-permute-start.7) | collective-permute-done | bytes 131104 | tf_op jit(solution)/shard_map/ppermute | solution.py:458
  55.1 0.6 copy-done.3
  55.7 0.1 copy-done.4
  55.8 5.6 %attend0.1 = (bf16[384,128]{1,0:T(8,128)(2,1)}, f32[24,128]{1,0:T(8,128)}) custom-call(s32[3]{0:T(128)} %pad_add_fusion.refs_0_, s32[192]{0:T(256)} %refs_1_.5, bf16[512,128]{1,0:T(8,128)(2,1)} %get-tuple-element.26.refs_2_, bf16[512,128]{1,0:T(8,128)(2,1)} %copy-done.4, bf16[512,128]{1,0:T(8,128)(2,1)} %copy-done.3, bf16[512,128]{1,0:T(8,128)(2,1)} %copy-done.2, ...), custom_call_target="tpu_custom_call" | custom-call | flops 25165824 | bytes 3145728 | tf_op jit(solution)/shard_map/attend0/pallas_call | solution.py:282
  61.5 1.5 %collective-permute-start.19 = (bf16[384,128]{1,0:T(8,128)(2,1)}, bf16[384,128]{1,0:T(8,128)(2,1)S(1)}, u32[]{:S(2)}, u32[]{:S(2)}) collective-permute-start(bf16[384,128]{1,0:T(8,128)(2,1)} %get-tuple-element.20.refs_1_), channel_id=1, source_target_pairs={{0,2},{2,0},{4,6},{6,4},{8,10},{10,8},{12,14},{14,12},{1,3},{3,1},... | collective-permute-start | bytes 294920 | tf_op jit(solution)/shard_map/ppermute | solution.py:475
  63.0 2.5 %collective-permute-start.18 = (bf16[384,128]{1,0:T(8,128)(2,1)}, bf16[384,128]{1,0:T(8,128)(2,1)S(1)}, u32[]{:S(2)}, u32[]{:S(2)}) collective-permute-start(bf16[384,128]{1,0:T(8,128)(2,1)} %get-tuple-element.20.refs_1_), channel_id=1, source_target_pairs={{0,12},{2,14},{4,8},{6,10},{8,4},{10,6},{12,0},{14,2},{1,13},{3,15... | collective-permute-start | bytes 294920 | tf_op jit(solution)/shard_map/ppermute | solution.py:473
  65.5 1.9 %collective-permute-start.16 = (bf16[384,128]{1,0:T(8,128)(2,1)}, bf16[384,128]{1,0:T(8,128)(2,1)S(1)}, u32[]{:S(2)}, u32[]{:S(2)}) collective-permute-start(bf16[384,128]{1,0:T(8,128)(2,1)} %get-tuple-element.20.refs_1_), channel_id=1, source_target_pairs={{0,4},{2,6},{4,0},{6,2},{8,12},{10,14},{12,8},{14,10},{1,5},{3,7},... | collective-permute-start | bytes 294920 | tf_op jit(solution)/shard_map/ppermute | solution.py:473
  67.4 0.6 copy-done.7
  68.0 5.6 %attend1.1.refs_1_ = bf16[384,128]{1,0:T(8,128)(2,1)} custom-call(s32[3]{0:T(128)} %pad_add_fusion.refs_0_, s32[192]{0:T(256)} %refs_1_.5, bf16[480,128]{1,0:T(8,128)(2,1)} %get-tuple-element.30.refs_2_, bf16[480,128]{1,0:T(8,128)(2,1)} %copy-done.7, bf16[480,128]{1,0:T(8,128)(2,1)} %copy-done.6, bf16[480,128]{1,0:T(8,128)(2,1)} %copy-done.5, ...), custom_call_target="tpu_custom_call" | custom-call | flops 25165824 | bytes 3145728 | tf_op jit(solution)/shard_map/attend1/pallas_call | solution.py:282
  73.6 2.5 %collective-permute-start.11 = (bf16[384,128]{1,0:T(8,128)(2,1)}, bf16[384,128]{1,0:T(8,128)(2,1)S(1)}, u32[]{:S(2)}, u32[]{:S(2)}) collective-permute-start(bf16[384,128]{1,0:T(8,128)(2,1)} %attend1.1.refs_1_), channel_id=1, source_target_pairs={{0,12},{2,14},{4,8},{6,10},{8,4},{10,6},{12,0},{14,2},{1,13},{3,15... | collective-permute-start | bytes 294920 | tf_op jit(solution)/shard_map/ppermute | solution.py:473
  76.1 1.9 %collective-permute-start.9 = (bf16[384,128]{1,0:T(8,128)(2,1)}, bf16[384,128]{1,0:T(8,128)(2,1)S(1)}, u32[]{:S(2)}, u32[]{:S(2)}) collective-permute-start(bf16[384,128]{1,0:T(8,128)(2,1)} %attend1.1.refs_1_), channel_id=1, source_target_pairs={{0,4},{2,6},{4,0},{6,2},{8,12},{10,14},{12,8},{14,10},{1,5},{3,7},... | collective-permute-start | bytes 294920 | tf_op jit(solution)/shard_map/ppermute | solution.py:473
  78.0 0.5 collective-permute-start.22
  78.5 1.5 %collective-permute-start.21 = (bf16[384,128]{1,0:T(8,128)(2,1)S(1)}, bf16[384,128]{1,0:T(8,128)(2,1)S(1)}, u32[]{:S(2)}, u32[]{:S(2)}) collective-permute-start(bf16[384,128]{1,0:T(8,128)(2,1)S(1)} %collective-permute-done.17.refs_3_), channel_id=1, source_target_pairs={{0,2},{2,0},{4,6},{6,4},{8,10},{10,8},{12,14},{14,12},{1,3},{3,1},... | collective-permute-start | bytes 294920 | tf_op jit(solution)/shard_map/ppermute | solution.py:475
  80.0 0.5 collective-permute-done.11.refs_4_
  80.5 0.5 collective-permute-start.20
  81.1 2.5 %collective-permute-done.10.refs_3_ = bf16[384,128]{1,0:T(8,128)(2,1)S(1)} collective-permute-done((bf16[384,128]{1,0:T(8,128)(2,1)}, bf16[384,128]{1,0:T(8,128)(2,1)S(1)}, u32[]{:S(2)}, u32[]{:S(2)}) %collective-permute-start.10) | collective-permute-done | bytes 98336 | tf_op jit(solution)/shard_map/ppermute | solution.py:473
  83.5 0.5 collective-permute-start.12
  84.1 1.5 %collective-permute-start.15 = (bf16[384,128]{1,0:T(8,128)(2,1)S(1)}, bf16[384,128]{1,0:T(8,128)(2,1)S(1)}, u32[]{:S(2)}, u32[]{:S(2)}) collective-permute-start(bf16[384,128]{1,0:T(8,128)(2,1)S(1)} %collective-permute-done.11.refs_4_), channel_id=1, source_target_pairs={{0,2},{2,0},{4,6},{6,4},{8,10},{10,8},{12,14},{14,12},{1,3},{3,1},... | collective-permute-start | bytes 294920 | tf_op jit(solution)/shard_map/ppermute | solution.py:475
  85.6 0.5 collective-permute-start.14
  86.1 1.5 %collective-permute-start.13 = (bf16[384,128]{1,0:T(8,128)(2,1)S(1)}, bf16[384,128]{1,0:T(8,128)(2,1)S(1)}, u32[]{:S(2)}, u32[]{:S(2)}) collective-permute-start(bf16[384,128]{1,0:T(8,128)(2,1)S(1)} %collective-permute-done.9.refs_2_), channel_id=1, source_target_pairs={{0,2},{2,0},{4,6},{6,4},{8,10},{10,8},{12,14},{14,12},{1,3},{3,1},... | collective-permute-start | bytes 294920 | tf_op jit(solution)/shard_map/ppermute | solution.py:475
  87.6 0.6 copy-done.20
  88.3 6.1 %output0.1.refs_11_ = f32[192,1024]{1,0:T(8,128)} custom-call(s32[3]{0:T(128)} %pad_add_fusion.refs_0_, bf16[384,128]{1,0:T(8,128)(2,1)} %get-tuple-element.20.refs_1_, bf16[384,128]{1,0:T(8,128)(2,1)} %copy-done.12, bf16[384,128]{1,0:T(8,128)(2,1)} %copy-done.10, bf16[384,128]{1,0:T(8,128)(2,1)} %copy-done.9, bf16[384,128]{1,0:T(8,128)(2,1)} %copy-done.8, ...), custom_call_target="tpu_custom_call" | custom-call | flops 805306368 | bytes 4194304 | tf_op jit(solution)/shard_map/output0/pallas_call | solution.py:381
  94.5 0.5 copy-done.15
  95.0 0.0 copy-done.17
  95.0 0.0 copy-done.19
  95.1 0.6 copy-done.21
  95.7 6.1 %output1.1 = (f32[96,1024]{1,0:T(8,128)}, bf16[96,1024]{1,0:T(8,128)(2,1)}) custom-call(s32[3]{0:T(128)} %pad_add_fusion.refs_0_, bf16[384,128]{1,0:T(8,128)(2,1)} %attend1.1.refs_1_, bf16[384,128]{1,0:T(8,128)(2,1)} %copy-done.14, bf16[384,128]{1,0:T(8,128)(2,1)} %copy-done.13, bf16[384,128]{1,0:T(8,128)(2,1)} %copy-done.11, bf16[384,128]{1,0:T(8,128)(2,1)} %copy-done.15, ...), custom_call_target="tpu_custom_call" | custom-call | flops 805306368 | bytes 4194304 | tf_op jit(solution)/shard_map/output1/pallas_call | solution.py:381
  101.8 1.6 %collective-permute-done.23 = bf16[96,1024]{1,0:T(8,128)(2,1)S(1)} collective-permute-done((bf16[96,1024]{1,0:T(8,128)(2,1)}, bf16[96,1024]{1,0:T(8,128)(2,1)S(1)}, u32[]{:S(2)}, u32[]{:S(2)}) %collective-permute-start.23) | collective-permute-done | bytes 196640 | tf_op jit(solution)/shard_map/ppermute | solution.py:487
  103.4 1.7 %add_convert_fusion = bf16[96,1024]{1,0:T(8,128)(2,1)} fusion(bf16[96,1024]{1,0:T(8,128)(2,1)S(1)} %collective-permute-done.23, f32[96,1024]{1,0:T(8,128)} %get-tuple-element.21, bf16[96,1024]{1,0:T(8,128)(2,1)S(1)} %copy-done.1), kind=kLoop, calls=%fused_computation | loop fusion | flops 491520 | bytes 983040 | tf_op jit(solution)/shard_map/convert_element_type | solution.py:488
  (61 shorter events, 0.1 us)
Async XLA Ops:
  0.0 1.7 %collective-permute-start = (bf16[96,1024]{1,0:T(8,128)(2,1)}, bf16[96,1024]{1,0:T(8,128)(2,1)S(1)}, u32[]{:S(2)}, u32[]{:S(2)}) collective-permute-start(bf16[96,1024]{1,0:T(8,128)(2,1)} %refs_1_.3), channel_id=1, source_target_pairs={{0,1},{1,0},{2,3},{3,2},{4,5},{5,4},{6,7},{7,6},{8,9},{9,8},{10,11... | collective-permute-start | bytes 589832 | tf_op jit(solution)/shard_map/ppermute | solution.py:428
  1.7 0.7 copy-start.23
  8.1 15.8 %collective-permute-start.5 = (bf16[4,512,128]{2,1,0:T(8,128)(2,1)}, bf16[4,512,128]{2,1,0:T(8,128)(2,1)S(1)}, u32[]{:S(2)}, u32[]{:S(2)}) collective-permute-start(bf16[4,512,128]{2,1,0:T(8,128)(2,1)} %get-tuple-element.18), channel_id=1, source_target_pairs={{0,2},{2,0},{4,6},{6,4},{8,10},{10,8},{12,14},{14,12},{1,3},{3,1},... | collective-permute-start | bytes 1572872 | tf_op jit(solution)/shard_map/ppermute | solution.py:452
  11.0 5.3 %copy-start.22 = (s32[192]{0:T(256)S(1)}, s32[192]{0:T(256)}, u32[]{:S(2)}) copy-start(s32[192]{0:T(256)} %refs_1_.5) | copy-start | bytes 2308
  11.0 12.9 %copy-start = (bf16[4,512,128]{2,1,0:T(8,128)(2,1)S(1)}, bf16[4,512,128]{2,1,0:T(8,128)(2,1)}, u32[]{:S(2)}) copy-start(bf16[4,512,128]{2,1,0:T(8,128)(2,1)} %get-tuple-element.17) | copy-start | bytes 1572868
  16.2 17.7 %collective-permute-start.1 = (bf16[4,480,128]{2,1,0:T(8,128)(2,1)}, bf16[4,480,128]{2,1,0:T(8,128)(2,1)S(1)}, u32[]{:S(2)}, u32[]{:S(2)}) collective-permute-start(bf16[4,480,128]{2,1,0:T(8,128)(2,1)} %get-tuple-element.16), channel_id=1, source_target_pairs={{0,2},{2,0},{4,6},{6,4},{8,10},{10,8},{12,14},{14,12},{1,3},{3,1},... | collective-permute-start | bytes 1474568 | tf_op jit(solution)/shard_map/ppermute | solution.py:452
  24.7 17.9 %collective-permute-start.8 = (bf16[512,128]{1,0:T(8,128)(2,1)S(1)}, bf16[512,128]{1,0:T(8,128)(2,1)S(1)}, u32[]{:S(2)}, u32[]{:S(2)}) collective-permute-start(bf16[512,128]{1,0:T(8,128)(2,1)S(1)} %get-tuple-element.23), channel_id=1, source_target_pairs={{0,12},{2,14},{4,8},{6,10},{8,4},{10,6},{12,0},{14,2},{1,13},{3,15... | collective-permute-start | bytes 393224 | tf_op jit(solution)/shard_map/ppermute | solution.py:458
  35.8 29.7 %collective-permute-start.4 = (bf16[480,128]{1,0:T(8,128)(2,1)S(1)}, bf16[480,128]{1,0:T(8,128)(2,1)S(1)}, u32[]{:S(2)}, u32[]{:S(2)}) collective-permute-start(bf16[480,128]{1,0:T(8,128)(2,1)S(1)} %get-tuple-element.27), channel_id=1, source_target_pairs={{0,12},{2,14},{4,8},{6,10},{8,4},{10,6},{12,0},{14,2},{1,13},{3,15... | collective-permute-start | bytes 368648 | tf_op jit(solution)/shard_map/ppermute | solution.py:458
  39.6 25.8 %collective-permute-start.3 = (bf16[480,128]{1,0:T(8,128)(2,1)S(1)}, bf16[480,128]{1,0:T(8,128)(2,1)S(1)}, u32[]{:S(2)}, u32[]{:S(2)}) collective-permute-start(bf16[480,128]{1,0:T(8,128)(2,1)S(1)} %get-tuple-element.28), channel_id=1, source_target_pairs={{0,8},{2,10},{4,12},{6,14},{8,0},{10,2},{12,4},{14,6},{1,9},{3,11}... | collective-permute-start | bytes 368648 | tf_op jit(solution)/shard_map/ppermute | solution.py:458
  39.6 27.7 %collective-permute-start.2 = (bf16[480,128]{1,0:T(8,128)(2,1)S(1)}, bf16[480,128]{1,0:T(8,128)(2,1)S(1)}, u32[]{:S(2)}, u32[]{:S(2)}) collective-permute-start(bf16[480,128]{1,0:T(8,128)(2,1)S(1)} %get-tuple-element.29), channel_id=1, source_target_pairs={{0,4},{2,6},{4,0},{6,2},{8,12},{10,14},{12,8},{14,10},{1,5},{3,7},... | collective-permute-start | bytes 368648 | tf_op jit(solution)/shard_map/ppermute | solution.py:458
  40.2 14.9 %collective-permute-start.7 = (bf16[512,128]{1,0:T(8,128)(2,1)S(1)}, bf16[512,128]{1,0:T(8,128)(2,1)S(1)}, u32[]{:S(2)}, u32[]{:S(2)}) collective-permute-start(bf16[512,128]{1,0:T(8,128)(2,1)S(1)} %get-tuple-element.24), channel_id=1, source_target_pairs={{0,8},{2,10},{4,12},{6,14},{8,0},{10,2},{12,4},{14,6},{1,9},{3,11}... | collective-permute-start | bytes 393224 | tf_op jit(solution)/shard_map/ppermute | solution.py:458
  42.5 12.6 %copy-start.2 = (bf16[512,128]{1,0:T(8,128)(2,1)}, bf16[512,128]{1,0:T(8,128)(2,1)S(1)}, u32[]{:S(2)}) copy-start(bf16[512,128]{1,0:T(8,128)(2,1)S(1)} %collective-permute-done.8.refs_5_) | copy-start | bytes 393220
  42.6 12.5 %collective-permute-start.6 = (bf16[512,128]{1,0:T(8,128)(2,1)S(1)}, bf16[512,128]{1,0:T(8,128)(2,1)S(1)}, u32[]{:S(2)}, u32[]{:S(2)}) collective-permute-start(bf16[512,128]{1,0:T(8,128)(2,1)S(1)} %get-tuple-element.25), channel_id=1, source_target_pairs={{0,4},{2,6},{4,0},{6,2},{8,12},{10,14},{12,8},{14,10},{1,5},{3,7},... | collective-permute-start | bytes 393224 | tf_op jit(solution)/shard_map/ppermute | solution.py:458
  55.1 0.7 copy-start.3
  55.1 0.7 copy-start.4
  61.5 14.6 %collective-permute-start.19 = (bf16[384,128]{1,0:T(8,128)(2,1)}, bf16[384,128]{1,0:T(8,128)(2,1)S(1)}, u32[]{:S(2)}, u32[]{:S(2)}) collective-permute-start(bf16[384,128]{1,0:T(8,128)(2,1)} %get-tuple-element.20.refs_1_), channel_id=1, source_target_pairs={{0,2},{2,0},{4,6},{6,4},{8,10},{10,8},{12,14},{14,12},{1,3},{3,1},... | collective-permute-start | bytes 294920 | tf_op jit(solution)/shard_map/ppermute | solution.py:475
  63.0 13.1 %collective-permute-start.18 = (bf16[384,128]{1,0:T(8,128)(2,1)}, bf16[384,128]{1,0:T(8,128)(2,1)S(1)}, u32[]{:S(2)}, u32[]{:S(2)}) collective-permute-start(bf16[384,128]{1,0:T(8,128)(2,1)} %get-tuple-element.20.refs_1_), channel_id=1, source_target_pairs={{0,12},{2,14},{4,8},{6,10},{8,4},{10,6},{12,0},{14,2},{1,13},{3,15... | collective-permute-start | bytes 294920 | tf_op jit(solution)/shard_map/ppermute | solution.py:473
  65.5 1.9 %copy-start.5 = (bf16[480,128]{1,0:T(8,128)(2,1)}, bf16[480,128]{1,0:T(8,128)(2,1)S(1)}, u32[]{:S(2)}) copy-start(bf16[480,128]{1,0:T(8,128)(2,1)S(1)} %collective-permute-done.4.refs_5_) | copy-start | bytes 368644
  65.5 12.5 %collective-permute-start.17 = (bf16[384,128]{1,0:T(8,128)(2,1)}, bf16[384,128]{1,0:T(8,128)(2,1)S(1)}, u32[]{:S(2)}, u32[]{:S(2)}) collective-permute-start(bf16[384,128]{1,0:T(8,128)(2,1)} %get-tuple-element.20.refs_1_), channel_id=1, source_target_pairs={{0,8},{2,10},{4,12},{6,14},{8,0},{10,2},{12,4},{14,6},{1,9},{3,11}... | collective-permute-start | bytes 294920 | tf_op jit(solution)/shard_map/ppermute | solution.py:473
  65.5 1.9 %copy-start.6 = (bf16[480,128]{1,0:T(8,128)(2,1)}, bf16[480,128]{1,0:T(8,128)(2,1)S(1)}, u32[]{:S(2)}) copy-start(bf16[480,128]{1,0:T(8,128)(2,1)S(1)} %collective-permute-done.3.refs_4_) | copy-start | bytes 368644
  65.5 13.0 %collective-permute-start.16 = (bf16[384,128]{1,0:T(8,128)(2,1)}, bf16[384,128]{1,0:T(8,128)(2,1)S(1)}, u32[]{:S(2)}, u32[]{:S(2)}) collective-permute-start(bf16[384,128]{1,0:T(8,128)(2,1)} %get-tuple-element.20.refs_1_), channel_id=1, source_target_pairs={{0,4},{2,6},{4,0},{6,2},{8,12},{10,14},{12,8},{14,10},{1,5},{3,7},... | collective-permute-start | bytes 294920 | tf_op jit(solution)/shard_map/ppermute | solution.py:473
  67.4 0.6 copy-start.7
  73.6 29.9 %copy-start.1 = (bf16[96,1024]{1,0:T(8,128)(2,1)S(1)}, bf16[96,1024]{1,0:T(8,128)(2,1)}, u32[]{:S(2)}) copy-start(bf16[96,1024]{1,0:T(8,128)(2,1)} %refs_1_.3) | copy-start | bytes 589828
  73.6 6.9 %collective-permute-start.11 = (bf16[384,128]{1,0:T(8,128)(2,1)}, bf16[384,128]{1,0:T(8,128)(2,1)S(1)}, u32[]{:S(2)}, u32[]{:S(2)}) collective-permute-start(bf16[384,128]{1,0:T(8,128)(2,1)} %attend1.1.refs_1_), channel_id=1, source_target_pairs={{0,12},{2,14},{4,8},{6,10},{8,4},{10,6},{12,0},{14,2},{1,13},{3,15... | collective-permute-start | bytes 294920 | tf_op jit(solution)/shard_map/ppermute | solution.py:473
  76.1 11.5 %copy-start.8 = (bf16[384,128]{1,0:T(8,128)(2,1)}, bf16[384,128]{1,0:T(8,128)(2,1)S(1)}, u32[]{:S(2)}) copy-start(bf16[384,128]{1,0:T(8,128)(2,1)S(1)} %collective-permute-done.19.refs_5_) | copy-start | bytes 294916
  76.1 7.4 %collective-permute-start.10 = (bf16[384,128]{1,0:T(8,128)(2,1)}, bf16[384,128]{1,0:T(8,128)(2,1)S(1)}, u32[]{:S(2)}, u32[]{:S(2)}) collective-permute-start(bf16[384,128]{1,0:T(8,128)(2,1)} %attend1.1.refs_1_), channel_id=1, source_target_pairs={{0,8},{2,10},{4,12},{6,14},{8,0},{10,2},{12,4},{14,6},{1,9},{3,11}... | collective-permute-start | bytes 294920 | tf_op jit(solution)/shard_map/ppermute | solution.py:473
  76.1 11.5 %copy-start.9 = (bf16[384,128]{1,0:T(8,128)(2,1)}, bf16[384,128]{1,0:T(8,128)(2,1)S(1)}, u32[]{:S(2)}) copy-start(bf16[384,128]{1,0:T(8,128)(2,1)S(1)} %collective-permute-done.18.refs_4_) | copy-start | bytes 294916
  76.1 8.0 %collective-permute-start.9 = (bf16[384,128]{1,0:T(8,128)(2,1)}, bf16[384,128]{1,0:T(8,128)(2,1)S(1)}, u32[]{:S(2)}, u32[]{:S(2)}) collective-permute-start(bf16[384,128]{1,0:T(8,128)(2,1)} %attend1.1.refs_1_), channel_id=1, source_target_pairs={{0,4},{2,6},{4,0},{6,2},{8,12},{10,14},{12,8},{14,10},{1,5},{3,7},... | collective-permute-start | bytes 294920 | tf_op jit(solution)/shard_map/ppermute | solution.py:473
  78.0 9.6 %copy-start.10 = (bf16[384,128]{1,0:T(8,128)(2,1)}, bf16[384,128]{1,0:T(8,128)(2,1)S(1)}, u32[]{:S(2)}) copy-start(bf16[384,128]{1,0:T(8,128)(2,1)S(1)} %collective-permute-done.17.refs_3_) | copy-start | bytes 294916
  78.0 7.6 %collective-permute-start.22 = (bf16[384,128]{1,0:T(8,128)(2,1)S(1)}, bf16[384,128]{1,0:T(8,128)(2,1)S(1)}, u32[]{:S(2)}, u32[]{:S(2)}) collective-permute-start(bf16[384,128]{1,0:T(8,128)(2,1)S(1)} %collective-permute-done.18.refs_4_), channel_id=1, source_target_pairs={{0,2},{2,0},{4,6},{6,4},{8,10},{10,8},{12,14},{14,12},{1,3},{3,1},... | collective-permute-start | bytes 294920 | tf_op jit(solution)/shard_map/ppermute | solution.py:475
  78.5 9.1 %copy-start.12 = (bf16[384,128]{1,0:T(8,128)(2,1)}, bf16[384,128]{1,0:T(8,128)(2,1)S(1)}, u32[]{:S(2)}) copy-start(bf16[384,128]{1,0:T(8,128)(2,1)S(1)} %collective-permute-done.16.refs_2_) | copy-start | bytes 294916
  78.5 7.6 %collective-permute-start.21 = (bf16[384,128]{1,0:T(8,128)(2,1)S(1)}, bf16[384,128]{1,0:T(8,128)(2,1)S(1)}, u32[]{:S(2)}, u32[]{:S(2)}) collective-permute-start(bf16[384,128]{1,0:T(8,128)(2,1)S(1)} %collective-permute-done.17.refs_3_), channel_id=1, source_target_pairs={{0,2},{2,0},{4,6},{6,4},{8,10},{10,8},{12,14},{14,12},{1,3},{3,1},... | collective-permute-start | bytes 294920 | tf_op jit(solution)/shard_map/ppermute | solution.py:475
  80.5 13.9 %copy-start.11 = (bf16[384,128]{1,0:T(8,128)(2,1)}, bf16[384,128]{1,0:T(8,128)(2,1)S(1)}, u32[]{:S(2)}) copy-start(bf16[384,128]{1,0:T(8,128)(2,1)S(1)} %collective-permute-done.11.refs_4_) | copy-start | bytes 294916
  80.5 7.1 %collective-permute-start.20 = (bf16[384,128]{1,0:T(8,128)(2,1)S(1)}, bf16[384,128]{1,0:T(8,128)(2,1)S(1)}, u32[]{:S(2)}, u32[]{:S(2)}) collective-permute-start(bf16[384,128]{1,0:T(8,128)(2,1)S(1)} %collective-permute-done.16.refs_2_), channel_id=1, source_target_pairs={{0,2},{2,0},{4,6},{6,4},{8,10},{10,8},{12,14},{14,12},{1,3},{3,1},... | collective-permute-start | bytes 294920 | tf_op jit(solution)/shard_map/ppermute | solution.py:475
  83.5 10.9 %copy-start.13 = (bf16[384,128]{1,0:T(8,128)(2,1)}, bf16[384,128]{1,0:T(8,128)(2,1)S(1)}, u32[]{:S(2)}) copy-start(bf16[384,128]{1,0:T(8,128)(2,1)S(1)} %collective-permute-done.10.refs_3_) | copy-start | bytes 294916
  83.5 10.9 %collective-permute-start.12 = (bf16[384,128]{1,0:T(8,128)(2,1)}, bf16[384,128]{1,0:T(8,128)(2,1)S(1)}, u32[]{:S(2)}, u32[]{:S(2)}) collective-permute-start(bf16[384,128]{1,0:T(8,128)(2,1)} %attend1.1.refs_1_), channel_id=1, source_target_pairs={{0,2},{2,0},{4,6},{6,4},{8,10},{10,8},{12,14},{14,12},{1,3},{3,1},... | collective-permute-start | bytes 294920 | tf_op jit(solution)/shard_map/ppermute | solution.py:475
  84.1 10.4 %copy-start.14 = (bf16[384,128]{1,0:T(8,128)(2,1)}, bf16[384,128]{1,0:T(8,128)(2,1)S(1)}, u32[]{:S(2)}) copy-start(bf16[384,128]{1,0:T(8,128)(2,1)S(1)} %collective-permute-done.9.refs_2_) | copy-start | bytes 294916
  84.1 10.3 %collective-permute-start.15 = (bf16[384,128]{1,0:T(8,128)(2,1)S(1)}, bf16[384,128]{1,0:T(8,128)(2,1)S(1)}, u32[]{:S(2)}, u32[]{:S(2)}) collective-permute-start(bf16[384,128]{1,0:T(8,128)(2,1)S(1)} %collective-permute-done.11.refs_4_), channel_id=1, source_target_pairs={{0,2},{2,0},{4,6},{6,4},{8,10},{10,8},{12,14},{14,12},{1,3},{3,1},... | collective-permute-start | bytes 294920 | tf_op jit(solution)/shard_map/ppermute | solution.py:475
  85.6 2.1 %copy-start.16 = (bf16[384,128]{1,0:T(8,128)(2,1)}, bf16[384,128]{1,0:T(8,128)(2,1)S(1)}, u32[]{:S(2)}) copy-start(bf16[384,128]{1,0:T(8,128)(2,1)S(1)} %collective-permute-done.22.refs_8_) | copy-start | bytes 294916
  85.6 8.8 %collective-permute-start.14 = (bf16[384,128]{1,0:T(8,128)(2,1)S(1)}, bf16[384,128]{1,0:T(8,128)(2,1)S(1)}, u32[]{:S(2)}, u32[]{:S(2)}) collective-permute-start(bf16[384,128]{1,0:T(8,128)(2,1)S(1)} %collective-permute-done.10.refs_3_), channel_id=1, source_target_pairs={{0,2},{2,0},{4,6},{6,4},{8,10},{10,8},{12,14},{14,12},{1,3},{3,1},... | collective-permute-start | bytes 294920 | tf_op jit(solution)/shard_map/ppermute | solution.py:475
  86.1 1.5 %copy-start.18 = (bf16[384,128]{1,0:T(8,128)(2,1)}, bf16[384,128]{1,0:T(8,128)(2,1)S(1)}, u32[]{:S(2)}) copy-start(bf16[384,128]{1,0:T(8,128)(2,1)S(1)} %collective-permute-done.21.refs_7_) | copy-start | bytes 294916
  86.1 8.3 %collective-permute-start.13 = (bf16[384,128]{1,0:T(8,128)(2,1)S(1)}, bf16[384,128]{1,0:T(8,128)(2,1)S(1)}, u32[]{:S(2)}, u32[]{:S(2)}) collective-permute-start(bf16[384,128]{1,0:T(8,128)(2,1)S(1)} %collective-permute-done.9.refs_2_), channel_id=1, source_target_pairs={{0,2},{2,0},{4,6},{6,4},{8,10},{10,8},{12,14},{14,12},{1,3},{3,1},... | collective-permute-start | bytes 294920 | tf_op jit(solution)/shard_map/ppermute | solution.py:475
  87.6 0.6 copy-start.20
  94.4 0.6 copy-start.15
  94.4 0.7 copy-start.17
  94.4 0.7 copy-start.19
  95.1 0.6 copy-start.21
  101.8 1.7 %collective-permute-start.23 = (bf16[96,1024]{1,0:T(8,128)(2,1)}, bf16[96,1024]{1,0:T(8,128)(2,1)S(1)}, u32[]{:S(2)}, u32[]{:S(2)}) collective-permute-start(bf16[96,1024]{1,0:T(8,128)(2,1)} %get-tuple-element.22), channel_id=1, source_target_pairs={{0,1},{1,0},{2,3},{3,2},{4,5},{5,4},{6,7},{7,6},{8,9},{9,8},{10,11... | collective-permute-start | bytes 589832 | tf_op jit(solution)/shard_map/ppermute | solution.py:487

commit v3 on v0

v3 whole, which is shorter than its diff:
```python
import functools
import math

import jax
import jax.numpy as jnp
from jax import lax
from jax.experimental import pallas as pl
from jax.experimental.pallas import tpu as pltpu
from jax.sharding import PartitionSpec as P

MODEL_WIDTH = 8192
QUERY_HEADS = 64
KEY_VALUE_HEADS = 8
HEAD_SIZE = 128
QUERIES_PER_KV = QUERY_HEADS // KEY_VALUE_HEADS
TILES = QUERIES_PER_KV + 2
SQUARE_ROWS = 32

EPSILON = 1e-06
ROPE_BASE = 1000000.0
CHUNKS = 2
SLOTS_PER_STEP = 8
VMEM_LIMIT = 32 * 1024 * 1024
F32 = jnp.float32
BF16 = jnp.bfloat16


def neighbour_pairs(nz):
    return [(z * 2 + y, z * 2 + 1 - y) for z in range(nz) for y in range(2)]


def column_groups(nz):
    return [[z * 2 + y for z in range(nz)] for y in range(2)]


def slot_one_hot(place_ref, slot_of_row, nz, per):
    rows = slot_of_row.shape[1]
    base = lax.broadcasted_iota(jnp.int32, (per, rows), 0)
    blocks = []
    for h in range(2):
        for z in range(nz):
            owner = z * 2 + (place_ref[1] ^ h)
            blocks.append(jnp.where(base + owner * per == slot_of_row, 1.0, 0.0).astype(F32))
    return jnp.concatenate(blocks, axis=0).astype(BF16)


def load_kernel(*refs, windows):
    count = len(windows)
    sources, targets, sems = refs[:count], refs[-1 - count : -1], refs[-1]
    copies = [
        pltpu.make_async_copy(source.at[window], target, sems.at[i])
        for i, (source, target, window) in enumerate(zip(sources, targets, windows))
    ]
    for copy in copies:
        copy.start()
    for copy in copies:
        copy.wait()


def load(name, arrays, windows, after=()):
    shapes = [
        tuple(w.size if isinstance(w, pl.Slice) else n for w, n in zip(window, a.shape))
        for a, window in zip(arrays, windows)
    ]
    size = sum(2 * math.prod(shape) for shape in shapes)
    return pl.pallas_call(
        functools.partial(load_kernel, windows=windows),
        in_specs=[pl.BlockSpec(memory_space=pltpu.HBM)] * len(arrays)
        + [pl.BlockSpec(memory_space=pl.ANY)] * len(after),
        out_specs=[pl.BlockSpec(memory_space=pltpu.VMEM)] * len(arrays),
        out_shape=[pltpu.VMEM(shape, a.dtype) for a, shape in zip(arrays, shapes)],
        scratch_shapes=[pltpu.SemaphoreType.DMA((len(arrays),))],
        compiler_params=pltpu.CompilerParams(vmem_limit_bytes=VMEM_LIMIT),
        cost_estimate=pl.CostEstimate(flops=0, bytes_accessed=size, transcendentals=0),
        name=name,
    )(*[pltpu.with_memory_space_constraint(a, pltpu.HBM) for a in arrays], *after)


def on_chip(count):
    return [pl.BlockSpec(memory_space=pltpu.VMEM)] * count


SCALARS = pl.BlockSpec(memory_space=pltpu.SMEM)


def project_kernel(*refs, nz, per, first, heads):
    place_ref = refs[0]
    half = nz * per
    if first:
        own_ref, other_ref, gain_ref, sor_ref, wq_ref, wk_ref, wv_ref = refs[1:8]
        keep_ref, send_ref, slotted_ref, acc = refs[8:]
        one_hot = slot_one_hot(place_ref, sor_ref[...], nz, per)
        own, other = own_ref[...], other_ref[...]
        lower = place_ref[2] == 0
        rows = jnp.concatenate(
            [jnp.where(lower, own, other), jnp.where(lower, other, own)], axis=0
        )
        hidden = jnp.dot(one_hot, rows, preferred_element_type=F32)
        gain = gain_ref[...].astype(F32)
        gain = jnp.concatenate([gain[j : j + 1] for j in range(gain.shape[0])], axis=1)
        slotted_ref[...] = (hidden * gain).astype(BF16)
        squares = jnp.sum(hidden * hidden, axis=1, keepdims=True)
        high = squares.astype(BF16).astype(F32)
        low = squares - high
        lane = lax.broadcasted_iota(jnp.int32, (per, HEAD_SIZE), 1)
        lane_high = place_ref[1] * 2
        for h, ref in enumerate((keep_ref, send_ref)):
            for z in range(nz):
                at = h * half + z * per
                packed = jnp.where(
                    lane == lane_high,
                    high[at : at + per],
                    jnp.where(lane == lane_high + 1, low[at : at + per], 0.0),
                )
                packed = jnp.concatenate(
                    [packed, jnp.zeros((SQUARE_ROWS - per, HEAD_SIZE), F32)], axis=0
                )
                ref[z, heads * TILES * per :, :] = packed.astype(BF16)
    else:
        slotted_ref, wq_ref, wk_ref, wv_ref = refs[1:5]
        keep_ref, send_ref, acc = refs[5:]

    columns = QUERIES_PER_KV * HEAD_SIZE
    slotted = slotted_ref[...]
    for g in range(heads):
        acc[:, :columns] = jnp.dot(
            slotted, wq_ref[:, g * columns : (g + 1) * columns], preferred_element_type=F32
        )
        narrow = slice(g * HEAD_SIZE, (g + 1) * HEAD_SIZE)
        acc[:, columns:] = jnp.dot(
            slotted,
            jnp.concatenate([wk_ref[:, narrow], wv_ref[:, narrow]], axis=1),
            preferred_element_type=F32,
        )
        for h, ref in enumerate((keep_ref, send_ref)):
            for z in range(nz):
                at = h * half + z * per
                block = jnp.concatenate(
                    [
                        acc[at : at + per, c * HEAD_SIZE : (c + 1) * HEAD_SIZE]
                        for c in range(TILES)
                    ],
                    axis=0,
                )
                ref[z, g * TILES * per : (g + 1) * TILES * per, :] = block.astype(BF16)


def project(place, inputs, weights, *, chunk, heads, nz, per):
    first = chunk == 0
    rows = 2 * nz * per
    depth = weights[0].shape[0]
    block_rows = heads * TILES * per + (SQUARE_ROWS if first else 0)
    out_block = jax.ShapeDtypeStruct((nz, block_rows, HEAD_SIZE), BF16)
    slotted = jax.ShapeDtypeStruct((rows, depth), BF16)
    out_shape = [out_block, out_block] + ([slotted] if first else [])
    return pl.pallas_call(
        functools.partial(project_kernel, nz=nz, per=per, first=first, heads=heads),
        in_specs=[SCALARS] + on_chip(len(inputs) + 3),
        out_specs=on_chip(len(out_shape)),
        out_shape=out_shape,
        scratch_shapes=[pltpu.VMEM((rows, TILES * HEAD_SIZE), F32)],
        compiler_params=pltpu.CompilerParams(vmem_limit_bytes=VMEM_LIMIT),
        cost_estimate=pl.CostEstimate(
            flops=20 * rows * depth * heads * TILES * HEAD_SIZE,
            bytes_accessed=20 * depth * heads * TILES * HEAD_SIZE,
            transcendentals=0,
        ),
        name="project" + str(chunk),
    )(place, *inputs, *weights)


def attend_kernel(*refs, first, heads, per, group, chunk):
    place_ref, lengths_ref, part_ref = refs[:3]
    rest = refs[3:]
    if first:
        qb_ref, kb_ref, vb_ref, cos_ref, sin_ref, k_ref, v_ref, out_ref, scale_ref = rest[:9]
    else:
        scale_in_ref, qb_ref, kb_ref, vb_ref, cos_ref, sin_ref, k_ref, v_ref, out_ref = rest[:9]
    fresh, result = rest[9:]
    body = heads * TILES * per
    head_rows = TILES * per
    parts = part_ref.shape[0]

    if first:
        squares = part_ref[0, body:, :].astype(F32)
        for z in range(1, parts):
            squares = squares + part_ref[z, body:, :].astype(F32)
        total = jnp.sum(squares[:per], axis=1, keepdims=True)
        scale = jnp.broadcast_to(lax.rsqrt(total / MODEL_WIDTH + EPSILON), (per, HEAD_SIZE))
        scale_ref[...] = scale
    else:
        scale = scale_in_ref[...]
    cos, sin = cos_ref[...], sin_ref[...]
    query_bias = qb_ref[...].astype(F32)
    key_bias = kb_ref[...].astype(F32)
    value_bias = vb_ref[...].astype(F32)
    for g in range(heads):
        rows = pl.ds(g * head_rows, head_rows)
        summed = part_ref[0, rows, :].astype(F32)
        for z in range(1, parts):
            summed = summed + part_ref[z, rows, :].astype(F32)
        head = chunk * heads + g
        for c in range(TILES):
            if c < QUERIES_PER_KV:
                at = head * QUERIES_PER_KV + c
                bias = query_bias[at : at + 1]
            else:
                bias = (key_bias if c == QUERIES_PER_KV else value_bias)[head : head + 1]
            tile = summed[c * per : (c + 1) * per] * scale + bias
            if c < TILES - 1:
                tile = tile * cos + pltpu.roll(tile, HEAD_SIZE // 2, 1) * sin
            fresh[pl.ds(g * head_rows + c * per, per), :] = tile.astype(BF16).astype(F32)

    positions = k_ref.shape[1]
    qrows = heads * QUERIES_PER_KV
    lanes = group * qrows
    extra = 16
    lane_block = lax.broadcasted_iota(jnp.int32, (HEAD_SIZE, lanes), 1) // QUERIES_PER_KV
    top_row = lax.broadcasted_iota(jnp.int32, (extra, HEAD_SIZE), 0) == 0
    lane_slot = lax.broadcasted_iota(jnp.int32, (1, lanes), 1) // qrows
    row = lax.broadcasted_iota(jnp.int32, (positions + extra, lanes), 0)
    base = (place_ref[0] * 2 + place_ref[1]) * per
    for start in range(0, per, group):
        slots = range(start, start + group)
        queries = jnp.concatenate(
            [
                fresh[pl.ds(g * head_rows + s, QUERIES_PER_KV, stride=per), :]
                for s in slots
                for g in range(heads)
            ],
            axis=0,
        )
        turned = queries.T
        scores = None
        for i, s in enumerate(slots):
            query, new_key = [], []
            for g in range(heads):
                query.append(jnp.where(lane_block == i * heads + g, turned, 0.0).astype(BF16))
                key = fresh[pl.ds(g * head_rows + QUERIES_PER_KV * per + s, 1), :]
                new_key.append(jnp.where(top_row, key, 0.0).astype(BF16))
            keys = jnp.concatenate([k_ref[s], jnp.concatenate(new_key, axis=1)], axis=0)
            term = jnp.dot(keys, jnp.concatenate(query, axis=0), preferred_element_type=F32)
            scores = term if scores is None else scores + term

        lengths = jnp.zeros((1, lanes), jnp.int32)
        for i, s in enumerate(slots):
            lengths = jnp.where(lane_slot == i, lengths_ref[base + s], lengths)
        valid = (row < lengths) | (row == positions)
        scores = jnp.where(valid, scores * (1.0 / math.sqrt(HEAD_SIZE)), -1e30)
        top = jnp.max(scores, axis=0, keepdims=True)
        exps = jnp.where(valid, jnp.exp(scores - top), 0.0)
        weights = exps * (1.0 / jnp.sum(exps, axis=0, keepdims=True))
        cache_weights = weights[:positions].T.astype(BF16)
        own_weights = weights[positions : positions + 8].T[:, 0:1].astype(BF16).astype(F32)
        for i, s in enumerate(slots):
            mixed = jnp.dot(
                cache_weights[i * qrows : (i + 1) * qrows], v_ref[s], preferred_element_type=F32
            )
            for g in range(heads):
                lo, hi = g * QUERIES_PER_KV, (g + 1) * QUERIES_PER_KV
                new_value = fresh[pl.ds(g * head_rows + (QUERIES_PER_KV + 1) * per + s, 1), :]
                result[pl.ds(g * QUERIES_PER_KV * per + s, QUERIES_PER_KV, stride=per), :] = (
                    mixed[lo:hi, g * HEAD_SIZE : (g + 1) * HEAD_SIZE]
                    + own_weights[i * qrows + lo : i * qrows + hi] * new_value
                )
    out_ref[...] = result[...].astype(BF16)


def attend(place, lengths, part, scale, biases, cos, sin, keys, values, *, chunk, heads):
    first = chunk == 0
    per, positions = keys.shape[0], keys.shape[1]
    ins = [part] + ([] if first else [scale]) + list(biases) + [cos, sin, keys, values]
    out_rows = heads * QUERIES_PER_KV * per
    out_shape = [jax.ShapeDtypeStruct((out_rows, HEAD_SIZE), BF16)]
    if first:
        out_shape.append(jax.ShapeDtypeStruct((per, HEAD_SIZE), F32))
    return pl.pallas_call(
        functools.partial(
            attend_kernel, first=first, heads=heads, per=per, group=SLOTS_PER_STEP, chunk=chunk
        ),
        in_specs=[SCALARS, SCALARS] + on_chip(len(ins)),
        out_specs=on_chip(len(out_shape)),
        out_shape=out_shape,
        scratch_shapes=[
            pltpu.VMEM((heads * TILES * per, HEAD_SIZE), F32),
            pltpu.VMEM((out_rows, HEAD_SIZE), F32),
        ],
        compiler_params=pltpu.CompilerParams(vmem_limit_bytes=VMEM_LIMIT),
        cost_estimate=pl.CostEstimate(
            flops=4 * per * heads * QUERIES_PER_KV * positions * HEAD_SIZE,
            bytes_accessed=4 * per * positions * heads * HEAD_SIZE,
            transcendentals=per * heads * QUERIES_PER_KV * positions,
        ),
        name="attend" + str(chunk),
    )(place, lengths, *ins)


def output_kernel(*refs, nz, per, first, last):
    place_ref, here_ref, there_ref, sor_ref, w_ref = refs[:5]
    rest = refs[5:]
    if not first:
        acc_in_ref, rest = rest[0], rest[1:]
    if last:
        mine_ref, send_ref, stacked, total = rest
    else:
        acc_out_ref, stacked = rest
    tiles = here_ref.shape[1] // per

    one_hot = slot_one_hot(place_ref, sor_ref[...], nz, per)
    wide = [ref[z].astype(F32) for ref in (here_ref, there_ref) for z in range(nz)]
    for c in range(tiles):
        stacked[:, c * HEAD_SIZE : (c + 1) * HEAD_SIZE] = jnp.concatenate(
            [block[c * per : (c + 1) * per] for block in wide], axis=0
        ).astype(BF16)
    permuted = lax.dot_general(
        one_hot, stacked[...], (((0,), (0,)), ((), ())), preferred_element_type=F32
    ).astype(BF16)
    stacked[...] = permuted
    product = jnp.dot(stacked[...], w_ref[...], preferred_element_type=F32)
    if not first:
        product = product + acc_in_ref[...]
    if last:
        half = product.shape[0] // 2
        total[...] = product
        mine_ref[...] = total[pl.ds(pl.multiple_of(place_ref[2] * half, half), half), :]
        send_ref[...] = total[
            pl.ds(pl.multiple_of((1 - place_ref[2]) * half, half), half), :
        ].astype(BF16)
    else:
        acc_out_ref[...] = product


def output(place, here, there, sor, w_out, acc, *, chunk, chunks, nz, per):
    first, last = chunk == 0, chunk == chunks - 1
    rows = 2 * nz * per
    depth, width = w_out.shape
    if last:
        out_shape = [
            jax.ShapeDtypeStruct((rows // 2, width), F32),
            jax.ShapeDtypeStruct((rows // 2, width), BF16),
        ]
    else:
        out_shape = [jax.ShapeDtypeStruct((rows, width), F32)]
    ins = [here, there, sor, w_out] + ([] if first else [acc])
    return pl.pallas_call(
        functools.partial(output_kernel, nz=nz, per=per, first=first, last=last),
        in_specs=[SCALARS] + on_chip(len(ins)),
        out_specs=on_chip(len(out_shape)),
        out_shape=out_shape,
        scratch_shapes=[pltpu.VMEM((rows, depth), BF16)]
        + ([pltpu.VMEM((rows, width), F32)] if last else []),
        compiler_params=pltpu.CompilerParams(vmem_limit_bytes=VMEM_LIMIT),
        cost_estimate=pl.CostEstimate(
            flops=2 * rows * depth * width, bytes_accessed=2 * depth * width, transcendentals=0
        ),
        name="output" + str(chunk),
    )(place, *ins)


def on_device(
    hidden_rows,
    norm_gain,
    w_query,
    key_weight,
    value_weight,
    query_bias,
    key_bias_vector,
    value_bias_vector,
    rotated_key_cache,
    stored_value_cache,
    slot_valid_lengths,
    slot_of_row,
    w_out,
    *,
    size,
):
    nz = size // 2
    per = rotated_key_cache.shape[0]
    kv_heads = key_weight.shape[1] // HEAD_SIZE
    heads = kv_heads // CHUNKS
    gx = lax.axis_index("gx")
    gy = lax.axis_index("gy")
    place = jnp.stack([gx // 2, gx % 2, gy]).astype(jnp.int32)

    other = lax.ppermute(hidden_rows, "gy", [(0, 1), (1, 0)])
    sor = slot_of_row[None, :]
    gain = norm_gain.reshape(-1, HEAD_SIZE)

    lengths = lax.dynamic_slice_in_dim(slot_valid_lengths, gx * per, per, 0)
    lane = jnp.arange(HEAD_SIZE)
    half_width = HEAD_SIZE // 2
    frequency = ROPE_BASE ** (-((lane % half_width).astype(F32) * 2.0 / HEAD_SIZE))
    angles = lengths.astype(F32)[:, None] * frequency[None, :]
    cos = jnp.cos(angles)
    sin = jnp.sin(angles) * jnp.where(lane < half_width, -1.0, 1.0)[None, :]
    biases = [b.reshape(-1, HEAD_SIZE) for b in (query_bias, key_bias_vector, value_bias_vector)]

    columns = heads * QUERIES_PER_KV * HEAD_SIZE
    narrow = heads * HEAD_SIZE
    everything = pl.ds(0, w_query.shape[0])
    positions = rotated_key_cache.shape[1]
    all_columns = pl.ds(0, w_out.shape[1])

    inputs = [hidden_rows, other, gain, sor]
    after = []
    kept, swapped = [], []
    for c in range(CHUNKS):
        weights = load(
            "load_weights" + str(c),
            [w_query, key_weight, value_weight],
            [(everything, pl.ds(c * n, n)) for n in (columns, narrow, narrow)],
            after,
        )
        outs = project(place, inputs, weights, chunk=c, heads=heads, nz=nz, per=per)
        if c == 0:
            inputs = [outs[2]]
        after = [outs[0]]
        kept.append(outs[0])
        swapped.append(lax.ppermute(outs[1], "gx", neighbour_pairs(nz)))
    caches, w_outs = [], []
    for c in range(CHUNKS):
        caches.append(
            load(
                "load_caches" + str(c),
                [rotated_key_cache, stored_value_cache],
                [(pl.ds(0, per), pl.ds(0, positions), pl.ds(c * narrow, narrow))] * 2,
                after,
            )
        )
        w_outs.append(
            load("load_out" + str(c), [w_out], [(pl.ds(c * columns, columns), all_columns)], after)
        )
    parts = []
    for c in range(CHUNKS):
        pair_sum = (kept[c].astype(F32) + swapped[c].astype(F32)).astype(BF16)
        parts.append(
            lax.all_to_all(pair_sum, "gx", 0, 0, axis_index_groups=column_groups(nz), tiled=True)
        )

    scale = None
    gathered = []
    for c in range(CHUNKS):
        outs = attend(
            place, slot_valid_lengths, parts[c], scale, biases, cos, sin, *caches[c],
            chunk=c, heads=heads,
        )
        if c == 0:
            scale = outs[1]
        spread = jnp.broadcast_to(outs[0][None], (nz,) + outs[0].shape)
        here = lax.all_to_all(
            spread, "gx", 0, 0, axis_index_groups=column_groups(nz), tiled=True
        )
        gathered.append((here, lax.ppermute(here, "gx", neighbour_pairs(nz))))

    acc = None
    for c in range(CHUNKS):
        outs = output(
            place, *gathered[c], sor, w_outs[c][0], acc, chunk=c, chunks=CHUNKS, nz=nz, per=per
        )
        acc = outs[0]
    mine, send = outs
    received = lax.ppermute(send, "gy", [(0, 1), (1, 0)])
    return (hidden_rows.astype(F32) + mine + received.astype(F32)).astype(BF16)


def solution(mesh):
    in_specs = (
        P(("grp", "gy"), "gx"),
        P("gx"),
        P("gx", "gy"),
        P("gx", "gy"),
        P("gx", "gy"),
        P("gy"),
        P("gy"),
        P("gy"),
        P(("grp", "gx"), None, "gy"),
        P(("grp", "gx"), None, "gy"),
        P("grp"),
        P("grp"),
        P("gy", "gx"),
    )
    out_specs = P(("grp", "gy"), "gx")
    return jax.shard_map(
        functools.partial(on_device, size=mesh.shape["gx"]),
        mesh=mesh,
        in_specs=in_specs,
        out_specs=out_specs,
        check_vma=False,
    )
```

time: 210 us -> 101 us (0.48)
  waiting for transfers between devices: 132 us -> 41.3 us
  Pallas kernels: 0 us -> 25.4 us
  blocking collectives: 25.2 us -> 0 us
  starting transfers between devices: 0.09 us -> 24.7 us
  matrix products: 17.9 us -> 0 us
  between operations: 13.3 us -> 0.2 us
  other arithmetic: 11.9 us -> 2.94 us
  local copies, waits for them, and re-layouts: 9.26 us -> 5.78 us
    reduce_scatter x2 -> x0, waiting for transfers between devices: 87.9 us -> none  [the longest x1 80.7 us: on_device(): lax.psum_scatter(jnp.concatenate([jnp.dot(slotted, w_query, preferred_ele...]
    all_gather x1 -> x0, waiting for transfers between devices: 44 us -> none  [on_device(): lax.all_gather(attended, 'gx', axis=0, tiled=True)]
    pallas_call x0 -> x12, Pallas kernels: none -> 25.4 us  [the longest x6 13.2 us: load(): pl.pallas_call(functools.partial(load_kernel, windows=windows), in_specs=...]
    psum x1 -> x0, blocking collectives: 23.1 us -> none  [on_device(): square_sum = lax.psum(local_squares, 'gx')]
    all_to_all x0 -> x4, waiting for transfers between devices: none -> 20.7 us  [the longest x2 13.1 us: on_device(): lax.all_to_all(spread, 'gx', 0, 0, axis_index_groups=column_groups(nz), t...]
    ppermute x0 -> x6, waiting for transfers between devices: none -> 20.6 us  [the longest x2 19.2 us: on_device(): swapped.append(lax.ppermute(outs[1], 'gx', neighbour_pairs(nz)))]
    dot_general x7 -> x0, matrix products: 17.9 us -> none  [the longest x1 6.56 us: on_device(): jnp.dot(lax.all_gather(attended, 'gx', axis=0, tiled=True), w_out, prefer...]
    all_to_all x0 -> x4, starting transfers between devices: none -> 17 us  [the longest x2 10.1 us: on_device(): lax.all_to_all(pair_sum, 'gx', 0, 0, axis_index_groups=column_groups(nz),...]
  transfers between devices with their start and end apart: 3 -> 10, of which waited for: 3 -> 6; matrix products, arithmetic and copies ran while one was open for 0% -> 1% of each run, Pallas kernels for 0% -> 22%
where the time goes in v3:
time: 101 us; the launch traced here: 100 us
  waiting for transfers between devices  41.3 us (41%)
  Pallas kernels  25.4 us (25%)
  starting transfers between devices  24.7 us (24%)
  local copies, waits for them, and re-layouts  5.78 us (6%)
  other arithmetic  2.94 us (3%)
    ppermute x2, waiting for transfers between devices, on_device(): swapped.append(lax.ppermute(outs[1], 'gx', neighbour_pairs(nz)))  19.2 us
    pallas_call x6, Pallas kernels, load(): pl.pallas_call(functools.partial(load_kernel, windows=windows), in_specs=...  13.2 us
    all_to_all x2, waiting for transfers between devices, on_device(): lax.all_to_all(spread, 'gx', 0, 0, axis_index_groups=column_groups(nz), t...  13.1 us
    all_to_all x2, starting transfers between devices, on_device(): lax.all_to_all(pair_sum, 'gx', 0, 0, axis_index_groups=column_groups(nz),...  10.1 us
    all_to_all x2, waiting for transfers between devices, on_device(): lax.all_to_all(pair_sum, 'gx', 0, 0, axis_index_groups=column_groups(nz),...  7.54 us
    all_to_all x2, starting transfers between devices, on_device(): lax.all_to_all(spread, 'gx', 0, 0, axis_index_groups=column_groups(nz), t...  6.92 us
    pallas_call x2, Pallas kernels, attend(): pl.pallas_call(functools.partial(attend_kernel, first=first, heads=heads,...  4.85 us
    unnamed x18, local copies, waits for them, and re-layouts  4.17 us
  transfers between devices with their start and end apart: 10, of which 6 were waited for; matrix products, arithmetic and copies ran while one was open for 1% of the time, Pallas kernels for 22%

profile of v3, /device:TPU:0, one launch (start us, length us, event | category | flops | bytes accessed | tf_op | source)
XLA Modules:
  0.0 100.4 jit_solution(12765986812972019541)
XLA Ops:
  0.0 0.5 collective-permute-start
  0.5 2.5 %load_weights0.1 = (bf16[1024,2048]{1,0:T(8,128)(2,1)S(1)}, bf16[1024,256]{1,0:T(8,128)(2,1)S(1)}, bf16[1024,256]{1,0:T(8,128)(2,1)S(1)}) custom-call(bf16[1024,4096]{1,0:T(8,128)(2,1)} %refs_0_.7, bf16[1024,512]{1,0:T(8,128)(2,1)} %refs_1_.9, bf16[1024,512]{1,0:T(8,128)(2,1)} %refs_2_.3), custom_call_target="tpu_custom_call" | custom-call | bytes 5242880 | tf_op jit(solution)/shard_map/load_weights0/pallas_call | solution.py:66
  3.0 0.1 pad_add_fusion.refs_0_
  3.1 0.0 collective-permute-done.refs_2_
  3.1 0.0 copy-done
  3.1 0.0 copy-done.2
  3.1 1.9 %project0.1 = (bf16[4,512,128]{2,1,0:T(8,128)(2,1)S(1)}, bf16[4,512,128]{2,1,0:T(8,128)(2,1)S(1)}, bf16[192,1024]{1,0:T(8,128)(2,1)S(1)}) custom-call(s32[3]{0:T(128)S(1)} %pad_add_fusion.refs_0_, bf16[96,1024]{1,0:T(8,128)(2,1)S(1)} %copy-done, bf16[96,1024]{1,0:T(8,128)(2,1)S(1)} %collective-permute-done.refs_2_, bf16[8,128]{1,0:T(8,128)(2,1)S(1)} %bitcast.17, ...), custom_call_target="tpu_custom_call" | custom-call | flops 10066329600 | bytes 52428800 | tf_op jit(solution)/shard_map/project0/pallas_call | solution.py:156
  5.0 2.6 %collective-permute-start.2 = (bf16[4,512,128]{2,1,0:T(8,128)(2,1)S(1)}, bf16[4,512,128]{2,1,0:T(8,128)(2,1)S(1)}, u32[]{:S(2)}, u32[]{:S(2)}) collective-permute-start(bf16[4,512,128]{2,1,0:T(8,128)(2,1)S(1)} %get-tuple-element.34), channel_id=1, source_target_pairs={{0,2},{2,0},{4,6},{6,4},{8,10},{10,8},{12,14},{14,12},{1,3},{3,1},... | collective-permute-start | bytes 1572872 | tf_op jit(solution)/shard_map/ppermute | solution.py:419
  7.6 2.5 %load_weights1.1 = (bf16[1024,2048]{1,0:T(8,128)(2,1)S(1)}, bf16[1024,256]{1,0:T(8,128)(2,1)S(1)}, bf16[1024,256]{1,0:T(8,128)(2,1)S(1)}) custom-call(bf16[1024,4096]{1,0:T(8,128)(2,1)} %refs_0_.7, bf16[1024,512]{1,0:T(8,128)(2,1)} %refs_1_.9, bf16[1024,512]{1,0:T(8,128)(2,1)} %refs_2_.3, bf16[4,512,128]{2,1,0:T(8,128)(2,1)S(1)} %get-tuple-element.28.refs_3_), custom_call_target="tpu_custom_call" | custom-call | bytes 5242880 | tf_op jit(solution)/shard_map/load_weights1/pallas_call | solution.py:66
  10.1 2.0 %copy-done.6 = bf16[1024,2048]{1,0:T(8,128)(2,1)} copy-done((bf16[1024,2048]{1,0:T(8,128)(2,1)}, bf16[1024,2048]{1,0:T(8,128)(2,1)S(1)}, u32[]{:S(2)}) %copy-start.6) | copy-done | bytes 4194328
  12.1 8.1 %collective-permute-done.2 = bf16[4,512,128]{2,1,0:T(8,128)(2,1)S(1)} collective-permute-done((bf16[4,512,128]{2,1,0:T(8,128)(2,1)S(1)}, bf16[4,512,128]{2,1,0:T(8,128)(2,1)S(1)}, u32[]{:S(2)}, u32[]{:S(2)}) %collective-permute-start.2) | collective-permute-done | bytes 524320 | tf_op jit(solution)/shard_map/ppermute | solution.py:419
  20.2 1.0 add_convert_fusion
  21.1 5.1 %all-to-all-start.1 = ((bf16[4,512,128]{2,1,0:T(8,128)(2,1)}), bf16[4,512,128]{2,1,0:T(8,128)(2,1)S(1)}, u32[]{:S(2)}, u32[]{:S(2)}) async-start(bf16[4,512,128]{2,1,0:T(8,128)(2,1)} %add_convert_fusion), calls=%async_computation.1 | async-start | bytes 1048576 | tf_op jit(solution)/shard_map/all_to_all | solution.py:437
  26.2 2.2 %copy-done.7 = bf16[1024,2048]{1,0:T(8,128)(2,1)S(1)} copy-done((bf16[1024,2048]{1,0:T(8,128)(2,1)S(1)}, bf16[1024,2048]{1,0:T(8,128)(2,1)}, u32[]{:S(2)}) %copy-start.7) | copy-done | bytes 4194328
  28.4 1.8 %project1.1 = (bf16[4,480,128]{2,1,0:T(8,128)(2,1)S(1)}, bf16[4,480,128]{2,1,0:T(8,128)(2,1)S(1)}) custom-call(s32[3]{0:T(128)S(1)} %pad_add_fusion.refs_0_, bf16[192,1024]{1,0:T(8,128)(2,1)S(1)} %get-tuple-element.27.refs_1_, bf16[1024,2048]{1,0:T(8,128)(2,1)S(1)} %copy-done.7, bf16[1024,256]{1,0:T(8,128)(2,1)S(1)} %get-tuple-element.30.refs_3_, ...), custom_call_target="tpu_custom_call" | custom-call | flops 10066329600 | bytes 52428800 | tf_op jit(solution)/shard_map/project1/pallas_call | solution.py:156
  30.2 1.6 %collective-permute-start.1 = (bf16[4,480,128]{2,1,0:T(8,128)(2,1)S(1)}, bf16[4,480,128]{2,1,0:T(8,128)(2,1)S(1)}, u32[]{:S(2)}, u32[]{:S(2)}) collective-permute-start(bf16[4,480,128]{2,1,0:T(8,128)(2,1)S(1)} %get-tuple-element.33), channel_id=1, source_target_pairs={{0,2},{2,0},{4,6},{6,4},{8,10},{10,8},{12,14},{14,12},{1,3},{3,1},... | collective-permute-start | bytes 1474568 | tf_op jit(solution)/shard_map/ppermute | solution.py:419
  31.8 11.0 %collective-permute-done.1 = bf16[4,480,128]{2,1,0:T(8,128)(2,1)S(1)} collective-permute-done((bf16[4,480,128]{2,1,0:T(8,128)(2,1)S(1)}, bf16[4,480,128]{2,1,0:T(8,128)(2,1)S(1)}, u32[]{:S(2)}, u32[]{:S(2)}) %collective-permute-start.1) | collective-permute-done | bytes 491552 | tf_op jit(solution)/shard_map/ppermute | solution.py:419
  42.8 0.9 add_convert_fusion.1
  43.8 0.0 all-to-all-done.1.refs_2_
  43.8 5.0 %all-to-all-start = ((bf16[4,480,128]{2,1,0:T(8,128)(2,1)}), bf16[4,480,128]{2,1,0:T(8,128)(2,1)S(1)}, u32[]{:S(2)}, u32[]{:S(2)}) async-start(bf16[4,480,128]{2,1,0:T(8,128)(2,1)} %add_convert_fusion.1), calls=%async_computation | async-start | bytes 983040 | tf_op jit(solution)/shard_map/all_to_all | solution.py:437
  48.7 0.0 copy-done.3
  48.7 0.1 dynamic-slice_convert_fusion
  48.8 0.1 fusion
  49.0 1.9 %load_caches0.1 = (bf16[24,128,256]{2,1,0:T(8,128)(2,1)S(1)}, bf16[24,128,256]{2,1,0:T(8,128)(2,1)S(1)}) custom-call(bf16[24,128,512]{2,1,0:T(8,128)(2,1)} %refs_0_.9, bf16[24,128,512]{2,1,0:T(8,128)(2,1)} %refs_1_.12, bf16[4,480,128]{2,1,0:T(8,128)(2,1)S(1)} %get-tuple-element.32.refs_2_.refs_1_), custom_call_target="tpu_custom_call" | custom-call | bytes 3145728 | tf_op jit(solution)/shard_map/load_caches0/pallas_call | solution.py:66
  50.9 0.0 copy-done.1
  50.9 0.0 copy-done.4
  50.9 0.0 copy-done.5
  50.9 2.5 %attend0.1 = (bf16[384,128]{1,0:T(8,128)(2,1)S(1)}, f32[24,128]{1,0:T(8,128)S(1)}) custom-call(s32[3]{0:T(128)S(1)} %pad_add_fusion.refs_0_, s32[192]{0:T(256)S(1)} %copy-done.3, bf16[4,512,128]{2,1,0:T(8,128)(2,1)S(1)} %all-to-all-done.1.refs_2_, bf16[32,128]{1,0:T(8,128)(2,1)S(1)} %bitcast.8, bf16[4,128]{1,0:T(4,128)(2,1)S(1)} %bitcast.13, ...), custom_call_target="tpu_custom_call" | custom-call | flops 25165824 | bytes 3145728 | tf_op jit(solution)/shard_map/attend0/pallas_call | solution.py:277
  53.4 7.5 %all-to-all-done.refs_2_ = bf16[4,480,128]{2,1,0:T(8,128)(2,1)S(1)} async-done(((bf16[4,480,128]{2,1,0:T(8,128)(2,1)}), bf16[4,480,128]{2,1,0:T(8,128)(2,1)S(1)}, u32[]{:S(2)}, u32[]{:S(2)}) %all-to-all-start) | async-done | bytes 491552 | tf_op jit(solution)/shard_map/all_to_all | solution.py:437
  60.9 0.8 broadcast_in_dim.30
  61.7 3.5 %all-to-all-start.3 = ((bf16[4,384,128]{2,1,0:T(8,128)(2,1)}), bf16[4,384,128]{2,1,0:T(8,128)(2,1)S(1)}, u32[]{:S(2)}, u32[]{:S(2)}) async-start(bf16[4,384,128]{2,1,0:T(8,128)(2,1)} %broadcast_in_dim.30), calls=%async_computation.3 | async-start | bytes 786432 | tf_op jit(solution)/shard_map/all_to_all | solution.py:450
  65.2 1.9 %load_caches1.1 = (bf16[24,128,256]{2,1,0:T(8,128)(2,1)S(1)}, bf16[24,128,256]{2,1,0:T(8,128)(2,1)S(1)}) custom-call(bf16[24,128,512]{2,1,0:T(8,128)(2,1)} %refs_0_.9, bf16[24,128,512]{2,1,0:T(8,128)(2,1)} %refs_1_.12, bf16[4,480,128]{2,1,0:T(8,128)(2,1)S(1)} %get-tuple-element.32.refs_2_.refs_1_), custom_call_target="tpu_custom_call" | custom-call | bytes 3145728 | tf_op jit(solution)/shard_map/load_caches1/pallas_call | solution.py:66
  67.1 2.4 %attend1.1 = bf16[384,128]{1,0:T(8,128)(2,1)S(1)} custom-call(s32[3]{0:T(128)S(1)} %pad_add_fusion.refs_0_, s32[192]{0:T(256)S(1)} %copy-done.3, bf16[4,480,128]{2,1,0:T(8,128)(2,1)S(1)} %all-to-all-done.refs_2_, f32[24,128]{1,0:T(8,128)S(1)} %get-tuple-element.37.refs_3_, bf16[32,128]{1,0:T(8,128)(2,1)S(1)} %bitcast.9, bf16[4,128]{1,0:T(4,128)(2,1)S(1)} %bitcast.14, ...), custom_call_target="tpu_custom_call" | custom-call | flops 25165824 | bytes 3145728 | tf_op jit(solution)/shard_map/attend1/pallas_call | solution.py:277
  69.5 5.2 %all-to-all-done.3.refs_1_ = bf16[4,384,128]{2,1,0:T(8,128)(2,1)S(1)} async-done(((bf16[4,384,128]{2,1,0:T(8,128)(2,1)}), bf16[4,384,128]{2,1,0:T(8,128)(2,1)S(1)}, u32[]{:S(2)}, u32[]{:S(2)}) %all-to-all-start.3) | async-done | bytes 393248 | tf_op jit(solution)/shard_map/all_to_all | solution.py:450
  74.7 0.8 broadcast_in_dim.29
  75.5 3.5 %all-to-all-start.2 = ((bf16[4,384,128]{2,1,0:T(8,128)(2,1)}), bf16[4,384,128]{2,1,0:T(8,128)(2,1)S(1)}, u32[]{:S(2)}, u32[]{:S(2)}) async-start(bf16[4,384,128]{2,1,0:T(8,128)(2,1)} %broadcast_in_dim.29), calls=%async_computation.2 | async-start | bytes 786432 | tf_op jit(solution)/shard_map/all_to_all | solution.py:450
  79.0 1.6 %collective-permute-start.4 = (bf16[4,384,128]{2,1,0:T(8,128)(2,1)S(1)}, bf16[4,384,128]{2,1,0:T(8,128)(2,1)S(1)}, u32[]{:S(2)}, u32[]{:S(2)}) collective-permute-start(bf16[4,384,128]{2,1,0:T(8,128)(2,1)S(1)} %all-to-all-done.3.refs_1_), channel_id=1, source_target_pairs={{0,2},{2,0},{4,6},{6,4},{8,10},{10,8},{12,14},{14,12},{1,3},{3,1},... | collective-permute-start | bytes 1179656 | tf_op jit(solution)/shard_map/ppermute | solution.py:453
  80.6 7.9 %all-to-all-done.2.refs_1_ = bf16[4,384,128]{2,1,0:T(8,128)(2,1)S(1)} async-done(((bf16[4,384,128]{2,1,0:T(8,128)(2,1)}), bf16[4,384,128]{2,1,0:T(8,128)(2,1)S(1)}, u32[]{:S(2)}, u32[]{:S(2)}) %all-to-all-start.2) | async-done | bytes 393248 | tf_op jit(solution)/shard_map/all_to_all | solution.py:450
  88.5 1.5 %collective-permute-start.3 = (bf16[4,384,128]{2,1,0:T(8,128)(2,1)S(1)}, bf16[4,384,128]{2,1,0:T(8,128)(2,1)S(1)}, u32[]{:S(2)}, u32[]{:S(2)}) collective-permute-start(bf16[4,384,128]{2,1,0:T(8,128)(2,1)S(1)} %all-to-all-done.2.refs_1_), channel_id=1, source_target_pairs={{0,2},{2,0},{4,6},{6,4},{8,10},{10,8},{12,14},{14,12},{1,3},{3,1},... | collective-permute-start | bytes 1179656 | tf_op jit(solution)/shard_map/ppermute | solution.py:453
  90.0 2.2 %load_out0.1.refs_4_ = bf16[2048,1024]{1,0:T(8,128)(2,1)S(1)} custom-call(bf16[4096,1024]{1,0:T(8,128)(2,1)} %refs_0_.11, bf16[4,480,128]{2,1,0:T(8,128)(2,1)S(1)} %get-tuple-element.32.refs_2_.refs_1_), custom_call_target="tpu_custom_call" | custom-call | bytes 4194304 | tf_op jit(solution)/shard_map/load_out0/pallas_call | solution.py:66
  92.2 2.2 %load_out1.1.refs_4_ = bf16[2048,1024]{1,0:T(8,128)(2,1)S(1)} custom-call(bf16[4096,1024]{1,0:T(8,128)(2,1)} %refs_0_.11, bf16[4,480,128]{2,1,0:T(8,128)(2,1)S(1)} %get-tuple-element.32.refs_2_.refs_1_), custom_call_target="tpu_custom_call" | custom-call | bytes 4194304 | tf_op jit(solution)/shard_map/load_out1/pallas_call | solution.py:66
  94.4 0.0 collective-permute-done.4.refs_2_
  94.4 1.8 %output0.1.refs_5_ = f32[192,1024]{1,0:T(8,128)S(1)} custom-call(s32[3]{0:T(128)S(1)} %pad_add_fusion.refs_0_, bf16[4,384,128]{2,1,0:T(8,128)(2,1)S(1)} %all-to-all-done.3.refs_1_, bf16[4,384,128]{2,1,0:T(8,128)(2,1)S(1)} %collective-permute-done.4.refs_2_, s32[1,192]{1,0:T(1,128)S(1)} %bitcast.11, bf16[2048,1024]{1,0:T(8,128)(2,1)S(1)} %load_out0.1.refs_4_), custom_call_target="tpu_custom_call" | custom-call | flops 805306368 | bytes 4194304 | tf_op jit(solution)/shard_map/output0/pallas_call | solution.py:345
  96.2 0.0 collective-permute-done.3.refs_2_
  96.2 1.9 %output1.1 = (f32[96,1024]{1,0:T(8,128)S(1)}, bf16[96,1024]{1,0:T(8,128)(2,1)S(1)}) custom-call(s32[3]{0:T(128)S(1)} %pad_add_fusion.refs_0_, bf16[4,384,128]{2,1,0:T(8,128)(2,1)S(1)} %all-to-all-done.2.refs_1_, bf16[4,384,128]{2,1,0:T(8,128)(2,1)S(1)} %collective-permute-done.3.refs_2_, s32[1,192]{1,0:T(1,128)S(1)} %bitcast.12, ...), custom_call_target="tpu_custom_call" | custom-call | flops 805306368 | bytes 4194304 | tf_op jit(solution)/shard_map/output1/pallas_call | solution.py:345
  98.1 0.1 collective-permute-start.5
  98.2 1.4 %collective-permute-done.5 = bf16[96,1024]{1,0:T(8,128)(2,1)S(1)} collective-permute-done((bf16[96,1024]{1,0:T(8,128)(2,1)S(1)}, bf16[96,1024]{1,0:T(8,128)(2,1)S(1)}, u32[]{:S(2)}, u32[]{:S(2)}) %collective-permute-start.5) | collective-permute-done | bytes 196640 | tf_op jit(solution)/shard_map/ppermute | solution.py:462
  99.6 0.8 add_convert_fusion.2
  (11 shorter events, 0.0 us)
Async XLA Ops:
  0.0 3.1 %collective-permute-start = (bf16[96,1024]{1,0:T(8,128)(2,1)}, bf16[96,1024]{1,0:T(8,128)(2,1)S(1)}, u32[]{:S(2)}, u32[]{:S(2)}) collective-permute-start(bf16[96,1024]{1,0:T(8,128)(2,1)} %refs_1_.8), channel_id=1, source_target_pairs={{0,1},{1,0},{2,3},{3,2},{4,5},{5,4},{6,7},{7,6},{8,9},{9,8},{10,11... | collective-permute-start | bytes 589832 | tf_op jit(solution)/shard_map/ppermute | solution.py:385
  0.5 2.6 %copy-start = (bf16[96,1024]{1,0:T(8,128)(2,1)S(1)}, bf16[96,1024]{1,0:T(8,128)(2,1)}, u32[]{:S(2)}) copy-start(bf16[96,1024]{1,0:T(8,128)(2,1)} %refs_1_.8) | copy-start | bytes 589828
  0.5 2.6 %copy-start.2 = (s32[192]{0:T(256)S(1)}, s32[192]{0:T(256)}, u32[]{:S(2)}) copy-start(s32[192]{0:T(256)} %param.24) | copy-start | bytes 2308
  0.5 2.6 %copy-start.8 = (bf16[1024]{0:T(1024)(128)(2,1)S(1)}, bf16[1024]{0:T(1024)(128)(2,1)}, u32[]{:S(2)}) copy-start(bf16[1024]{0:T(1024)(128)(2,1)} %param.14) | copy-start | bytes 6148
  5.0 15.2 %collective-permute-start.2 = (bf16[4,512,128]{2,1,0:T(8,128)(2,1)S(1)}, bf16[4,512,128]{2,1,0:T(8,128)(2,1)S(1)}, u32[]{:S(2)}, u32[]{:S(2)}) collective-permute-start(bf16[4,512,128]{2,1,0:T(8,128)(2,1)S(1)} %get-tuple-element.34), channel_id=1, source_target_pairs={{0,2},{2,0},{4,6},{6,4},{8,10},{10,8},{12,14},{14,12},{1,3},{3,1},... | collective-permute-start | bytes 1572872 | tf_op jit(solution)/shard_map/ppermute | solution.py:419
  10.1 2.0 %copy-start.6 = (bf16[1024,2048]{1,0:T(8,128)(2,1)}, bf16[1024,2048]{1,0:T(8,128)(2,1)S(1)}, u32[]{:S(2)}) copy-start(bf16[1024,2048]{1,0:T(8,128)(2,1)S(1)} %get-tuple-element.29.refs_2_) | copy-start | bytes 12582916
  21.1 22.6 %all-to-all-start.1 = ((bf16[4,512,128]{2,1,0:T(8,128)(2,1)}), bf16[4,512,128]{2,1,0:T(8,128)(2,1)S(1)}, u32[]{:S(2)}, u32[]{:S(2)}) async-start(bf16[4,512,128]{2,1,0:T(8,128)(2,1)} %add_convert_fusion), calls=%async_computation.1 | async-start | bytes 1048576 | tf_op jit(solution)/shard_map/all_to_all | solution.py:437
  26.2 2.2 %copy-start.7 = (bf16[1024,2048]{1,0:T(8,128)(2,1)S(1)}, bf16[1024,2048]{1,0:T(8,128)(2,1)}, u32[]{:S(2)}) copy-start(bf16[1024,2048]{1,0:T(8,128)(2,1)} %copy-done.6) | copy-start | bytes 12582916
  28.4 20.3 %copy-start.3 = (s32[192]{0:T(256)S(1)}, s32[192]{0:T(256)}, u32[]{:S(2)}) copy-start(s32[192]{0:T(256)} %refs_1_.13) | copy-start | bytes 2308
  30.2 12.6 %collective-permute-start.1 = (bf16[4,480,128]{2,1,0:T(8,128)(2,1)S(1)}, bf16[4,480,128]{2,1,0:T(8,128)(2,1)S(1)}, u32[]{:S(2)}, u32[]{:S(2)}) collective-permute-start(bf16[4,480,128]{2,1,0:T(8,128)(2,1)S(1)} %get-tuple-element.33), channel_id=1, source_target_pairs={{0,2},{2,0},{4,6},{6,4},{8,10},{10,8},{12,14},{14,12},{1,3},{3,1},... | collective-permute-start | bytes 1474568 | tf_op jit(solution)/shard_map/ppermute | solution.py:419
  43.8 7.1 %copy-start.1 = (bf16[4096]{0:T(1024)(128)(2,1)S(1)}, bf16[4096]{0:T(1024)(128)(2,1)}, u32[]{:S(2)}) copy-start(bf16[4096]{0:T(1024)(128)(2,1)} %param.18) | copy-start | bytes 24580
  43.8 7.1 %copy-start.4 = (bf16[512]{0:T(512)(128)(2,1)S(1)}, bf16[512]{0:T(512)(128)(2,1)}, u32[]{:S(2)}) copy-start(bf16[512]{0:T(512)(128)(2,1)} %param.19) | copy-start | bytes 3076
  43.8 7.1 %copy-start.5 = (bf16[512]{0:T(512)(128)(2,1)S(1)}, bf16[512]{0:T(512)(128)(2,1)}, u32[]{:S(2)}) copy-start(bf16[512]{0:T(512)(128)(2,1)} %param.20) | copy-start | bytes 3076
  43.8 17.2 %all-to-all-start = ((bf16[4,480,128]{2,1,0:T(8,128)(2,1)}), bf16[4,480,128]{2,1,0:T(8,128)(2,1)S(1)}, u32[]{:S(2)}, u32[]{:S(2)}) async-start(bf16[4,480,128]{2,1,0:T(8,128)(2,1)} %add_convert_fusion.1), calls=%async_computation | async-start | bytes 983040 | tf_op jit(solution)/shard_map/all_to_all | solution.py:437
  61.7 13.0 %all-to-all-start.3 = ((bf16[4,384,128]{2,1,0:T(8,128)(2,1)}), bf16[4,384,128]{2,1,0:T(8,128)(2,1)S(1)}, u32[]{:S(2)}, u32[]{:S(2)}) async-start(bf16[4,384,128]{2,1,0:T(8,128)(2,1)} %broadcast_in_dim.30), calls=%async_computation.3 | async-start | bytes 786432 | tf_op jit(solution)/shard_map/all_to_all | solution.py:450
  75.5 12.9 %all-to-all-start.2 = ((bf16[4,384,128]{2,1,0:T(8,128)(2,1)}), bf16[4,384,128]{2,1,0:T(8,128)(2,1)S(1)}, u32[]{:S(2)}, u32[]{:S(2)}) async-start(bf16[4,384,128]{2,1,0:T(8,128)(2,1)} %broadcast_in_dim.29), calls=%async_computation.2 | async-start | bytes 786432 | tf_op jit(solution)/shard_map/all_to_all | solution.py:450
  79.0 15.4 %collective-permute-start.4 = (bf16[4,384,128]{2,1,0:T(8,128)(2,1)S(1)}, bf16[4,384,128]{2,1,0:T(8,128)(2,1)S(1)}, u32[]{:S(2)}, u32[]{:S(2)}) collective-permute-start(bf16[4,384,128]{2,1,0:T(8,128)(2,1)S(1)} %all-to-all-done.3.refs_1_), channel_id=1, source_target_pairs={{0,2},{2,0},{4,6},{6,4},{8,10},{10,8},{12,14},{14,12},{1,3},{3,1},... | collective-permute-start | bytes 1179656 | tf_op jit(solution)/shard_map/ppermute | solution.py:453
  88.5 7.8 %collective-permute-start.3 = (bf16[4,384,128]{2,1,0:T(8,128)(2,1)S(1)}, bf16[4,384,128]{2,1,0:T(8,128)(2,1)S(1)}, u32[]{:S(2)}, u32[]{:S(2)}) collective-permute-start(bf16[4,384,128]{2,1,0:T(8,128)(2,1)S(1)} %all-to-all-done.2.refs_1_), channel_id=1, source_target_pairs={{0,2},{2,0},{4,6},{6,4},{8,10},{10,8},{12,14},{14,12},{1,3},{3,1},... | collective-permute-start | bytes 1179656 | tf_op jit(solution)/shard_map/ppermute | solution.py:453
  98.1 1.5 %collective-permute-start.5 = (bf16[96,1024]{1,0:T(8,128)(2,1)S(1)}, bf16[96,1024]{1,0:T(8,128)(2,1)S(1)}, u32[]{:S(2)}, u32[]{:S(2)}) collective-permute-start(bf16[96,1024]{1,0:T(8,128)(2,1)S(1)} %get-tuple-element.42), channel_id=1, source_target_pairs={{0,1},{1,0},{2,3},{3,2},{4,5},{5,4},{6,7},{7,6},{8,9},{9,8},{10,11... | collective-permute-start | bytes 589832 | tf_op jit(solution)/shard_map/ppermute | solution.py:462

commit v4 on v3

v4 whole, which is shorter than its diff:
```python
import functools
import math

import jax
import jax.numpy as jnp
from jax import lax
from jax.experimental import pallas as pl
from jax.experimental.pallas import tpu as pltpu
from jax.sharding import PartitionSpec as P

MODEL_WIDTH = 8192
QUERY_HEADS = 64
KEY_VALUE_HEADS = 8
HEAD_SIZE = 128
QUERIES_PER_KV = QUERY_HEADS // KEY_VALUE_HEADS
TILES = QUERIES_PER_KV + 2
SQUARE_ROWS = 32

EPSILON = 1e-06
ROPE_BASE = 1000000.0
CHUNKS = 2
SLOTS_PER_STEP = 8
VMEM_LIMIT = 16 * 1024 * 1024
ORDER = (
    ("project", 0),
    ("project", 1),
    ("load_caches", 0),
    ("far", 0),
    ("load_caches", 1),
    ("near", 0),
    ("load_out", 0),
    ("far", 1),
    ("attend", 0),
    ("near", 1),
    ("load_out", 1),
    ("gather", 0),
    ("attend", 1),
    ("gather", 1),
    ("output", 0),
    ("output", 1),
)
F32 = jnp.float32
BF16 = jnp.bfloat16


def neighbour_pairs(nz):
    return [(z * 2 + y, z * 2 + 1 - y) for z in range(nz) for y in range(2)]


def stride_pairs(nz, stride):
    return [(z * 2 + y, (z ^ stride) * 2 + y) for z in range(nz) for y in range(2)]


def strides(nz):
    return [1 << i for i in range(nz.bit_length() - 1)]


def place_order(nz):
    return sorted(range(nz), key=lambda q: [(q & b) != 0 for b in strides(nz)])


def slot_one_hot(place_ref, slot_of_row, nz, per):
    rows = slot_of_row.shape[1]
    base = lax.broadcasted_iota(jnp.int32, (per, rows), 0)
    blocks = []
    for h in range(2):
        for q in place_order(nz):
            owner = (place_ref[0] ^ q) * 2 + (place_ref[1] ^ h)
            blocks.append(jnp.where(base + owner * per == slot_of_row, 1.0, 0.0).astype(F32))
    return jnp.concatenate(blocks, axis=0).astype(BF16)


TOKEN = (8, HEAD_SIZE)


def call(kernel, name, token, scalars, arrays, out_shapes, scratch):
    def body(*refs):
        first_out = 1 + len(scalars) + len(arrays)
        refs[first_out][...] = jnp.zeros(TOKEN, F32)
        kernel(*refs[1:first_out], *refs[first_out + 1 :])

    vmem = pl.BlockSpec(memory_space=pltpu.VMEM)
    outs = pl.pallas_call(
        body,
        in_specs=[vmem]
        + [pl.BlockSpec(memory_space=pltpu.SMEM)] * len(scalars)
        + [vmem] * len(arrays),
        out_specs=[vmem] * (1 + len(out_shapes)),
        out_shape=[pltpu.VMEM(TOKEN, F32)]
        + [jax.ShapeDtypeStruct(shape, dtype) for shape, dtype in out_shapes],
        scratch_shapes=scratch,
        compiler_params=pltpu.CompilerParams(vmem_limit_bytes=VMEM_LIMIT),
        cost_estimate=pl.CostEstimate(flops=0, bytes_accessed=0, transcendentals=0),
        name=name,
    )(token, *scalars, *arrays)
    return outs[0], outs[1:]


def load_kernel(*refs, windows):
    count = len(windows)
    sources, token_ref, targets, sems = (
        refs[:count], refs[count + 1], refs[count + 2 : -1], refs[-1],
    )
    copies = [
        pltpu.make_async_copy(source.at[window], target, sems.at[i])
        for i, (source, target, window) in enumerate(zip(sources, targets, windows))
    ]
    for copy in copies:
        copy.start()
    token_ref[...] = jnp.zeros(TOKEN, F32)
    for copy in copies:
        copy.wait()


def load(name, token, arrays, windows):
    shapes = [
        tuple(w.size if isinstance(w, pl.Slice) else n for w, n in zip(window, a.shape))
        for a, window in zip(arrays, windows)
    ]
    vmem = pl.BlockSpec(memory_space=pltpu.VMEM)
    outs = pl.pallas_call(
        functools.partial(load_kernel, windows=windows),
        in_specs=[pl.BlockSpec(memory_space=pltpu.HBM)] * len(arrays) + [vmem],
        out_specs=[vmem] * (1 + len(arrays)),
        out_shape=[pltpu.VMEM(TOKEN, F32)]
        + [pltpu.VMEM(shape, a.dtype) for a, shape in zip(arrays, shapes)],
        scratch_shapes=[pltpu.SemaphoreType.DMA((len(arrays),))],
        compiler_params=pltpu.CompilerParams(vmem_limit_bytes=VMEM_LIMIT),
        cost_estimate=pl.CostEstimate(flops=0, bytes_accessed=0, transcendentals=0),
        name=name,
    )(*[pltpu.with_memory_space_constraint(a, pltpu.HBM) for a in arrays], token)
    return outs[0], outs[1:]


def project_kernel(*refs, nz, per, first, heads):
    place_ref = refs[0]
    if first:
        own_ref, other_ref, gain_ref, sor_ref, wq_ref, wk_ref, wv_ref = refs[1:8]
        *out_refs, slotted_ref, acc = refs[8:]
        one_hot = slot_one_hot(place_ref, sor_ref[...], nz, per)
        own, other = own_ref[...], other_ref[...]
        lower = place_ref[2] == 0
        rows = jnp.concatenate(
            [jnp.where(lower, own, other), jnp.where(lower, other, own)], axis=0
        )
        hidden = jnp.dot(one_hot, rows, preferred_element_type=F32)
        gain = gain_ref[...].astype(F32)
        gain = jnp.concatenate([gain[j : j + 1] for j in range(gain.shape[0])], axis=1)
        slotted_ref[...] = (hidden * gain).astype(BF16)
        squares = jnp.sum(hidden * hidden, axis=1, keepdims=True)
        high = squares.astype(BF16).astype(F32)
        low = squares - high
        lane = lax.broadcasted_iota(jnp.int32, (per, HEAD_SIZE), 1)
        lane_high = place_ref[1] * 2
        for b, ref in enumerate(out_refs):
            for z in range(nz // 2):
                at = (b * (nz // 2) + z) * per
                packed = jnp.where(
                    lane == lane_high,
                    high[at : at + per],
                    jnp.where(lane == lane_high + 1, low[at : at + per], 0.0),
                )
                packed = jnp.concatenate(
                    [packed, jnp.zeros((SQUARE_ROWS - per, HEAD_SIZE), F32)], axis=0
                )
                ref[z, heads * TILES * per :, :] = packed.astype(BF16)
    else:
        slotted_ref, wq_ref, wk_ref, wv_ref = refs[1:5]
        *out_refs, acc = refs[5:]

    columns = QUERIES_PER_KV * HEAD_SIZE
    slotted = slotted_ref[...]
    for g in range(heads):
        acc[:, :columns] = jnp.dot(
            slotted, wq_ref[:, g * columns : (g + 1) * columns], preferred_element_type=F32
        )
        narrow = slice(g * HEAD_SIZE, (g + 1) * HEAD_SIZE)
        acc[:, columns:] = jnp.dot(
            slotted,
            jnp.concatenate([wk_ref[:, narrow], wv_ref[:, narrow]], axis=1),
            preferred_element_type=F32,
        )
        for b, ref in enumerate(out_refs):
            for z in range(nz // 2):
                at = (b * (nz // 2) + z) * per
                block = jnp.concatenate(
                    [
                        acc[at : at + per, c * HEAD_SIZE : (c + 1) * HEAD_SIZE]
                        for c in range(TILES)
                    ],
                    axis=0,
                )
                ref[z, g * TILES * per : (g + 1) * TILES * per, :] = block.astype(BF16)


def project(token, place, inputs, weights, *, chunk, heads, nz, per):
    first = chunk == 0
    rows = 2 * nz * per
    depth = weights[0].shape[0]
    block_rows = heads * TILES * per + (SQUARE_ROWS if first else 0)
    out_shapes = [((nz // 2, block_rows, HEAD_SIZE), BF16)] * 4
    return call(
        functools.partial(project_kernel, nz=nz, per=per, first=first, heads=heads),
        "project" + str(chunk),
        token,
        [place],
        [*inputs, *weights],
        out_shapes + ([((rows, depth), BF16)] if first else []),
        [pltpu.VMEM((rows, TILES * HEAD_SIZE), F32)],
    )


def add_kernel(*refs, terms):
    outs = refs[terms:]
    each = outs[0].shape[0]
    for z in range(refs[0].shape[0]):
        total = refs[0][z].astype(F32)
        for ref in refs[1:terms]:
            total = total + ref[z].astype(F32)
        outs[z // each][z % each] = total.astype(BF16)


def add(name, token, arrays, parts):
    count, rows, width = arrays[0].shape
    shape = (count // parts, rows, width)
    return call(
        functools.partial(add_kernel, terms=len(arrays)),
        name,
        token,
        [],
        arrays,
        [(shape, BF16)] * parts,
        [],
    )


def join_kernel(a_ref, b_ref, out_ref):
    count = a_ref.shape[0]
    out_ref[:count] = a_ref[...]
    out_ref[count:] = b_ref[...]


def join(name, token, a, b):
    shape = (a.shape[0] + b.shape[0],) + a.shape[1:]
    token, (joined,) = call(join_kernel, name, token, [], [a, b], [(shape, BF16)], [])
    return token, joined


def attend_kernel(*refs, first, heads, per, group, chunk):
    place_ref, lengths_ref, mine_ref, last_ref = refs[:4]
    rest = refs[4:]
    if first:
        qb_ref, kb_ref, vb_ref, cos_ref, sin_ref, k_ref, v_ref, out_ref, scale_ref = rest[:9]
    else:
        scale_in_ref, qb_ref, kb_ref, vb_ref, cos_ref, sin_ref, k_ref, v_ref, out_ref = rest[:9]
    fresh, result = rest[9:]
    body = heads * TILES * per
    head_rows = TILES * per

    if first:
        squares = mine_ref[0, body:, :].astype(F32) + last_ref[0, body:, :].astype(F32)
        total = jnp.sum(squares[:per], axis=1, keepdims=True)
        scale = jnp.broadcast_to(lax.rsqrt(total / MODEL_WIDTH + EPSILON), (per, HEAD_SIZE))
        scale_ref[...] = scale
    else:
        scale = scale_in_ref[...]
    cos, sin = cos_ref[...], sin_ref[...]
    query_bias = qb_ref[...].astype(F32)
    key_bias = kb_ref[...].astype(F32)
    value_bias = vb_ref[...].astype(F32)
    for g in range(heads):
        rows = pl.ds(g * head_rows, head_rows)
        summed = mine_ref[0, rows, :].astype(F32) + last_ref[0, rows, :].astype(F32)
        head = chunk * heads + g
        for c in range(TILES):
            if c < QUERIES_PER_KV:
                at = head * QUERIES_PER_KV + c
                bias = query_bias[at : at + 1]
            else:
                bias = (key_bias if c == QUERIES_PER_KV else value_bias)[head : head + 1]
            tile = summed[c * per : (c + 1) * per] * scale + bias
            if c < TILES - 1:
                tile = tile * cos + pltpu.roll(tile, HEAD_SIZE // 2, 1) * sin
            fresh[pl.ds(g * head_rows + c * per, per), :] = tile.astype(BF16).astype(F32)

    positions = k_ref.shape[1]
    qrows = heads * QUERIES_PER_KV
    lanes = group * qrows
    extra = 16
    lane_block = lax.broadcasted_iota(jnp.int32, (HEAD_SIZE, lanes), 1) // QUERIES_PER_KV
    top_row = lax.broadcasted_iota(jnp.int32, (extra, HEAD_SIZE), 0) == 0
    lane_slot = lax.broadcasted_iota(jnp.int32, (1, lanes), 1) // qrows
    row = lax.broadcasted_iota(jnp.int32, (positions + extra, lanes), 0)
    base = (place_ref[0] * 2 + place_ref[1]) * per
    for start in range(0, per, group):
        slots = range(start, start + group)
        queries = jnp.concatenate(
            [
                fresh[pl.ds(g * head_rows + s, QUERIES_PER_KV, stride=per), :]
                for s in slots
                for g in range(heads)
            ],
            axis=0,
        )
        turned = queries.T
        scores = None
        for i, s in enumerate(slots):
            query, new_key = [], []
            for g in range(heads):
                query.append(jnp.where(lane_block == i * heads + g, turned, 0.0).astype(BF16))
                key = fresh[pl.ds(g * head_rows + QUERIES_PER_KV * per + s, 1), :]
                new_key.append(jnp.where(top_row, key, 0.0).astype(BF16))
            keys = jnp.concatenate([k_ref[s], jnp.concatenate(new_key, axis=1)], axis=0)
            term = jnp.dot(keys, jnp.concatenate(query, axis=0), preferred_element_type=F32)
            scores = term if scores is None else scores + term

        lengths = jnp.zeros((1, lanes), jnp.int32)
        for i, s in enumerate(slots):
            lengths = jnp.where(lane_slot == i, lengths_ref[base + s], lengths)
        valid = (row < lengths) | (row == positions)
        scores = jnp.where(valid, scores * (1.0 / math.sqrt(HEAD_SIZE)), -1e30)
        top = jnp.max(scores, axis=0, keepdims=True)
        exps = jnp.where(valid, jnp.exp(scores - top), 0.0)
        weights = exps * (1.0 / jnp.sum(exps, axis=0, keepdims=True))
        cache_weights = weights[:positions].T.astype(BF16)
        own_weights = weights[positions : positions + 8].T[:, 0:1].astype(BF16).astype(F32)
        for i, s in enumerate(slots):
            mixed = jnp.dot(
                cache_weights[i * qrows : (i + 1) * qrows], v_ref[s], preferred_element_type=F32
            )
            for g in range(heads):
                lo, hi = g * QUERIES_PER_KV, (g + 1) * QUERIES_PER_KV
                new_value = fresh[pl.ds(g * head_rows + (QUERIES_PER_KV + 1) * per + s, 1), :]
                result[pl.ds(g * QUERIES_PER_KV * per + s, QUERIES_PER_KV, stride=per), :] = (
                    mixed[lo:hi, g * HEAD_SIZE : (g + 1) * HEAD_SIZE]
                    + own_weights[i * qrows + lo : i * qrows + hi] * new_value
                )
    out_ref[0] = result[...].astype(BF16)


def attend(token, place, lengths, parts, scale, biases, cos, sin, keys, values, *, chunk, heads):
    first = chunk == 0
    per = keys.shape[0]
    out_rows = heads * QUERIES_PER_KV * per
    return call(
        functools.partial(
            attend_kernel, first=first, heads=heads, per=per, group=SLOTS_PER_STEP, chunk=chunk
        ),
        "attend" + str(chunk),
        token,
        [place, lengths],
        list(parts) + ([] if first else [scale]) + list(biases) + [cos, sin, keys, values],
        [((1, out_rows, HEAD_SIZE), BF16)] + ([((per, HEAD_SIZE), F32)] if first else []),
        [
            pltpu.VMEM((heads * TILES * per, HEAD_SIZE), F32),
            pltpu.VMEM((out_rows, HEAD_SIZE), F32),
        ],
    )


def output_kernel(*refs, nz, per, first, last):
    place_ref, block_refs, sor_ref, w_ref = refs[0], refs[1:5], refs[5], refs[6]
    rest = refs[7:]
    if not first:
        acc_in_ref, rest = rest[0], rest[1:]
    if last:
        mine_ref, send_ref, stacked, total = rest
    else:
        acc_out_ref, stacked = rest
    tiles = block_refs[0].shape[1] // per

    one_hot = slot_one_hot(place_ref, sor_ref[...], nz, per)
    wide = [ref[z].astype(F32) for ref in block_refs for z in range(nz // 2)]
    for c in range(tiles):
        stacked[:, c * HEAD_SIZE : (c + 1) * HEAD_SIZE] = jnp.concatenate(
            [block[c * per : (c + 1) * per] for block in wide], axis=0
        ).astype(BF16)
    permuted = lax.dot_general(
        one_hot, stacked[...], (((0,), (0,)), ((), ())), preferred_element_type=F32
    ).astype(BF16)
    stacked[...] = permuted
    product = jnp.dot(stacked[...], w_ref[...], preferred_element_type=F32)
    if not first:
        product = product + acc_in_ref[...]
    if last:
        half = product.shape[0] // 2
        total[...] = product
        mine_ref[...] = total[pl.ds(pl.multiple_of(place_ref[2] * half, half), half), :]
        send_ref[...] = total[
            pl.ds(pl.multiple_of((1 - place_ref[2]) * half, half), half), :
        ].astype(BF16)
    else:
        acc_out_ref[...] = product


def output(token, place, blocks, sor, w_out, acc, *, chunk, chunks, nz, per):
    first, last = chunk == 0, chunk == chunks - 1
    rows = 2 * nz * per
    depth, width = w_out.shape
    if last:
        out_shapes = [((rows // 2, width), F32), ((rows // 2, width), BF16)]
    else:
        out_shapes = [((rows, width), F32)]
    return call(
        functools.partial(output_kernel, nz=nz, per=per, first=first, last=last),
        "output" + str(chunk),
        token,
        [place],
        [*blocks, sor, w_out] + ([] if first else [acc]),
        out_shapes,
        [pltpu.VMEM((rows, depth), BF16)] + ([pltpu.VMEM((rows, width), F32)] if last else []),
    )


def on_device(
    hidden_rows,
    norm_gain,
    w_query,
    key_weight,
    value_weight,
    query_bias,
    key_bias_vector,
    value_bias_vector,
    rotated_key_cache,
    stored_value_cache,
    slot_valid_lengths,
    slot_of_row,
    w_out,
    *,
    size,
):
    nz = size // 2
    assert size % 2 == 0 and nz & (nz - 1) == 0 and nz > 2
    per = rotated_key_cache.shape[0]
    kv_heads = key_weight.shape[1] // HEAD_SIZE
    heads = kv_heads // CHUNKS
    gx = lax.axis_index("gx")
    gy = lax.axis_index("gy")
    place = jnp.stack([gx // 2, gx % 2, gy]).astype(jnp.int32)

    other = lax.ppermute(hidden_rows, "gy", [(0, 1), (1, 0)])
    sor = slot_of_row[None, :]
    gain = norm_gain.reshape(-1, HEAD_SIZE)

    lengths = lax.dynamic_slice_in_dim(slot_valid_lengths, gx * per, per, 0)
    lane = jnp.arange(HEAD_SIZE)
    half_width = HEAD_SIZE // 2
    frequency = ROPE_BASE ** (-((lane % half_width).astype(F32) * 2.0 / HEAD_SIZE))
    angles = lengths.astype(F32)[:, None] * frequency[None, :]
    cos = jnp.cos(angles)
    sin = jnp.sin(angles) * jnp.where(lane < half_width, -1.0, 1.0)[None, :]
    biases = [b.reshape(-1, HEAD_SIZE) for b in (query_bias, key_bias_vector, value_bias_vector)]

    columns = heads * QUERIES_PER_KV * HEAD_SIZE
    narrow = heads * HEAD_SIZE
    everything = pl.ds(0, w_query.shape[0])
    positions = rotated_key_cache.shape[1]
    all_columns = pl.ds(0, w_out.shape[1])
    same_z = neighbour_pairs(nz)
    scale = acc = None
    inputs = [hidden_rows, other, gain, sor]
    near, far, near_sent, far_sent = {}, {}, {}, {}
    caches, w_outs, held, partial = {}, {}, {}, {}

    def do_project(token, c):
        nonlocal inputs
        token, weights = load(
            "load_weights" + str(c),
            token,
            [w_query, key_weight, value_weight],
            [(everything, pl.ds(c * n, n)) for n in (columns, narrow, narrow)],
        )
        token, outs = project(
            token, place, inputs, weights, chunk=c, heads=heads, nz=nz, per=per
        )
        near[c], far[c], near_out, far_out = outs[:4]
        if c == 0:
            inputs = [outs[4]]
        far_sent[c] = lax.ppermute(far_out, "gx", same_z)
        near_sent[c] = lax.ppermute(near_out, "gx", same_z)
        return token

    def do_load_caches(token, c):
        token, caches[c] = load(
            "load_caches" + str(c),
            token,
            [rotated_key_cache, stored_value_cache],
            [(pl.ds(0, per), pl.ds(0, positions), pl.ds(c * narrow, narrow))] * 2,
        )
        return token

    def do_load_out(token, c):
        token, (w_outs[c],) = load(
            "load_out" + str(c), token, [w_out], [(pl.ds(c * columns, columns), all_columns)]
        )
        return token

    def do_far(token, c):
        token, (total,) = add("add_far" + str(c), token, [far[c], far_sent[c]], 1)
        far[c] = lax.ppermute(total, "gx", stride_pairs(nz, 1))
        return token

    def do_near(token, c):
        terms = [near[c], near_sent[c], far[c]]
        for stride in strides(nz)[1:]:
            token, (kept, sent) = add("add_near" + str(c) + "_" + str(stride), token, terms, 2)
            terms = [kept, lax.ppermute(sent, "gx", stride_pairs(nz, stride))]
        partial[c] = terms
        return token

    def do_attend(token, c):
        nonlocal scale
        token, outs = attend(
            token, place, slot_valid_lengths, partial[c], scale, biases, cos, sin, *caches[c],
            chunk=c, heads=heads,
        )
        if c == 0:
            scale = outs[1]
        stride = strides(nz)[-1]
        held[c] = outs[0], lax.ppermute(outs[0], "gx", stride_pairs(nz, stride))
        return token

    def do_gather(token, c):
        blocks, received = held[c]
        for stride in reversed(strides(nz)[:-1]):
            token, blocks = join("join" + str(c) + "_" + str(stride), token, blocks, received)
            received = lax.ppermute(blocks, "gx", stride_pairs(nz, stride))
        held[c] = [
            blocks,
            received,
            lax.ppermute(blocks, "gx", same_z),
            lax.ppermute(received, "gx", same_z),
        ]
        return token

    def do_output(token, c):
        nonlocal acc
        token, acc = output(
            token, place, held[c], sor, w_outs[c], acc if c == 0 else acc[0],
            chunk=c, chunks=CHUNKS, nz=nz, per=per,
        )
        return token

    token = jnp.zeros(TOKEN, F32)
    steps = {
        "project": do_project,
        "load_caches": do_load_caches,
        "load_out": do_load_out,
        "far": do_far,
        "near": do_near,
        "attend": do_attend,
        "gather": do_gather,
        "output": do_output,
    }
    for step, c in ORDER:
        token = steps[step](token, c)
    mine, send = acc
    received = lax.ppermute(send, "gy", [(0, 1), (1, 0)])
    return (hidden_rows.astype(F32) + mine + received.astype(F32)).astype(BF16)


def solution(mesh):
    in_specs = (
        P(("grp", "gy"), "gx"),
        P("gx"),
        P("gx", "gy"),
        P("gx", "gy"),
        P("gx", "gy"),
        P("gy"),
        P("gy"),
        P("gy"),
        P(("grp", "gx"), None, "gy"),
        P(("grp", "gx"), None, "gy"),
        P("grp"),
        P("grp"),
        P("gy", "gx"),
    )
    out_specs = P(("grp", "gy"), "gx")
    return jax.shard_map(
        functools.partial(on_device, size=mesh.shape["gx"]),
        mesh=mesh,
        in_specs=in_specs,
        out_specs=out_specs,
        check_vma=False,
    )
```

time: 101 us -> 84.9 us (0.84)
  waiting for transfers between devices: 41.3 us -> 30.2 us
  local copies, waits for them, and re-layouts: 5.78 us -> 0.06 us
  Pallas kernels: 25.4 us -> 30.6 us
  starting transfers between devices: 24.7 us -> 22.5 us
  other arithmetic: 2.94 us -> 1.04 us
    all_to_all x4 -> x0, waiting for transfers between devices: 20.7 us -> none  [the longest x2 13.1 us: on_device(): lax.all_to_all(spread, 'gx', 0, 0, axis_index_groups=column_groups(nz), t...]
    all_to_all x4 -> x0, starting transfers between devices: 17 us -> none  [the longest x2 10.1 us: on_device(): lax.all_to_all(pair_sum, 'gx', 0, 0, axis_index_groups=column_groups(nz),...]
    ppermute x4 -> x16, starting transfers between devices: 7.23 us -> 22.1 us  [the longest x2 6.03 us: do_near(): terms = [kept, lax.ppermute(sent, 'gx', stride_pairs(nz, stride))]]
    ppermute x4 -> x16, waiting for transfers between devices: 19.2 us -> 28.8 us  [the longest x2 10.4 us: do_attend(): held[c] = (outs[0], lax.ppermute(outs[0], 'gx', stride_pairs(nz, stride)))]
    pallas_call x6 -> x12, Pallas kernels: 12.2 us -> 17 us  [call(): pl.pallas_call(body, in_specs=[vmem] + [pl.BlockSpec(memory_space=pltpu.S...]
    unnamed x18 -> x28, local copies, waits for them, and re-layouts: 4.17 us -> 0.06 us
    convert_element_type x2 -> x0, other arithmetic: 1.89 us -> none  [on_device(): pair_sum = (kept[c].astype(F32) + swapped[c].astype(F32)).astype(BF16)]
    broadcast_in_dim x2 -> x1, local copies, waits for them, and re-layouts: 1.61 us -> 0.01 us  [on_device(): token = jnp.zeros(TOKEN, F32)]
  transfers between devices with their start and end apart: 10 -> 18, of which waited for: 6 -> 11; matrix products, arithmetic and copies ran while one was open for 1% -> 0% of each run, Pallas kernels for 22% -> 28%
where the time goes in v4:
time: 84.9 us; the launch traced here: 84.7 us
  Pallas kernels  30.6 us (36%)
  waiting for transfers between devices  30.2 us (36%)
  starting transfers between devices  22.5 us (27%)
  other arithmetic  1.04 us (1%)
    pallas_call x12, Pallas kernels, call(): pl.pallas_call(body, in_specs=[vmem] + [pl.BlockSpec(memory_space=pltpu.S...  17 us
    pallas_call x6, Pallas kernels, load(): pl.pallas_call(functools.partial(load_kernel, windows=windows), in_specs=...  13.6 us
    ppermute x2, waiting for transfers between devices, do_attend(): held[c] = (outs[0], lax.ppermute(outs[0], 'gx', stride_pairs(nz, stride)))  10.4 us
    ppermute x2, waiting for transfers between devices, do_gather(): lax.ppermute(received, 'gx', same_z)  6.32 us
    ppermute x2, starting transfers between devices, do_near(): terms = [kept, lax.ppermute(sent, 'gx', stride_pairs(nz, stride))]  6.03 us
    ppermute x2, waiting for transfers between devices, do_near(): terms = [kept, lax.ppermute(sent, 'gx', stride_pairs(nz, stride))]  4.45 us
    ppermute x2, starting transfers between devices, do_project(): far_sent[c] = lax.ppermute(far_out, 'gx', same_z)  4.06 us
    ppermute x2, starting transfers between devices, do_far(): far[c] = lax.ppermute(total, 'gx', stride_pairs(nz, 1))  3.87 us
  transfers between devices with their start and end apart: 18, of which 11 were waited for; matrix products, arithmetic and copies ran while one was open for 0% of the time, Pallas kernels for 28%

profile of v4, /device:TPU:0, one launch (start us, length us, event | category | flops | bytes accessed | tf_op | source)
XLA Modules:
  0.0 84.7 jit_solution(8277819065823240765)
XLA Ops:
  0.0 0.5 collective-permute-start
  0.5 2.5 %load_weights0.1 = (f32[8,128]{1,0:T(8,128)S(1)}, bf16[1024,2048]{1,0:T(8,128)(2,1)S(1)}, bf16[1024,256]{1,0:T(8,128)(2,1)S(1)}, bf16[1024,256]{1,0:T(8,128)(2,1)S(1)}) custom-call(bf16[1024,4096]{1,0:T(8,128)(2,1)} %refs_0_.7, bf16[1024,512]{1,0:T(8,128)(2,1)} %refs_1_.5, bf16[1024,512]{1,0:T(8,128)(2,1)} %refs_2_.7, f32[8,128]{1,0:T(8,128)S(1)} %broadcast_in_dim.17.refs_3_), custom_call_target="tpu_custom_call" | custom-call | tf_op jit(solution)/shard_map/load_weights0/pallas_call | solution.py:121
  3.0 0.1 pad_add_fusion.refs_1_
  3.1 2.6 %project0.1 = (f32[8,128]{1,0:T(8,128)S(1)}, bf16[2,512,128]{2,1,0:T(8,128)(2,1)S(1)}, bf16[2,512,128]{2,1,0:T(8,128)(2,1)S(1)}, bf16[2,512,128]{2,1,0:T(8,128)(...) custom-call(f32[8,128]{1,0:T(8,128)S(1)} %get-tuple-element.57.refs_0_, s32[3]{0:T(128)S(1)} %pad_add_fusion.refs_1_, ...), custom_call_target="tpu_custom_call" | custom-call | tf_op jit(solution)/shard_map/project0/pallas_call | solution.py:83
  5.7 2.5 %collective-permute-start.1 = (bf16[2,512,128]{2,1,0:T(8,128)(2,1)S(1)}, bf16[2,512,128]{2,1,0:T(8,128)(2,1)S(1)}, u32[]{:S(2)}, u32[]{:S(2)}) collective-permute-start(bf16[2,512,128]{2,1,0:T(8,128)(2,1)S(1)} %get-tuple-element.70), channel_id=1, source_target_pairs={{0,2},{2,0},{4,6},{6,4},{8,10},{10,8},{12,14},{14,12},{1,3},{3,1},... | collective-permute-start | bytes 786440 | tf_op jit(solution)/shard_map/ppermute | solution.py:479
  8.3 0.0 collective-permute-start.2
  8.3 2.5 %load_weights1.1 = (f32[8,128]{1,0:T(8,128)S(1)}, bf16[1024,2048]{1,0:T(8,128)(2,1)S(1)}, bf16[1024,256]{1,0:T(8,128)(2,1)S(1)}, bf16[1024,256]{1,0:T(8,128)(2,1)S(1)}) custom-call(bf16[1024,4096]{1,0:T(8,128)(2,1)} %refs_0_.7, bf16[1024,512]{1,0:T(8,128)(2,1)} %refs_1_.5, bf16[1024,512]{1,0:T(8,128)(2,1)} %refs_2_.7, f32[8,128]{1,0:T(8,128)S(1)} %get-tuple-element.61.refs_3_), custom_call_target="tpu_custom_call" | custom-call | tf_op jit(solution)/shard_map/load_weights1/pallas_call | solution.py:121
  10.8 2.5 %project1.1 = (f32[8,128]{1,0:T(8,128)S(1)}, bf16[2,480,128]{2,1,0:T(8,128)(2,1)S(1)}, bf16[2,480,128]{2,1,0:T(8,128)(2,1)S(1)}, bf16[2,480,128]{2,1,0:T(8,128)(2,1)S(1)}, bf16[2,480,128]{2,1,0:T(8,128)(2,1)}) custom-call(f32[8,128]{1,0:T(8,128)S(1)} %get-tuple-element.62.refs_0_, s32[3]{0:T(128)S(1)} %pad_add_fusion.refs_1_, ...), custom_call_target="tpu_custom_call" | custom-call | tf_op jit(solution)/shard_map/project1/pallas_call | solution.py:83
  13.3 2.2 %load_caches0.1 = (f32[8,128]{1,0:T(8,128)S(1)}, bf16[24,128,256]{2,1,0:T(8,128)(2,1)S(1)}, bf16[24,128,256]{2,1,0:T(8,128)(2,1)S(1)}) custom-call(bf16[24,128,512]{2,1,0:T(8,128)(2,1)} %refs_0_.9, bf16[24,128,512]{2,1,0:T(8,128)(2,1)} %refs_1_.7, f32[8,128]{1,0:T(8,128)S(1)} %get-tuple-element.67.refs_2_), custom_call_target="tpu_custom_call" | custom-call | tf_op jit(solution)/shard_map/load_caches0/pallas_call | solution.py:121
  15.5 0.8 add_far0.1
  16.2 2.1 %collective-permute-start.3 = (bf16[2,512,128]{2,1,0:T(8,128)(2,1)}, bf16[2,512,128]{2,1,0:T(8,128)(2,1)}, u32[]{:S(2)}, u32[]{:S(2)}) collective-permute-start(bf16[2,512,128]{2,1,0:T(8,128)(2,1)} %get-tuple-element.75), channel_id=1, source_target_pairs={{0,4},{2,6},{4,0},{6,2},{8,12},{10,14},{12,8},{14,10},{1,5},{3,7},... | collective-permute-start | bytes 786440 | tf_op jit(solution)/shard_map/ppermute | solution.py:500
  18.3 1.5 %collective-permute-start.4 = (bf16[2,480,128]{2,1,0:T(8,128)(2,1)}, bf16[2,480,128]{2,1,0:T(8,128)(2,1)}, u32[]{:S(2)}, u32[]{:S(2)}) collective-permute-start(bf16[2,480,128]{2,1,0:T(8,128)(2,1)} %get-tuple-element.79), channel_id=1, source_target_pairs={{0,2},{2,0},{4,6},{6,4},{8,10},{10,8},{12,14},{14,12},{1,3},{3,1},... | collective-permute-start | bytes 737288 | tf_op jit(solution)/shard_map/ppermute | solution.py:479
  19.8 0.6 collective-permute-start.6
  20.4 1.9 %load_caches1.1 = (f32[8,128]{1,0:T(8,128)S(1)}, bf16[24,128,256]{2,1,0:T(8,128)(2,1)S(1)}, bf16[24,128,256]{2,1,0:T(8,128)(2,1)S(1)}) custom-call(bf16[24,128,512]{2,1,0:T(8,128)(2,1)} %refs_0_.9, bf16[24,128,512]{2,1,0:T(8,128)(2,1)} %refs_1_.7, f32[8,128]{1,0:T(8,128)S(1)} %get-tuple-element.71.refs_2_), custom_call_target="tpu_custom_call" | custom-call | tf_op jit(solution)/shard_map/load_caches1/pallas_call | solution.py:121
  22.3 2.7 %collective-permute-done.3.refs_3_ = bf16[2,512,128]{2,1,0:T(8,128)(2,1)} collective-permute-done((bf16[2,512,128]{2,1,0:T(8,128)(2,1)}, bf16[2,512,128]{2,1,0:T(8,128)(2,1)}, u32[]{:S(2)}, u32[]{:S(2)}) %collective-permute-start.3) | collective-permute-done | bytes 262176 | tf_op jit(solution)/shard_map/ppermute | solution.py:500
  25.0 1.1 %add_near0_2.1 = (f32[8,128]{1,0:T(8,128)S(1)}, bf16[1,512,128]{2,1,0:T(8,128)(2,1)S(1)}, bf16[1,512,128]{2,1,0:T(8,128)(2,1)S(1)}) custom-call(f32[8,128]{1,0:T(8,128)S(1)} %get-tuple-element.72.refs_0_, bf16[2,512,128]{2,1,0:T(8,128)(2,1)S(1)} %copy-done.2, bf16[2,512,128]{2,1,0:T(8,128)(2,1)} %collective-permute-done.2.refs_2_, ...), custom_call_target="tpu_custom_call" | custom-call | tf_op jit(solution)/shard_map/add_near0_2/pallas_call | solution.py:83
  26.2 2.3 %load_out0.1 = (f32[8,128]{1,0:T(8,128)S(1)}, bf16[2048,1024]{1,0:T(8,128)(2,1)S(1)}) custom-call(bf16[4096,1024]{1,0:T(8,128)(2,1)} %refs_0_.11, f32[8,128]{1,0:T(8,128)S(1)} %get-tuple-element.76.refs_1_), custom_call_target="tpu_custom_call" | custom-call | tf_op jit(solution)/shard_map/load_out0/pallas_call | solution.py:121
  28.6 1.0 %add_far1.1 = (f32[8,128]{1,0:T(8,128)S(1)}, bf16[2,480,128]{2,1,0:T(8,128)(2,1)S(1)}) custom-call(f32[8,128]{1,0:T(8,128)S(1)} %get-tuple-element.77.refs_0_, bf16[2,480,128]{2,1,0:T(8,128)(2,1)S(1)} %copy-done.6, bf16[2,480,128]{2,1,0:T(8,128)(2,1)} %collective-permute-done.4.refs_2_), custom_call_target="tpu_custom_call" | custom-call | tf_op jit(solution)/shard_map/add_far1/pallas_call | solution.py:83
  29.6 1.8 %collective-permute-start.7 = (bf16[2,480,128]{2,1,0:T(8,128)(2,1)S(1)}, bf16[2,480,128]{2,1,0:T(8,128)(2,1)S(1)}, u32[]{:S(2)}, u32[]{:S(2)}) collective-permute-start(bf16[2,480,128]{2,1,0:T(8,128)(2,1)S(1)} %get-tuple-element.88), channel_id=1, source_target_pairs={{0,4},{2,6},{4,0},{6,2},{8,12},{10,14},{12,8},{14,10},{1,5},{3,7},... | collective-permute-start | bytes 737288 | tf_op jit(solution)/shard_map/ppermute | solution.py:500
  31.4 0.1 dynamic-slice_convert_fusion
  31.5 2.6 %collective-permute-start.5 = (bf16[1,512,128]{2,1,0:T(8,128)(2,1)S(1)}, bf16[1,512,128]{2,1,0:T(8,128)(2,1)S(1)}, u32[]{:S(2)}, u32[]{:S(2)}) collective-permute-start(bf16[1,512,128]{2,1,0:T(8,128)(2,1)S(1)} %get-tuple-element.82), channel_id=1, source_target_pairs={{0,8},{2,10},{4,12},{6,14},{8,0},{10,2},{12,4},{14,6},{1,9},{3,11}... | collective-permute-start | bytes 393224 | tf_op jit(solution)/shard_map/ppermute | solution.py:507
  34.0 0.1 fusion
  34.2 4.4 %collective-permute-done.5.refs_4_ = bf16[1,512,128]{2,1,0:T(8,128)(2,1)S(1)} collective-permute-done((bf16[1,512,128]{2,1,0:T(8,128)(2,1)S(1)}, bf16[1,512,128]{2,1,0:T(8,128)(2,1)S(1)}, u32[]{:S(2)}, u32[]{:S(2)}) %collective-permute-start.5) | collective-permute-done | bytes 131104 | tf_op jit(solution)/shard_map/ppermute | solution.py:507
  38.6 2.5 %attend0.1 = (f32[8,128]{1,0:T(8,128)S(1)}, bf16[1,384,128]{2,1,0:T(8,128)(2,1)S(1)}, f32[24,128]{1,0:T(8,128)S(1)}) custom-call(f32[8,128]{1,0:T(8,128)S(1)} %get-tuple-element.80.refs_0_, s32[3]{0:T(128)S(1)} %pad_add_fusion.refs_1_, s32[192]{0:T(256)S(1)} %copy-done.9, bf16[1,512,128]{2,1,0:T(8,128)(2,1)S(1)} %get-tuple-element.81.refs_3_, ...), custom_call_target="tpu_custom_call" | custom-call | tf_op jit(solution)/shard_map/attend0/pallas_call | solution.py:83
  41.1 0.1 add_near1_2.1
  41.2 3.4 %collective-permute-start.9 = (bf16[1,480,128]{2,1,0:T(8,128)(2,1)S(1)}, bf16[1,480,128]{2,1,0:T(8,128)(2,1)S(1)}, u32[]{:S(2)}, u32[]{:S(2)}) collective-permute-start(bf16[1,480,128]{2,1,0:T(8,128)(2,1)S(1)} %get-tuple-element.94), channel_id=1, source_target_pairs={{0,8},{2,10},{4,12},{6,14},{8,0},{10,2},{12,4},{14,6},{1,9},{3,11}... | collective-permute-start | bytes 368648 | tf_op jit(solution)/shard_map/ppermute | solution.py:507
  44.7 0.1 collective-permute-start.8
  44.8 2.2 %load_out1.1 = (f32[8,128]{1,0:T(8,128)S(1)}, bf16[2048,1024]{1,0:T(8,128)(2,1)S(1)}) custom-call(bf16[4096,1024]{1,0:T(8,128)(2,1)} %refs_0_.11, f32[8,128]{1,0:T(8,128)S(1)} %get-tuple-element.89.refs_1_), custom_call_target="tpu_custom_call" | custom-call | tf_op jit(solution)/shard_map/load_out1/pallas_call | solution.py:121
  47.0 6.7 %collective-permute-done.8.refs_2_ = bf16[1,384,128]{2,1,0:T(8,128)(2,1)S(1)} collective-permute-done((bf16[1,384,128]{2,1,0:T(8,128)(2,1)S(1)}, bf16[1,384,128]{2,1,0:T(8,128)(2,1)S(1)}, u32[]{:S(2)}, u32[]{:S(2)}) %collective-permute-start.8) | collective-permute-done | bytes 98336 | tf_op jit(solution)/shard_map/ppermute | solution.py:520
  53.7 2.4 %attend1.1 = (f32[8,128]{1,0:T(8,128)S(1)}, bf16[1,384,128]{2,1,0:T(8,128)(2,1)S(1)}) custom-call(f32[8,128]{1,0:T(8,128)S(1)} %get-tuple-element.92.refs_0_, s32[3]{0:T(128)S(1)} %pad_add_fusion.refs_1_, s32[192]{0:T(256)S(1)} %copy-done.9, bf16[1,480,128]{2,1,0:T(8,128)(2,1)S(1)} %get-tuple-element.93.refs_3_, ...), custom_call_target="tpu_custom_call" | custom-call | tf_op jit(solution)/shard_map/attend1/pallas_call | solution.py:83
  56.1 0.1 collective-permute-start.10
  56.2 2.2 %collective-permute-start.11 = (bf16[2,384,128]{2,1,0:T(8,128)(2,1)S(1)}, bf16[2,384,128]{2,1,0:T(8,128)(2,1)S(1)}, u32[]{:S(2)}, u32[]{:S(2)}) collective-permute-start(bf16[2,384,128]{2,1,0:T(8,128)(2,1)S(1)} %get-tuple-element.101.refs_2_), channel_id=1, source_target_pairs={{0,4},{2,6},{4,0},{6,2},{8,12},{10,14},{12,8},{14,10},{1,5},{3,7},... | collective-permute-start | bytes 589832 | tf_op jit(solution)/shard_map/ppermute | solution.py:527
  58.3 3.7 %collective-permute-done.10.refs_2_ = bf16[1,384,128]{2,1,0:T(8,128)(2,1)S(1)} collective-permute-done((bf16[1,384,128]{2,1,0:T(8,128)(2,1)S(1)}, bf16[1,384,128]{2,1,0:T(8,128)(2,1)S(1)}, u32[]{:S(2)}, u32[]{:S(2)}) %collective-permute-start.10) | collective-permute-done | bytes 98336 | tf_op jit(solution)/shard_map/ppermute | solution.py:520
  62.1 0.1 collective-permute-start.14
  62.2 1.6 %collective-permute-start.12 = (bf16[2,384,128]{2,1,0:T(8,128)(2,1)S(1)}, bf16[2,384,128]{2,1,0:T(8,128)(2,1)S(1)}, u32[]{:S(2)}, u32[]{:S(2)}) collective-permute-start(bf16[2,384,128]{2,1,0:T(8,128)(2,1)S(1)} %get-tuple-element.101.refs_2_), channel_id=1, source_target_pairs={{0,2},{2,0},{4,6},{6,4},{8,10},{10,8},{12,14},{14,12},{1,3},{3,1},... | collective-permute-start | bytes 589832 | tf_op jit(solution)/shard_map/ppermute | solution.py:531
  63.7 1.7 %collective-permute-done.11.refs_3_ = bf16[2,384,128]{2,1,0:T(8,128)(2,1)S(1)} collective-permute-done((bf16[2,384,128]{2,1,0:T(8,128)(2,1)S(1)}, bf16[2,384,128]{2,1,0:T(8,128)(2,1)S(1)}, u32[]{:S(2)}, u32[]{:S(2)}) %collective-permute-start.11) | collective-permute-done | bytes 196640 | tf_op jit(solution)/shard_map/ppermute | solution.py:527
  65.4 1.6 %collective-permute-start.13 = (bf16[2,384,128]{2,1,0:T(8,128)(2,1)S(1)}, bf16[2,384,128]{2,1,0:T(8,128)(2,1)S(1)}, u32[]{:S(2)}, u32[]{:S(2)}) collective-permute-start(bf16[2,384,128]{2,1,0:T(8,128)(2,1)S(1)} %collective-permute-done.11.refs_3_), channel_id=1, source_target_pairs={{0,2},{2,0},{4,6},{6,4},{8,10},{10,8},{12,14},{14,12},{1,3},{3,1},... | collective-permute-start | bytes 589832 | tf_op jit(solution)/shard_map/ppermute | solution.py:532
  66.9 0.5 collective-permute-start.15
  67.4 0.9 %collective-permute-done.14.refs_3_ = bf16[2,384,128]{2,1,0:T(8,128)(2,1)S(1)} collective-permute-done((bf16[2,384,128]{2,1,0:T(8,128)(2,1)S(1)}, bf16[2,384,128]{2,1,0:T(8,128)(2,1)S(1)}, u32[]{:S(2)}, u32[]{:S(2)}) %collective-permute-start.14) | collective-permute-done | bytes 196640 | tf_op jit(solution)/shard_map/ppermute | solution.py:527
  68.3 1.6 %collective-permute-start.16 = (bf16[2,384,128]{2,1,0:T(8,128)(2,1)S(1)}, bf16[2,384,128]{2,1,0:T(8,128)(2,1)S(1)}, u32[]{:S(2)}, u32[]{:S(2)}) collective-permute-start(bf16[2,384,128]{2,1,0:T(8,128)(2,1)S(1)} %collective-permute-done.14.refs_3_), channel_id=1, source_target_pairs={{0,2},{2,0},{4,6},{6,4},{8,10},{10,8},{12,14},{14,12},{1,3},{3,1},... | collective-permute-start | bytes 589832 | tf_op jit(solution)/shard_map/ppermute | solution.py:532
  69.9 0.1 collective-permute-done.12.refs_4_
  70.0 4.2 %collective-permute-done.13.refs_5_ = bf16[2,384,128]{2,1,0:T(8,128)(2,1)S(1)} collective-permute-done((bf16[2,384,128]{2,1,0:T(8,128)(2,1)S(1)}, bf16[2,384,128]{2,1,0:T(8,128)(2,1)S(1)}, u32[]{:S(2)}, u32[]{:S(2)}) %collective-permute-start.13) | collective-permute-done | bytes 196640 | tf_op jit(solution)/shard_map/ppermute | solution.py:532
  74.2 1.8 %output0.1 = (f32[8,128]{1,0:T(8,128)S(1)}, f32[192,1024]{1,0:T(8,128)S(1)}) custom-call(f32[8,128]{1,0:T(8,128)S(1)} %get-tuple-element.100.refs_0_, s32[3]{0:T(128)S(1)} %pad_add_fusion.refs_1_, bf16[2,384,128]{2,1,0:T(8,128)(2,1)S(1)} %get-tuple-element.101.refs_2_, bf16[2,384,128]{2,1,0:T(8,128)(2,1)S(1)} %collective-permute-done.11.refs_3_, ...), custom_call_target="tpu_custom_call" | custom-call | tf_op jit(solution)/shard_map/output0/pallas_call | solution.py:83
  76.0 2.1 %collective-permute-done.15.refs_4_ = bf16[2,384,128]{2,1,0:T(8,128)(2,1)S(1)} collective-permute-done((bf16[2,384,128]{2,1,0:T(8,128)(2,1)S(1)}, bf16[2,384,128]{2,1,0:T(8,128)(2,1)S(1)}, u32[]{:S(2)}, u32[]{:S(2)}) %collective-permute-start.15) | collective-permute-done | bytes 196640 | tf_op jit(solution)/shard_map/ppermute | solution.py:531
  78.2 2.1 %collective-permute-done.16.refs_5_ = bf16[2,384,128]{2,1,0:T(8,128)(2,1)S(1)} collective-permute-done((bf16[2,384,128]{2,1,0:T(8,128)(2,1)S(1)}, bf16[2,384,128]{2,1,0:T(8,128)(2,1)S(1)}, u32[]{:S(2)}, u32[]{:S(2)}) %collective-permute-start.16) | collective-permute-done | bytes 196640 | tf_op jit(solution)/shard_map/ppermute | solution.py:532
  80.3 2.2 %output1.1 = (f32[8,128]{1,0:T(8,128)}, f32[96,1024]{1,0:T(8,128)S(1)}, bf16[96,1024]{1,0:T(8,128)(2,1)S(1)}) custom-call(f32[8,128]{1,0:T(8,128)S(1)} %get-tuple-element.103.refs_0_, s32[3]{0:T(128)S(1)} %pad_add_fusion.refs_1_, bf16[2,384,128]{2,1,0:T(8,128)(2,1)S(1)} %get-tuple-element.104.refs_2_, ...), custom_call_target="tpu_custom_call" | custom-call | tf_op jit(solution)/shard_map/output1/pallas_call | solution.py:83
  82.5 1.4 %collective-permute-done.17 = bf16[96,1024]{1,0:T(8,128)(2,1)S(1)} collective-permute-done((bf16[96,1024]{1,0:T(8,128)(2,1)S(1)}, bf16[96,1024]{1,0:T(8,128)(2,1)S(1)}, u32[]{:S(2)}, u32[]{:S(2)}) %collective-permute-start.17) | collective-permute-done | bytes 196640 | tf_op jit(solution)/shard_map/ppermute | solution.py:558
  84.0 0.7 add_convert_fusion
  (40 shorter events, 0.1 us)
Async XLA Ops:
  0.0 3.1 %collective-permute-start = (bf16[96,1024]{1,0:T(8,128)(2,1)}, bf16[96,1024]{1,0:T(8,128)(2,1)S(1)}, u32[]{:S(2)}, u32[]{:S(2)}) collective-permute-start(bf16[96,1024]{1,0:T(8,128)(2,1)} %refs_2_.6), channel_id=1, source_target_pairs={{0,1},{1,0},{2,3},{3,2},{4,5},{5,4},{6,7},{7,6},{8,9},{9,8},{10,11... | collective-permute-start | bytes 589832 | tf_op jit(solution)/shard_map/ppermute | solution.py:441
  0.5 2.6 %copy-start = (bf16[96,1024]{1,0:T(8,128)(2,1)S(1)}, bf16[96,1024]{1,0:T(8,128)(2,1)}, u32[]{:S(2)}) copy-start(bf16[96,1024]{1,0:T(8,128)(2,1)} %refs_2_.6) | copy-start | bytes 589828
  0.5 2.6 %copy-start.8 = (s32[192]{0:T(256)S(1)}, s32[192]{0:T(256)}, u32[]{:S(2)}) copy-start(s32[192]{0:T(256)} %param.24) | copy-start | bytes 2308
  0.5 2.6 %copy-start.12 = (bf16[1024]{0:T(1024)(128)(2,1)S(1)}, bf16[1024]{0:T(1024)(128)(2,1)}, u32[]{:S(2)}) copy-start(bf16[1024]{0:T(1024)(128)(2,1)} %param.14) | copy-start | bytes 6148
  5.7 5.1 %copy-start.1 = (bf16[2,512,128]{2,1,0:T(8,128)(2,1)}, bf16[2,512,128]{2,1,0:T(8,128)(2,1)S(1)}, u32[]{:S(2)}) copy-start(bf16[2,512,128]{2,1,0:T(8,128)(2,1)S(1)} %get-tuple-element.73.refs_1_) | copy-start | bytes 786436
  5.7 9.7 %collective-permute-start.1 = (bf16[2,512,128]{2,1,0:T(8,128)(2,1)S(1)}, bf16[2,512,128]{2,1,0:T(8,128)(2,1)S(1)}, u32[]{:S(2)}, u32[]{:S(2)}) collective-permute-start(bf16[2,512,128]{2,1,0:T(8,128)(2,1)S(1)} %get-tuple-element.70), channel_id=1, source_target_pairs={{0,2},{2,0},{4,6},{6,4},{8,10},{10,8},{12,14},{14,12},{1,3},{3,1},... | collective-permute-start | bytes 786440 | tf_op jit(solution)/shard_map/ppermute | solution.py:479
  8.3 14.0 %collective-permute-start.2 = (bf16[2,512,128]{2,1,0:T(8,128)(2,1)}, bf16[2,512,128]{2,1,0:T(8,128)(2,1)}, u32[]{:S(2)}, u32[]{:S(2)}) collective-permute-start(bf16[2,512,128]{2,1,0:T(8,128)(2,1)} %get-tuple-element.74), channel_id=1, source_target_pairs={{0,2},{2,0},{4,6},{6,4},{8,10},{10,8},{12,14},{14,12},{1,3},{3,1},... | collective-permute-start | bytes 786440 | tf_op jit(solution)/shard_map/ppermute | solution.py:480
  13.3 3.0 %copy-start.3 = (bf16[2,480,128]{2,1,0:T(8,128)(2,1)}, bf16[2,480,128]{2,1,0:T(8,128)(2,1)S(1)}, u32[]{:S(2)}) copy-start(bf16[2,480,128]{2,1,0:T(8,128)(2,1)S(1)} %get-tuple-element.86.refs_1_) | copy-start | bytes 737284
  13.3 3.0 %copy-start.5 = (bf16[2,480,128]{2,1,0:T(8,128)(2,1)}, bf16[2,480,128]{2,1,0:T(8,128)(2,1)S(1)}, u32[]{:S(2)}) copy-start(bf16[2,480,128]{2,1,0:T(8,128)(2,1)S(1)} %get-tuple-element.78.refs_1_) | copy-start | bytes 737284
  13.3 5.0 %copy-start.13 = (bf16[2,480,128]{2,1,0:T(8,128)(2,1)}, bf16[2,480,128]{2,1,0:T(8,128)(2,1)S(1)}, u32[]{:S(2)}) copy-start(bf16[2,480,128]{2,1,0:T(8,128)(2,1)S(1)} %get-tuple-element.87) | copy-start | bytes 737284
  16.2 8.8 %collective-permute-start.3 = (bf16[2,512,128]{2,1,0:T(8,128)(2,1)}, bf16[2,512,128]{2,1,0:T(8,128)(2,1)}, u32[]{:S(2)}, u32[]{:S(2)}) collective-permute-start(bf16[2,512,128]{2,1,0:T(8,128)(2,1)} %get-tuple-element.75), channel_id=1, source_target_pairs={{0,4},{2,6},{4,0},{6,2},{8,12},{10,14},{12,8},{14,10},{1,5},{3,7},... | collective-permute-start | bytes 786440 | tf_op jit(solution)/shard_map/ppermute | solution.py:500
  18.3 10.3 %collective-permute-start.4 = (bf16[2,480,128]{2,1,0:T(8,128)(2,1)}, bf16[2,480,128]{2,1,0:T(8,128)(2,1)}, u32[]{:S(2)}, u32[]{:S(2)}) collective-permute-start(bf16[2,480,128]{2,1,0:T(8,128)(2,1)} %get-tuple-element.79), channel_id=1, source_target_pairs={{0,2},{2,0},{4,6},{6,4},{8,10},{10,8},{12,14},{14,12},{1,3},{3,1},... | collective-permute-start | bytes 737288 | tf_op jit(solution)/shard_map/ppermute | solution.py:479
  19.8 5.2 %copy-start.2 = (bf16[2,512,128]{2,1,0:T(8,128)(2,1)S(1)}, bf16[2,512,128]{2,1,0:T(8,128)(2,1)}, u32[]{:S(2)}) copy-start(bf16[2,512,128]{2,1,0:T(8,128)(2,1)} %copy-done.1) | copy-start | bytes 786436
  19.8 21.3 %collective-permute-start.6 = (bf16[2,480,128]{2,1,0:T(8,128)(2,1)}, bf16[2,480,128]{2,1,0:T(8,128)(2,1)S(1)}, u32[]{:S(2)}, u32[]{:S(2)}) collective-permute-start(bf16[2,480,128]{2,1,0:T(8,128)(2,1)} %copy-done.13), channel_id=1, source_target_pairs={{0,2},{2,0},{4,6},{6,4},{8,10},{10,8},{12,14},{14,12},{1,3},{3,1},... | collective-permute-start | bytes 737288 | tf_op jit(solution)/shard_map/ppermute | solution.py:480
  26.1 2.4 %copy-start.6 = (bf16[2,480,128]{2,1,0:T(8,128)(2,1)S(1)}, bf16[2,480,128]{2,1,0:T(8,128)(2,1)}, u32[]{:S(2)}) copy-start(bf16[2,480,128]{2,1,0:T(8,128)(2,1)} %copy-done.5) | copy-start | bytes 737284
  26.1 5.2 %copy-start.9 = (s32[192]{0:T(256)S(1)}, s32[192]{0:T(256)}, u32[]{:S(2)}) copy-start(s32[192]{0:T(256)} %refs_2_.9) | copy-start | bytes 2308
  26.2 12.5 %copy-start.7 = (bf16[4096]{0:T(1024)(128)(2,1)S(1)}, bf16[4096]{0:T(1024)(128)(2,1)}, u32[]{:S(2)}) copy-start(bf16[4096]{0:T(1024)(128)(2,1)} %param.18) | copy-start | bytes 24580
  26.2 12.5 %copy-start.10 = (bf16[512]{0:T(512)(128)(2,1)S(1)}, bf16[512]{0:T(512)(128)(2,1)}, u32[]{:S(2)}) copy-start(bf16[512]{0:T(512)(128)(2,1)} %param.19) | copy-start | bytes 3076
  26.2 12.5 %copy-start.11 = (bf16[512]{0:T(512)(128)(2,1)S(1)}, bf16[512]{0:T(512)(128)(2,1)}, u32[]{:S(2)}) copy-start(bf16[512]{0:T(512)(128)(2,1)} %param.20) | copy-start | bytes 3076
  26.2 14.9 %copy-start.4 = (bf16[2,480,128]{2,1,0:T(8,128)(2,1)S(1)}, bf16[2,480,128]{2,1,0:T(8,128)(2,1)}, u32[]{:S(2)}) copy-start(bf16[2,480,128]{2,1,0:T(8,128)(2,1)} %copy-done.3) | copy-start | bytes 737284
  29.6 11.5 %collective-permute-start.7 = (bf16[2,480,128]{2,1,0:T(8,128)(2,1)S(1)}, bf16[2,480,128]{2,1,0:T(8,128)(2,1)S(1)}, u32[]{:S(2)}, u32[]{:S(2)}) collective-permute-start(bf16[2,480,128]{2,1,0:T(8,128)(2,1)S(1)} %get-tuple-element.88), channel_id=1, source_target_pairs={{0,4},{2,6},{4,0},{6,2},{8,12},{10,14},{12,8},{14,10},{1,5},{3,7},... | collective-permute-start | bytes 737288 | tf_op jit(solution)/shard_map/ppermute | solution.py:500
  31.5 7.2 %collective-permute-start.5 = (bf16[1,512,128]{2,1,0:T(8,128)(2,1)S(1)}, bf16[1,512,128]{2,1,0:T(8,128)(2,1)S(1)}, u32[]{:S(2)}, u32[]{:S(2)}) collective-permute-start(bf16[1,512,128]{2,1,0:T(8,128)(2,1)S(1)} %get-tuple-element.82), channel_id=1, source_target_pairs={{0,8},{2,10},{4,12},{6,14},{8,0},{10,2},{12,4},{14,6},{1,9},{3,11}... | collective-permute-start | bytes 393224 | tf_op jit(solution)/shard_map/ppermute | solution.py:507
  41.2 12.5 %collective-permute-start.9 = (bf16[1,480,128]{2,1,0:T(8,128)(2,1)S(1)}, bf16[1,480,128]{2,1,0:T(8,128)(2,1)S(1)}, u32[]{:S(2)}, u32[]{:S(2)}) collective-permute-start(bf16[1,480,128]{2,1,0:T(8,128)(2,1)S(1)} %get-tuple-element.94), channel_id=1, source_target_pairs={{0,8},{2,10},{4,12},{6,14},{8,0},{10,2},{12,4},{14,6},{1,9},{3,11}... | collective-permute-start | bytes 368648 | tf_op jit(solution)/shard_map/ppermute | solution.py:507
  44.7 9.0 %collective-permute-start.8 = (bf16[1,384,128]{2,1,0:T(8,128)(2,1)S(1)}, bf16[1,384,128]{2,1,0:T(8,128)(2,1)S(1)}, u32[]{:S(2)}, u32[]{:S(2)}) collective-permute-start(bf16[1,384,128]{2,1,0:T(8,128)(2,1)S(1)} %get-tuple-element.91.refs_1_), channel_id=1, source_target_pairs={{0,8},{2,10},{4,12},{6,14},{8,0},{10,2},{12,4},{14,6},{1,9},{3,11}... | collective-permute-start | bytes 294920 | tf_op jit(solution)/shard_map/ppermute | solution.py:520
  56.1 5.9 %collective-permute-start.10 = (bf16[1,384,128]{2,1,0:T(8,128)(2,1)S(1)}, bf16[1,384,128]{2,1,0:T(8,128)(2,1)S(1)}, u32[]{:S(2)}, u32[]{:S(2)}) collective-permute-start(bf16[1,384,128]{2,1,0:T(8,128)(2,1)S(1)} %get-tuple-element.99.refs_1_), channel_id=1, source_target_pairs={{0,8},{2,10},{4,12},{6,14},{8,0},{10,2},{12,4},{14,6},{1,9},{3,11}... | collective-permute-start | bytes 294920 | tf_op jit(solution)/shard_map/ppermute | solution.py:520
  56.2 9.2 %collective-permute-start.11 = (bf16[2,384,128]{2,1,0:T(8,128)(2,1)S(1)}, bf16[2,384,128]{2,1,0:T(8,128)(2,1)S(1)}, u32[]{:S(2)}, u32[]{:S(2)}) collective-permute-start(bf16[2,384,128]{2,1,0:T(8,128)(2,1)S(1)} %get-tuple-element.101.refs_2_), channel_id=1, source_target_pairs={{0,4},{2,6},{4,0},{6,2},{8,12},{10,14},{12,8},{14,10},{1,5},{3,7},... | collective-permute-start | bytes 589832 | tf_op jit(solution)/shard_map/ppermute | solution.py:527
  62.1 6.2 %collective-permute-start.14 = (bf16[2,384,128]{2,1,0:T(8,128)(2,1)S(1)}, bf16[2,384,128]{2,1,0:T(8,128)(2,1)S(1)}, u32[]{:S(2)}, u32[]{:S(2)}) collective-permute-start(bf16[2,384,128]{2,1,0:T(8,128)(2,1)S(1)} %get-tuple-element.104.refs_2_), channel_id=1, source_target_pairs={{0,4},{2,6},{4,0},{6,2},{8,12},{10,14},{12,8},{14,10},{1,5},{3,7},... | collective-permute-start | bytes 589832 | tf_op jit(solution)/shard_map/ppermute | solution.py:527
  62.2 7.8 %collective-permute-start.12 = (bf16[2,384,128]{2,1,0:T(8,128)(2,1)S(1)}, bf16[2,384,128]{2,1,0:T(8,128)(2,1)S(1)}, u32[]{:S(2)}, u32[]{:S(2)}) collective-permute-start(bf16[2,384,128]{2,1,0:T(8,128)(2,1)S(1)} %get-tuple-element.101.refs_2_), channel_id=1, source_target_pairs={{0,2},{2,0},{4,6},{6,4},{8,10},{10,8},{12,14},{14,12},{1,3},{3,1},... | collective-permute-start | bytes 589832 | tf_op jit(solution)/shard_map/ppermute | solution.py:531
  65.4 8.8 %collective-permute-start.13 = (bf16[2,384,128]{2,1,0:T(8,128)(2,1)S(1)}, bf16[2,384,128]{2,1,0:T(8,128)(2,1)S(1)}, u32[]{:S(2)}, u32[]{:S(2)}) collective-permute-start(bf16[2,384,128]{2,1,0:T(8,128)(2,1)S(1)} %collective-permute-done.11.refs_3_), channel_id=1, source_target_pairs={{0,2},{2,0},{4,6},{6,4},{8,10},{10,8},{12,14},{14,12},{1,3},{3,1},... | collective-permute-start | bytes 589832 | tf_op jit(solution)/shard_map/ppermute | solution.py:532
  66.9 11.3 %collective-permute-start.15 = (bf16[2,384,128]{2,1,0:T(8,128)(2,1)S(1)}, bf16[2,384,128]{2,1,0:T(8,128)(2,1)S(1)}, u32[]{:S(2)}, u32[]{:S(2)}) collective-permute-start(bf16[2,384,128]{2,1,0:T(8,128)(2,1)S(1)} %get-tuple-element.104.refs_2_), channel_id=1, source_target_pairs={{0,2},{2,0},{4,6},{6,4},{8,10},{10,8},{12,14},{14,12},{1,3},{3,1},... | collective-permute-start | bytes 589832 | tf_op jit(solution)/shard_map/ppermute | solution.py:531
  68.3 12.0 %collective-permute-start.16 = (bf16[2,384,128]{2,1,0:T(8,128)(2,1)S(1)}, bf16[2,384,128]{2,1,0:T(8,128)(2,1)S(1)}, u32[]{:S(2)}, u32[]{:S(2)}) collective-permute-start(bf16[2,384,128]{2,1,0:T(8,128)(2,1)S(1)} %collective-permute-done.14.refs_3_), channel_id=1, source_target_pairs={{0,2},{2,0},{4,6},{6,4},{8,10},{10,8},{12,14},{14,12},{1,3},{3,1},... | collective-permute-start | bytes 589832 | tf_op jit(solution)/shard_map/ppermute | solution.py:532
  82.5 1.4 %collective-permute-start.17 = (bf16[96,1024]{1,0:T(8,128)(2,1)S(1)}, bf16[96,1024]{1,0:T(8,128)(2,1)S(1)}, u32[]{:S(2)}, u32[]{:S(2)}) collective-permute-start(bf16[96,1024]{1,0:T(8,128)(2,1)S(1)} %get-tuple-element.108), channel_id=1, source_target_pairs={{0,1},{1,0},{2,3},{3,2},{4,5},{5,4},{6,7},{7,6},{8,9},{9,8},{10,11... | collective-permute-start | bytes 589832 | tf_op jit(solution)/shard_map/ppermute | solution.py:558

commit v5 on v4

--- a/solution.py
+++ b/solution.py
@@ -18,26 +18,41 @@
 
 EPSILON = 1e-06
 ROPE_BASE = 1000000.0
-CHUNKS = 2
-SLOTS_PER_STEP = 8
-VMEM_LIMIT = 16 * 1024 * 1024
+CHUNK_HEADS = (1, 2, 1)
+F32 = jnp.float32
+BF16 = jnp.bfloat16
+MIB = 1024 * 1024
+SLOTS_AT_ONCE = {1: 24, 2: 8, 3: 8, 4: 4}
+COSTS = {'attend1': 3000, 'load_caches2': 300, 'load_weights1': 100000, 'project1': 30000, 'load_caches0': 10000, 'project2': 30000, 'attend2': 3000, 'join1': 3000, 'add_far1': 100000, 'add_near2_2': 300, 'load_out0': 100000, 'add_near1_2': 30000, 'output2': 3000, 'load_weights2': 10000, 'load_caches1': 3000}
+GATHER = ('y halved', 'y halved', 'y halved')
 ORDER = (
     ("project", 0),
     ("project", 1),
+    ("far", 0),
     ("load_caches", 0),
-    ("far", 0),
+    ("load_out", 0),
+    ("near", 0),
+    ("attend", 0),
+    ("far", 1),
+    ("gather", 0),
+    ("project", 2),
+    ("near", 1),
     ("load_caches", 1),
-    ("near", 0),
-    ("load_out", 0),
-    ("far", 1),
-    ("attend", 0),
-    ("near", 1),
+    ("far", 2),
+    ("attend", 1),
+    ("forward", 0),
+    ("load_caches", 2),
+    ("near", 2),
+    ("gather", 1),
+    ("attend", 2),
+    ("forward", 1),
+    ("output", 0),
+    ("load_out", 2),
+    ("gather", 2),
     ("load_out", 1),
-    ("gather", 0),
-    ("attend", 1),
-    ("gather", 1),
-    ("output", 0),
+    ("forward", 2),
     ("output", 1),
+    ("output", 2),
 )
 F32 = jnp.float32
 BF16 = jnp.bfloat16
@@ -73,7 +88,11 @@
 TOKEN = (8, HEAD_SIZE)
 
 
-def call(kernel, name, token, scalars, arrays, out_shapes, scratch):
+def estimate(name):
+    return pl.CostEstimate(flops=0, bytes_accessed=COSTS.get(name, 0) * 1000, transcendentals=0)
+
+
+def call(kernel, name, token, scalars, arrays, out_shapes, scratch, vmem_mib):
     def body(*refs):
         first_out = 1 + len(scalars) + len(arrays)
         refs[first_out][...] = jnp.zeros(TOKEN, F32)
@@ -87,10 +106,10 @@
         + [vmem] * len(arrays),
         out_specs=[vmem] * (1 + len(out_shapes)),
         out_shape=[pltpu.VMEM(TOKEN, F32)]
-        + [jax.ShapeDtypeStruct(shape, dtype) for shape, dtype in out_shapes],
+        + [pltpu.VMEM(shape, dtype) for shape, dtype in out_shapes],
         scratch_shapes=scratch,
-        compiler_params=pltpu.CompilerParams(vmem_limit_bytes=VMEM_LIMIT),
-        cost_estimate=pl.CostEstimate(flops=0, bytes_accessed=0, transcendentals=0),
+        compiler_params=pltpu.CompilerParams(vmem_limit_bytes=vmem_mib * MIB),
+        cost_estimate=estimate(name),
         name=name,
     )(token, *scalars, *arrays)
     return outs[0], outs[1:]
@@ -125,8 +144,8 @@
         out_shape=[pltpu.VMEM(TOKEN, F32)]
         + [pltpu.VMEM(shape, a.dtype) for a, shape in zip(arrays, shapes)],
         scratch_shapes=[pltpu.SemaphoreType.DMA((len(arrays),))],
-        compiler_params=pltpu.CompilerParams(vmem_limit_bytes=VMEM_LIMIT),
-        cost_estimate=pl.CostEstimate(flops=0, bytes_accessed=0, transcendentals=0),
+        compiler_params=pltpu.CompilerParams(vmem_limit_bytes=MIB),
+        cost_estimate=estimate(name),
         name=name,
     )(*[pltpu.with_memory_space_constraint(a, pltpu.HBM) for a in arrays], token)
     return outs[0], outs[1:]
@@ -153,8 +172,8 @@
         lane = lax.broadcasted_iota(jnp.int32, (per, HEAD_SIZE), 1)
         lane_high = place_ref[1] * 2
         for b, ref in enumerate(out_refs):
-            for z in range(nz // 2):
-                at = (b * (nz // 2) + z) * per
+            for z in range(nz):
+                at = (b * nz + z) * per
                 packed = jnp.where(
                     lane == lane_high,
                     high[at : at + per],
@@ -181,8 +200,8 @@
             preferred_element_type=F32,
         )
         for b, ref in enumerate(out_refs):
-            for z in range(nz // 2):
-                at = (b * (nz // 2) + z) * per
+            for z in range(nz):
+                at = (b * nz + z) * per
                 block = jnp.concatenate(
                     [
                         acc[at : at + per, c * HEAD_SIZE : (c + 1) * HEAD_SIZE]
@@ -198,7 +217,7 @@
     rows = 2 * nz * per
     depth = weights[0].shape[0]
     block_rows = heads * TILES * per + (SQUARE_ROWS if first else 0)
-    out_shapes = [((nz // 2, block_rows, HEAD_SIZE), BF16)] * 4
+    out_shapes = [((nz, block_rows, HEAD_SIZE), BF16)] * 2
     return call(
         functools.partial(project_kernel, nz=nz, per=per, first=first, heads=heads),
         "project" + str(chunk),
@@ -207,30 +226,32 @@
         [*inputs, *weights],
         out_shapes + ([((rows, depth), BF16)] if first else []),
         [pltpu.VMEM((rows, TILES * HEAD_SIZE), F32)],
+        12,
     )
 
 
-def add_kernel(*refs, terms):
+def add_kernel(*refs, starts, count):
+    terms = len(starts)
     outs = refs[terms:]
     each = outs[0].shape[0]
-    for z in range(refs[0].shape[0]):
-        total = refs[0][z].astype(F32)
-        for ref in refs[1:terms]:
-            total = total + ref[z].astype(F32)
+    for z in range(count):
+        total = refs[0][starts[0] + z].astype(F32)
+        for ref, start in zip(refs[1:terms], starts[1:]):
+            total = total + ref[start + z].astype(F32)
         outs[z // each][z % each] = total.astype(BF16)
 
 
-def add(name, token, arrays, parts):
-    count, rows, width = arrays[0].shape
-    shape = (count // parts, rows, width)
+def add(name, token, arrays, starts, count, parts):
+    shape = (count // parts,) + arrays[0].shape[1:]
     return call(
-        functools.partial(add_kernel, terms=len(arrays)),
+        functools.partial(add_kernel, starts=starts, count=count),
         name,
         token,
         [],
         arrays,
         [(shape, BF16)] * parts,
         [],
+        2,
     )
 
 
@@ -242,11 +263,11 @@
 
 def join(name, token, a, b):
     shape = (a.shape[0] + b.shape[0],) + a.shape[1:]
-    token, (joined,) = call(join_kernel, name, token, [], [a, b], [(shape, BF16)], [])
+    token, (joined,) = call(join_kernel, name, token, [], [a, b], [(shape, BF16)], [], 2)
     return token, joined
 
 
-def attend_kernel(*refs, first, heads, per, group, chunk):
+def attend_kernel(*refs, first, heads, per, group, start_head):
     place_ref, lengths_ref, mine_ref, last_ref = refs[:4]
     rest = refs[4:]
     if first:
@@ -271,7 +292,7 @@
     for g in range(heads):
         rows = pl.ds(g * head_rows, head_rows)
         summed = mine_ref[0, rows, :].astype(F32) + last_ref[0, rows, :].astype(F32)
-        head = chunk * heads + g
+        head = start_head + g
         for c in range(TILES):
             if c < QUERIES_PER_KV:
                 at = head * QUERIES_PER_KV + c
@@ -322,11 +343,13 @@
         top = jnp.max(scores, axis=0, keepdims=True)
         exps = jnp.where(valid, jnp.exp(scores - top), 0.0)
         weights = exps * (1.0 / jnp.sum(exps, axis=0, keepdims=True))
-        cache_weights = weights[:positions].T.astype(BF16)
+        cache_weights = weights[:positions].T
         own_weights = weights[positions : positions + 8].T[:, 0:1].astype(BF16).astype(F32)
         for i, s in enumerate(slots):
             mixed = jnp.dot(
-                cache_weights[i * qrows : (i + 1) * qrows], v_ref[s], preferred_element_type=F32
+                cache_weights[i * qrows : (i + 1) * qrows].astype(BF16),
+                v_ref[s],
+                preferred_element_type=F32,
             )
             for g in range(heads):
                 lo, hi = g * QUERIES_PER_KV, (g + 1) * QUERIES_PER_KV
@@ -344,7 +367,12 @@
     out_rows = heads * QUERIES_PER_KV * per
     return call(
         functools.partial(
-            attend_kernel, first=first, heads=heads, per=per, group=SLOTS_PER_STEP, chunk=chunk
+            attend_kernel,
+            first=first,
+            heads=heads,
+            per=per,
+            group=SLOTS_AT_ONCE[heads],
+            start_head=sum(CHUNK_HEADS[:chunk]),
         ),
         "attend" + str(chunk),
         token,
@@ -355,12 +383,14 @@
             pltpu.VMEM((heads * TILES * per, HEAD_SIZE), F32),
             pltpu.VMEM((out_rows, HEAD_SIZE), F32),
         ],
+        8,
     )
 
 
-def output_kernel(*refs, nz, per, first, last):
-    place_ref, block_refs, sor_ref, w_ref = refs[0], refs[1:5], refs[5], refs[6]
-    rest = refs[7:]
+def output_kernel(*refs, labels, nz, per, first, last):
+    count = len(labels)
+    place_ref, block_refs, sor_ref, w_ref = refs[0], refs[1 : 1 + count], refs[1 + count], refs[2 + count]
+    rest = refs[3 + count :]
     if not first:
         acc_in_ref, rest = rest[0], rest[1:]
     if last:
@@ -370,7 +400,12 @@
     tiles = block_refs[0].shape[1] // per
 
     one_hot = slot_one_hot(place_ref, sor_ref[...], nz, per)
-    wide = [ref[z].astype(F32) for ref in block_refs for z in range(nz // 2)]
+    wide = {
+        label: ref[z].astype(F32)
+        for ref, own in zip(block_refs, labels)
+        for z, label in enumerate(own)
+    }
+    wide = [wide[h, q] for h in range(2) for q in place_order(nz)]
     for c in range(tiles):
         stacked[:, c * HEAD_SIZE : (c + 1) * HEAD_SIZE] = jnp.concatenate(
             [block[c * per : (c + 1) * per] for block in wide], axis=0
@@ -393,7 +428,7 @@
         acc_out_ref[...] = product
 
 
-def output(token, place, blocks, sor, w_out, acc, *, chunk, chunks, nz, per):
+def output(token, place, blocks, labels, sor, w_out, acc, *, chunk, chunks, nz, per):
     first, last = chunk == 0, chunk == chunks - 1
     rows = 2 * nz * per
     depth, width = w_out.shape
@@ -402,13 +437,16 @@
     else:
         out_shapes = [((rows, width), F32)]
     return call(
-        functools.partial(output_kernel, nz=nz, per=per, first=first, last=last),
+        functools.partial(
+            output_kernel, labels=labels, nz=nz, per=per, first=first, last=last
+        ),
         "output" + str(chunk),
         token,
         [place],
         [*blocks, sor, w_out] + ([] if first else [acc]),
         out_shapes,
         [pltpu.VMEM((rows, depth), BF16)] + ([pltpu.VMEM((rows, width), F32)] if last else []),
+        12,
     )
 
 
@@ -433,7 +471,8 @@
     assert size % 2 == 0 and nz & (nz - 1) == 0 and nz > 2
     per = rotated_key_cache.shape[0]
     kv_heads = key_weight.shape[1] // HEAD_SIZE
-    heads = kv_heads // CHUNKS
+    assert sum(CHUNK_HEADS) == kv_heads and per == SLOTS_AT_ONCE[1]
+    chunks = len(CHUNK_HEADS)
     gx = lax.axis_index("gx")
     gy = lax.axis_index("gy")
     place = jnp.stack([gx // 2, gx % 2, gy]).astype(jnp.int32)
@@ -451,16 +490,25 @@
     sin = jnp.sin(angles) * jnp.where(lane < half_width, -1.0, 1.0)[None, :]
     biases = [b.reshape(-1, HEAD_SIZE) for b in (query_bias, key_bias_vector, value_bias_vector)]
 
-    columns = heads * QUERIES_PER_KV * HEAD_SIZE
-    narrow = heads * HEAD_SIZE
+    def head_window(c, width):
+        return pl.ds(sum(CHUNK_HEADS[:c]) * width, CHUNK_HEADS[c] * width)
+
+    wide = QUERIES_PER_KV * HEAD_SIZE
     everything = pl.ds(0, w_query.shape[0])
     positions = rotated_key_cache.shape[1]
     all_columns = pl.ds(0, w_out.shape[1])
     same_z = neighbour_pairs(nz)
     scale = acc = None
     inputs = [hidden_rows, other, gain, sor]
-    near, far, near_sent, far_sent = {}, {}, {}, {}
-    caches, w_outs, held, partial = {}, {}, {}, {}
+    kept, swapped, reduced = {}, {}, {}
+    caches, w_outs, gathered, waiting = {}, {}, {}, {}
+
+    def over_y(blocks, labels):
+        return lax.ppermute(blocks, "gx", same_z), [(1 - h, q) for h, q in labels]
+
+    def over_z(blocks, labels, stride):
+        moved = lax.ppermute(blocks, "gx", stride_pairs(nz, stride))
+        return moved, [(h, q ^ stride) for h, q in labels]
 
     def do_project(token, c):
         nonlocal inputs
@@ -468,16 +516,15 @@
             "load_weights" + str(c),
             token,
             [w_query, key_weight, value_weight],
-            [(everything, pl.ds(c * n, n)) for n in (columns, narrow, narrow)],
+            [(everything, head_window(c, n)) for n in (wide, HEAD_SIZE, HEAD_SIZE)],
         )
         token, outs = project(
-            token, place, inputs, weights, chunk=c, heads=heads, nz=nz, per=per
-        )
-        near[c], far[c], near_out, far_out = outs[:4]
+            token, place, inputs, weights, chunk=c, heads=CHUNK_HEADS[c], nz=nz, per=per
+        )
+        kept[c] = outs[0]
         if c == 0:
-            inputs = [outs[4]]
-        far_sent[c] = lax.ppermute(far_out, "gx", same_z)
-        near_sent[c] = lax.ppermute(near_out, "gx", same_z)
+            inputs = [outs[2]]
+        swapped[c] = lax.ppermute(outs[1], "gx", same_z)
         return token
 
     def do_load_caches(token, c):
@@ -485,59 +532,77 @@
             "load_caches" + str(c),
             token,
             [rotated_key_cache, stored_value_cache],
-            [(pl.ds(0, per), pl.ds(0, positions), pl.ds(c * narrow, narrow))] * 2,
+            [(pl.ds(0, per), pl.ds(0, positions), head_window(c, HEAD_SIZE))] * 2,
         )
         return token
 
     def do_load_out(token, c):
         token, (w_outs[c],) = load(
-            "load_out" + str(c), token, [w_out], [(pl.ds(c * columns, columns), all_columns)]
+            "load_out" + str(c), token, [w_out], [(head_window(c, wide), all_columns)]
         )
         return token
 
     def do_far(token, c):
-        token, (total,) = add("add_far" + str(c), token, [far[c], far_sent[c]], 1)
-        far[c] = lax.ppermute(total, "gx", stride_pairs(nz, 1))
+        half = nz // 2
+        token, (total,) = add(
+            "add_far" + str(c), token, [kept[c], swapped[c]], [half, half], half, 1
+        )
+        reduced[c] = lax.ppermute(total, "gx", stride_pairs(nz, 1))
         return token
 
     def do_near(token, c):
-        terms = [near[c], near_sent[c], far[c]]
+        terms, starts, count = [kept[c], swapped[c], reduced[c]], [0, 0, 0], nz // 2
         for stride in strides(nz)[1:]:
-            token, (kept, sent) = add("add_near" + str(c) + "_" + str(stride), token, terms, 2)
-            terms = [kept, lax.ppermute(sent, "gx", stride_pairs(nz, stride))]
-        partial[c] = terms
+            token, (mine, sent) = add(
+                "add_near" + str(c) + "_" + str(stride), token, terms, starts, count, 2
+            )
+            terms = [mine, lax.ppermute(sent, "gx", stride_pairs(nz, stride))]
+            starts, count = [0, 0], count // 2
+        reduced[c] = terms
         return token
 
     def do_attend(token, c):
         nonlocal scale
         token, outs = attend(
-            token, place, slot_valid_lengths, partial[c], scale, biases, cos, sin, *caches[c],
-            chunk=c, heads=heads,
+            token, place, slot_valid_lengths, reduced[c], scale, biases, cos, sin, *caches[c],
+            chunk=c, heads=CHUNK_HEADS[c],
         )
         if c == 0:
             scale = outs[1]
-        stride = strides(nz)[-1]
-        held[c] = outs[0], lax.ppermute(outs[0], "gx", stride_pairs(nz, stride))
+        own = outs[0], [(0, 0)]
+        first_move = over_y(*own) if GATHER[c] == "y first" else over_z(*own, strides(nz)[-1])
+        waiting[c] = own, first_move
         return token
 
     def do_gather(token, c):
-        blocks, received = held[c]
-        for stride in reversed(strides(nz)[:-1]):
-            token, blocks = join("join" + str(c) + "_" + str(stride), token, blocks, received)
-            received = lax.ppermute(blocks, "gx", stride_pairs(nz, stride))
-        held[c] = [
-            blocks,
-            received,
-            lax.ppermute(blocks, "gx", same_z),
-            lax.ppermute(received, "gx", same_z),
-        ]
+        held, moved = waiting[c]
+        for stride in reversed(strides(nz) if GATHER[c] == "y first" else strides(nz)[:-1]):
+            if GATHER[c] == "y first" and stride == 1:
+                break
+            token, joined = join("join" + str(c) + "_" + str(stride), token, held[0], moved[0])
+            held = joined, held[1] + moved[1]
+            moved = over_z(*held, stride)
+        waiting[c] = held, moved
+        gathered[c] = [held, moved]
+        if GATHER[c] == "y halved":
+            gathered[c].append(over_y(*held))
+        return token
+
+    def do_forward(token, c):
+        held, moved = waiting[c]
+        if GATHER[c] == "y halved":
+            gathered[c].append(over_y(*moved))
+            return token
+        token, joined = join("join" + str(c), token, held[0], moved[0])
+        held = joined, held[1] + moved[1]
+        gathered[c] = [held, over_z(*held, 1) if GATHER[c] == "y first" else over_y(*held)]
         return token
 
     def do_output(token, c):
         nonlocal acc
         token, acc = output(
-            token, place, held[c], sor, w_outs[c], acc if c == 0 else acc[0],
-            chunk=c, chunks=CHUNKS, nz=nz, per=per,
+            token, place, [a for a, _ in gathered[c]], [own for _, own in gathered[c]], sor,
+            w_outs[c], acc if c == 0 else acc[0], chunk=c, chunks=chunks, nz=nz, per=per,
         )
         return token
 
@@ -550,6 +615,7 @@
         "near": do_near,
         "attend": do_attend,
         "gather": do_gather,
+        "forward": do_forward,
         "output": do_output,
     }
     for step, c in ORDER:

time: 84.9 us -> 85.5 us (level)
  waiting for transfers between devices: 30.2 us -> 17.3 us
  starting transfers between devices: 22.5 us -> 34.1 us
  Pallas kernels: 30.6 us -> 32.3 us
    ppermute x16 -> x21, waiting for transfers between devices: 28.8 us -> 15.9 us  [the longest x6 9.42 us: over_z(): moved = lax.ppermute(blocks, 'gx', stride_pairs(nz, stride))]
    ppermute x16 -> x21, starting transfers between devices: 22.1 us -> 33.7 us  [the longest x6 8.5 us: over_z(): moved = lax.ppermute(blocks, 'gx', stride_pairs(nz, stride))]
    pallas_call x6 -> x9, Pallas kernels: 13.6 us -> 16.1 us  [load(): pl.pallas_call(functools.partial(load_kernel, windows=windows), in_specs=...]
    pallas_call x12 -> x18, Pallas kernels: 17 us -> 16.3 us  [call(): pl.pallas_call(body, in_specs=[vmem] + [pl.BlockSpec(memory_space=pltpu.S...]
  transfers between devices with their start and end apart: 18 -> 23, of which waited for: 11 -> 8; matrix products, arithmetic and copies ran while one was open for 0% -> 0% of each run, Pallas kernels for 28% -> 34%
where the time goes in v5:
time: 85.5 us; the launch traced here: 85.2 us
  starting transfers between devices  34.1 us (40%)
  Pallas kernels  32.3 us (38%)
  waiting for transfers between devices  17.3 us (20%)
  other arithmetic  1.04 us (1%)
    pallas_call x18, Pallas kernels, call(): pl.pallas_call(body, in_specs=[vmem] + [pl.BlockSpec(memory_space=pltpu.S...  16.3 us
    pallas_call x9, Pallas kernels, load(): pl.pallas_call(functools.partial(load_kernel, windows=windows), in_specs=...  16.1 us
    ppermute x6, waiting for transfers between devices, over_z(): moved = lax.ppermute(blocks, 'gx', stride_pairs(nz, stride))  9.42 us
    ppermute x6, starting transfers between devices, over_z(): moved = lax.ppermute(blocks, 'gx', stride_pairs(nz, stride))  8.5 us
    ppermute x3, starting transfers between devices, do_near(): terms = [mine, lax.ppermute(sent, 'gx', stride_pairs(nz, stride))]  8.07 us
    ppermute x6, starting transfers between devices, over_y(): return (lax.ppermute(blocks, 'gx', same_z), [(1 - h, q) for h, q in labels])  6.6 us
    ppermute x3, starting transfers between devices, do_far(): reduced[c] = lax.ppermute(total, 'gx', stride_pairs(nz, 1))  6.13 us
    ppermute x3, starting transfers between devices, do_project(): swapped[c] = lax.ppermute(outs[1], 'gx', same_z)  4.38 us
  transfers between devices with their start and end apart: 23, of which 8 were waited for; matrix products, arithmetic and copies ran while one was open for 0% of the time, Pallas kernels for 34%

profile of v5, /device:TPU:0, one launch (start us, length us, event | category | flops | bytes accessed | tf_op | source)
XLA Modules:
  0.0 85.2 jit_solution(12896413509043010809)
XLA Ops:
  0.0 0.5 collective-permute-start
  0.5 1.7 %load_weights0.1 = (f32[8,128]{1,0:T(8,128)S(1)}, bf16[1024,1024]{1,0:T(8,128)(2,1)S(1)}, bf16[1024,128]{1,0:T(8,128)(2,1)S(1)}, bf16[1024,128]{1,0:T(8,128)(2,1)S(1)}) custom-call(bf16[1024,4096]{1,0:T(8,128)(2,1)} %refs_0_.13, bf16[1024,512]{1,0:T(8,128)(2,1)} %refs_1_.9, bf16[1024,512]{1,0:T(8,128)(2,1)} %refs_2_.11, f32[8,128]{1,0:T(8,128)S(1)} %broadcast_in_dim.17.refs_3_), custom_call_target="tpu_custom_call" | custom-call | tf_op jit(solution)/shard_map/load_weights0/pallas_call | solution.py:140
  2.3 1.5 %project0.1 = (f32[8,128]{1,0:T(8,128)S(1)}, bf16[4,272,128]{2,1,0:T(8,128)(2,1)S(1)}, bf16[4,272,128]{2,1,0:T(8,128)(2,1)S(1)}, bf16[192,1024]{1,0:T(8,128)(2,1)S(1)}) custom-call(f32[8,128]{1,0:T(8,128)S(1)} %get-tuple-element.76.refs_0_, s32[3]{0:T(128)S(1)} %pad_add_fusion.refs_1_, bf16[96,1024]{1,0:T(8,128)(2,1)S(1)} %copy-done, ...), custom_call_target="tpu_custom_call" | custom-call | tf_op jit(solution)/shard_map/project0/pallas_call | solution.py:102
  3.8 2.6 %collective-permute-start.1 = (bf16[4,272,128]{2,1,0:T(8,128)(2,1)S(1)}, bf16[4,272,128]{2,1,0:T(8,128)(2,1)S(1)}, u32[]{:S(2)}, u32[]{:S(2)}) collective-permute-start(bf16[4,272,128]{2,1,0:T(8,128)(2,1)S(1)} %get-tuple-element.88), channel_id=1, source_target_pairs={{0,2},{2,0},{4,6},{6,4},{8,10},{10,8},{12,14},{14,12},{1,3},{3,1},... | collective-permute-start | bytes 835592 | tf_op jit(solution)/shard_map/ppermute | solution.py:527
  6.4 2.5 %load_weights1.1 = (f32[8,128]{1,0:T(8,128)S(1)}, bf16[1024,2048]{1,0:T(8,128)(2,1)S(1)}, bf16[1024,256]{1,0:T(8,128)(2,1)S(1)}, bf16[1024,256]{1,0:T(8,128)(2,1)S(1)}) custom-call(bf16[1024,4096]{1,0:T(8,128)(2,1)} %refs_0_.13, bf16[1024,512]{1,0:T(8,128)(2,1)} %refs_1_.9, bf16[1024,512]{1,0:T(8,128)(2,1)} %refs_2_.11, f32[8,128]{1,0:T(8,128)S(1)} %get-tuple-element.80.refs_3_), custom_call_target="tpu_custom_call" | custom-call | bytes 100000000 | tf_op jit(solution)/shard_map/load_weights1/pallas_call | solution.py:140
  8.9 1.7 %project1.1 = (f32[8,128]{1,0:T(8,128)S(1)}, bf16[4,480,128]{2,1,0:T(8,128)(2,1)S(1)}, bf16[4,480,128]{2,1,0:T(8,128)(2,1)S(1)}) custom-call(f32[8,128]{1,0:T(8,128)S(1)} %get-tuple-element.81.refs_0_, s32[3]{0:T(128)S(1)} %pad_add_fusion.refs_1_, bf16[192,1024]{1,0:T(8,128)(2,1)S(1)} %get-tuple-element.82.refs_2_, ...), custom_call_target="tpu_custom_call" | custom-call | bytes 30000000 | tf_op jit(solution)/shard_map/project1/pallas_call | solution.py:102
  10.7 3.1 %collective-permute-done.1.refs_2_ = bf16[4,272,128]{2,1,0:T(8,128)(2,1)S(1)} collective-permute-done((bf16[4,272,128]{2,1,0:T(8,128)(2,1)S(1)}, bf16[4,272,128]{2,1,0:T(8,128)(2,1)S(1)}, u32[]{:S(2)}, u32[]{:S(2)}) %collective-permute-start.1) | collective-permute-done | bytes 278560 | tf_op jit(solution)/shard_map/ppermute | solution.py:527
  13.8 2.1 %collective-permute-start.2 = (bf16[2,272,128]{2,1,0:T(8,128)(2,1)S(1)}, bf16[2,272,128]{2,1,0:T(8,128)(2,1)S(1)}, u32[]{:S(2)}, u32[]{:S(2)}) collective-permute-start(bf16[2,272,128]{2,1,0:T(8,128)(2,1)S(1)} %get-tuple-element.92), channel_id=1, source_target_pairs={{0,4},{2,6},{4,0},{6,2},{8,12},{10,14},{12,8},{14,10},{1,5},{3,7},... | collective-permute-start | bytes 417800 | tf_op jit(solution)/shard_map/ppermute | solution.py:550
  16.0 1.4 %load_caches0.1 = (f32[8,128]{1,0:T(8,128)S(1)}, bf16[24,128,128]{2,1,0:T(8,128)(2,1)S(1)}, bf16[24,128,128]{2,1,0:T(8,128)(2,1)S(1)}) custom-call(bf16[24,128,512]{2,1,0:T(8,128)(2,1)} %refs_0_.15, bf16[24,128,512]{2,1,0:T(8,128)(2,1)} %refs_1_.11, f32[8,128]{1,0:T(8,128)S(1)} %get-tuple-element.89.refs_2_), custom_call_target="tpu_custom_call" | custom-call | bytes 10000000 | tf_op jit(solution)/shard_map/load_caches0/pallas_call | solution.py:140
  17.5 1.6 %load_out0.1 = (f32[8,128]{1,0:T(8,128)S(1)}, bf16[1024,1024]{1,0:T(8,128)(2,1)S(1)}) custom-call(bf16[4096,1024]{1,0:T(8,128)(2,1)} %refs_0_.17, f32[8,128]{1,0:T(8,128)S(1)} %get-tuple-element.90.refs_1_), custom_call_target="tpu_custom_call" | custom-call | bytes 100000000 | tf_op jit(solution)/shard_map/load_out0/pallas_call | solution.py:140
  19.1 0.2 collective-permute-done.2.refs_3_
  19.3 2.8 %collective-permute-start.3 = (bf16[1,272,128]{2,1,0:T(8,128)(2,1)S(1)}, bf16[1,272,128]{2,1,0:T(8,128)(2,1)S(1)}, u32[]{:S(2)}, u32[]{:S(2)}) collective-permute-start(bf16[1,272,128]{2,1,0:T(8,128)(2,1)S(1)} %get-tuple-element.95), channel_id=1, source_target_pairs={{0,8},{2,10},{4,12},{6,14},{8,0},{10,2},{12,4},{14,6},{1,9},{3,11}... | collective-permute-start | bytes 208904 | tf_op jit(solution)/shard_map/ppermute | solution.py:559
  22.1 0.1 fusion
  22.2 2.4 %collective-permute-done.3.refs_4_ = bf16[1,272,128]{2,1,0:T(8,128)(2,1)S(1)} collective-permute-done((bf16[1,272,128]{2,1,0:T(8,128)(2,1)S(1)}, bf16[1,272,128]{2,1,0:T(8,128)(2,1)S(1)}, u32[]{:S(2)}, u32[]{:S(2)}) %collective-permute-start.3) | collective-permute-done | bytes 69664 | tf_op jit(solution)/shard_map/ppermute | solution.py:559
  24.6 2.2 %attend0.1 = (f32[8,128]{1,0:T(8,128)S(1)}, bf16[1,192,128]{2,1,0:T(8,128)(2,1)S(1)}, f32[24,128]{1,0:T(8,128)S(1)}) custom-call(f32[8,128]{1,0:T(8,128)S(1)} %get-tuple-element.93.refs_0_, s32[3]{0:T(128)S(1)} %pad_add_fusion.refs_1_, s32[192]{0:T(256)S(1)} %copy-done.3, bf16[1,272,128]{2,1,0:T(8,128)(2,1)S(1)} %get-tuple-element.94.refs_3_, ...), custom_call_target="tpu_custom_call" | custom-call | tf_op jit(solution)/shard_map/attend0/pallas_call | solution.py:102
  26.9 1.8 %collective-permute-start.6 = (bf16[2,480,128]{2,1,0:T(8,128)(2,1)S(1)}, bf16[2,480,128]{2,1,0:T(8,128)(2,1)S(1)}, u32[]{:S(2)}, u32[]{:S(2)}) collective-permute-start(bf16[2,480,128]{2,1,0:T(8,128)(2,1)S(1)} %get-tuple-element.109), channel_id=1, source_target_pairs={{0,4},{2,6},{4,0},{6,2},{8,12},{10,14},{12,8},{14,10},{1,5},{3,7},... | collective-permute-start | bytes 737288 | tf_op jit(solution)/shard_map/ppermute | solution.py:550
  28.6 3.2 %collective-permute-start.5 = (bf16[1,192,128]{2,1,0:T(8,128)(2,1)S(1)}, bf16[1,192,128]{2,1,0:T(8,128)(2,1)S(1)}, u32[]{:S(2)}, u32[]{:S(2)}) collective-permute-start(bf16[1,192,128]{2,1,0:T(8,128)(2,1)S(1)} %get-tuple-element.102.refs_1_), channel_id=1, source_target_pairs={{0,8},{2,10},{4,12},{6,14},{8,0},{10,2},{12,4},{14,6},{1,9},{3,11}... | collective-permute-start | bytes 147464 | tf_op jit(solution)/shard_map/ppermute | solution.py:510
  31.9 2.1 %collective-permute-done.5.refs_2_ = bf16[1,192,128]{2,1,0:T(8,128)(2,1)S(1)} collective-permute-done((bf16[1,192,128]{2,1,0:T(8,128)(2,1)S(1)}, bf16[1,192,128]{2,1,0:T(8,128)(2,1)S(1)}, u32[]{:S(2)}, u32[]{:S(2)}) %collective-permute-start.5) | collective-permute-done | bytes 49184 | tf_op jit(solution)/shard_map/ppermute | solution.py:510
  33.9 1.7 %load_weights2.1 = (f32[8,128]{1,0:T(8,128)S(1)}, bf16[1024,1024]{1,0:T(8,128)(2,1)S(1)}, bf16[1024,128]{1,0:T(8,128)(2,1)S(1)}, bf16[1024,128]{1,0:T(8,128)(2,1)S(1)}) custom-call(bf16[1024,4096]{1,0:T(8,128)(2,1)} %refs_0_.13, bf16[1024,512]{1,0:T(8,128)(2,1)} %refs_1_.9, bf16[1024,512]{1,0:T(8,128)(2,1)} %refs_2_.11, f32[8,128]{1,0:T(8,128)S(1)} %get-tuple-element.103.refs_3_), custom_call_target="tpu_custom_call" | custom-call | bytes 10000000 | tf_op jit(solution)/shard_map/load_weights2/pallas_call | solution.py:140
  35.7 1.2 %project2.1 = (f32[8,128]{1,0:T(8,128)S(1)}, bf16[4,240,128]{2,1,0:T(8,128)(2,1)S(1)}, bf16[4,240,128]{2,1,0:T(8,128)(2,1)S(1)}) custom-call(f32[8,128]{1,0:T(8,128)S(1)} %get-tuple-element.104.refs_0_, s32[3]{0:T(128)S(1)} %pad_add_fusion.refs_1_, bf16[192,1024]{1,0:T(8,128)(2,1)S(1)} %get-tuple-element.82.refs_2_, ...), custom_call_target="tpu_custom_call" | custom-call | bytes 30000000 | tf_op jit(solution)/shard_map/project2/pallas_call | solution.py:102
  36.9 1.7 %collective-permute-start.7 = (bf16[4,240,128]{2,1,0:T(8,128)(2,1)S(1)}, bf16[4,240,128]{2,1,0:T(8,128)(2,1)S(1)}, u32[]{:S(2)}, u32[]{:S(2)}) collective-permute-start(bf16[4,240,128]{2,1,0:T(8,128)(2,1)S(1)} %get-tuple-element.113), channel_id=1, source_target_pairs={{0,2},{2,0},{4,6},{6,4},{8,10},{10,8},{12,14},{14,12},{1,3},{3,1},... | collective-permute-start | bytes 737288 | tf_op jit(solution)/shard_map/ppermute | solution.py:527
  38.7 3.0 %collective-permute-start.8 = (bf16[1,480,128]{2,1,0:T(8,128)(2,1)S(1)}, bf16[1,480,128]{2,1,0:T(8,128)(2,1)S(1)}, u32[]{:S(2)}, u32[]{:S(2)}) collective-permute-start(bf16[1,480,128]{2,1,0:T(8,128)(2,1)S(1)} %get-tuple-element.116), channel_id=1, source_target_pairs={{0,8},{2,10},{4,12},{6,14},{8,0},{10,2},{12,4},{14,6},{1,9},{3,11}... | collective-permute-start | bytes 368648 | tf_op jit(solution)/shard_map/ppermute | solution.py:559
  41.7 1.9 %load_caches1.1 = (f32[8,128]{1,0:T(8,128)S(1)}, bf16[24,128,256]{2,1,0:T(8,128)(2,1)S(1)}, bf16[24,128,256]{2,1,0:T(8,128)(2,1)S(1)}) custom-call(bf16[24,128,512]{2,1,0:T(8,128)(2,1)} %refs_0_.15, bf16[24,128,512]{2,1,0:T(8,128)(2,1)} %refs_1_.11, f32[8,128]{1,0:T(8,128)S(1)} %get-tuple-element.110.refs_2_), custom_call_target="tpu_custom_call" | custom-call | bytes 3000000 | tf_op jit(solution)/shard_map/load_caches1/pallas_call | solution.py:140
  43.6 2.3 %collective-permute-start.9 = (bf16[2,240,128]{2,1,0:T(8,128)(2,1)S(1)}, bf16[2,240,128]{2,1,0:T(8,128)(2,1)S(1)}, u32[]{:S(2)}, u32[]{:S(2)}) collective-permute-start(bf16[2,240,128]{2,1,0:T(8,128)(2,1)S(1)} %get-tuple-element.122), channel_id=1, source_target_pairs={{0,4},{2,6},{4,0},{6,2},{8,12},{10,14},{12,8},{14,10},{1,5},{3,7},... | collective-permute-start | bytes 368648 | tf_op jit(solution)/shard_map/ppermute | solution.py:550
  45.9 2.4 %attend1.1 = (f32[8,128]{1,0:T(8,128)S(1)}, bf16[1,384,128]{2,1,0:T(8,128)(2,1)S(1)}) custom-call(f32[8,128]{1,0:T(8,128)S(1)} %get-tuple-element.114.refs_0_, s32[3]{0:T(128)S(1)} %pad_add_fusion.refs_1_, s32[192]{0:T(256)S(1)} %copy-done.3, bf16[1,480,128]{2,1,0:T(8,128)(2,1)S(1)} %get-tuple-element.115.refs_3_, ...), custom_call_target="tpu_custom_call" | custom-call | bytes 3000000 | tf_op jit(solution)/shard_map/attend1/pallas_call | solution.py:102
  48.3 1.7 %collective-permute-start.10 = (bf16[1,384,128]{2,1,0:T(8,128)(2,1)S(1)}, bf16[1,384,128]{2,1,0:T(8,128)(2,1)S(1)}, u32[]{:S(2)}, u32[]{:S(2)}) collective-permute-start(bf16[1,384,128]{2,1,0:T(8,128)(2,1)S(1)} %get-tuple-element.124.refs_1_), channel_id=1, source_target_pairs={{0,8},{2,10},{4,12},{6,14},{8,0},{10,2},{12,4},{14,6},{1,9},{3,11}... | collective-permute-start | bytes 294920 | tf_op jit(solution)/shard_map/ppermute | solution.py:510
  49.9 0.7 collective-permute-start.12
  50.7 1.4 %load_caches2.1 = (f32[8,128]{1,0:T(8,128)S(1)}, bf16[24,128,128]{2,1,0:T(8,128)(2,1)S(1)}, bf16[24,128,128]{2,1,0:T(8,128)(2,1)S(1)}) custom-call(bf16[24,128,512]{2,1,0:T(8,128)(2,1)} %refs_0_.15, bf16[24,128,512]{2,1,0:T(8,128)(2,1)} %refs_1_.11, f32[8,128]{1,0:T(8,128)S(1)} %get-tuple-element.120.refs_2_), custom_call_target="tpu_custom_call" | custom-call | bytes 300000 | tf_op jit(solution)/shard_map/load_caches2/pallas_call | solution.py:140
  52.1 4.1 %collective-permute-done.10.refs_2_ = bf16[1,384,128]{2,1,0:T(8,128)(2,1)S(1)} collective-permute-done((bf16[1,384,128]{2,1,0:T(8,128)(2,1)S(1)}, bf16[1,384,128]{2,1,0:T(8,128)(2,1)S(1)}, u32[]{:S(2)}, u32[]{:S(2)}) %collective-permute-start.10) | collective-permute-done | bytes 98336 | tf_op jit(solution)/shard_map/ppermute | solution.py:510
  56.2 0.2 collective-permute-start.16
  56.4 2.3 %collective-permute-start.11 = (bf16[1,240,128]{2,1,0:T(8,128)(2,1)S(1)}, bf16[1,240,128]{2,1,0:T(8,128)(2,1)S(1)}, u32[]{:S(2)}, u32[]{:S(2)}) collective-permute-start(bf16[1,240,128]{2,1,0:T(8,128)(2,1)S(1)} %get-tuple-element.127), channel_id=1, source_target_pairs={{0,8},{2,10},{4,12},{6,14},{8,0},{10,2},{12,4},{14,6},{1,9},{3,11}... | collective-permute-start | bytes 184328 | tf_op jit(solution)/shard_map/ppermute | solution.py:559
  58.7 1.1 %collective-permute-start.13 = (bf16[2,192,128]{2,1,0:T(8,128)(2,1)S(1)}, bf16[2,192,128]{2,1,0:T(8,128)(2,1)S(1)}, u32[]{:S(2)}, u32[]{:S(2)}) collective-permute-start(bf16[2,192,128]{2,1,0:T(8,128)(2,1)S(1)} %get-tuple-element.131.refs_2_), channel_id=1, source_target_pairs={{0,2},{2,0},{4,6},{6,4},{8,10},{10,8},{12,14},{14,12},{1,3},{3,1},... | collective-permute-start | bytes 294920 | tf_op jit(solution)/shard_map/ppermute | solution.py:507
  59.8 0.9 %collective-permute-start.14 = (bf16[2,192,128]{2,1,0:T(8,128)(2,1)S(1)}, bf16[2,192,128]{2,1,0:T(8,128)(2,1)S(1)}, u32[]{:S(2)}, u32[]{:S(2)}) collective-permute-start(bf16[2,192,128]{2,1,0:T(8,128)(2,1)S(1)} %collective-permute-done.12.refs_3_), channel_id=1, source_target_pairs={{0,2},{2,0},{4,6},{6,4},{8,10},{10,8},{12,14},{14,12},{1,3},{3,1},... | collective-permute-start | bytes 294920 | tf_op jit(solution)/shard_map/ppermute | solution.py:507
  60.8 0.8 collective-permute-done.11.refs_4_
  61.6 2.1 %attend2.1 = (f32[8,128]{1,0:T(8,128)S(1)}, bf16[1,192,128]{2,1,0:T(8,128)(2,1)S(1)}) custom-call(f32[8,128]{1,0:T(8,128)S(1)} %get-tuple-element.125.refs_0_, s32[3]{0:T(128)S(1)} %pad_add_fusion.refs_1_, s32[192]{0:T(256)S(1)} %copy-done.3, bf16[1,240,128]{2,1,0:T(8,128)(2,1)S(1)} %get-tuple-element.126.refs_3_, ...), custom_call_target="tpu_custom_call" | custom-call | bytes 3000000 | tf_op jit(solution)/shard_map/attend2/pallas_call | solution.py:102
  63.7 2.6 %collective-permute-start.15 = (bf16[1,192,128]{2,1,0:T(8,128)(2,1)S(1)}, bf16[1,192,128]{2,1,0:T(8,128)(2,1)S(1)}, u32[]{:S(2)}, u32[]{:S(2)}) collective-permute-start(bf16[1,192,128]{2,1,0:T(8,128)(2,1)S(1)} %get-tuple-element.135.refs_1_), channel_id=1, source_target_pairs={{0,8},{2,10},{4,12},{6,14},{8,0},{10,2},{12,4},{14,6},{1,9},{3,11}... | collective-permute-start | bytes 147464 | tf_op jit(solution)/shard_map/ppermute | solution.py:510
  66.3 1.1 %collective-permute-start.17 = (bf16[2,384,128]{2,1,0:T(8,128)(2,1)S(1)}, bf16[2,384,128]{2,1,0:T(8,128)(2,1)S(1)}, u32[]{:S(2)}, u32[]{:S(2)}) collective-permute-start(bf16[2,384,128]{2,1,0:T(8,128)(2,1)S(1)} %get-tuple-element.138.refs_2_), channel_id=1, source_target_pairs={{0,2},{2,0},{4,6},{6,4},{8,10},{10,8},{12,14},{14,12},{1,3},{3,1},... | collective-permute-start | bytes 589832 | tf_op jit(solution)/shard_map/ppermute | solution.py:507
  67.5 1.3 %output0.1 = (f32[8,128]{1,0:T(8,128)S(1)}, f32[192,1024]{1,0:T(8,128)S(1)}) custom-call(f32[8,128]{1,0:T(8,128)S(1)} %get-tuple-element.130.refs_0_, s32[3]{0:T(128)S(1)} %pad_add_fusion.refs_1_, bf16[2,192,128]{2,1,0:T(8,128)(2,1)S(1)} %get-tuple-element.131.refs_2_, bf16[2,192,128]{2,1,0:T(8,128)(2,1)S(1)} %collective-permute-done.12.refs_3_, ...), custom_call_target="tpu_custom_call" | custom-call | tf_op jit(solution)/shard_map/output0/pallas_call | solution.py:102
  68.8 1.6 %load_out2.1 = (f32[8,128]{1,0:T(8,128)S(1)}, bf16[1024,1024]{1,0:T(8,128)(2,1)S(1)}) custom-call(bf16[4096,1024]{1,0:T(8,128)(2,1)} %refs_0_.17, f32[8,128]{1,0:T(8,128)S(1)} %get-tuple-element.133.refs_1_), custom_call_target="tpu_custom_call" | custom-call | tf_op jit(solution)/shard_map/load_out2/pallas_call | solution.py:140
  70.4 1.0 %collective-permute-start.18 = (bf16[2,384,128]{2,1,0:T(8,128)(2,1)S(1)}, bf16[2,384,128]{2,1,0:T(8,128)(2,1)S(1)}, u32[]{:S(2)}, u32[]{:S(2)}) collective-permute-start(bf16[2,384,128]{2,1,0:T(8,128)(2,1)S(1)} %collective-permute-done.16.refs_3_), channel_id=1, source_target_pairs={{0,2},{2,0},{4,6},{6,4},{8,10},{10,8},{12,14},{14,12},{1,3},{3,1},... | collective-permute-start | bytes 589832 | tf_op jit(solution)/shard_map/ppermute | solution.py:507
  71.5 1.3 %collective-permute-start.20 = (bf16[2,192,128]{2,1,0:T(8,128)(2,1)S(1)}, bf16[2,192,128]{2,1,0:T(8,128)(2,1)S(1)}, u32[]{:S(2)}, u32[]{:S(2)}) collective-permute-start(bf16[2,192,128]{2,1,0:T(8,128)(2,1)S(1)} %get-tuple-element.142.refs_2_), channel_id=1, source_target_pairs={{0,2},{2,0},{4,6},{6,4},{8,10},{10,8},{12,14},{14,12},{1,3},{3,1},... | collective-permute-start | bytes 294920 | tf_op jit(solution)/shard_map/ppermute | solution.py:507
  72.8 3.3 %collective-permute-done.19.refs_3_ = bf16[2,192,128]{2,1,0:T(8,128)(2,1)S(1)} collective-permute-done((bf16[2,192,128]{2,1,0:T(8,128)(2,1)S(1)}, bf16[2,192,128]{2,1,0:T(8,128)(2,1)S(1)}, u32[]{:S(2)}, u32[]{:S(2)}) %collective-permute-start.19) | collective-permute-done | bytes 98336 | tf_op jit(solution)/shard_map/ppermute | solution.py:510
  76.1 1.1 %collective-permute-start.21 = (bf16[2,192,128]{2,1,0:T(8,128)(2,1)S(1)}, bf16[2,192,128]{2,1,0:T(8,128)(2,1)S(1)}, u32[]{:S(2)}, u32[]{:S(2)}) collective-permute-start(bf16[2,192,128]{2,1,0:T(8,128)(2,1)S(1)} %collective-permute-done.19.refs_3_), channel_id=1, source_target_pairs={{0,2},{2,0},{4,6},{6,4},{8,10},{10,8},{12,14},{14,12},{1,3},{3,1},... | collective-permute-start | bytes 294920 | tf_op jit(solution)/shard_map/ppermute | solution.py:507
  77.2 2.2 %load_out1.1 = (f32[8,128]{1,0:T(8,128)S(1)}, bf16[2048,1024]{1,0:T(8,128)(2,1)S(1)}) custom-call(bf16[4096,1024]{1,0:T(8,128)(2,1)} %refs_0_.17, f32[8,128]{1,0:T(8,128)S(1)} %get-tuple-element.136.refs_1_), custom_call_target="tpu_custom_call" | custom-call | tf_op jit(solution)/shard_map/load_out1/pallas_call | solution.py:140
  79.4 1.8 %output1.1 = (f32[8,128]{1,0:T(8,128)S(1)}, f32[192,1024]{1,0:T(8,128)S(1)}) custom-call(f32[8,128]{1,0:T(8,128)S(1)} %get-tuple-element.137.refs_0_, s32[3]{0:T(128)S(1)} %pad_add_fusion.refs_1_, bf16[2,384,128]{2,1,0:T(8,128)(2,1)S(1)} %get-tuple-element.138.refs_2_, bf16[2,384,128]{2,1,0:T(8,128)(2,1)S(1)} %collective-permute-done.16.refs_3_, ...), custom_call_target="tpu_custom_call" | custom-call | tf_op jit(solution)/shard_map/output1/pallas_call | solution.py:102
  81.3 1.7 %output2.1 = (f32[8,128]{1,0:T(8,128)}, f32[96,1024]{1,0:T(8,128)S(1)}, bf16[96,1024]{1,0:T(8,128)(2,1)S(1)}) custom-call(f32[8,128]{1,0:T(8,128)S(1)} %get-tuple-element.141.refs_0_, s32[3]{0:T(128)S(1)} %pad_add_fusion.refs_1_, bf16[2,192,128]{2,1,0:T(8,128)(2,1)S(1)} %get-tuple-element.142.refs_2_, ...), custom_call_target="tpu_custom_call" | custom-call | bytes 3000000 | tf_op jit(solution)/shard_map/output2/pallas_call | solution.py:102
  83.0 1.4 %collective-permute-done.22 = bf16[96,1024]{1,0:T(8,128)(2,1)S(1)} collective-permute-done((bf16[96,1024]{1,0:T(8,128)(2,1)S(1)}, bf16[96,1024]{1,0:T(8,128)(2,1)S(1)}, u32[]{:S(2)}, u32[]{:S(2)}) %collective-permute-start.22) | collective-permute-done | bytes 196640 | tf_op jit(solution)/shard_map/ppermute | solution.py:624
  84.5 0.7 add_convert_fusion
  (45 shorter events, 0.8 us)
Async XLA Ops:
  0.0 2.3 %collective-permute-start = (bf16[96,1024]{1,0:T(8,128)(2,1)}, bf16[96,1024]{1,0:T(8,128)(2,1)S(1)}, u32[]{:S(2)}, u32[]{:S(2)}) collective-permute-start(bf16[96,1024]{1,0:T(8,128)(2,1)} %refs_2_.8), channel_id=1, source_target_pairs={{0,1},{1,0},{2,3},{3,2},{4,5},{5,4},{6,7},{7,6},{8,9},{9,8},{10,11... | collective-permute-start | bytes 589832 | tf_op jit(solution)/shard_map/ppermute | solution.py:480
  0.5 1.8 %copy-start = (bf16[96,1024]{1,0:T(8,128)(2,1)S(1)}, bf16[96,1024]{1,0:T(8,128)(2,1)}, u32[]{:S(2)}) copy-start(bf16[96,1024]{1,0:T(8,128)(2,1)} %refs_2_.8) | copy-start | bytes 589828
  0.5 1.8 %copy-start.2 = (s32[192]{0:T(256)S(1)}, s32[192]{0:T(256)}, u32[]{:S(2)}) copy-start(s32[192]{0:T(256)} %param.24) | copy-start | bytes 2308
  0.5 1.9 %copy-start.6 = (bf16[1024]{0:T(1024)(128)(2,1)S(1)}, bf16[1024]{0:T(1024)(128)(2,1)}, u32[]{:S(2)}) copy-start(bf16[1024]{0:T(1024)(128)(2,1)} %param.14) | copy-start | bytes 6148
  3.8 10.0 %collective-permute-start.1 = (bf16[4,272,128]{2,1,0:T(8,128)(2,1)S(1)}, bf16[4,272,128]{2,1,0:T(8,128)(2,1)S(1)}, u32[]{:S(2)}, u32[]{:S(2)}) collective-permute-start(bf16[4,272,128]{2,1,0:T(8,128)(2,1)S(1)} %get-tuple-element.88), channel_id=1, source_target_pairs={{0,2},{2,0},{4,6},{6,4},{8,10},{10,8},{12,14},{14,12},{1,3},{3,1},... | collective-permute-start | bytes 835592 | tf_op jit(solution)/shard_map/ppermute | solution.py:527
  8.9 7.0 %copy-start.3 = (s32[192]{0:T(256)S(1)}, s32[192]{0:T(256)}, u32[]{:S(2)}) copy-start(s32[192]{0:T(256)} %refs_2_.13) | copy-start | bytes 2308
  10.7 16.1 %collective-permute-start.4 = (bf16[4,480,128]{2,1,0:T(8,128)(2,1)S(1)}, bf16[4,480,128]{2,1,0:T(8,128)(2,1)S(1)}, u32[]{:S(2)}, u32[]{:S(2)}) collective-permute-start(bf16[4,480,128]{2,1,0:T(8,128)(2,1)S(1)} %get-tuple-element.100), channel_id=1, source_target_pairs={{0,2},{2,0},{4,6},{6,4},{8,10},{10,8},{12,14},{14,12},{1,3},{3,1},... | collective-permute-start | bytes 1474568 | tf_op jit(solution)/shard_map/ppermute | solution.py:527
  13.8 5.4 %collective-permute-start.2 = (bf16[2,272,128]{2,1,0:T(8,128)(2,1)S(1)}, bf16[2,272,128]{2,1,0:T(8,128)(2,1)S(1)}, u32[]{:S(2)}, u32[]{:S(2)}) collective-permute-start(bf16[2,272,128]{2,1,0:T(8,128)(2,1)S(1)} %get-tuple-element.92), channel_id=1, source_target_pairs={{0,4},{2,6},{4,0},{6,2},{8,12},{10,14},{12,8},{14,10},{1,5},{3,7},... | collective-permute-start | bytes 417800 | tf_op jit(solution)/shard_map/ppermute | solution.py:550
  17.4 7.2 %copy-start.1 = (bf16[4096]{0:T(1024)(128)(2,1)S(1)}, bf16[4096]{0:T(1024)(128)(2,1)}, u32[]{:S(2)}) copy-start(bf16[4096]{0:T(1024)(128)(2,1)} %param.18) | copy-start | bytes 24580
  17.4 7.2 %copy-start.4 = (bf16[512]{0:T(512)(128)(2,1)S(1)}, bf16[512]{0:T(512)(128)(2,1)}, u32[]{:S(2)}) copy-start(bf16[512]{0:T(512)(128)(2,1)} %param.19) | copy-start | bytes 3076
  17.4 7.2 %copy-start.5 = (bf16[512]{0:T(512)(128)(2,1)S(1)}, bf16[512]{0:T(512)(128)(2,1)}, u32[]{:S(2)}) copy-start(bf16[512]{0:T(512)(128)(2,1)} %param.20) | copy-start | bytes 3076
  19.3 5.3 %collective-permute-start.3 = (bf16[1,272,128]{2,1,0:T(8,128)(2,1)S(1)}, bf16[1,272,128]{2,1,0:T(8,128)(2,1)S(1)}, u32[]{:S(2)}, u32[]{:S(2)}) collective-permute-start(bf16[1,272,128]{2,1,0:T(8,128)(2,1)S(1)} %get-tuple-element.95), channel_id=1, source_target_pairs={{0,8},{2,10},{4,12},{6,14},{8,0},{10,2},{12,4},{14,6},{1,9},{3,11}... | collective-permute-start | bytes 208904 | tf_op jit(solution)/shard_map/ppermute | solution.py:559
  26.9 11.7 %collective-permute-start.6 = (bf16[2,480,128]{2,1,0:T(8,128)(2,1)S(1)}, bf16[2,480,128]{2,1,0:T(8,128)(2,1)S(1)}, u32[]{:S(2)}, u32[]{:S(2)}) collective-permute-start(bf16[2,480,128]{2,1,0:T(8,128)(2,1)S(1)} %get-tuple-element.109), channel_id=1, source_target_pairs={{0,4},{2,6},{4,0},{6,2},{8,12},{10,14},{12,8},{14,10},{1,5},{3,7},... | collective-permute-start | bytes 737288 | tf_op jit(solution)/shard_map/ppermute | solution.py:550
  28.6 5.3 %collective-permute-start.5 = (bf16[1,192,128]{2,1,0:T(8,128)(2,1)S(1)}, bf16[1,192,128]{2,1,0:T(8,128)(2,1)S(1)}, u32[]{:S(2)}, u32[]{:S(2)}) collective-permute-start(bf16[1,192,128]{2,1,0:T(8,128)(2,1)S(1)} %get-tuple-element.102.refs_1_), channel_id=1, source_target_pairs={{0,8},{2,10},{4,12},{6,14},{8,0},{10,2},{12,4},{14,6},{1,9},{3,11}... | collective-permute-start | bytes 147464 | tf_op jit(solution)/shard_map/ppermute | solution.py:510
  36.9 6.7 %collective-permute-start.7 = (bf16[4,240,128]{2,1,0:T(8,128)(2,1)S(1)}, bf16[4,240,128]{2,1,0:T(8,128)(2,1)S(1)}, u32[]{:S(2)}, u32[]{:S(2)}) collective-permute-start(bf16[4,240,128]{2,1,0:T(8,128)(2,1)S(1)} %get-tuple-element.113), channel_id=1, source_target_pairs={{0,2},{2,0},{4,6},{6,4},{8,10},{10,8},{12,14},{14,12},{1,3},{3,1},... | collective-permute-start | bytes 737288 | tf_op jit(solution)/shard_map/ppermute | solution.py:527
  38.7 7.2 %collective-permute-start.8 = (bf16[1,480,128]{2,1,0:T(8,128)(2,1)S(1)}, bf16[1,480,128]{2,1,0:T(8,128)(2,1)S(1)}, u32[]{:S(2)}, u32[]{:S(2)}) collective-permute-start(bf16[1,480,128]{2,1,0:T(8,128)(2,1)S(1)} %get-tuple-element.116), channel_id=1, source_target_pairs={{0,8},{2,10},{4,12},{6,14},{8,0},{10,2},{12,4},{14,6},{1,9},{3,11}... | collective-permute-start | bytes 368648 | tf_op jit(solution)/shard_map/ppermute | solution.py:559
  43.6 8.4 %collective-permute-start.9 = (bf16[2,240,128]{2,1,0:T(8,128)(2,1)S(1)}, bf16[2,240,128]{2,1,0:T(8,128)(2,1)S(1)}, u32[]{:S(2)}, u32[]{:S(2)}) collective-permute-start(bf16[2,240,128]{2,1,0:T(8,128)(2,1)S(1)} %get-tuple-element.122), channel_id=1, source_target_pairs={{0,4},{2,6},{4,0},{6,2},{8,12},{10,14},{12,8},{14,10},{1,5},{3,7},... | collective-permute-start | bytes 368648 | tf_op jit(solution)/shard_map/ppermute | solution.py:550
  48.3 7.9 %collective-permute-start.10 = (bf16[1,384,128]{2,1,0:T(8,128)(2,1)S(1)}, bf16[1,384,128]{2,1,0:T(8,128)(2,1)S(1)}, u32[]{:S(2)}, u32[]{:S(2)}) collective-permute-start(bf16[1,384,128]{2,1,0:T(8,128)(2,1)S(1)} %get-tuple-element.124.refs_1_), channel_id=1, source_target_pairs={{0,8},{2,10},{4,12},{6,14},{8,0},{10,2},{12,4},{14,6},{1,9},{3,11}... | collective-permute-start | bytes 294920 | tf_op jit(solution)/shard_map/ppermute | solution.py:510
  49.9 9.9 %collective-permute-start.12 = (bf16[2,192,128]{2,1,0:T(8,128)(2,1)S(1)}, bf16[2,192,128]{2,1,0:T(8,128)(2,1)S(1)}, u32[]{:S(2)}, u32[]{:S(2)}) collective-permute-start(bf16[2,192,128]{2,1,0:T(8,128)(2,1)S(1)} %get-tuple-element.131.refs_2_), channel_id=1, source_target_pairs={{0,4},{2,6},{4,0},{6,2},{8,12},{10,14},{12,8},{14,10},{1,5},{3,7},... | collective-permute-start | bytes 294920 | tf_op jit(solution)/shard_map/ppermute | solution.py:510
  56.2 14.2 %collective-permute-start.16 = (bf16[2,384,128]{2,1,0:T(8,128)(2,1)S(1)}, bf16[2,384,128]{2,1,0:T(8,128)(2,1)S(1)}, u32[]{:S(2)}, u32[]{:S(2)}) collective-permute-start(bf16[2,384,128]{2,1,0:T(8,128)(2,1)S(1)} %get-tuple-element.138.refs_2_), channel_id=1, source_target_pairs={{0,4},{2,6},{4,0},{6,2},{8,12},{10,14},{12,8},{14,10},{1,5},{3,7},... | collective-permute-start | bytes 589832 | tf_op jit(solution)/shard_map/ppermute | solution.py:510
  56.4 5.2 %collective-permute-start.11 = (bf16[1,240,128]{2,1,0:T(8,128)(2,1)S(1)}, bf16[1,240,128]{2,1,0:T(8,128)(2,1)S(1)}, u32[]{:S(2)}, u32[]{:S(2)}) collective-permute-start(bf16[1,240,128]{2,1,0:T(8,128)(2,1)S(1)} %get-tuple-element.127), channel_id=1, source_target_pairs={{0,8},{2,10},{4,12},{6,14},{8,0},{10,2},{12,4},{14,6},{1,9},{3,11}... | collective-permute-start | bytes 184328 | tf_op jit(solution)/shard_map/ppermute | solution.py:559
  58.7 8.7 %collective-permute-start.13 = (bf16[2,192,128]{2,1,0:T(8,128)(2,1)S(1)}, bf16[2,192,128]{2,1,0:T(8,128)(2,1)S(1)}, u32[]{:S(2)}, u32[]{:S(2)}) collective-permute-start(bf16[2,192,128]{2,1,0:T(8,128)(2,1)S(1)} %get-tuple-element.131.refs_2_), channel_id=1, source_target_pairs={{0,2},{2,0},{4,6},{6,4},{8,10},{10,8},{12,14},{14,12},{1,3},{3,1},... | collective-permute-start | bytes 294920 | tf_op jit(solution)/shard_map/ppermute | solution.py:507
  59.8 7.7 %collective-permute-start.14 = (bf16[2,192,128]{2,1,0:T(8,128)(2,1)S(1)}, bf16[2,192,128]{2,1,0:T(8,128)(2,1)S(1)}, u32[]{:S(2)}, u32[]{:S(2)}) collective-permute-start(bf16[2,192,128]{2,1,0:T(8,128)(2,1)S(1)} %collective-permute-done.12.refs_3_), channel_id=1, source_target_pairs={{0,2},{2,0},{4,6},{6,4},{8,10},{10,8},{12,14},{14,12},{1,3},{3,1},... | collective-permute-start | bytes 294920 | tf_op jit(solution)/shard_map/ppermute | solution.py:507
  63.7 7.7 %collective-permute-start.15 = (bf16[1,192,128]{2,1,0:T(8,128)(2,1)S(1)}, bf16[1,192,128]{2,1,0:T(8,128)(2,1)S(1)}, u32[]{:S(2)}, u32[]{:S(2)}) collective-permute-start(bf16[1,192,128]{2,1,0:T(8,128)(2,1)S(1)} %get-tuple-element.135.refs_1_), channel_id=1, source_target_pairs={{0,8},{2,10},{4,12},{6,14},{8,0},{10,2},{12,4},{14,6},{1,9},{3,11}... | collective-permute-start | bytes 147464 | tf_op jit(solution)/shard_map/ppermute | solution.py:510
  66.3 13.1 %collective-permute-start.17 = (bf16[2,384,128]{2,1,0:T(8,128)(2,1)S(1)}, bf16[2,384,128]{2,1,0:T(8,128)(2,1)S(1)}, u32[]{:S(2)}, u32[]{:S(2)}) collective-permute-start(bf16[2,384,128]{2,1,0:T(8,128)(2,1)S(1)} %get-tuple-element.138.refs_2_), channel_id=1, source_target_pairs={{0,2},{2,0},{4,6},{6,4},{8,10},{10,8},{12,14},{14,12},{1,3},{3,1},... | collective-permute-start | bytes 589832 | tf_op jit(solution)/shard_map/ppermute | solution.py:507
  70.4 9.0 %collective-permute-start.18 = (bf16[2,384,128]{2,1,0:T(8,128)(2,1)S(1)}, bf16[2,384,128]{2,1,0:T(8,128)(2,1)S(1)}, u32[]{:S(2)}, u32[]{:S(2)}) collective-permute-start(bf16[2,384,128]{2,1,0:T(8,128)(2,1)S(1)} %collective-permute-done.16.refs_3_), channel_id=1, source_target_pairs={{0,2},{2,0},{4,6},{6,4},{8,10},{10,8},{12,14},{14,12},{1,3},{3,1},... | collective-permute-start | bytes 589832 | tf_op jit(solution)/shard_map/ppermute | solution.py:507
  71.4 4.7 %collective-permute-start.19 = (bf16[2,192,128]{2,1,0:T(8,128)(2,1)S(1)}, bf16[2,192,128]{2,1,0:T(8,128)(2,1)S(1)}, u32[]{:S(2)}, u32[]{:S(2)}) collective-permute-start(bf16[2,192,128]{2,1,0:T(8,128)(2,1)S(1)} %get-tuple-element.142.refs_2_), channel_id=1, source_target_pairs={{0,4},{2,6},{4,0},{6,2},{8,12},{10,14},{12,8},{14,10},{1,5},{3,7},... | collective-permute-start | bytes 294920 | tf_op jit(solution)/shard_map/ppermute | solution.py:510
  71.5 9.8 %collective-permute-start.20 = (bf16[2,192,128]{2,1,0:T(8,128)(2,1)S(1)}, bf16[2,192,128]{2,1,0:T(8,128)(2,1)S(1)}, u32[]{:S(2)}, u32[]{:S(2)}) collective-permute-start(bf16[2,192,128]{2,1,0:T(8,128)(2,1)S(1)} %get-tuple-element.142.refs_2_), channel_id=1, source_target_pairs={{0,2},{2,0},{4,6},{6,4},{8,10},{10,8},{12,14},{14,12},{1,3},{3,1},... | collective-permute-start | bytes 294920 | tf_op jit(solution)/shard_map/ppermute | solution.py:507
  76.1 5.2 %collective-permute-start.21 = (bf16[2,192,128]{2,1,0:T(8,128)(2,1)S(1)}, bf16[2,192,128]{2,1,0:T(8,128)(2,1)S(1)}, u32[]{:S(2)}, u32[]{:S(2)}) collective-permute-start(bf16[2,192,128]{2,1,0:T(8,128)(2,1)S(1)} %collective-permute-done.19.refs_3_), channel_id=1, source_target_pairs={{0,2},{2,0},{4,6},{6,4},{8,10},{10,8},{12,14},{14,12},{1,3},{3,1},... | collective-permute-start | bytes 294920 | tf_op jit(solution)/shard_map/ppermute | solution.py:507
  83.0 1.4 %collective-permute-start.22 = (bf16[96,1024]{1,0:T(8,128)(2,1)S(1)}, bf16[96,1024]{1,0:T(8,128)(2,1)S(1)}, u32[]{:S(2)}, u32[]{:S(2)}) collective-permute-start(bf16[96,1024]{1,0:T(8,128)(2,1)S(1)} %get-tuple-element.146), channel_id=1, source_target_pairs={{0,1},{1,0},{2,3},{3,2},{4,5},{5,4},{6,7},{7,6},{8,9},{9,8},{10,11... | collective-permute-start | bytes 589832 | tf_op jit(solution)/shard_map/ppermute | solution.py:624

commit v6 on v5

--- a/solution.py
+++ b/solution.py
@@ -23,34 +23,35 @@
 BF16 = jnp.bfloat16
 MIB = 1024 * 1024
 SLOTS_AT_ONCE = {1: 24, 2: 8, 3: 8, 4: 4}
-COSTS = {'attend1': 3000, 'load_caches2': 300, 'load_weights1': 100000, 'project1': 30000, 'load_caches0': 10000, 'project2': 30000, 'attend2': 3000, 'join1': 3000, 'add_far1': 100000, 'add_near2_2': 300, 'load_out0': 100000, 'add_near1_2': 30000, 'output2': 3000, 'load_weights2': 10000, 'load_caches1': 3000}
+PEAK_FLOP_PER_US = 1.1535e9
+COSTS = {'project0': 1.35, 'load_caches0': 1.12, 'load_out0': 1.32, 'add_far0': 0.15, 'add_near0_2': 0.15, 'attend0': 2.1, 'join0_2': 0.1, 'join0': 0.1, 'output0': 2, 'load_weights1': 2.5, 'project1': 1, 'load_caches1': 1.9, 'load_out1': 2.3, 'add_far1': 0.15, 'add_near1_2': 0.15, 'attend1': 1, 'join1_2': 1, 'output1': 1.9, 'load_weights2': 1.42, 'project2': 1.35, 'load_caches2': 16, 'load_out2': 1.32, 'add_far2': 0.15, 'add_near2_2': 0.15, 'attend2': 2.1, 'join2_2': 8, 'join2': 8, 'output2': 1.28}
 GATHER = ('y halved', 'y halved', 'y halved')
 ORDER = (
+    ("load_caches", 0),
     ("project", 0),
     ("project", 1),
     ("far", 0),
-    ("load_caches", 0),
     ("load_out", 0),
+    ("load_caches", 1),
+    ("project", 2),
     ("near", 0),
+    ("far", 1),
     ("attend", 0),
-    ("far", 1),
+    ("far", 2),
+    ("near", 1),
     ("gather", 0),
-    ("project", 2),
-    ("near", 1),
-    ("load_caches", 1),
-    ("far", 2),
-    ("attend", 1),
     ("forward", 0),
     ("load_caches", 2),
+    ("attend", 1),
     ("near", 2),
+    ("attend", 2),
     ("gather", 1),
-    ("attend", 2),
-    ("forward", 1),
-    ("output", 0),
     ("load_out", 2),
     ("gather", 2),
+    ("forward", 1),
+    ("forward", 2),
+    ("output", 0),
     ("load_out", 1),
-    ("forward", 2),
     ("output", 1),
     ("output", 2),
 )
@@ -89,7 +90,8 @@
 
 
 def estimate(name):
-    return pl.CostEstimate(flops=0, bytes_accessed=COSTS.get(name, 0) * 1000, transcendentals=0)
+    flops = int(COSTS.get(name, 0) * PEAK_FLOP_PER_US)
+    return pl.CostEstimate(flops=flops, bytes_accessed=0, transcendentals=0)
 
 
 def call(kernel, name, token, scalars, arrays, out_shapes, scratch, vmem_mib):

time: 85.5 us -> 77.1 us (0.902)
  waiting for transfers between devices: 17.3 us -> 12.1 us
  starting transfers between devices: 34.1 us -> 30.2 us
    ppermute x6, waiting for transfers between devices: 9.42 us -> 1.46 us  [over_z(): moved = lax.ppermute(blocks, 'gx', stride_pairs(nz, stride))]
    ppermute x3, starting transfers between devices: 8.07 us -> 5.35 us  [do_near(): terms = [mine, lax.ppermute(sent, 'gx', stride_pairs(nz, stride))]]
    ppermute x6, waiting for transfers between devices: 0.02 us -> 1.91 us  [over_y(): return (lax.ppermute(blocks, 'gx', same_z), [(1 - h, q) for h, q in labels])]
  transfers between devices with their start and end apart: 23 -> 23, of which waited for: 8 -> 9; matrix products, arithmetic and copies ran while one was open for 0% -> 1% of each run, Pallas kernels for 34% -> 38%
where the time goes in v6:
time: 77.1 us; the launch traced here: 76.8 us
  Pallas kernels  32.3 us (42%)
  starting transfers between devices  30.2 us (39%)
  waiting for transfers between devices  12.1 us (16%)
  other arithmetic  1.72 us (2%)
    pallas_call x18, Pallas kernels, call(): pl.pallas_call(body, in_specs=[vmem] + [pl.BlockSpec(memory_space=pltpu.S...  16.2 us
    pallas_call x9, Pallas kernels, load(): pl.pallas_call(functools.partial(load_kernel, windows=windows), in_specs=...  16.1 us
    ppermute x6, starting transfers between devices, over_z(): moved = lax.ppermute(blocks, 'gx', stride_pairs(nz, stride))  8.2 us
    ppermute x6, starting transfers between devices, over_y(): return (lax.ppermute(blocks, 'gx', same_z), [(1 - h, q) for h, q in labels])  6.37 us
    ppermute x3, starting transfers between devices, do_far(): reduced[c] = lax.ppermute(total, 'gx', stride_pairs(nz, 1))  5.62 us
    ppermute x3, starting transfers between devices, do_near(): terms = [mine, lax.ppermute(sent, 'gx', stride_pairs(nz, stride))]  5.35 us
    ppermute x3, starting transfers between devices, do_project(): swapped[c] = lax.ppermute(outs[1], 'gx', same_z)  4.25 us
    ppermute x3, waiting for transfers between devices, do_near(): terms = [mine, lax.ppermute(sent, 'gx', stride_pairs(nz, stride))]  3.87 us
  transfers between devices with their start and end apart: 23, of which 9 were waited for; matrix products, arithmetic and copies ran while one was open for 1% of the time, Pallas kernels for 38%

profile of v6, /device:TPU:0, one launch (start us, length us, event | category | flops | bytes accessed | tf_op | source)
XLA Modules:
  0.0 76.8 jit_solution(450935055744699503)
XLA Ops:
  0.0 0.5 collective-permute-start
  0.5 0.8 dynamic-slice_convert_fusion
  1.2 1.4 %load_caches0.1 = (f32[8,128]{1,0:T(8,128)S(1)}, bf16[24,128,128]{2,1,0:T(8,128)(2,1)S(1)}, bf16[24,128,128]{2,1,0:T(8,128)(2,1)S(1)}) custom-call(bf16[24,128,512]{2,1,0:T(8,128)(2,1)} %refs_0_.15, bf16[24,128,512]{2,1,0:T(8,128)(2,1)} %refs_1_.11, f32[8,128]{1,0:T(8,128)S(1)} %broadcast_in_dim.17.refs_2_), custom_call_target="tpu_custom_call" | custom-call | flops 1291920000 | tf_op jit(solution)/shard_map/load_caches0/pallas_call | solution.py:142
  2.7 1.8 %load_weights0.1 = (f32[8,128]{1,0:T(8,128)S(1)}, bf16[1024,1024]{1,0:T(8,128)(2,1)S(1)}, bf16[1024,128]{1,0:T(8,128)(2,1)S(1)}, bf16[1024,128]{1,0:T(8,128)(2,1)S(1)}) custom-call(bf16[1024,4096]{1,0:T(8,128)(2,1)} %refs_0_.14, bf16[1024,512]{1,0:T(8,128)(2,1)} %refs_1_.10, bf16[1024,512]{1,0:T(8,128)(2,1)} %refs_2_.10, f32[8,128]{1,0:T(8,128)S(1)} %get-tuple-element.76.refs_3_), custom_call_target="tpu_custom_call" | custom-call | tf_op jit(solution)/shard_map/load_weights0/pallas_call | solution.py:142
  4.5 1.5 %project0.1 = (f32[8,128]{1,0:T(8,128)S(1)}, bf16[4,272,128]{2,1,0:T(8,128)(2,1)S(1)}, bf16[4,272,128]{2,1,0:T(8,128)(2,1)S(1)}, bf16[192,1024]{1,0:T(8,128)(2,1)S(1)}) custom-call(f32[8,128]{1,0:T(8,128)S(1)} %get-tuple-element.77.refs_0_, s32[3]{0:T(128)S(1)} %pad_add_fusion.refs_1_, bf16[96,1024]{1,0:T(8,128)(2,1)S(1)} %copy-done, ...), custom_call_target="tpu_custom_call" | custom-call | flops 1557224960 | tf_op jit(solution)/shard_map/project0/pallas_call | solution.py:104
  6.0 2.6 %collective-permute-start.1 = (bf16[4,272,128]{2,1,0:T(8,128)(2,1)S(1)}, bf16[4,272,128]{2,1,0:T(8,128)(2,1)S(1)}, u32[]{:S(2)}, u32[]{:S(2)}) collective-permute-start(bf16[4,272,128]{2,1,0:T(8,128)(2,1)S(1)} %get-tuple-element.89), channel_id=1, source_target_pairs={{0,2},{2,0},{4,6},{6,4},{8,10},{10,8},{12,14},{14,12},{1,3},{3,1},... | collective-permute-start | bytes 835592 | tf_op jit(solution)/shard_map/ppermute | solution.py:529
  8.6 2.5 %load_weights1.1 = (f32[8,128]{1,0:T(8,128)S(1)}, bf16[1024,2048]{1,0:T(8,128)(2,1)S(1)}, bf16[1024,256]{1,0:T(8,128)(2,1)S(1)}, bf16[1024,256]{1,0:T(8,128)(2,1)S(1)}) custom-call(bf16[1024,4096]{1,0:T(8,128)(2,1)} %refs_0_.14, bf16[1024,512]{1,0:T(8,128)(2,1)} %refs_1_.10, bf16[1024,512]{1,0:T(8,128)(2,1)} %refs_2_.10, f32[8,128]{1,0:T(8,128)S(1)} %get-tuple-element.81.refs_3_), custom_call_target="tpu_custom_call" | custom-call | flops 2883749888 | tf_op jit(solution)/shard_map/load_weights1/pallas_call | solution.py:142
  11.1 1.7 %project1.1 = (f32[8,128]{1,0:T(8,128)S(1)}, bf16[4,480,128]{2,1,0:T(8,128)(2,1)S(1)}, bf16[4,480,128]{2,1,0:T(8,128)(2,1)S(1)}) custom-call(f32[8,128]{1,0:T(8,128)S(1)} %get-tuple-element.82.refs_0_, s32[3]{0:T(128)S(1)} %pad_add_fusion.refs_1_, bf16[192,1024]{1,0:T(8,128)(2,1)S(1)} %get-tuple-element.83.refs_2_, ...), custom_call_target="tpu_custom_call" | custom-call | flops 1153500032 | tf_op jit(solution)/shard_map/project1/pallas_call | solution.py:104
  12.9 3.1 %collective-permute-done.1.refs_2_ = bf16[4,272,128]{2,1,0:T(8,128)(2,1)S(1)} collective-permute-done((bf16[4,272,128]{2,1,0:T(8,128)(2,1)S(1)}, bf16[4,272,128]{2,1,0:T(8,128)(2,1)S(1)}, u32[]{:S(2)}, u32[]{:S(2)}) %collective-permute-start.1) | collective-permute-done | bytes 278560 | tf_op jit(solution)/shard_map/ppermute | solution.py:529
  16.1 1.6 %load_out0.1 = (f32[8,128]{1,0:T(8,128)S(1)}, bf16[1024,1024]{1,0:T(8,128)(2,1)S(1)}) custom-call(bf16[4096,1024]{1,0:T(8,128)(2,1)} %refs_0_.17, f32[8,128]{1,0:T(8,128)S(1)} %get-tuple-element.90.refs_1_), custom_call_target="tpu_custom_call" | custom-call | flops 1522620032 | tf_op jit(solution)/shard_map/load_out0/pallas_call | solution.py:142
  17.7 1.9 %load_caches1.1 = (f32[8,128]{1,0:T(8,128)S(1)}, bf16[24,128,256]{2,1,0:T(8,128)(2,1)S(1)}, bf16[24,128,256]{2,1,0:T(8,128)(2,1)S(1)}) custom-call(bf16[24,128,512]{2,1,0:T(8,128)(2,1)} %refs_0_.15, bf16[24,128,512]{2,1,0:T(8,128)(2,1)} %refs_1_.11, f32[8,128]{1,0:T(8,128)S(1)} %get-tuple-element.91.refs_2_), custom_call_target="tpu_custom_call" | custom-call | flops 2191650048 | tf_op jit(solution)/shard_map/load_caches1/pallas_call | solution.py:142
  19.6 2.1 %collective-permute-start.2 = (bf16[2,272,128]{2,1,0:T(8,128)(2,1)S(1)}, bf16[2,272,128]{2,1,0:T(8,128)(2,1)S(1)}, u32[]{:S(2)}, u32[]{:S(2)}) collective-permute-start(bf16[2,272,128]{2,1,0:T(8,128)(2,1)S(1)} %get-tuple-element.98), channel_id=1, source_target_pairs={{0,4},{2,6},{4,0},{6,2},{8,12},{10,14},{12,8},{14,10},{1,5},{3,7},... | collective-permute-start | bytes 417800 | tf_op jit(solution)/shard_map/ppermute | solution.py:552
  21.7 1.7 %load_weights2.1 = (f32[8,128]{1,0:T(8,128)S(1)}, bf16[1024,1024]{1,0:T(8,128)(2,1)S(1)}, bf16[1024,128]{1,0:T(8,128)(2,1)S(1)}, bf16[1024,128]{1,0:T(8,128)(2,1)S(1)}) custom-call(bf16[1024,4096]{1,0:T(8,128)(2,1)} %refs_0_.14, bf16[1024,512]{1,0:T(8,128)(2,1)} %refs_1_.10, bf16[1024,512]{1,0:T(8,128)(2,1)} %refs_2_.10, f32[8,128]{1,0:T(8,128)S(1)} %get-tuple-element.92.refs_3_), custom_call_target="tpu_custom_call" | custom-call | flops 1637970048 | tf_op jit(solution)/shard_map/load_weights2/pallas_call | solution.py:142
  23.5 1.2 %project2.1 = (f32[8,128]{1,0:T(8,128)S(1)}, bf16[4,240,128]{2,1,0:T(8,128)(2,1)S(1)}, bf16[4,240,128]{2,1,0:T(8,128)(2,1)S(1)}) custom-call(f32[8,128]{1,0:T(8,128)S(1)} %get-tuple-element.93.refs_0_, s32[3]{0:T(128)S(1)} %pad_add_fusion.refs_1_, bf16[192,1024]{1,0:T(8,128)(2,1)S(1)} %get-tuple-element.83.refs_2_, ...), custom_call_target="tpu_custom_call" | custom-call | flops 1557224960 | tf_op jit(solution)/shard_map/project2/pallas_call | solution.py:104
  24.7 0.3 collective-permute-done.2.refs_3_
  25.1 2.8 %collective-permute-start.4 = (bf16[1,272,128]{2,1,0:T(8,128)(2,1)S(1)}, bf16[1,272,128]{2,1,0:T(8,128)(2,1)S(1)}, u32[]{:S(2)}, u32[]{:S(2)}) collective-permute-start(bf16[1,272,128]{2,1,0:T(8,128)(2,1)S(1)} %get-tuple-element.104), channel_id=1, source_target_pairs={{0,8},{2,10},{4,12},{6,14},{8,0},{10,2},{12,4},{14,6},{1,9},{3,11}... | collective-permute-start | bytes 208904 | tf_op jit(solution)/shard_map/ppermute | solution.py:561
  28.0 1.6 %collective-permute-start.5 = (bf16[4,240,128]{2,1,0:T(8,128)(2,1)S(1)}, bf16[4,240,128]{2,1,0:T(8,128)(2,1)S(1)}, u32[]{:S(2)}, u32[]{:S(2)}) collective-permute-start(bf16[4,240,128]{2,1,0:T(8,128)(2,1)S(1)} %get-tuple-element.109), channel_id=1, source_target_pairs={{0,2},{2,0},{4,6},{6,4},{8,10},{10,8},{12,14},{14,12},{1,3},{3,1},... | collective-permute-start | bytes 737288 | tf_op jit(solution)/shard_map/ppermute | solution.py:529
  29.7 1.6 %collective-permute-start.6 = (bf16[2,480,128]{2,1,0:T(8,128)(2,1)S(1)}, bf16[2,480,128]{2,1,0:T(8,128)(2,1)S(1)}, u32[]{:S(2)}, u32[]{:S(2)}) collective-permute-start(bf16[2,480,128]{2,1,0:T(8,128)(2,1)S(1)} %get-tuple-element.111), channel_id=1, source_target_pairs={{0,4},{2,6},{4,0},{6,2},{8,12},{10,14},{12,8},{14,10},{1,5},{3,7},... | collective-permute-start | bytes 737288 | tf_op jit(solution)/shard_map/ppermute | solution.py:552
  31.4 2.2 %attend0.1 = (f32[8,128]{1,0:T(8,128)S(1)}, bf16[1,192,128]{2,1,0:T(8,128)(2,1)S(1)}, f32[24,128]{1,0:T(8,128)S(1)}) custom-call(f32[8,128]{1,0:T(8,128)S(1)} %get-tuple-element.102.refs_0_, s32[3]{0:T(128)S(1)} %pad_add_fusion.refs_1_, s32[192]{0:T(256)S(1)} %copy-done.3, bf16[1,272,128]{2,1,0:T(8,128)(2,1)S(1)} %get-tuple-element.103.refs_3_, ...), custom_call_target="tpu_custom_call" | custom-call | flops 2422350080 | tf_op jit(solution)/shard_map/attend0/pallas_call | solution.py:104
  33.5 2.3 %collective-permute-start.7 = (bf16[1,192,128]{2,1,0:T(8,128)(2,1)S(1)}, bf16[1,192,128]{2,1,0:T(8,128)(2,1)S(1)}, u32[]{:S(2)}, u32[]{:S(2)}) collective-permute-start(bf16[1,192,128]{2,1,0:T(8,128)(2,1)S(1)} %get-tuple-element.113.refs_1_), channel_id=1, source_target_pairs={{0,8},{2,10},{4,12},{6,14},{8,0},{10,2},{12,4},{14,6},{1,9},{3,11}... | collective-permute-start | bytes 147464 | tf_op jit(solution)/shard_map/ppermute | solution.py:512
  35.9 1.9 %collective-permute-start.9 = (bf16[2,240,128]{2,1,0:T(8,128)(2,1)S(1)}, bf16[2,240,128]{2,1,0:T(8,128)(2,1)S(1)}, u32[]{:S(2)}, u32[]{:S(2)}) collective-permute-start(bf16[2,240,128]{2,1,0:T(8,128)(2,1)S(1)} %get-tuple-element.122), channel_id=1, source_target_pairs={{0,4},{2,6},{4,0},{6,2},{8,12},{10,14},{12,8},{14,10},{1,5},{3,7},... | collective-permute-start | bytes 368648 | tf_op jit(solution)/shard_map/ppermute | solution.py:552
  37.8 1.1 %collective-permute-start.8 = (bf16[1,480,128]{2,1,0:T(8,128)(2,1)S(1)}, bf16[1,480,128]{2,1,0:T(8,128)(2,1)S(1)}, u32[]{:S(2)}, u32[]{:S(2)}) collective-permute-start(bf16[1,480,128]{2,1,0:T(8,128)(2,1)S(1)} %get-tuple-element.117), channel_id=1, source_target_pairs={{0,8},{2,10},{4,12},{6,14},{8,0},{10,2},{12,4},{14,6},{1,9},{3,11}... | collective-permute-start | bytes 368648 | tf_op jit(solution)/shard_map/ppermute | solution.py:561
  39.0 1.4 %collective-permute-done.7.refs_2_ = bf16[1,192,128]{2,1,0:T(8,128)(2,1)S(1)} collective-permute-done((bf16[1,192,128]{2,1,0:T(8,128)(2,1)S(1)}, bf16[1,192,128]{2,1,0:T(8,128)(2,1)S(1)}, u32[]{:S(2)}, u32[]{:S(2)}) %collective-permute-start.7) | collective-permute-done | bytes 49184 | tf_op jit(solution)/shard_map/ppermute | solution.py:512
  40.3 1.4 %load_caches2.1 = (f32[8,128]{1,0:T(8,128)S(1)}, bf16[24,128,128]{2,1,0:T(8,128)(2,1)S(1)}, bf16[24,128,128]{2,1,0:T(8,128)(2,1)S(1)}) custom-call(bf16[24,128,512]{2,1,0:T(8,128)(2,1)} %refs_0_.15, bf16[24,128,512]{2,1,0:T(8,128)(2,1)} %refs_1_.11, f32[8,128]{1,0:T(8,128)S(1)} %get-tuple-element.114.refs_2_), custom_call_target="tpu_custom_call" | custom-call | flops 18456000512 | tf_op jit(solution)/shard_map/load_caches2/pallas_call | solution.py:142
  41.8 1.1 %collective-permute-start.13 = (bf16[2,192,128]{2,1,0:T(8,128)(2,1)S(1)}, bf16[2,192,128]{2,1,0:T(8,128)(2,1)S(1)}, u32[]{:S(2)}, u32[]{:S(2)}) collective-permute-start(bf16[2,192,128]{2,1,0:T(8,128)(2,1)S(1)} %get-tuple-element.134.refs_2_), channel_id=1, source_target_pairs={{0,4},{2,6},{4,0},{6,2},{8,12},{10,14},{12,8},{14,10},{1,5},{3,7},... | collective-permute-start | bytes 294920 | tf_op jit(solution)/shard_map/ppermute | solution.py:512
  42.9 2.1 %collective-permute-done.8.refs_4_ = bf16[1,480,128]{2,1,0:T(8,128)(2,1)S(1)} collective-permute-done((bf16[1,480,128]{2,1,0:T(8,128)(2,1)S(1)}, bf16[1,480,128]{2,1,0:T(8,128)(2,1)S(1)}, u32[]{:S(2)}, u32[]{:S(2)}) %collective-permute-start.8) | collective-permute-done | bytes 122912 | tf_op jit(solution)/shard_map/ppermute | solution.py:561
  45.0 2.4 %attend1.1 = (f32[8,128]{1,0:T(8,128)S(1)}, bf16[1,384,128]{2,1,0:T(8,128)(2,1)S(1)}) custom-call(f32[8,128]{1,0:T(8,128)S(1)} %get-tuple-element.115.refs_0_, s32[3]{0:T(128)S(1)} %pad_add_fusion.refs_1_, s32[192]{0:T(256)S(1)} %copy-done.3, bf16[1,480,128]{2,1,0:T(8,128)(2,1)S(1)} %get-tuple-element.116.refs_3_, ...), custom_call_target="tpu_custom_call" | custom-call | flops 1153500032 | tf_op jit(solution)/shard_map/attend1/pallas_call | solution.py:104
  47.4 1.4 %collective-permute-start.10 = (bf16[1,240,128]{2,1,0:T(8,128)(2,1)S(1)}, bf16[1,240,128]{2,1,0:T(8,128)(2,1)S(1)}, u32[]{:S(2)}, u32[]{:S(2)}) collective-permute-start(bf16[1,240,128]{2,1,0:T(8,128)(2,1)S(1)} %get-tuple-element.125), channel_id=1, source_target_pairs={{0,8},{2,10},{4,12},{6,14},{8,0},{10,2},{12,4},{14,6},{1,9},{3,11}... | collective-permute-start | bytes 184328 | tf_op jit(solution)/shard_map/ppermute | solution.py:561
  48.8 1.4 %collective-permute-start.14 = (bf16[2,192,128]{2,1,0:T(8,128)(2,1)S(1)}, bf16[2,192,128]{2,1,0:T(8,128)(2,1)S(1)}, u32[]{:S(2)}, u32[]{:S(2)}) collective-permute-start(bf16[2,192,128]{2,1,0:T(8,128)(2,1)S(1)} %get-tuple-element.134.refs_2_), channel_id=1, source_target_pairs={{0,2},{2,0},{4,6},{6,4},{8,10},{10,8},{12,14},{14,12},{1,3},{3,1},... | collective-permute-start | bytes 294920 | tf_op jit(solution)/shard_map/ppermute | solution.py:509
  50.3 0.6 collective-permute-start.15
  50.9 1.6 %collective-permute-start.11 = (bf16[1,384,128]{2,1,0:T(8,128)(2,1)S(1)}, bf16[1,384,128]{2,1,0:T(8,128)(2,1)S(1)}, u32[]{:S(2)}, u32[]{:S(2)}) collective-permute-start(bf16[1,384,128]{2,1,0:T(8,128)(2,1)S(1)} %get-tuple-element.129.refs_1_), channel_id=1, source_target_pairs={{0,8},{2,10},{4,12},{6,14},{8,0},{10,2},{12,4},{14,6},{1,9},{3,11}... | collective-permute-start | bytes 294920 | tf_op jit(solution)/shard_map/ppermute | solution.py:512
  52.4 1.8 %collective-permute-done.10.refs_4_ = bf16[1,240,128]{2,1,0:T(8,128)(2,1)S(1)} collective-permute-done((bf16[1,240,128]{2,1,0:T(8,128)(2,1)S(1)}, bf16[1,240,128]{2,1,0:T(8,128)(2,1)S(1)}, u32[]{:S(2)}, u32[]{:S(2)}) %collective-permute-start.10) | collective-permute-done | bytes 61472 | tf_op jit(solution)/shard_map/ppermute | solution.py:561
  54.2 2.1 %attend2.1 = (f32[8,128]{1,0:T(8,128)S(1)}, bf16[1,192,128]{2,1,0:T(8,128)(2,1)S(1)}) custom-call(f32[8,128]{1,0:T(8,128)S(1)} %get-tuple-element.123.refs_0_, s32[3]{0:T(128)S(1)} %pad_add_fusion.refs_1_, s32[192]{0:T(256)S(1)} %copy-done.3, bf16[1,240,128]{2,1,0:T(8,128)(2,1)S(1)} %get-tuple-element.124.refs_3_, ...), custom_call_target="tpu_custom_call" | custom-call | flops 2422350080 | tf_op jit(solution)/shard_map/attend2/pallas_call | solution.py:104
  56.5 3.0 %collective-permute-start.16 = (bf16[2,384,128]{2,1,0:T(8,128)(2,1)S(1)}, bf16[2,384,128]{2,1,0:T(8,128)(2,1)S(1)}, u32[]{:S(2)}, u32[]{:S(2)}) collective-permute-start(bf16[2,384,128]{2,1,0:T(8,128)(2,1)S(1)} %get-tuple-element.138.refs_2_), channel_id=1, source_target_pairs={{0,4},{2,6},{4,0},{6,2},{8,12},{10,14},{12,8},{14,10},{1,5},{3,7},... | collective-permute-start | bytes 589832 | tf_op jit(solution)/shard_map/ppermute | solution.py:512
  59.5 1.3 %collective-permute-start.17 = (bf16[2,384,128]{2,1,0:T(8,128)(2,1)S(1)}, bf16[2,384,128]{2,1,0:T(8,128)(2,1)S(1)}, u32[]{:S(2)}, u32[]{:S(2)}) collective-permute-start(bf16[2,384,128]{2,1,0:T(8,128)(2,1)S(1)} %get-tuple-element.138.refs_2_), channel_id=1, source_target_pairs={{0,2},{2,0},{4,6},{6,4},{8,10},{10,8},{12,14},{14,12},{1,3},{3,1},... | collective-permute-start | bytes 589832 | tf_op jit(solution)/shard_map/ppermute | solution.py:509
  60.8 1.6 %load_out2.1 = (f32[8,128]{1,0:T(8,128)S(1)}, bf16[1024,1024]{1,0:T(8,128)(2,1)S(1)}) custom-call(bf16[4096,1024]{1,0:T(8,128)(2,1)} %refs_0_.17, f32[8,128]{1,0:T(8,128)S(1)} %get-tuple-element.130.refs_1_), custom_call_target="tpu_custom_call" | custom-call | flops 1522620032 | tf_op jit(solution)/shard_map/load_out2/pallas_call | solution.py:142
  62.4 0.1 collective-permute-start.19
  62.6 0.9 %collective-permute-start.20 = (bf16[2,192,128]{2,1,0:T(8,128)(2,1)S(1)}, bf16[2,192,128]{2,1,0:T(8,128)(2,1)S(1)}, u32[]{:S(2)}, u32[]{:S(2)}) collective-permute-start(bf16[2,192,128]{2,1,0:T(8,128)(2,1)S(1)} %get-tuple-element.142.refs_2_), channel_id=1, source_target_pairs={{0,2},{2,0},{4,6},{6,4},{8,10},{10,8},{12,14},{14,12},{1,3},{3,1},... | collective-permute-start | bytes 294920 | tf_op jit(solution)/shard_map/ppermute | solution.py:509
  63.4 1.3 %output0.1 = (f32[8,128]{1,0:T(8,128)S(1)}, f32[192,1024]{1,0:T(8,128)S(1)}) custom-call(f32[8,128]{1,0:T(8,128)S(1)} %get-tuple-element.133.refs_0_, s32[3]{0:T(128)S(1)} %pad_add_fusion.refs_1_, bf16[2,192,128]{2,1,0:T(8,128)(2,1)S(1)} %get-tuple-element.134.refs_2_, bf16[2,192,128]{2,1,0:T(8,128)(2,1)S(1)} %collective-permute-done.13.refs_3_, ...), custom_call_target="tpu_custom_call" | custom-call | flops 2307000064 | tf_op jit(solution)/shard_map/output0/pallas_call | solution.py:104
  64.7 1.2 %collective-permute-start.18 = (bf16[2,384,128]{2,1,0:T(8,128)(2,1)S(1)}, bf16[2,384,128]{2,1,0:T(8,128)(2,1)S(1)}, u32[]{:S(2)}, u32[]{:S(2)}) collective-permute-start(bf16[2,384,128]{2,1,0:T(8,128)(2,1)S(1)} %collective-permute-done.16.refs_3_), channel_id=1, source_target_pairs={{0,2},{2,0},{4,6},{6,4},{8,10},{10,8},{12,14},{14,12},{1,3},{3,1},... | collective-permute-start | bytes 589832 | tf_op jit(solution)/shard_map/ppermute | solution.py:509
  66.0 2.2 %load_out1.1 = (f32[8,128]{1,0:T(8,128)S(1)}, bf16[2048,1024]{1,0:T(8,128)(2,1)S(1)}) custom-call(bf16[4096,1024]{1,0:T(8,128)(2,1)} %refs_0_.17, f32[8,128]{1,0:T(8,128)S(1)} %get-tuple-element.136.refs_1_), custom_call_target="tpu_custom_call" | custom-call | flops 2653050112 | tf_op jit(solution)/shard_map/load_out1/pallas_call | solution.py:142
  68.2 0.9 %collective-permute-start.21 = (bf16[2,192,128]{2,1,0:T(8,128)(2,1)S(1)}, bf16[2,192,128]{2,1,0:T(8,128)(2,1)S(1)}, u32[]{:S(2)}, u32[]{:S(2)}) collective-permute-start(bf16[2,192,128]{2,1,0:T(8,128)(2,1)S(1)} %collective-permute-done.19.refs_3_), channel_id=1, source_target_pairs={{0,2},{2,0},{4,6},{6,4},{8,10},{10,8},{12,14},{14,12},{1,3},{3,1},... | collective-permute-start | bytes 294920 | tf_op jit(solution)/shard_map/ppermute | solution.py:509
  69.1 1.4 %collective-permute-done.18.refs_5_ = bf16[2,384,128]{2,1,0:T(8,128)(2,1)S(1)} collective-permute-done((bf16[2,384,128]{2,1,0:T(8,128)(2,1)S(1)}, bf16[2,384,128]{2,1,0:T(8,128)(2,1)S(1)}, u32[]{:S(2)}, u32[]{:S(2)}) %collective-permute-start.18) | collective-permute-done | bytes 196640 | tf_op jit(solution)/shard_map/ppermute | solution.py:509
  70.5 1.8 %output1.1 = (f32[8,128]{1,0:T(8,128)S(1)}, f32[192,1024]{1,0:T(8,128)S(1)}) custom-call(f32[8,128]{1,0:T(8,128)S(1)} %get-tuple-element.137.refs_0_, s32[3]{0:T(128)S(1)} %pad_add_fusion.refs_1_, bf16[2,384,128]{2,1,0:T(8,128)(2,1)S(1)} %get-tuple-element.138.refs_2_, bf16[2,384,128]{2,1,0:T(8,128)(2,1)S(1)} %collective-permute-done.16.refs_3_, ...), custom_call_target="tpu_custom_call" | custom-call | flops 2191650048 | tf_op jit(solution)/shard_map/output1/pallas_call | solution.py:104
  72.3 0.5 collective-permute-done.21.refs_5_
  72.9 1.7 %output2.1 = (f32[8,128]{1,0:T(8,128)}, f32[96,1024]{1,0:T(8,128)S(1)}, bf16[96,1024]{1,0:T(8,128)(2,1)S(1)}) custom-call(f32[8,128]{1,0:T(8,128)S(1)} %get-tuple-element.141.refs_0_, s32[3]{0:T(128)S(1)} %pad_add_fusion.refs_1_, bf16[2,192,128]{2,1,0:T(8,128)(2,1)S(1)} %get-tuple-element.142.refs_2_, ...), custom_call_target="tpu_custom_call" | custom-call | flops 1476480000 | tf_op jit(solution)/shard_map/output2/pallas_call | solution.py:104
  74.6 1.4 %collective-permute-done.22 = bf16[96,1024]{1,0:T(8,128)(2,1)S(1)} collective-permute-done((bf16[96,1024]{1,0:T(8,128)(2,1)S(1)}, bf16[96,1024]{1,0:T(8,128)(2,1)S(1)}, u32[]{:S(2)}, u32[]{:S(2)}) %collective-permute-start.22) | collective-permute-done | bytes 196640 | tf_op jit(solution)/shard_map/ppermute | solution.py:626
  76.0 0.8 add_convert_fusion
  (45 shorter events, 0.9 us)
Async XLA Ops:
  0.0 4.5 %collective-permute-start = (bf16[96,1024]{1,0:T(8,128)(2,1)}, bf16[96,1024]{1,0:T(8,128)(2,1)S(1)}, u32[]{:S(2)}, u32[]{:S(2)}) collective-permute-start(bf16[96,1024]{1,0:T(8,128)(2,1)} %refs_2_.8), channel_id=1, source_target_pairs={{0,1},{1,0},{2,3},{3,2},{4,5},{5,4},{6,7},{7,6},{8,9},{9,8},{10,11... | collective-permute-start | bytes 589832 | tf_op jit(solution)/shard_map/ppermute | solution.py:482
  2.6 1.9 %copy-start = (bf16[96,1024]{1,0:T(8,128)(2,1)S(1)}, bf16[96,1024]{1,0:T(8,128)(2,1)}, u32[]{:S(2)}) copy-start(bf16[96,1024]{1,0:T(8,128)(2,1)} %refs_2_.8) | copy-start | bytes 589828
  2.6 1.9 %copy-start.2 = (bf16[1024]{0:T(1024)(128)(2,1)S(1)}, bf16[1024]{0:T(1024)(128)(2,1)}, u32[]{:S(2)}) copy-start(bf16[1024]{0:T(1024)(128)(2,1)} %param.14) | copy-start | bytes 6148
  2.6 1.9 %copy-start.6 = (s32[192]{0:T(256)S(1)}, s32[192]{0:T(256)}, u32[]{:S(2)}) copy-start(s32[192]{0:T(256)} %param.24) | copy-start | bytes 2308
  6.0 10.0 %collective-permute-start.1 = (bf16[4,272,128]{2,1,0:T(8,128)(2,1)S(1)}, bf16[4,272,128]{2,1,0:T(8,128)(2,1)S(1)}, u32[]{:S(2)}, u32[]{:S(2)}) collective-permute-start(bf16[4,272,128]{2,1,0:T(8,128)(2,1)S(1)} %get-tuple-element.89), channel_id=1, source_target_pairs={{0,2},{2,0},{4,6},{6,4},{8,10},{10,8},{12,14},{14,12},{1,3},{3,1},... | collective-permute-start | bytes 835592 | tf_op jit(solution)/shard_map/ppermute | solution.py:529
  12.8 16.8 %collective-permute-start.3 = (bf16[4,480,128]{2,1,0:T(8,128)(2,1)S(1)}, bf16[4,480,128]{2,1,0:T(8,128)(2,1)S(1)}, u32[]{:S(2)}, u32[]{:S(2)}) collective-permute-start(bf16[4,480,128]{2,1,0:T(8,128)(2,1)S(1)} %get-tuple-element.101), channel_id=1, source_target_pairs={{0,2},{2,0},{4,6},{6,4},{8,10},{10,8},{12,14},{14,12},{1,3},{3,1},... | collective-permute-start | bytes 1474568 | tf_op jit(solution)/shard_map/ppermute | solution.py:529
  19.6 5.5 %collective-permute-start.2 = (bf16[2,272,128]{2,1,0:T(8,128)(2,1)S(1)}, bf16[2,272,128]{2,1,0:T(8,128)(2,1)S(1)}, u32[]{:S(2)}, u32[]{:S(2)}) collective-permute-start(bf16[2,272,128]{2,1,0:T(8,128)(2,1)S(1)} %get-tuple-element.98), channel_id=1, source_target_pairs={{0,4},{2,6},{4,0},{6,2},{8,12},{10,14},{12,8},{14,10},{1,5},{3,7},... | collective-permute-start | bytes 417800 | tf_op jit(solution)/shard_map/ppermute | solution.py:552
  23.4 7.9 %copy-start.1 = (bf16[4096]{0:T(1024)(128)(2,1)S(1)}, bf16[4096]{0:T(1024)(128)(2,1)}, u32[]{:S(2)}) copy-start(bf16[4096]{0:T(1024)(128)(2,1)} %param.18) | copy-start | bytes 24580
  23.5 7.9 %copy-start.3 = (s32[192]{0:T(256)S(1)}, s32[192]{0:T(256)}, u32[]{:S(2)}) copy-start(s32[192]{0:T(256)} %refs_2_.13) | copy-start | bytes 2308
  23.5 7.9 %copy-start.4 = (bf16[512]{0:T(512)(128)(2,1)S(1)}, bf16[512]{0:T(512)(128)(2,1)}, u32[]{:S(2)}) copy-start(bf16[512]{0:T(512)(128)(2,1)} %param.19) | copy-start | bytes 3076
  23.5 7.9 %copy-start.5 = (bf16[512]{0:T(512)(128)(2,1)S(1)}, bf16[512]{0:T(512)(128)(2,1)}, u32[]{:S(2)}) copy-start(bf16[512]{0:T(512)(128)(2,1)} %param.20) | copy-start | bytes 3076
  25.1 6.2 %collective-permute-start.4 = (bf16[1,272,128]{2,1,0:T(8,128)(2,1)S(1)}, bf16[1,272,128]{2,1,0:T(8,128)(2,1)S(1)}, u32[]{:S(2)}, u32[]{:S(2)}) collective-permute-start(bf16[1,272,128]{2,1,0:T(8,128)(2,1)S(1)} %get-tuple-element.104), channel_id=1, source_target_pairs={{0,8},{2,10},{4,12},{6,14},{8,0},{10,2},{12,4},{14,6},{1,9},{3,11}... | collective-permute-start | bytes 208904 | tf_op jit(solution)/shard_map/ppermute | solution.py:561
  28.0 7.8 %collective-permute-start.5 = (bf16[4,240,128]{2,1,0:T(8,128)(2,1)S(1)}, bf16[4,240,128]{2,1,0:T(8,128)(2,1)S(1)}, u32[]{:S(2)}, u32[]{:S(2)}) collective-permute-start(bf16[4,240,128]{2,1,0:T(8,128)(2,1)S(1)} %get-tuple-element.109), channel_id=1, source_target_pairs={{0,2},{2,0},{4,6},{6,4},{8,10},{10,8},{12,14},{14,12},{1,3},{3,1},... | collective-permute-start | bytes 737288 | tf_op jit(solution)/shard_map/ppermute | solution.py:529
  29.7 8.0 %collective-permute-start.6 = (bf16[2,480,128]{2,1,0:T(8,128)(2,1)S(1)}, bf16[2,480,128]{2,1,0:T(8,128)(2,1)S(1)}, u32[]{:S(2)}, u32[]{:S(2)}) collective-permute-start(bf16[2,480,128]{2,1,0:T(8,128)(2,1)S(1)} %get-tuple-element.111), channel_id=1, source_target_pairs={{0,4},{2,6},{4,0},{6,2},{8,12},{10,14},{12,8},{14,10},{1,5},{3,7},... | collective-permute-start | bytes 737288 | tf_op jit(solution)/shard_map/ppermute | solution.py:552
  33.5 6.8 %collective-permute-start.7 = (bf16[1,192,128]{2,1,0:T(8,128)(2,1)S(1)}, bf16[1,192,128]{2,1,0:T(8,128)(2,1)S(1)}, u32[]{:S(2)}, u32[]{:S(2)}) collective-permute-start(bf16[1,192,128]{2,1,0:T(8,128)(2,1)S(1)} %get-tuple-element.113.refs_1_), channel_id=1, source_target_pairs={{0,8},{2,10},{4,12},{6,14},{8,0},{10,2},{12,4},{14,6},{1,9},{3,11}... | collective-permute-start | bytes 147464 | tf_op jit(solution)/shard_map/ppermute | solution.py:512
  35.9 11.5 %collective-permute-start.9 = (bf16[2,240,128]{2,1,0:T(8,128)(2,1)S(1)}, bf16[2,240,128]{2,1,0:T(8,128)(2,1)S(1)}, u32[]{:S(2)}, u32[]{:S(2)}) collective-permute-start(bf16[2,240,128]{2,1,0:T(8,128)(2,1)S(1)} %get-tuple-element.122), channel_id=1, source_target_pairs={{0,4},{2,6},{4,0},{6,2},{8,12},{10,14},{12,8},{14,10},{1,5},{3,7},... | collective-permute-start | bytes 368648 | tf_op jit(solution)/shard_map/ppermute | solution.py:552
  37.8 7.2 %collective-permute-start.8 = (bf16[1,480,128]{2,1,0:T(8,128)(2,1)S(1)}, bf16[1,480,128]{2,1,0:T(8,128)(2,1)S(1)}, u32[]{:S(2)}, u32[]{:S(2)}) collective-permute-start(bf16[1,480,128]{2,1,0:T(8,128)(2,1)S(1)} %get-tuple-element.117), channel_id=1, source_target_pairs={{0,8},{2,10},{4,12},{6,14},{8,0},{10,2},{12,4},{14,6},{1,9},{3,11}... | collective-permute-start | bytes 368648 | tf_op jit(solution)/shard_map/ppermute | solution.py:561
  41.8 8.5 %collective-permute-start.13 = (bf16[2,192,128]{2,1,0:T(8,128)(2,1)S(1)}, bf16[2,192,128]{2,1,0:T(8,128)(2,1)S(1)}, u32[]{:S(2)}, u32[]{:S(2)}) collective-permute-start(bf16[2,192,128]{2,1,0:T(8,128)(2,1)S(1)} %get-tuple-element.134.refs_2_), channel_id=1, source_target_pairs={{0,4},{2,6},{4,0},{6,2},{8,12},{10,14},{12,8},{14,10},{1,5},{3,7},... | collective-permute-start | bytes 294920 | tf_op jit(solution)/shard_map/ppermute | solution.py:512
  47.4 6.8 %collective-permute-start.10 = (bf16[1,240,128]{2,1,0:T(8,128)(2,1)S(1)}, bf16[1,240,128]{2,1,0:T(8,128)(2,1)S(1)}, u32[]{:S(2)}, u32[]{:S(2)}) collective-permute-start(bf16[1,240,128]{2,1,0:T(8,128)(2,1)S(1)} %get-tuple-element.125), channel_id=1, source_target_pairs={{0,8},{2,10},{4,12},{6,14},{8,0},{10,2},{12,4},{14,6},{1,9},{3,11}... | collective-permute-start | bytes 184328 | tf_op jit(solution)/shard_map/ppermute | solution.py:561
  48.8 13.7 %collective-permute-start.14 = (bf16[2,192,128]{2,1,0:T(8,128)(2,1)S(1)}, bf16[2,192,128]{2,1,0:T(8,128)(2,1)S(1)}, u32[]{:S(2)}, u32[]{:S(2)}) collective-permute-start(bf16[2,192,128]{2,1,0:T(8,128)(2,1)S(1)} %get-tuple-element.134.refs_2_), channel_id=1, source_target_pairs={{0,2},{2,0},{4,6},{6,4},{8,10},{10,8},{12,14},{14,12},{1,3},{3,1},... | collective-permute-start | bytes 294920 | tf_op jit(solution)/shard_map/ppermute | solution.py:509
  50.3 13.2 %collective-permute-start.15 = (bf16[2,192,128]{2,1,0:T(8,128)(2,1)S(1)}, bf16[2,192,128]{2,1,0:T(8,128)(2,1)S(1)}, u32[]{:S(2)}, u32[]{:S(2)}) collective-permute-start(bf16[2,192,128]{2,1,0:T(8,128)(2,1)S(1)} %collective-permute-done.13.refs_3_), channel_id=1, source_target_pairs={{0,2},{2,0},{4,6},{6,4},{8,10},{10,8},{12,14},{14,12},{1,3},{3,1},... | collective-permute-start | bytes 294920 | tf_op jit(solution)/shard_map/ppermute | solution.py:509
  50.9 5.6 %collective-permute-start.11 = (bf16[1,384,128]{2,1,0:T(8,128)(2,1)S(1)}, bf16[1,384,128]{2,1,0:T(8,128)(2,1)S(1)}, u32[]{:S(2)}, u32[]{:S(2)}) collective-permute-start(bf16[1,384,128]{2,1,0:T(8,128)(2,1)S(1)} %get-tuple-element.129.refs_1_), channel_id=1, source_target_pairs={{0,8},{2,10},{4,12},{6,14},{8,0},{10,2},{12,4},{14,6},{1,9},{3,11}... | collective-permute-start | bytes 294920 | tf_op jit(solution)/shard_map/ppermute | solution.py:512
  56.3 6.1 %collective-permute-start.12 = (bf16[1,192,128]{2,1,0:T(8,128)(2,1)S(1)}, bf16[1,192,128]{2,1,0:T(8,128)(2,1)S(1)}, u32[]{:S(2)}, u32[]{:S(2)}) collective-permute-start(bf16[1,192,128]{2,1,0:T(8,128)(2,1)S(1)} %get-tuple-element.132.refs_1_), channel_id=1, source_target_pairs={{0,8},{2,10},{4,12},{6,14},{8,0},{10,2},{12,4},{14,6},{1,9},{3,11}... | collective-permute-start | bytes 147464 | tf_op jit(solution)/shard_map/ppermute | solution.py:512
  56.5 8.3 %collective-permute-start.16 = (bf16[2,384,128]{2,1,0:T(8,128)(2,1)S(1)}, bf16[2,384,128]{2,1,0:T(8,128)(2,1)S(1)}, u32[]{:S(2)}, u32[]{:S(2)}) collective-permute-start(bf16[2,384,128]{2,1,0:T(8,128)(2,1)S(1)} %get-tuple-element.138.refs_2_), channel_id=1, source_target_pairs={{0,4},{2,6},{4,0},{6,2},{8,12},{10,14},{12,8},{14,10},{1,5},{3,7},... | collective-permute-start | bytes 589832 | tf_op jit(solution)/shard_map/ppermute | solution.py:512
  59.5 9.7 %collective-permute-start.17 = (bf16[2,384,128]{2,1,0:T(8,128)(2,1)S(1)}, bf16[2,384,128]{2,1,0:T(8,128)(2,1)S(1)}, u32[]{:S(2)}, u32[]{:S(2)}) collective-permute-start(bf16[2,384,128]{2,1,0:T(8,128)(2,1)S(1)} %get-tuple-element.138.refs_2_), channel_id=1, source_target_pairs={{0,2},{2,0},{4,6},{6,4},{8,10},{10,8},{12,14},{14,12},{1,3},{3,1},... | collective-permute-start | bytes 589832 | tf_op jit(solution)/shard_map/ppermute | solution.py:509
  62.4 5.8 %collective-permute-start.19 = (bf16[2,192,128]{2,1,0:T(8,128)(2,1)S(1)}, bf16[2,192,128]{2,1,0:T(8,128)(2,1)S(1)}, u32[]{:S(2)}, u32[]{:S(2)}) collective-permute-start(bf16[2,192,128]{2,1,0:T(8,128)(2,1)S(1)} %get-tuple-element.142.refs_2_), channel_id=1, source_target_pairs={{0,4},{2,6},{4,0},{6,2},{8,12},{10,14},{12,8},{14,10},{1,5},{3,7},... | collective-permute-start | bytes 294920 | tf_op jit(solution)/shard_map/ppermute | solution.py:512
  62.6 9.8 %collective-permute-start.20 = (bf16[2,192,128]{2,1,0:T(8,128)(2,1)S(1)}, bf16[2,192,128]{2,1,0:T(8,128)(2,1)S(1)}, u32[]{:S(2)}, u32[]{:S(2)}) collective-permute-start(bf16[2,192,128]{2,1,0:T(8,128)(2,1)S(1)} %get-tuple-element.142.refs_2_), channel_id=1, source_target_pairs={{0,2},{2,0},{4,6},{6,4},{8,10},{10,8},{12,14},{14,12},{1,3},{3,1},... | collective-permute-start | bytes 294920 | tf_op jit(solution)/shard_map/ppermute | solution.py:509
  64.7 5.7 %collective-permute-start.18 = (bf16[2,384,128]{2,1,0:T(8,128)(2,1)S(1)}, bf16[2,384,128]{2,1,0:T(8,128)(2,1)S(1)}, u32[]{:S(2)}, u32[]{:S(2)}) collective-permute-start(bf16[2,384,128]{2,1,0:T(8,128)(2,1)S(1)} %collective-permute-done.16.refs_3_), channel_id=1, source_target_pairs={{0,2},{2,0},{4,6},{6,4},{8,10},{10,8},{12,14},{14,12},{1,3},{3,1},... | collective-permute-start | bytes 589832 | tf_op jit(solution)/shard_map/ppermute | solution.py:509
  68.2 4.7 %collective-permute-start.21 = (bf16[2,192,128]{2,1,0:T(8,128)(2,1)S(1)}, bf16[2,192,128]{2,1,0:T(8,128)(2,1)S(1)}, u32[]{:S(2)}, u32[]{:S(2)}) collective-permute-start(bf16[2,192,128]{2,1,0:T(8,128)(2,1)S(1)} %collective-permute-done.19.refs_3_), channel_id=1, source_target_pairs={{0,2},{2,0},{4,6},{6,4},{8,10},{10,8},{12,14},{14,12},{1,3},{3,1},... | collective-permute-start | bytes 294920 | tf_op jit(solution)/shard_map/ppermute | solution.py:509
  74.6 1.4 %collective-permute-start.22 = (bf16[96,1024]{1,0:T(8,128)(2,1)S(1)}, bf16[96,1024]{1,0:T(8,128)(2,1)S(1)}, u32[]{:S(2)}, u32[]{:S(2)}) collective-permute-start(bf16[96,1024]{1,0:T(8,128)(2,1)S(1)} %get-tuple-element.146), channel_id=1, source_target_pairs={{0,1},{1,0},{2,3},{3,2},{4,5},{5,4},{6,7},{7,6},{8,9},{9,8},{10,11... | collective-permute-start | bytes 589832 | tf_op jit(solution)/shard_map/ppermute | solution.py:626

commit v7 on v6

--- a/solution.py
+++ b/solution.py
@@ -24,34 +24,37 @@
 MIB = 1024 * 1024
 SLOTS_AT_ONCE = {1: 24, 2: 8, 3: 8, 4: 4}
 PEAK_FLOP_PER_US = 1.1535e9
-COSTS = {'project0': 1.35, 'load_caches0': 1.12, 'load_out0': 1.32, 'add_far0': 0.15, 'add_near0_2': 0.15, 'attend0': 2.1, 'join0_2': 0.1, 'join0': 0.1, 'output0': 2, 'load_weights1': 2.5, 'project1': 1, 'load_caches1': 1.9, 'load_out1': 2.3, 'add_far1': 0.15, 'add_near1_2': 0.15, 'attend1': 1, 'join1_2': 1, 'output1': 1.9, 'load_weights2': 1.42, 'project2': 1.35, 'load_caches2': 16, 'load_out2': 1.32, 'add_far2': 0.15, 'add_near2_2': 0.15, 'attend2': 2.1, 'join2_2': 8, 'join2': 8, 'output2': 1.28}
-GATHER = ('y halved', 'y halved', 'y halved')
+COSTS = {'project0': 1.35, 'attend0': 2.1, 'join0_2': 0.1, 'join0': 0.1, 'output0': 8, 'project1': 1, 'add_near1_2': 2, 'attend1': 1, 'join1_2': 1, 'output1': 8, 'project2': 1.35, 'add_far2': 0.15, 'add_near2_2': 0.3, 'attend2': 2.1, 'join2_2': 8, 'output2': 1.28, 'join1_1': 2, 'join2_1': 4, 'add_far0': 2, 'join2': 4}
+GATHER = ("all_gather", "y halved", "y halved")
 ORDER = (
-    ("load_caches", 0),
+    ("caches", 0),
+    ("weights", 0),
     ("project", 0),
+    ("weights", 1),
     ("project", 1),
     ("far", 0),
-    ("load_out", 0),
-    ("load_caches", 1),
+    ("out", 0),
+    ("caches", 1),
+    ("near", 0),
+    ("weights", 2),
     ("project", 2),
-    ("near", 0),
     ("far", 1),
     ("attend", 0),
     ("far", 2),
     ("near", 1),
     ("gather", 0),
+    ("caches", 2),
+    ("near", 2),
+    ("attend", 1),
     ("forward", 0),
-    ("load_caches", 2),
-    ("attend", 1),
-    ("near", 2),
     ("attend", 2),
     ("gather", 1),
-    ("load_out", 2),
+    ("out", 2),
     ("gather", 2),
+    ("output", 0),
     ("forward", 1),
     ("forward", 2),
-    ("output", 0),
-    ("load_out", 1),
+    ("out", 1),
     ("output", 1),
     ("output", 2),
 )
@@ -75,13 +78,16 @@
     return sorted(range(nz), key=lambda q: [(q & b) != 0 for b in strides(nz)])
 
 
-def slot_one_hot(place_ref, slot_of_row, nz, per):
+def slot_one_hot(place_ref, slot_of_row, nz, per, absolute=False):
     rows = slot_of_row.shape[1]
     base = lax.broadcasted_iota(jnp.int32, (per, rows), 0)
     blocks = []
     for h in range(2):
         for q in place_order(nz):
-            owner = (place_ref[0] ^ q) * 2 + (place_ref[1] ^ h)
+            if absolute:
+                owner = len(blocks)
+            else:
+                owner = (place_ref[0] ^ q) * 2 + (place_ref[1] ^ h)
             blocks.append(jnp.where(base + owner * per == slot_of_row, 1.0, 0.0).astype(F32))
     return jnp.concatenate(blocks, axis=0).astype(BF16)
 
@@ -94,63 +100,58 @@
     return pl.CostEstimate(flops=flops, bytes_accessed=0, transcendentals=0)
 
 
-def call(kernel, name, token, scalars, arrays, out_shapes, scratch, vmem_mib):
+def copies_of(sources, windows, targets, sems):
+    return [
+        pltpu.make_async_copy(source.at[window], target, sems.at[i])
+        for i, (source, window, target) in enumerate(zip(sources, windows, targets))
+    ]
+
+
+def call(kernel, name, token, scalars, arrays, out_shapes, scratch, vmem_mib, loads=()):
+    sources = [array for array, _ in loads]
+    windows = [window for _, window in loads]
+    loaded_shapes = [
+        tuple(w.size if isinstance(w, pl.Slice) else n for w, n in zip(window, array.shape))
+        for array, window in loads
+    ]
+
     def body(*refs):
-        first_out = 1 + len(scalars) + len(arrays)
-        refs[first_out][...] = jnp.zeros(TOKEN, F32)
-        kernel(*refs[1:first_out], *refs[first_out + 1 :])
+        refs = list(refs)
+        del refs[0]
+        source_refs = [refs.pop(0) for _ in loads]
+        in_refs = [refs.pop(0) for _ in range(len(scalars) + len(arrays))]
+        token_ref = refs.pop(0)
+        target_refs = [refs.pop(0) for _ in loads]
+        copies = copies_of(source_refs, windows, target_refs, refs.pop() if loads else None)
+        for copy in copies:
+            copy.start()
+        token_ref[...] = jnp.zeros(TOKEN, F32)
+        kernel(*in_refs, *refs)
+        for copy in copies:
+            copy.wait()
 
     vmem = pl.BlockSpec(memory_space=pltpu.VMEM)
     outs = pl.pallas_call(
         body,
         in_specs=[vmem]
+        + [pl.BlockSpec(memory_space=pltpu.HBM)] * len(loads)
         + [pl.BlockSpec(memory_space=pltpu.SMEM)] * len(scalars)
         + [vmem] * len(arrays),
-        out_specs=[vmem] * (1 + len(out_shapes)),
+        out_specs=[vmem] * (1 + len(loads) + len(out_shapes)),
         out_shape=[pltpu.VMEM(TOKEN, F32)]
+        + [pltpu.VMEM(shape, array.dtype) for shape, array in zip(loaded_shapes, sources)]
         + [pltpu.VMEM(shape, dtype) for shape, dtype in out_shapes],
-        scratch_shapes=scratch,
+        scratch_shapes=list(scratch) + ([pltpu.SemaphoreType.DMA((len(loads),))] if loads else []),
         compiler_params=pltpu.CompilerParams(vmem_limit_bytes=vmem_mib * MIB),
         cost_estimate=estimate(name),
         name=name,
-    )(token, *scalars, *arrays)
-    return outs[0], outs[1:]
-
-
-def load_kernel(*refs, windows):
-    count = len(windows)
-    sources, token_ref, targets, sems = (
-        refs[:count], refs[count + 1], refs[count + 2 : -1], refs[-1],
+    )(
+        token,
+        *[pltpu.with_memory_space_constraint(array, pltpu.HBM) for array in sources],
+        *scalars,
+        *arrays,
     )
-    copies = [
-        pltpu.make_async_copy(source.at[window], target, sems.at[i])
-        for i, (source, target, window) in enumerate(zip(sources, targets, windows))
-    ]
-    for copy in copies:
-        copy.start()
-    token_ref[...] = jnp.zeros(TOKEN, F32)
-    for copy in copies:
-        copy.wait()
-
-
-def load(name, token, arrays, windows):
-    shapes = [
-        tuple(w.size if isinstance(w, pl.Slice) else n for w, n in zip(window, a.shape))
-        for a, window in zip(arrays, windows)
-    ]
-    vmem = pl.BlockSpec(memory_space=pltpu.VMEM)
-    outs = pl.pallas_call(
-        functools.partial(load_kernel, windows=windows),
-        in_specs=[pl.BlockSpec(memory_space=pltpu.HBM)] * len(arrays) + [vmem],
-        out_specs=[vmem] * (1 + len(arrays)),
-        out_shape=[pltpu.VMEM(TOKEN, F32)]
-        + [pltpu.VMEM(shape, a.dtype) for a, shape in zip(arrays, shapes)],
-        scratch_shapes=[pltpu.SemaphoreType.DMA((len(arrays),))],
-        compiler_params=pltpu.CompilerParams(vmem_limit_bytes=MIB),
-        cost_estimate=estimate(name),
-        name=name,
-    )(*[pltpu.with_memory_space_constraint(a, pltpu.HBM) for a in arrays], token)
-    return outs[0], outs[1:]
+    return outs[0], outs[1 : 1 + len(loads)], outs[1 + len(loads) :]
 
 
 def project_kernel(*refs, nz, per, first, heads):
@@ -214,7 +215,7 @@
                 ref[z, g * TILES * per : (g + 1) * TILES * per, :] = block.astype(BF16)
 
 
-def project(token, place, inputs, weights, *, chunk, heads, nz, per):
+def project(token, place, inputs, weights, loads, *, chunk, heads, nz, per):
     first = chunk == 0
     rows = 2 * nz * per
     depth = weights[0].shape[0]
@@ -229,6 +230,7 @@
         out_shapes + ([((rows, depth), BF16)] if first else []),
         [pltpu.VMEM((rows, TILES * HEAD_SIZE), F32)],
         12,
+        loads,
     )
 
 
@@ -245,7 +247,7 @@
 
 def add(name, token, arrays, starts, count, parts):
     shape = (count // parts,) + arrays[0].shape[1:]
-    return call(
+    token, _, sums = call(
         functools.partial(add_kernel, starts=starts, count=count),
         name,
         token,
@@ -255,6 +257,7 @@
         [],
         2,
     )
+    return token, sums
 
 
 def join_kernel(a_ref, b_ref, out_ref):
@@ -265,7 +268,7 @@
 
 def join(name, token, a, b):
     shape = (a.shape[0] + b.shape[0],) + a.shape[1:]
-    token, (joined,) = call(join_kernel, name, token, [], [a, b], [(shape, BF16)], [], 2)
+    token, _, (joined,) = call(join_kernel, name, token, [], [a, b], [(shape, BF16)], [], 2)
     return token, joined
 
 
@@ -314,6 +317,7 @@
     top_row = lax.broadcasted_iota(jnp.int32, (extra, HEAD_SIZE), 0) == 0
     lane_slot = lax.broadcasted_iota(jnp.int32, (1, lanes), 1) // qrows
     row = lax.broadcasted_iota(jnp.int32, (positions + extra, lanes), 0)
+    row_slot = lax.broadcasted_iota(jnp.int32, (lanes, positions), 0) // qrows
     base = (place_ref[0] * 2 + place_ref[1]) * per
     for start in range(0, per, group):
         slots = range(start, start + group)
@@ -326,16 +330,20 @@
             axis=0,
         )
         turned = queries.T
-        scores = None
+        query, new_key = [], []
         for i, s in enumerate(slots):
-            query, new_key = [], []
             for g in range(heads):
                 query.append(jnp.where(lane_block == i * heads + g, turned, 0.0).astype(BF16))
                 key = fresh[pl.ds(g * head_rows + QUERIES_PER_KV * per + s, 1), :]
                 new_key.append(jnp.where(top_row, key, 0.0).astype(BF16))
-            keys = jnp.concatenate([k_ref[s], jnp.concatenate(new_key, axis=1)], axis=0)
-            term = jnp.dot(keys, jnp.concatenate(query, axis=0), preferred_element_type=F32)
-            scores = term if scores is None else scores + term
+        keys = jnp.concatenate(
+            [
+                jnp.concatenate([k_ref[s] for s in slots], axis=1),
+                jnp.concatenate(new_key, axis=1),
+            ],
+            axis=0,
+        )
+        scores = jnp.dot(keys, jnp.concatenate(query, axis=0), preferred_element_type=F32)
 
         lengths = jnp.zeros((1, lanes), jnp.int32)
         for i, s in enumerate(slots):
@@ -347,23 +355,27 @@
         weights = exps * (1.0 / jnp.sum(exps, axis=0, keepdims=True))
         cache_weights = weights[:positions].T
         own_weights = weights[positions : positions + 8].T[:, 0:1].astype(BF16).astype(F32)
+        spread = jnp.concatenate(
+            [jnp.where(row_slot == i, cache_weights, 0.0).astype(BF16) for i in range(group)],
+            axis=1,
+        )
+        values = v_ref[start : start + group].reshape(group * positions, heads * HEAD_SIZE)
+        mixed = jnp.dot(spread, values, preferred_element_type=F32)
         for i, s in enumerate(slots):
-            mixed = jnp.dot(
-                cache_weights[i * qrows : (i + 1) * qrows].astype(BF16),
-                v_ref[s],
-                preferred_element_type=F32,
-            )
             for g in range(heads):
-                lo, hi = g * QUERIES_PER_KV, (g + 1) * QUERIES_PER_KV
+                lo = i * qrows + g * QUERIES_PER_KV
+                hi = lo + QUERIES_PER_KV
                 new_value = fresh[pl.ds(g * head_rows + (QUERIES_PER_KV + 1) * per + s, 1), :]
                 result[pl.ds(g * QUERIES_PER_KV * per + s, QUERIES_PER_KV, stride=per), :] = (
                     mixed[lo:hi, g * HEAD_SIZE : (g + 1) * HEAD_SIZE]
-                    + own_weights[i * qrows + lo : i * qrows + hi] * new_value
+                    + own_weights[lo:hi] * new_value
                 )
     out_ref[0] = result[...].astype(BF16)
 
 
-def attend(token, place, lengths, parts, scale, biases, cos, sin, keys, values, *, chunk, heads):
+def attend(
+    token, place, lengths, parts, scale, biases, cos, sin, keys, values, loads, *, chunk, heads
+):
     first = chunk == 0
     per = keys.shape[0]
     out_rows = heads * QUERIES_PER_KV * per
@@ -386,28 +398,36 @@
             pltpu.VMEM((out_rows, HEAD_SIZE), F32),
         ],
         8,
+        loads,
     )
 
 
-def output_kernel(*refs, labels, nz, per, first, last):
+def output_kernel(*refs, labels, nz, per, first, last, absolute):
     count = len(labels)
     place_ref, block_refs, sor_ref, w_ref = refs[0], refs[1 : 1 + count], refs[1 + count], refs[2 + count]
     rest = refs[3 + count :]
     if not first:
         acc_in_ref, rest = rest[0], rest[1:]
     if last:
-        mine_ref, send_ref, stacked, total = rest
+        mine_ref, send_ref, stacked = rest
     else:
         acc_out_ref, stacked = rest
     tiles = block_refs[0].shape[1] // per
 
-    one_hot = slot_one_hot(place_ref, sor_ref[...], nz, per)
+    half = sor_ref.shape[1] // 2
+    slot_of_row = sor_ref[...]
+    swapped = jnp.concatenate([slot_of_row[:, half:], slot_of_row[:, :half]], axis=1)
+    slot_of_row = jnp.where(place_ref[2] == 0, slot_of_row, swapped)
+    one_hot = slot_one_hot(place_ref, slot_of_row, nz, per, absolute)
     wide = {
         label: ref[z].astype(F32)
         for ref, own in zip(block_refs, labels)
         for z, label in enumerate(own)
     }
-    wide = [wide[h, q] for h in range(2) for q in place_order(nz)]
+    if absolute:
+        wide = [wide[owner] for owner in range(2 * nz)]
+    else:
+        wide = [wide[h, q] for h in range(2) for q in place_order(nz)]
     for c in range(tiles):
         stacked[:, c * HEAD_SIZE : (c + 1) * HEAD_SIZE] = jnp.concatenate(
             [block[c * per : (c + 1) * per] for block in wide], axis=0
@@ -420,17 +440,13 @@
     if not first:
         product = product + acc_in_ref[...]
     if last:
-        half = product.shape[0] // 2
-        total[...] = product
-        mine_ref[...] = total[pl.ds(pl.multiple_of(place_ref[2] * half, half), half), :]
-        send_ref[...] = total[
-            pl.ds(pl.multiple_of((1 - place_ref[2]) * half, half), half), :
-        ].astype(BF16)
+        mine_ref[...] = product[:half]
+        send_ref[...] = product[half:].astype(BF16)
     else:
         acc_out_ref[...] = product
 
 
-def output(token, place, blocks, labels, sor, w_out, acc, *, chunk, chunks, nz, per):
+def output(token, place, blocks, labels, sor, w_out, acc, loads, *, chunk, chunks, nz, per):
     first, last = chunk == 0, chunk == chunks - 1
     rows = 2 * nz * per
     depth, width = w_out.shape
@@ -440,15 +456,22 @@
         out_shapes = [((rows, width), F32)]
     return call(
         functools.partial(
-            output_kernel, labels=labels, nz=nz, per=per, first=first, last=last
+            output_kernel,
+            labels=labels,
+            nz=nz,
+            per=per,
+            first=first,
+            last=last,
+            absolute=GATHER[chunk] == "all_gather",
         ),
         "output" + str(chunk),
         token,
         [place],
         [*blocks, sor, w_out] + ([] if first else [acc]),
         out_shapes,
-        [pltpu.VMEM((rows, depth), BF16)] + ([pltpu.VMEM((rows, width), F32)] if last else []),
+        [pltpu.VMEM((rows, depth), BF16)],
         12,
+        loads,
     )
 
 
@@ -503,7 +526,7 @@
     scale = acc = None
     inputs = [hidden_rows, other, gain, sor]
     kept, swapped, reduced = {}, {}, {}
-    caches, w_outs, gathered, waiting = {}, {}, {}, {}
+    loaded, gathered, waiting = {}, {}, {}
 
     def over_y(blocks, labels):
         return lax.ppermute(blocks, "gx", same_z), [(1 - h, q) for h, q in labels]
@@ -512,39 +535,47 @@
         moved = lax.ppermute(blocks, "gx", stride_pairs(nz, stride))
         return moved, [(h, q ^ stride) for h, q in labels]
 
-    def do_project(token, c):
+    def windows_of(kind, c):
+        if kind == "weights":
+            return [
+                (array, (everything, head_window(c, n)))
+                for array, n in (
+                    (w_query, wide), (key_weight, HEAD_SIZE), (value_weight, HEAD_SIZE),
+                )
+            ]
+        if kind == "caches":
+            window = (pl.ds(0, per), pl.ds(0, positions), head_window(c, HEAD_SIZE))
+            return [(rotated_key_cache, window), (stored_value_cache, window)]
+        return [(w_out, (head_window(c, wide), all_columns))]
+
+    def file_loaded(wanted, arrays):
+        arrays = list(arrays)
+        for kind, c in wanted:
+            loaded[kind, c] = [arrays.pop(0) for _ in windows_of(kind, c)]
+
+    def loads_of(wanted):
+        return [pair for kind, c in wanted for pair in windows_of(kind, c)]
+
+    def do_load(token, wanted):
+        name = "load" + "".join("_" + kind + str(c) for kind, c in wanted)
+        token, arrays, _ = call(lambda: None, name, token, [], [], [], [], 1, loads_of(wanted))
+        file_loaded(wanted, arrays)
+        return token
+
+    def do_project(token, c, wanted):
         nonlocal inputs
-        token, weights = load(
-            "load_weights" + str(c),
-            token,
-            [w_query, key_weight, value_weight],
-            [(everything, head_window(c, n)) for n in (wide, HEAD_SIZE, HEAD_SIZE)],
-        )
-        token, outs = project(
-            token, place, inputs, weights, chunk=c, heads=CHUNK_HEADS[c], nz=nz, per=per
-        )
+        token, arrays, outs = project(
+            token, place, inputs, loaded["weights", c], loads_of(wanted),
+            chunk=c, heads=CHUNK_HEADS[c], nz=nz, per=per,
+        )
+        file_loaded(wanted, arrays)
         kept[c] = outs[0]
         if c == 0:
             inputs = [outs[2]]
         swapped[c] = lax.ppermute(outs[1], "gx", same_z)
         return token
 
-    def do_load_caches(token, c):
-        token, caches[c] = load(
-            "load_caches" + str(c),
-            token,
-            [rotated_key_cache, stored_value_cache],
-            [(pl.ds(0, per), pl.ds(0, positions), head_window(c, HEAD_SIZE))] * 2,
-        )
-        return token
-
-    def do_load_out(token, c):
-        token, (w_outs[c],) = load(
-            "load_out" + str(c), token, [w_out], [(head_window(c, wide), all_columns)]
-        )
-        return token
-
-    def do_far(token, c):
+    def do_far(token, c, wanted):
         half = nz // 2
         token, (total,) = add(
             "add_far" + str(c), token, [kept[c], swapped[c]], [half, half], half, 1
@@ -552,7 +583,7 @@
         reduced[c] = lax.ppermute(total, "gx", stride_pairs(nz, 1))
         return token
 
-    def do_near(token, c):
+    def do_near(token, c, wanted):
         terms, starts, count = [kept[c], swapped[c], reduced[c]], [0, 0, 0], nz // 2
         for stride in strides(nz)[1:]:
             token, (mine, sent) = add(
@@ -563,20 +594,27 @@
         reduced[c] = terms
         return token
 
-    def do_attend(token, c):
+    def do_attend(token, c, wanted):
         nonlocal scale
-        token, outs = attend(
-            token, place, slot_valid_lengths, reduced[c], scale, biases, cos, sin, *caches[c],
-            chunk=c, heads=CHUNK_HEADS[c],
-        )
+        token, arrays, outs = attend(
+            token, place, slot_valid_lengths, reduced[c], scale, biases, cos, sin, *loaded["caches", c],
+            loads_of(wanted), chunk=c, heads=CHUNK_HEADS[c],
+        )
+        file_loaded(wanted, arrays)
         if c == 0:
             scale = outs[1]
+        if GATHER[c] == "all_gather":
+            whole = lax.all_gather(outs[0], "gx", axis=0, tiled=True)
+            gathered[c] = [(whole, list(range(2 * nz)))]
+            return token
         own = outs[0], [(0, 0)]
         first_move = over_y(*own) if GATHER[c] == "y first" else over_z(*own, strides(nz)[-1])
         waiting[c] = own, first_move
         return token
 
-    def do_gather(token, c):
+    def do_gather(token, c, wanted):
+        if GATHER[c] == "all_gather":
+            return token
         held, moved = waiting[c]
         for stride in reversed(strides(nz) if GATHER[c] == "y first" else strides(nz)[:-1]):
             if GATHER[c] == "y first" and stride == 1:
@@ -590,7 +628,9 @@
             gathered[c].append(over_y(*held))
         return token
 
-    def do_forward(token, c):
+    def do_forward(token, c, wanted):
+        if GATHER[c] == "all_gather":
+            return token
         held, moved = waiting[c]
         if GATHER[c] == "y halved":
             gathered[c].append(over_y(*moved))
@@ -600,19 +640,19 @@
         gathered[c] = [held, over_z(*held, 1) if GATHER[c] == "y first" else over_y(*held)]
         return token
 
-    def do_output(token, c):
+    def do_output(token, c, wanted):
         nonlocal acc
-        token, acc = output(
+        token, arrays, acc = output(
             token, place, [a for a, _ in gathered[c]], [own for _, own in gathered[c]], sor,
-            w_outs[c], acc if c == 0 else acc[0], chunk=c, chunks=chunks, nz=nz, per=per,
-        )
+            *loaded["out", c], acc if c == 0 else acc[0], loads_of(wanted),
+            chunk=c, chunks=chunks, nz=nz, per=per,
+        )
+        file_loaded(wanted, arrays)
         return token
 
     token = jnp.zeros(TOKEN, F32)
     steps = {
         "project": do_project,
-        "load_caches": do_load_caches,
-        "load_out": do_load_out,
         "far": do_far,
         "near": do_near,
         "attend": do_attend,
@@ -620,8 +660,18 @@
         "forward": do_forward,
         "output": do_output,
     }
+    needs = {"project": "weights", "attend": "caches", "output": "out"}
+    wanted = []
     for step, c in ORDER:
-        token = steps[step](token, c)
+        if step not in steps:
+            wanted.append((step, c))
+            continue
+        if step not in needs or (needs[step], c) in wanted:
+            if wanted:
+                token = do_load(token, wanted)
+            wanted = []
+        token = steps[step](token, c, wanted)
+        wanted = []
     mine, send = acc
     received = lax.ppermute(send, "gy", [(0, 1), (1, 0)])
     return (hidden_rows.astype(F32) + mine + received.astype(F32)).astype(BF16)

time: 77.1 us -> 97.3 us (1.26)
  blocking collectives: 0 us -> 31.2 us
  starting transfers between devices: 30.2 us -> 24.1 us
  Pallas kernels: 32.3 us -> 30.2 us
  waiting for transfers between devices: 12.1 us -> 10.2 us
    all_gather x0 -> x1, blocking collectives: none -> 31.2 us  [do_attend(): whole = lax.all_gather(outs[0], 'gx', axis=0, tiled=True)]
    ppermute x6 -> x4, starting transfers between devices: 8.2 us -> 3.42 us  [over_z(): moved = lax.ppermute(blocks, 'gx', stride_pairs(nz, stride))]
    ppermute x3, waiting for transfers between devices: 3.87 us -> 0.01 us  [do_near(): terms = [mine, lax.ppermute(sent, 'gx', stride_pairs(nz, stride))]]
    pallas_call x27 -> x24, Pallas kernels: 32.3 us -> 30.2 us  [call(): pl.pallas_call(body, in_specs=[vmem] + [pl.BlockSpec(memory_space=pltpu.H...]
    ppermute x3, waiting for transfers between devices: 0.32 us -> 2.1 us  [do_far(): reduced[c] = lax.ppermute(total, 'gx', stride_pairs(nz, 1))]
    ppermute x6 -> x4, starting transfers between devices: 6.37 us -> 5.91 us  [over_y(): return (lax.ppermute(blocks, 'gx', same_z), [(1 - h, q) for h, q in labels])]
  transfers between devices with their start and end apart: 23 -> 19, of which waited for: 9 -> 7; matrix products, arithmetic and copies ran while one was open for 1% -> 0% of each run, Pallas kernels for 38% -> 28%
where the time goes in v7:
time: 97.3 us; the launch traced here: 97 us
  blocking collectives  31.2 us (32%)
  Pallas kernels  30.2 us (31%)
  starting transfers between devices  24.1 us (25%)
  waiting for transfers between devices  10.2 us (10%)
  other arithmetic  1.04 us (1%)
    all_gather x1, blocking collectives, do_attend(): whole = lax.all_gather(outs[0], 'gx', axis=0, tiled=True)  31.2 us
    pallas_call x24, Pallas kernels, call(): pl.pallas_call(body, in_specs=[vmem] + [pl.BlockSpec(memory_space=pltpu.H...  30.2 us
    ppermute x4, starting transfers between devices, over_y(): return (lax.ppermute(blocks, 'gx', same_z), [(1 - h, q) for h, q in labels])  5.91 us
    ppermute x3, starting transfers between devices, do_far(): reduced[c] = lax.ppermute(total, 'gx', stride_pairs(nz, 1))  5.36 us
    ppermute x3, starting transfers between devices, do_near(): terms = [mine, lax.ppermute(sent, 'gx', stride_pairs(nz, stride))]  4.62 us
    ppermute x3, starting transfers between devices, do_project(): swapped[c] = lax.ppermute(outs[1], 'gx', same_z)  4.38 us
    ppermute x3, waiting for transfers between devices, do_project(): swapped[c] = lax.ppermute(outs[1], 'gx', same_z)  3.82 us
    ppermute x4, starting transfers between devices, over_z(): moved = lax.ppermute(blocks, 'gx', stride_pairs(nz, stride))  3.42 us
  transfers between devices with their start and end apart: 19, of which 7 were waited for; matrix products, arithmetic and copies ran while one was open for 0% of the time, Pallas kernels for 28%

profile of v7, /device:TPU:0, one launch (start us, length us, event | category | flops | bytes accessed | tf_op | source)
XLA Modules:
  0.0 97.0 jit_solution(7632852445306289060)
XLA Ops:
  0.0 0.5 collective-permute-start
  0.5 2.3 %load_caches0_weights0.1 = (f32[8,128]{1,0:T(8,128)S(1)}, bf16[24,128,128]{2,1,0:T(8,128)(2,1)S(1)}, bf16[24,128,128]{2,1,0:T(8,128)(2,1)S(1)}, bf16[1024,1024]{...) custom-call(f32[8,128]{1,0:T(8,128)S(1)} %broadcast_in_dim.17.refs_0_, ...), custom_call_target="tpu_custom_call" | custom-call | tf_op jit(solution)/shard_map/load_caches0_weights0/pallas_call | solution.py:134
  2.7 0.1 pad_add_fusion.refs_1_
  2.8 1.5 %project0.1 = (f32[8,128]{1,0:T(8,128)S(1)}, bf16[4,272,128]{2,1,0:T(8,128)(2,1)S(1)}, bf16[4,272,128]{2,1,0:T(8,128)(2,1)S(1)}, bf16[192,1024]{1,0:T(8,128)(2,1)S(1)}) custom-call(f32[8,128]{1,0:T(8,128)S(1)} %get-tuple-element.72.refs_0_, s32[3]{0:T(128)S(1)} %pad_add_fusion.refs_1_, bf16[96,1024]{1,0:T(8,128)(2,1)S(1)} %copy-done, ...), custom_call_target="tpu_custom_call" | custom-call | flops 1557224960 | tf_op jit(solution)/shard_map/project0/pallas_call | solution.py:134
  4.3 2.6 %collective-permute-start.1 = (bf16[4,272,128]{2,1,0:T(8,128)(2,1)S(1)}, bf16[4,272,128]{2,1,0:T(8,128)(2,1)S(1)}, u32[]{:S(2)}, u32[]{:S(2)}) collective-permute-start(bf16[4,272,128]{2,1,0:T(8,128)(2,1)S(1)} %get-tuple-element.84), channel_id=1, source_target_pairs={{0,2},{2,0},{4,6},{6,4},{8,10},{10,8},{12,14},{14,12},{1,3},{3,1},... | collective-permute-start | bytes 835592 | tf_op jit(solution)/shard_map/ppermute | solution.py:575
  6.9 2.5 %load_weights1.1 = (f32[8,128]{1,0:T(8,128)S(1)}, bf16[1024,2048]{1,0:T(8,128)(2,1)S(1)}, bf16[1024,256]{1,0:T(8,128)(2,1)S(1)}, bf16[1024,256]{1,0:T(8,128)(2,1)S(1)}) custom-call(f32[8,128]{1,0:T(8,128)S(1)} %get-tuple-element.76.refs_0_, bf16[1024,4096]{1,0:T(8,128)(2,1)} %refs_1_.10, bf16[1024,512]{1,0:T(8,128)(2,1)} %refs_2_.13, bf16[1024,512]{1,0:T(8,128)(2,1)} %refs_3_.7), custom_call_target="tpu_custom_call" | custom-call | tf_op jit(solution)/shard_map/load_weights1/pallas_call | solution.py:134
  9.4 1.8 %project1.1 = (f32[8,128]{1,0:T(8,128)S(1)}, bf16[4,480,128]{2,1,0:T(8,128)(2,1)S(1)}, bf16[4,480,128]{2,1,0:T(8,128)(2,1)S(1)}) custom-call(f32[8,128]{1,0:T(8,128)S(1)} %get-tuple-element.77.refs_0_, s32[3]{0:T(128)S(1)} %pad_add_fusion.refs_1_, bf16[192,1024]{1,0:T(8,128)(2,1)S(1)} %get-tuple-element.78.refs_2_, ...), custom_call_target="tpu_custom_call" | custom-call | flops 1153500032 | tf_op jit(solution)/shard_map/project1/pallas_call | solution.py:134
  11.2 0.1 collective-permute-start.3
  11.3 3.1 %collective-permute-done.1.refs_2_ = bf16[4,272,128]{2,1,0:T(8,128)(2,1)S(1)} collective-permute-done((bf16[4,272,128]{2,1,0:T(8,128)(2,1)S(1)}, bf16[4,272,128]{2,1,0:T(8,128)(2,1)S(1)}, u32[]{:S(2)}, u32[]{:S(2)}) %collective-permute-start.1) | collective-permute-done | bytes 278560 | tf_op jit(solution)/shard_map/ppermute | solution.py:575
  14.4 2.1 %collective-permute-start.2 = (bf16[2,272,128]{2,1,0:T(8,128)(2,1)S(1)}, bf16[2,272,128]{2,1,0:T(8,128)(2,1)S(1)}, u32[]{:S(2)}, u32[]{:S(2)}) collective-permute-start(bf16[2,272,128]{2,1,0:T(8,128)(2,1)S(1)} %get-tuple-element.87), channel_id=1, source_target_pairs={{0,4},{2,6},{4,0},{6,2},{8,12},{10,14},{12,8},{14,10},{1,5},{3,7},... | collective-permute-start | bytes 417800 | tf_op jit(solution)/shard_map/ppermute | solution.py:583
  16.5 0.1 dynamic-slice_convert_fusion
  16.5 2.5 %load_out0_caches1.1 = (f32[8,128]{1,0:T(8,128)S(1)}, bf16[1024,1024]{1,0:T(8,128)(2,1)S(1)}, bf16[24,128,256]{2,1,0:T(8,128)(2,1)S(1)}, bf16[24,128,256]{2,1,0:T(8,128)(2,1)S(1)}) custom-call(f32[8,128]{1,0:T(8,128)S(1)} %get-tuple-element.85.refs_0_, bf16[4096,1024]{1,0:T(8,128)(2,1)} %refs_1_.13, bf16[24,128,512]{2,1,0:T(8,128)(2,1)} %refs_1_.11, ...), custom_call_target="tpu_custom_call" | custom-call | tf_op jit(solution)/shard_map/load_out0_caches1/pallas_call | solution.py:134
  19.1 0.7 collective-permute-done.2.refs_3_
  19.9 1.7 %load_weights2.1 = (f32[8,128]{1,0:T(8,128)S(1)}, bf16[1024,1024]{1,0:T(8,128)(2,1)S(1)}, bf16[1024,128]{1,0:T(8,128)(2,1)S(1)}, bf16[1024,128]{1,0:T(8,128)(2,1)S(1)}) custom-call(f32[8,128]{1,0:T(8,128)S(1)} %get-tuple-element.88.refs_0_, bf16[1024,4096]{1,0:T(8,128)(2,1)} %refs_1_.10, bf16[1024,512]{1,0:T(8,128)(2,1)} %refs_2_.13, bf16[1024,512]{1,0:T(8,128)(2,1)} %refs_3_.7), custom_call_target="tpu_custom_call" | custom-call | tf_op jit(solution)/shard_map/load_weights2/pallas_call | solution.py:134
  21.6 2.8 %collective-permute-start.4 = (bf16[1,272,128]{2,1,0:T(8,128)(2,1)S(1)}, bf16[1,272,128]{2,1,0:T(8,128)(2,1)S(1)}, u32[]{:S(2)}, u32[]{:S(2)}) collective-permute-start(bf16[1,272,128]{2,1,0:T(8,128)(2,1)S(1)} %get-tuple-element.98), channel_id=1, source_target_pairs={{0,8},{2,10},{4,12},{6,14},{8,0},{10,2},{12,4},{14,6},{1,9},{3,11}... | collective-permute-start | bytes 208904 | tf_op jit(solution)/shard_map/ppermute | solution.py:592
  24.4 1.2 %project2.1 = (f32[8,128]{1,0:T(8,128)S(1)}, bf16[4,240,128]{2,1,0:T(8,128)(2,1)S(1)}, bf16[4,240,128]{2,1,0:T(8,128)(2,1)S(1)}) custom-call(f32[8,128]{1,0:T(8,128)S(1)} %get-tuple-element.89.refs_0_, s32[3]{0:T(128)S(1)} %pad_add_fusion.refs_1_, bf16[192,1024]{1,0:T(8,128)(2,1)S(1)} %get-tuple-element.78.refs_2_, ...), custom_call_target="tpu_custom_call" | custom-call | flops 1557224960 | tf_op jit(solution)/shard_map/project2/pallas_call | solution.py:134
  25.6 1.7 %collective-permute-start.5 = (bf16[4,240,128]{2,1,0:T(8,128)(2,1)S(1)}, bf16[4,240,128]{2,1,0:T(8,128)(2,1)S(1)}, u32[]{:S(2)}, u32[]{:S(2)}) collective-permute-start(bf16[4,240,128]{2,1,0:T(8,128)(2,1)S(1)} %get-tuple-element.103), channel_id=1, source_target_pairs={{0,2},{2,0},{4,6},{6,4},{8,10},{10,8},{12,14},{14,12},{1,3},{3,1},... | collective-permute-start | bytes 737288 | tf_op jit(solution)/shard_map/ppermute | solution.py:575
  27.3 0.1 add_far1.1
  27.4 1.6 %collective-permute-start.6 = (bf16[2,480,128]{2,1,0:T(8,128)(2,1)S(1)}, bf16[2,480,128]{2,1,0:T(8,128)(2,1)S(1)}, u32[]{:S(2)}, u32[]{:S(2)}) collective-permute-start(bf16[2,480,128]{2,1,0:T(8,128)(2,1)S(1)} %get-tuple-element.105), channel_id=1, source_target_pairs={{0,4},{2,6},{4,0},{6,2},{8,12},{10,14},{12,8},{14,10},{1,5},{3,7},... | collective-permute-start | bytes 737288 | tf_op jit(solution)/shard_map/ppermute | solution.py:583
  29.0 0.1 fusion
  29.2 2.0 %attend0.1 = (f32[8,128]{1,0:T(8,128)S(1)}, bf16[1,192,128]{2,1,0:T(8,128)(2,1)S(1)}, f32[24,128]{1,0:T(8,128)S(1)}) custom-call(f32[8,128]{1,0:T(8,128)S(1)} %get-tuple-element.96.refs_0_, s32[3]{0:T(128)S(1)} %pad_add_fusion.refs_1_, s32[192]{0:T(256)S(1)} %copy-done.3, bf16[1,272,128]{2,1,0:T(8,128)(2,1)S(1)} %get-tuple-element.97.refs_3_, ...), custom_call_target="tpu_custom_call" | custom-call | flops 2422350080 | tf_op jit(solution)/shard_map/attend0/pallas_call | solution.py:134
  31.1 0.7 collective-permute-done.5.refs_2_
  31.9 1.6 %collective-permute-start.7 = (bf16[2,240,128]{2,1,0:T(8,128)(2,1)S(1)}, bf16[2,240,128]{2,1,0:T(8,128)(2,1)S(1)}, u32[]{:S(2)}, u32[]{:S(2)}) collective-permute-start(bf16[2,240,128]{2,1,0:T(8,128)(2,1)S(1)} %get-tuple-element.108), channel_id=1, source_target_pairs={{0,4},{2,6},{4,0},{6,2},{8,12},{10,14},{12,8},{14,10},{1,5},{3,7},... | collective-permute-start | bytes 368648 | tf_op jit(solution)/shard_map/ppermute | solution.py:583
  33.6 1.4 %collective-permute-done.6.refs_3_ = bf16[2,480,128]{2,1,0:T(8,128)(2,1)S(1)} collective-permute-done((bf16[2,480,128]{2,1,0:T(8,128)(2,1)S(1)}, bf16[2,480,128]{2,1,0:T(8,128)(2,1)S(1)}, u32[]{:S(2)}, u32[]{:S(2)}) %collective-permute-start.6) | collective-permute-done | bytes 245792 | tf_op jit(solution)/shard_map/ppermute | solution.py:583
  35.0 0.1 add_near1_2.1
  35.1 1.8 %collective-permute-start.8 = (bf16[1,480,128]{2,1,0:T(8,128)(2,1)S(1)}, bf16[1,480,128]{2,1,0:T(8,128)(2,1)S(1)}, u32[]{:S(2)}, u32[]{:S(2)}) collective-permute-start(bf16[1,480,128]{2,1,0:T(8,128)(2,1)S(1)} %get-tuple-element.111), channel_id=1, source_target_pairs={{0,8},{2,10},{4,12},{6,14},{8,0},{10,2},{12,4},{14,6},{1,9},{3,11}... | collective-permute-start | bytes 368648 | tf_op jit(solution)/shard_map/ppermute | solution.py:592
  36.8 31.2 %all_gather.3.refs_2_ = bf16[8,192,128]{2,1,0:T(8,128)(2,1)S(1)} all-gather(bf16[1,192,128]{2,1,0:T(8,128)(2,1)S(1)} %get-tuple-element.126), channel_id=1, replica_groups=mesh['grp'=2,'gx'=8,'gy'=2] {'gx'}, dimensions={0}, use_global_device_ids=true | all-gather | bytes 442368 | tf_op jit(solution)/shard_map/all_gather | solution.py:607
  68.0 1.4 %load_caches2.1 = (f32[8,128]{1,0:T(8,128)S(1)}, bf16[24,128,128]{2,1,0:T(8,128)(2,1)S(1)}, bf16[24,128,128]{2,1,0:T(8,128)(2,1)S(1)}) custom-call(f32[8,128]{1,0:T(8,128)S(1)} %get-tuple-element.106.refs_0_, bf16[24,128,512]{2,1,0:T(8,128)(2,1)} %refs_1_.11, bf16[24,128,512]{2,1,0:T(8,128)(2,1)} %refs_2_.15), custom_call_target="tpu_custom_call" | custom-call | tf_op jit(solution)/shard_map/load_caches2/pallas_call | solution.py:134
  69.5 0.1 collective-permute-start.9
  69.6 2.4 %attend1.1 = (f32[8,128]{1,0:T(8,128)S(1)}, bf16[1,384,128]{2,1,0:T(8,128)(2,1)S(1)}) custom-call(f32[8,128]{1,0:T(8,128)S(1)} %get-tuple-element.109.refs_0_, s32[3]{0:T(128)S(1)} %pad_add_fusion.refs_1_, s32[192]{0:T(256)S(1)} %copy-done.3, bf16[1,480,128]{2,1,0:T(8,128)(2,1)S(1)} %get-tuple-element.110.refs_3_, ...), custom_call_target="tpu_custom_call" | custom-call | flops 1153500032 | tf_op jit(solution)/shard_map/attend1/pallas_call | solution.py:134
  72.0 3.0 %collective-permute-start.10 = (bf16[1,384,128]{2,1,0:T(8,128)(2,1)S(1)}, bf16[1,384,128]{2,1,0:T(8,128)(2,1)S(1)}, u32[]{:S(2)}, u32[]{:S(2)}) collective-permute-start(bf16[1,384,128]{2,1,0:T(8,128)(2,1)S(1)} %get-tuple-element.121.refs_1_), channel_id=1, source_target_pairs={{0,8},{2,10},{4,12},{6,14},{8,0},{10,2},{12,4},{14,6},{1,9},{3,11}... | collective-permute-start | bytes 294920 | tf_op jit(solution)/shard_map/ppermute | solution.py:535
  74.9 1.9 %attend2.1 = (f32[8,128]{1,0:T(8,128)S(1)}, bf16[1,192,128]{2,1,0:T(8,128)(2,1)S(1)}) custom-call(f32[8,128]{1,0:T(8,128)S(1)} %get-tuple-element.115.refs_0_, s32[3]{0:T(128)S(1)} %pad_add_fusion.refs_1_, s32[192]{0:T(256)S(1)} %copy-done.3, bf16[1,240,128]{2,1,0:T(8,128)(2,1)S(1)} %get-tuple-element.116.refs_3_, ...), custom_call_target="tpu_custom_call" | custom-call | flops 2422350080 | tf_op jit(solution)/shard_map/attend2/pallas_call | solution.py:134
  76.8 0.1 collective-permute-start.11
  76.9 1.7 %collective-permute-done.10.refs_2_ = bf16[1,384,128]{2,1,0:T(8,128)(2,1)S(1)} collective-permute-done((bf16[1,384,128]{2,1,0:T(8,128)(2,1)S(1)}, bf16[1,384,128]{2,1,0:T(8,128)(2,1)S(1)}, u32[]{:S(2)}, u32[]{:S(2)}) %collective-permute-start.10) | collective-permute-done | bytes 98336 | tf_op jit(solution)/shard_map/ppermute | solution.py:535
  78.6 0.2 collective-permute-start.12
  78.9 2.2 %collective-permute-start.13 = (bf16[2,384,128]{2,1,0:T(8,128)(2,1)S(1)}, bf16[2,384,128]{2,1,0:T(8,128)(2,1)S(1)}, u32[]{:S(2)}, u32[]{:S(2)}) collective-permute-start(bf16[2,384,128]{2,1,0:T(8,128)(2,1)S(1)} %get-tuple-element.130.refs_2_), channel_id=1, source_target_pairs={{0,2},{2,0},{4,6},{6,4},{8,10},{10,8},{12,14},{14,12},{1,3},{3,1},... | collective-permute-start | bytes 589832 | tf_op jit(solution)/shard_map/ppermute | solution.py:532
  81.0 1.6 %load_out2.1 = (f32[8,128]{1,0:T(8,128)S(1)}, bf16[1024,1024]{1,0:T(8,128)(2,1)S(1)}) custom-call(f32[8,128]{1,0:T(8,128)S(1)} %get-tuple-element.122.refs_0_, bf16[4096,1024]{1,0:T(8,128)(2,1)} %refs_1_.13), custom_call_target="tpu_custom_call" | custom-call | tf_op jit(solution)/shard_map/load_out2/pallas_call | solution.py:134
  82.7 0.1 collective-permute-start.15
  82.8 1.7 %collective-permute-start.16 = (bf16[2,192,128]{2,1,0:T(8,128)(2,1)S(1)}, bf16[2,192,128]{2,1,0:T(8,128)(2,1)S(1)}, u32[]{:S(2)}, u32[]{:S(2)}) collective-permute-start(bf16[2,192,128]{2,1,0:T(8,128)(2,1)S(1)} %get-tuple-element.134.refs_2_), channel_id=1, source_target_pairs={{0,2},{2,0},{4,6},{6,4},{8,10},{10,8},{12,14},{14,12},{1,3},{3,1},... | collective-permute-start | bytes 294920 | tf_op jit(solution)/shard_map/ppermute | solution.py:532
  84.5 0.4 collective-permute-start.14
  84.8 1.3 %output0.1 = (f32[8,128]{1,0:T(8,128)S(1)}, f32[192,1024]{1,0:T(8,128)S(1)}) custom-call(f32[8,128]{1,0:T(8,128)S(1)} %get-tuple-element.125.refs_0_, s32[3]{0:T(128)S(1)} %pad_add_fusion.refs_1_, bf16[8,192,128]{2,1,0:T(8,128)(2,1)S(1)} %all_gather.3.refs_2_, s32[1,192]{1,0:T(1,128)S(1)} %bitcast.19, bf16[1024,1024]{1,0:T(8,128)(2,1)S(1)} %get-tuple-element.127.refs_4_), custom_call_target="tpu_custom_call" | custom-call | flops 9228000256 | tf_op jit(solution)/shard_map/output0/pallas_call | solution.py:134
  86.2 2.2 %load_out1.1 = (f32[8,128]{1,0:T(8,128)S(1)}, bf16[2048,1024]{1,0:T(8,128)(2,1)S(1)}) custom-call(f32[8,128]{1,0:T(8,128)S(1)} %get-tuple-element.128.refs_0_, bf16[4096,1024]{1,0:T(8,128)(2,1)} %refs_1_.13), custom_call_target="tpu_custom_call" | custom-call | tf_op jit(solution)/shard_map/load_out1/pallas_call | solution.py:134
  88.4 1.7 %collective-permute-start.17 = (bf16[2,192,128]{2,1,0:T(8,128)(2,1)S(1)}, bf16[2,192,128]{2,1,0:T(8,128)(2,1)S(1)}, u32[]{:S(2)}, u32[]{:S(2)}) collective-permute-start(bf16[2,192,128]{2,1,0:T(8,128)(2,1)S(1)} %collective-permute-done.15.refs_3_), channel_id=1, source_target_pairs={{0,2},{2,0},{4,6},{6,4},{8,10},{10,8},{12,14},{14,12},{1,3},{3,1},... | collective-permute-start | bytes 294920 | tf_op jit(solution)/shard_map/ppermute | solution.py:532
  90.1 1.8 %output1.1 = (f32[8,128]{1,0:T(8,128)S(1)}, f32[192,1024]{1,0:T(8,128)S(1)}) custom-call(f32[8,128]{1,0:T(8,128)S(1)} %get-tuple-element.129.refs_0_, s32[3]{0:T(128)S(1)} %pad_add_fusion.refs_1_, bf16[2,384,128]{2,1,0:T(8,128)(2,1)S(1)} %get-tuple-element.130.refs_2_, bf16[2,384,128]{2,1,0:T(8,128)(2,1)S(1)} %collective-permute-done.12.refs_3_, ...), custom_call_target="tpu_custom_call" | custom-call | flops 9228000256 | tf_op jit(solution)/shard_map/output1/pallas_call | solution.py:134
  92.0 1.1 %collective-permute-done.17.refs_5_ = bf16[2,192,128]{2,1,0:T(8,128)(2,1)S(1)} collective-permute-done((bf16[2,192,128]{2,1,0:T(8,128)(2,1)S(1)}, bf16[2,192,128]{2,1,0:T(8,128)(2,1)S(1)}, u32[]{:S(2)}, u32[]{:S(2)}) %collective-permute-start.17) | collective-permute-done | bytes 98336 | tf_op jit(solution)/shard_map/ppermute | solution.py:532
  93.1 1.8 %output2.1 = (f32[8,128]{1,0:T(8,128)}, f32[96,1024]{1,0:T(8,128)S(1)}, bf16[96,1024]{1,0:T(8,128)(2,1)S(1)}) custom-call(f32[8,128]{1,0:T(8,128)S(1)} %get-tuple-element.133.refs_0_, s32[3]{0:T(128)S(1)} %pad_add_fusion.refs_1_, bf16[2,192,128]{2,1,0:T(8,128)(2,1)S(1)} %get-tuple-element.134.refs_2_, ...), custom_call_target="tpu_custom_call" | custom-call | flops 1476480000 | tf_op jit(solution)/shard_map/output2/pallas_call | solution.py:134
  94.8 1.4 %collective-permute-done.18 = bf16[96,1024]{1,0:T(8,128)(2,1)S(1)} collective-permute-done((bf16[96,1024]{1,0:T(8,128)(2,1)S(1)}, bf16[96,1024]{1,0:T(8,128)(2,1)S(1)}, u32[]{:S(2)}, u32[]{:S(2)}) %collective-permute-start.18) | collective-permute-done | bytes 196640 | tf_op jit(solution)/shard_map/ppermute | solution.py:676
  96.3 0.7 add_convert_fusion
  (35 shorter events, 0.3 us)
Async XLA Ops:
  0.0 2.8 %collective-permute-start = (bf16[96,1024]{1,0:T(8,128)(2,1)}, bf16[96,1024]{1,0:T(8,128)(2,1)S(1)}, u32[]{:S(2)}, u32[]{:S(2)}) collective-permute-start(bf16[96,1024]{1,0:T(8,128)(2,1)} %refs_2_.10), channel_id=1, source_target_pairs={{0,1},{1,0},{2,3},{3,2},{4,5},{5,4},{6,7},{7,6},{8,9},{9,8},{10,11... | collective-permute-start | bytes 589832 | tf_op jit(solution)/shard_map/ppermute | solution.py:505
  0.5 2.4 %copy-start = (bf16[96,1024]{1,0:T(8,128)(2,1)S(1)}, bf16[96,1024]{1,0:T(8,128)(2,1)}, u32[]{:S(2)}) copy-start(bf16[96,1024]{1,0:T(8,128)(2,1)} %refs_2_.10) | copy-start | bytes 589828
  0.5 2.4 %copy-start.2 = (bf16[1024]{0:T(1024)(128)(2,1)S(1)}, bf16[1024]{0:T(1024)(128)(2,1)}, u32[]{:S(2)}) copy-start(bf16[1024]{0:T(1024)(128)(2,1)} %param.14) | copy-start | bytes 6148
  0.5 2.4 %copy-start.6 = (s32[192]{0:T(256)S(1)}, s32[192]{0:T(256)}, u32[]{:S(2)}) copy-start(s32[192]{0:T(256)} %param.24) | copy-start | bytes 2308
  4.3 10.0 %collective-permute-start.1 = (bf16[4,272,128]{2,1,0:T(8,128)(2,1)S(1)}, bf16[4,272,128]{2,1,0:T(8,128)(2,1)S(1)}, u32[]{:S(2)}, u32[]{:S(2)}) collective-permute-start(bf16[4,272,128]{2,1,0:T(8,128)(2,1)S(1)} %get-tuple-element.84), channel_id=1, source_target_pairs={{0,2},{2,0},{4,6},{6,4},{8,10},{10,8},{12,14},{14,12},{1,3},{3,1},... | collective-permute-start | bytes 835592 | tf_op jit(solution)/shard_map/ppermute | solution.py:575
  11.2 16.1 %collective-permute-start.3 = (bf16[4,480,128]{2,1,0:T(8,128)(2,1)S(1)}, bf16[4,480,128]{2,1,0:T(8,128)(2,1)S(1)}, u32[]{:S(2)}, u32[]{:S(2)}) collective-permute-start(bf16[4,480,128]{2,1,0:T(8,128)(2,1)S(1)} %get-tuple-element.95), channel_id=1, source_target_pairs={{0,2},{2,0},{4,6},{6,4},{8,10},{10,8},{12,14},{14,12},{1,3},{3,1},... | collective-permute-start | bytes 1474568 | tf_op jit(solution)/shard_map/ppermute | solution.py:575
  14.3 2.1 %copy-start.3 = (s32[192]{0:T(256)S(1)}, s32[192]{0:T(256)}, u32[]{:S(2)}) copy-start(s32[192]{0:T(256)} %refs_2_.17) | copy-start | bytes 2308
  14.4 5.4 %collective-permute-start.2 = (bf16[2,272,128]{2,1,0:T(8,128)(2,1)S(1)}, bf16[2,272,128]{2,1,0:T(8,128)(2,1)S(1)}, u32[]{:S(2)}, u32[]{:S(2)}) collective-permute-start(bf16[2,272,128]{2,1,0:T(8,128)(2,1)S(1)} %get-tuple-element.87), channel_id=1, source_target_pairs={{0,4},{2,6},{4,0},{6,2},{8,12},{10,14},{12,8},{14,10},{1,5},{3,7},... | collective-permute-start | bytes 417800 | tf_op jit(solution)/shard_map/ppermute | solution.py:583
  21.6 7.6 %collective-permute-start.4 = (bf16[1,272,128]{2,1,0:T(8,128)(2,1)S(1)}, bf16[1,272,128]{2,1,0:T(8,128)(2,1)S(1)}, u32[]{:S(2)}, u32[]{:S(2)}) collective-permute-start(bf16[1,272,128]{2,1,0:T(8,128)(2,1)S(1)} %get-tuple-element.98), channel_id=1, source_target_pairs={{0,8},{2,10},{4,12},{6,14},{8,0},{10,2},{12,4},{14,6},{1,9},{3,11}... | collective-permute-start | bytes 208904 | tf_op jit(solution)/shard_map/ppermute | solution.py:592
  24.4 4.8 %copy-start.1 = (bf16[4096]{0:T(1024)(128)(2,1)S(1)}, bf16[4096]{0:T(1024)(128)(2,1)}, u32[]{:S(2)}) copy-start(bf16[4096]{0:T(1024)(128)(2,1)} %param.18) | copy-start | bytes 24580
  24.4 4.8 %copy-start.4 = (bf16[512]{0:T(512)(128)(2,1)S(1)}, bf16[512]{0:T(512)(128)(2,1)}, u32[]{:S(2)}) copy-start(bf16[512]{0:T(512)(128)(2,1)} %param.19) | copy-start | bytes 3076
  24.4 4.8 %copy-start.5 = (bf16[512]{0:T(512)(128)(2,1)S(1)}, bf16[512]{0:T(512)(128)(2,1)}, u32[]{:S(2)}) copy-start(bf16[512]{0:T(512)(128)(2,1)} %param.20) | copy-start | bytes 3076
  25.6 6.3 %collective-permute-start.5 = (bf16[4,240,128]{2,1,0:T(8,128)(2,1)S(1)}, bf16[4,240,128]{2,1,0:T(8,128)(2,1)S(1)}, u32[]{:S(2)}, u32[]{:S(2)}) collective-permute-start(bf16[4,240,128]{2,1,0:T(8,128)(2,1)S(1)} %get-tuple-element.103), channel_id=1, source_target_pairs={{0,2},{2,0},{4,6},{6,4},{8,10},{10,8},{12,14},{14,12},{1,3},{3,1},... | collective-permute-start | bytes 737288 | tf_op jit(solution)/shard_map/ppermute | solution.py:575
  27.4 7.6 %collective-permute-start.6 = (bf16[2,480,128]{2,1,0:T(8,128)(2,1)S(1)}, bf16[2,480,128]{2,1,0:T(8,128)(2,1)S(1)}, u32[]{:S(2)}, u32[]{:S(2)}) collective-permute-start(bf16[2,480,128]{2,1,0:T(8,128)(2,1)S(1)} %get-tuple-element.105), channel_id=1, source_target_pairs={{0,4},{2,6},{4,0},{6,2},{8,12},{10,14},{12,8},{14,10},{1,5},{3,7},... | collective-permute-start | bytes 737288 | tf_op jit(solution)/shard_map/ppermute | solution.py:583
  31.9 37.5 %collective-permute-start.7 = (bf16[2,240,128]{2,1,0:T(8,128)(2,1)S(1)}, bf16[2,240,128]{2,1,0:T(8,128)(2,1)S(1)}, u32[]{:S(2)}, u32[]{:S(2)}) collective-permute-start(bf16[2,240,128]{2,1,0:T(8,128)(2,1)S(1)} %get-tuple-element.108), channel_id=1, source_target_pairs={{0,4},{2,6},{4,0},{6,2},{8,12},{10,14},{12,8},{14,10},{1,5},{3,7},... | collective-permute-start | bytes 368648 | tf_op jit(solution)/shard_map/ppermute | solution.py:583
  35.1 34.5 %collective-permute-start.8 = (bf16[1,480,128]{2,1,0:T(8,128)(2,1)S(1)}, bf16[1,480,128]{2,1,0:T(8,128)(2,1)S(1)}, u32[]{:S(2)}, u32[]{:S(2)}) collective-permute-start(bf16[1,480,128]{2,1,0:T(8,128)(2,1)S(1)} %get-tuple-element.111), channel_id=1, source_target_pairs={{0,8},{2,10},{4,12},{6,14},{8,0},{10,2},{12,4},{14,6},{1,9},{3,11}... | collective-permute-start | bytes 368648 | tf_op jit(solution)/shard_map/ppermute | solution.py:592
  69.5 5.5 %collective-permute-start.9 = (bf16[1,240,128]{2,1,0:T(8,128)(2,1)S(1)}, bf16[1,240,128]{2,1,0:T(8,128)(2,1)S(1)}, u32[]{:S(2)}, u32[]{:S(2)}) collective-permute-start(bf16[1,240,128]{2,1,0:T(8,128)(2,1)S(1)} %get-tuple-element.117), channel_id=1, source_target_pairs={{0,8},{2,10},{4,12},{6,14},{8,0},{10,2},{12,4},{14,6},{1,9},{3,11}... | collective-permute-start | bytes 184328 | tf_op jit(solution)/shard_map/ppermute | solution.py:592
  72.0 6.6 %collective-permute-start.10 = (bf16[1,384,128]{2,1,0:T(8,128)(2,1)S(1)}, bf16[1,384,128]{2,1,0:T(8,128)(2,1)S(1)}, u32[]{:S(2)}, u32[]{:S(2)}) collective-permute-start(bf16[1,384,128]{2,1,0:T(8,128)(2,1)S(1)} %get-tuple-element.121.refs_1_), channel_id=1, source_target_pairs={{0,8},{2,10},{4,12},{6,14},{8,0},{10,2},{12,4},{14,6},{1,9},{3,11}... | collective-permute-start | bytes 294920 | tf_op jit(solution)/shard_map/ppermute | solution.py:535
  76.8 5.8 %collective-permute-start.11 = (bf16[1,192,128]{2,1,0:T(8,128)(2,1)S(1)}, bf16[1,192,128]{2,1,0:T(8,128)(2,1)S(1)}, u32[]{:S(2)}, u32[]{:S(2)}) collective-permute-start(bf16[1,192,128]{2,1,0:T(8,128)(2,1)S(1)} %get-tuple-element.124.refs_1_), channel_id=1, source_target_pairs={{0,8},{2,10},{4,12},{6,14},{8,0},{10,2},{12,4},{14,6},{1,9},{3,11}... | collective-permute-start | bytes 147464 | tf_op jit(solution)/shard_map/ppermute | solution.py:535
  78.6 5.8 %collective-permute-start.12 = (bf16[2,384,128]{2,1,0:T(8,128)(2,1)S(1)}, bf16[2,384,128]{2,1,0:T(8,128)(2,1)S(1)}, u32[]{:S(2)}, u32[]{:S(2)}) collective-permute-start(bf16[2,384,128]{2,1,0:T(8,128)(2,1)S(1)} %get-tuple-element.130.refs_2_), channel_id=1, source_target_pairs={{0,4},{2,6},{4,0},{6,2},{8,12},{10,14},{12,8},{14,10},{1,5},{3,7},... | collective-permute-start | bytes 589832 | tf_op jit(solution)/shard_map/ppermute | solution.py:535
  78.9 11.3 %collective-permute-start.13 = (bf16[2,384,128]{2,1,0:T(8,128)(2,1)S(1)}, bf16[2,384,128]{2,1,0:T(8,128)(2,1)S(1)}, u32[]{:S(2)}, u32[]{:S(2)}) collective-permute-start(bf16[2,384,128]{2,1,0:T(8,128)(2,1)S(1)} %get-tuple-element.130.refs_2_), channel_id=1, source_target_pairs={{0,2},{2,0},{4,6},{6,4},{8,10},{10,8},{12,14},{14,12},{1,3},{3,1},... | collective-permute-start | bytes 589832 | tf_op jit(solution)/shard_map/ppermute | solution.py:532
  82.7 5.7 %collective-permute-start.15 = (bf16[2,192,128]{2,1,0:T(8,128)(2,1)S(1)}, bf16[2,192,128]{2,1,0:T(8,128)(2,1)S(1)}, u32[]{:S(2)}, u32[]{:S(2)}) collective-permute-start(bf16[2,192,128]{2,1,0:T(8,128)(2,1)S(1)} %get-tuple-element.134.refs_2_), channel_id=1, source_target_pairs={{0,4},{2,6},{4,0},{6,2},{8,12},{10,14},{12,8},{14,10},{1,5},{3,7},... | collective-permute-start | bytes 294920 | tf_op jit(solution)/shard_map/ppermute | solution.py:535
  82.8 9.2 %collective-permute-start.16 = (bf16[2,192,128]{2,1,0:T(8,128)(2,1)S(1)}, bf16[2,192,128]{2,1,0:T(8,128)(2,1)S(1)}, u32[]{:S(2)}, u32[]{:S(2)}) collective-permute-start(bf16[2,192,128]{2,1,0:T(8,128)(2,1)S(1)} %get-tuple-element.134.refs_2_), channel_id=1, source_target_pairs={{0,2},{2,0},{4,6},{6,4},{8,10},{10,8},{12,14},{14,12},{1,3},{3,1},... | collective-permute-start | bytes 294920 | tf_op jit(solution)/shard_map/ppermute | solution.py:532
  84.5 5.7 %collective-permute-start.14 = (bf16[2,384,128]{2,1,0:T(8,128)(2,1)S(1)}, bf16[2,384,128]{2,1,0:T(8,128)(2,1)S(1)}, u32[]{:S(2)}, u32[]{:S(2)}) collective-permute-start(bf16[2,384,128]{2,1,0:T(8,128)(2,1)S(1)} %collective-permute-done.12.refs_3_), channel_id=1, source_target_pairs={{0,2},{2,0},{4,6},{6,4},{8,10},{10,8},{12,14},{14,12},{1,3},{3,1},... | collective-permute-start | bytes 589832 | tf_op jit(solution)/shard_map/ppermute | solution.py:532
  88.4 4.7 %collective-permute-start.17 = (bf16[2,192,128]{2,1,0:T(8,128)(2,1)S(1)}, bf16[2,192,128]{2,1,0:T(8,128)(2,1)S(1)}, u32[]{:S(2)}, u32[]{:S(2)}) collective-permute-start(bf16[2,192,128]{2,1,0:T(8,128)(2,1)S(1)} %collective-permute-done.15.refs_3_), channel_id=1, source_target_pairs={{0,2},{2,0},{4,6},{6,4},{8,10},{10,8},{12,14},{14,12},{1,3},{3,1},... | collective-permute-start | bytes 294920 | tf_op jit(solution)/shard_map/ppermute | solution.py:532
  94.8 1.4 %collective-permute-start.18 = (bf16[96,1024]{1,0:T(8,128)(2,1)S(1)}, bf16[96,1024]{1,0:T(8,128)(2,1)S(1)}, u32[]{:S(2)}, u32[]{:S(2)}) collective-permute-start(bf16[96,1024]{1,0:T(8,128)(2,1)S(1)} %get-tuple-element.138), channel_id=1, source_target_pairs={{0,1},{1,0},{2,3},{3,2},{4,5},{5,4},{6,7},{7,6},{8,9},{9,8},{10,11... | collective-permute-start | bytes 589832 | tf_op jit(solution)/shard_map/ppermute | solution.py:676

commit v8 on v7

--- a/solution.py
+++ b/solution.py
@@ -24,37 +24,37 @@
 MIB = 1024 * 1024
 SLOTS_AT_ONCE = {1: 24, 2: 8, 3: 8, 4: 4}
 PEAK_FLOP_PER_US = 1.1535e9
-COSTS = {'project0': 1.35, 'attend0': 2.1, 'join0_2': 0.1, 'join0': 0.1, 'output0': 8, 'project1': 1, 'add_near1_2': 2, 'attend1': 1, 'join1_2': 1, 'output1': 8, 'project2': 1.35, 'add_far2': 0.15, 'add_near2_2': 0.3, 'attend2': 2.1, 'join2_2': 8, 'output2': 1.28, 'join1_1': 2, 'join2_1': 4, 'add_far0': 2, 'join2': 4}
-GATHER = ("all_gather", "y halved", "y halved")
+COSTS = {'attend0': 4, 'output0': 4, 'project1': 1, 'attend1': 8, 'attend2': 1, 'join0_1': 4, 'add_far0': 1, 'add_far2': 1, 'add_near0_2': 1, 'project2': 4, 'join0': 1, 'project0': 1, 'join2': 2}
+GATHER = ('y halved', 'y halved', 'y halved')
 ORDER = (
-    ("caches", 0),
+    ("weights", 2),
     ("weights", 0),
     ("project", 0),
     ("weights", 1),
+    ("caches", 0),
     ("project", 1),
+    ("project", 2),
+    ("out", 0),
     ("far", 0),
-    ("out", 0),
     ("caches", 1),
     ("near", 0),
-    ("weights", 2),
-    ("project", 2),
     ("far", 1),
     ("attend", 0),
     ("far", 2),
     ("near", 1),
     ("gather", 0),
     ("caches", 2),
+    ("forward", 0),
     ("near", 2),
+    ("out", 2),
     ("attend", 1),
-    ("forward", 0),
+    ("out", 1),
     ("attend", 2),
     ("gather", 1),
-    ("out", 2),
+    ("output", 0),
     ("gather", 2),
-    ("output", 0),
+    ("forward", 2),
     ("forward", 1),
-    ("forward", 2),
-    ("out", 1),
     ("output", 1),
     ("output", 2),
 )

time: 97.3 us -> 74.9 us (0.77)
  blocking collectives: 31.2 us -> 0 us
  starting transfers between devices: 24.1 us -> 33 us
  Pallas kernels: 30.2 us -> 28.6 us
  waiting for transfers between devices: 10.2 us -> 11.7 us
    all_gather x1 -> x0, blocking collectives: 31.2 us -> none  [do_attend(): whole = lax.all_gather(outs[0], 'gx', axis=0, tiled=True)]
    ppermute x4 -> x6, waiting for transfers between devices: 1.72 us -> 7.79 us  [over_z(): moved = lax.ppermute(blocks, 'gx', stride_pairs(nz, stride))]
    ppermute x4 -> x6, starting transfers between devices: 3.42 us -> 9.4 us  [over_z(): moved = lax.ppermute(blocks, 'gx', stride_pairs(nz, stride))]
    ppermute x3, waiting for transfers between devices: 3.82 us -> 0.01 us  [do_project(): swapped[c] = lax.ppermute(outs[1], 'gx', same_z)]
    ppermute x4 -> x6, starting transfers between devices: 5.91 us -> 8.32 us  [over_y(): return (lax.ppermute(blocks, 'gx', same_z), [(1 - h, q) for h, q in labels])]
    pallas_call x24 -> x23, Pallas kernels: 30.2 us -> 28.6 us  [call(): pl.pallas_call(body, in_specs=[vmem] + [pl.BlockSpec(memory_space=pltpu.H...]
    ppermute x3, starting transfers between devices: 4.62 us -> 5.96 us  [do_near(): terms = [mine, lax.ppermute(sent, 'gx', stride_pairs(nz, stride))]]
  transfers between devices with their start and end apart: 19 -> 23, of which waited for: 7 -> 6; matrix products, arithmetic and copies ran while one was open for 0% -> 0% of each run, Pallas kernels for 28% -> 34%
where the time goes in v8:
time: 74.9 us; the launch traced here: 74.7 us
  starting transfers between devices  33 us (44%)
  Pallas kernels  28.6 us (38%)
  waiting for transfers between devices  11.7 us (16%)
  other arithmetic  1.04 us (1%)
    pallas_call x23, Pallas kernels, call(): pl.pallas_call(body, in_specs=[vmem] + [pl.BlockSpec(memory_space=pltpu.H...  28.6 us
    ppermute x6, starting transfers between devices, over_z(): moved = lax.ppermute(blocks, 'gx', stride_pairs(nz, stride))  9.4 us
    ppermute x6, starting transfers between devices, over_y(): return (lax.ppermute(blocks, 'gx', same_z), [(1 - h, q) for h, q in labels])  8.32 us
    ppermute x6, waiting for transfers between devices, over_z(): moved = lax.ppermute(blocks, 'gx', stride_pairs(nz, stride))  7.79 us
    ppermute x3, starting transfers between devices, do_near(): terms = [mine, lax.ppermute(sent, 'gx', stride_pairs(nz, stride))]  5.96 us
    ppermute x3, starting transfers between devices, do_far(): reduced[c] = lax.ppermute(total, 'gx', stride_pairs(nz, 1))  4.57 us
    ppermute x3, starting transfers between devices, do_project(): swapped[c] = lax.ppermute(outs[1], 'gx', same_z)  4.32 us
    ppermute x3, waiting for transfers between devices, do_far(): reduced[c] = lax.ppermute(total, 'gx', stride_pairs(nz, 1))  1.7 us
  transfers between devices with their start and end apart: 23, of which 6 were waited for; matrix products, arithmetic and copies ran while one was open for 0% of the time, Pallas kernels for 34%

profile of v8, /device:TPU:0, one launch (start us, length us, event | category | flops | bytes accessed | tf_op | source)
XLA Modules:
  0.0 74.7 jit_solution(13538764565418213479)
XLA Ops:
  0.0 0.5 collective-permute-start
  0.5 2.6 %load_weights2_weights0.1 = (f32[8,128]{1,0:T(8,128)S(1)}, bf16[1024,1024]{1,0:T(8,128)(2,1)S(1)}, bf16[1024,128]{1,0:T(8,128)(2,1)S(1)}, bf16[1024,128]{1,0:T(8...) custom-call(f32[8,128]{1,0:T(8,128)S(1)} %broadcast_in_dim.17.refs_0_, ...), custom_call_target="tpu_custom_call" | custom-call | tf_op jit(solution)/shard_map/load_weights2_weights0/pallas_call | solution.py:134
  3.1 0.1 pad_add_fusion.refs_1_.refs_2_
  3.2 1.5 %project0.1 = (f32[8,128]{1,0:T(8,128)S(1)}, bf16[4,272,128]{2,1,0:T(8,128)(2,1)S(1)}, bf16[4,272,128]{2,1,0:T(8,128)(2,1)S(1)}, bf16[192,1024]{1,0:T(8,128)(2,1)S(1)}) custom-call(f32[8,128]{1,0:T(8,128)S(1)} %get-tuple-element.72.refs_0_, s32[3]{0:T(128)S(1)} %pad_add_fusion.refs_1_.refs_2_, bf16[96,1024]{1,0:T(8,128)(2,1)S(1)} %copy-done, ...), custom_call_target="tpu_custom_call" | custom-call | flops 1153500032 | tf_op jit(solution)/shard_map/project0/pallas_call | solution.py:134
  4.6 2.6 %collective-permute-start.1 = (bf16[4,272,128]{2,1,0:T(8,128)(2,1)S(1)}, bf16[4,272,128]{2,1,0:T(8,128)(2,1)S(1)}, u32[]{:S(2)}, u32[]{:S(2)}) collective-permute-start(bf16[4,272,128]{2,1,0:T(8,128)(2,1)S(1)} %get-tuple-element.89), channel_id=1, source_target_pairs={{0,2},{2,0},{4,6},{6,4},{8,10},{10,8},{12,14},{14,12},{1,3},{3,1},... | collective-permute-start | bytes 835592 | tf_op jit(solution)/shard_map/ppermute | solution.py:575
  7.3 3.0 %load_weights1_caches0.1 = (f32[8,128]{1,0:T(8,128)S(1)}, bf16[1024,2048]{1,0:T(8,128)(2,1)S(1)}, bf16[1024,256]{1,0:T(8,128)(2,1)S(1)}, bf16[1024,256]{1,0:T(8,...) custom-call(f32[8,128]{1,0:T(8,128)S(1)} %get-tuple-element.76.refs_0_, ...), custom_call_target="tpu_custom_call" | custom-call | tf_op jit(solution)/shard_map/load_weights1_caches0/pallas_call | solution.py:134
  10.3 1.7 %project1.1 = (f32[8,128]{1,0:T(8,128)S(1)}, bf16[4,480,128]{2,1,0:T(8,128)(2,1)S(1)}, bf16[4,480,128]{2,1,0:T(8,128)(2,1)S(1)}) custom-call(f32[8,128]{1,0:T(8,128)S(1)} %get-tuple-element.77.refs_0_, s32[3]{0:T(128)S(1)} %pad_add_fusion.refs_1_.refs_2_, bf16[192,1024]{1,0:T(8,128)(2,1)S(1)} %get-tuple-element.78.refs_2_, ...), custom_call_target="tpu_custom_call" | custom-call | flops 1153500032 | tf_op jit(solution)/shard_map/project1/pallas_call | solution.py:134
  12.0 0.1 collective-permute-start.3
  12.1 1.2 %project2.1 = (f32[8,128]{1,0:T(8,128)S(1)}, bf16[4,240,128]{2,1,0:T(8,128)(2,1)S(1)}, bf16[4,240,128]{2,1,0:T(8,128)(2,1)S(1)}) custom-call(f32[8,128]{1,0:T(8,128)S(1)} %get-tuple-element.82.refs_0_, s32[3]{0:T(128)S(1)} %pad_add_fusion.refs_1_.refs_2_, bf16[192,1024]{1,0:T(8,128)(2,1)S(1)} %get-tuple-element.78.refs_2_, ...), custom_call_target="tpu_custom_call" | custom-call | flops 4614000128 | tf_op jit(solution)/shard_map/project2/pallas_call | solution.py:134
  13.4 1.6 %load_out0.1 = (f32[8,128]{1,0:T(8,128)S(1)}, bf16[1024,1024]{1,0:T(8,128)(2,1)S(1)}) custom-call(f32[8,128]{1,0:T(8,128)S(1)} %get-tuple-element.86.refs_0_, bf16[4096,1024]{1,0:T(8,128)(2,1)} %refs_1_.13), custom_call_target="tpu_custom_call" | custom-call | tf_op jit(solution)/shard_map/load_out0/pallas_call | solution.py:134
  15.0 2.1 %collective-permute-start.2 = (bf16[2,272,128]{2,1,0:T(8,128)(2,1)S(1)}, bf16[2,272,128]{2,1,0:T(8,128)(2,1)S(1)}, u32[]{:S(2)}, u32[]{:S(2)}) collective-permute-start(bf16[2,272,128]{2,1,0:T(8,128)(2,1)S(1)} %get-tuple-element.92), channel_id=1, source_target_pairs={{0,4},{2,6},{4,0},{6,2},{8,12},{10,14},{12,8},{14,10},{1,5},{3,7},... | collective-permute-start | bytes 417800 | tf_op jit(solution)/shard_map/ppermute | solution.py:583
  17.2 0.1 dynamic-slice_convert_fusion
  17.3 1.9 %load_caches1.1 = (f32[8,128]{1,0:T(8,128)S(1)}, bf16[24,128,256]{2,1,0:T(8,128)(2,1)S(1)}, bf16[24,128,256]{2,1,0:T(8,128)(2,1)S(1)}) custom-call(f32[8,128]{1,0:T(8,128)S(1)} %get-tuple-element.90.refs_0_, bf16[24,128,512]{2,1,0:T(8,128)(2,1)} %refs_1_.11, bf16[24,128,512]{2,1,0:T(8,128)(2,1)} %refs_2_.11), custom_call_target="tpu_custom_call" | custom-call | tf_op jit(solution)/shard_map/load_caches1/pallas_call | solution.py:134
  19.2 1.7 %collective-permute-done.2.refs_3_ = bf16[2,272,128]{2,1,0:T(8,128)(2,1)S(1)} collective-permute-done((bf16[2,272,128]{2,1,0:T(8,128)(2,1)S(1)}, bf16[2,272,128]{2,1,0:T(8,128)(2,1)S(1)}, u32[]{:S(2)}, u32[]{:S(2)}) %collective-permute-start.2) | collective-permute-done | bytes 139296 | tf_op jit(solution)/shard_map/ppermute | solution.py:583
  20.9 0.1 add_near0_2.1
  21.0 2.8 %collective-permute-start.4 = (bf16[1,272,128]{2,1,0:T(8,128)(2,1)S(1)}, bf16[1,272,128]{2,1,0:T(8,128)(2,1)S(1)}, u32[]{:S(2)}, u32[]{:S(2)}) collective-permute-start(bf16[1,272,128]{2,1,0:T(8,128)(2,1)S(1)} %get-tuple-element.98), channel_id=1, source_target_pairs={{0,8},{2,10},{4,12},{6,14},{8,0},{10,2},{12,4},{14,6},{1,9},{3,11}... | collective-permute-start | bytes 208904 | tf_op jit(solution)/shard_map/ppermute | solution.py:592
  23.8 0.1 fusion
  23.9 1.6 %collective-permute-start.5 = (bf16[4,240,128]{2,1,0:T(8,128)(2,1)S(1)}, bf16[4,240,128]{2,1,0:T(8,128)(2,1)S(1)}, u32[]{:S(2)}, u32[]{:S(2)}) collective-permute-start(bf16[4,240,128]{2,1,0:T(8,128)(2,1)S(1)} %get-tuple-element.103), channel_id=1, source_target_pairs={{0,2},{2,0},{4,6},{6,4},{8,10},{10,8},{12,14},{14,12},{1,3},{3,1},... | collective-permute-start | bytes 737288 | tf_op jit(solution)/shard_map/ppermute | solution.py:575
  25.5 0.1 add_far1.1
  25.6 1.6 %collective-permute-start.6 = (bf16[2,480,128]{2,1,0:T(8,128)(2,1)S(1)}, bf16[2,480,128]{2,1,0:T(8,128)(2,1)S(1)}, u32[]{:S(2)}, u32[]{:S(2)}) collective-permute-start(bf16[2,480,128]{2,1,0:T(8,128)(2,1)S(1)} %get-tuple-element.105), channel_id=1, source_target_pairs={{0,4},{2,6},{4,0},{6,2},{8,12},{10,14},{12,8},{14,10},{1,5},{3,7},... | collective-permute-start | bytes 737288 | tf_op jit(solution)/shard_map/ppermute | solution.py:583
  27.2 2.0 %attend0.1 = (f32[8,128]{1,0:T(8,128)S(1)}, bf16[1,192,128]{2,1,0:T(8,128)(2,1)S(1)}, f32[24,128]{1,0:T(8,128)S(1)}) custom-call(f32[8,128]{1,0:T(8,128)S(1)} %get-tuple-element.96.refs_0_, s32[3]{0:T(128)S(1)} %pad_add_fusion.refs_1_.refs_2_, s32[192]{0:T(256)S(1)} %copy-done.3, bf16[1,272,128]{2,1,0:T(8,128)(2,1)S(1)} %get-tuple-element.97.refs_3_, ...), custom_call_target="tpu_custom_call" | custom-call | flops 4614000128 | tf_op jit(solution)/shard_map/attend0/pallas_call | solution.py:134
  29.2 3.3 %collective-permute-start.7 = (bf16[1,192,128]{2,1,0:T(8,128)(2,1)S(1)}, bf16[1,192,128]{2,1,0:T(8,128)(2,1)S(1)}, u32[]{:S(2)}, u32[]{:S(2)}) collective-permute-start(bf16[1,192,128]{2,1,0:T(8,128)(2,1)S(1)} %get-tuple-element.107.refs_1_), channel_id=1, source_target_pairs={{0,8},{2,10},{4,12},{6,14},{8,0},{10,2},{12,4},{14,6},{1,9},{3,11}... | collective-permute-start | bytes 147464 | tf_op jit(solution)/shard_map/ppermute | solution.py:535
  32.5 0.8 %collective-permute-start.8 = (bf16[2,240,128]{2,1,0:T(8,128)(2,1)S(1)}, bf16[2,240,128]{2,1,0:T(8,128)(2,1)S(1)}, u32[]{:S(2)}, u32[]{:S(2)}) collective-permute-start(bf16[2,240,128]{2,1,0:T(8,128)(2,1)S(1)} %get-tuple-element.110), channel_id=1, source_target_pairs={{0,4},{2,6},{4,0},{6,2},{8,12},{10,14},{12,8},{14,10},{1,5},{3,7},... | collective-permute-start | bytes 368648 | tf_op jit(solution)/shard_map/ppermute | solution.py:583
  33.3 0.1 add_near1_2.1
  33.4 3.0 %collective-permute-start.9 = (bf16[1,480,128]{2,1,0:T(8,128)(2,1)S(1)}, bf16[1,480,128]{2,1,0:T(8,128)(2,1)S(1)}, u32[]{:S(2)}, u32[]{:S(2)}) collective-permute-start(bf16[1,480,128]{2,1,0:T(8,128)(2,1)S(1)} %get-tuple-element.113), channel_id=1, source_target_pairs={{0,8},{2,10},{4,12},{6,14},{8,0},{10,2},{12,4},{14,6},{1,9},{3,11}... | collective-permute-start | bytes 368648 | tf_op jit(solution)/shard_map/ppermute | solution.py:592
  36.5 2.5 %collective-permute-start.12 = (bf16[2,192,128]{2,1,0:T(8,128)(2,1)S(1)}, bf16[2,192,128]{2,1,0:T(8,128)(2,1)S(1)}, u32[]{:S(2)}, u32[]{:S(2)}) collective-permute-start(bf16[2,192,128]{2,1,0:T(8,128)(2,1)S(1)} %get-tuple-element.125.refs_2_), channel_id=1, source_target_pairs={{0,4},{2,6},{4,0},{6,2},{8,12},{10,14},{12,8},{14,10},{1,5},{3,7},... | collective-permute-start | bytes 294920 | tf_op jit(solution)/shard_map/ppermute | solution.py:535
  39.0 1.4 %collective-permute-start.13 = (bf16[2,192,128]{2,1,0:T(8,128)(2,1)S(1)}, bf16[2,192,128]{2,1,0:T(8,128)(2,1)S(1)}, u32[]{:S(2)}, u32[]{:S(2)}) collective-permute-start(bf16[2,192,128]{2,1,0:T(8,128)(2,1)S(1)} %get-tuple-element.125.refs_2_), channel_id=1, source_target_pairs={{0,2},{2,0},{4,6},{6,4},{8,10},{10,8},{12,14},{14,12},{1,3},{3,1},... | collective-permute-start | bytes 294920 | tf_op jit(solution)/shard_map/ppermute | solution.py:532
  40.4 1.4 %load_caches2.1 = (f32[8,128]{1,0:T(8,128)S(1)}, bf16[24,128,128]{2,1,0:T(8,128)(2,1)S(1)}, bf16[24,128,128]{2,1,0:T(8,128)(2,1)S(1)}) custom-call(f32[8,128]{1,0:T(8,128)S(1)} %get-tuple-element.108.refs_0_, bf16[24,128,512]{2,1,0:T(8,128)(2,1)} %refs_1_.11, bf16[24,128,512]{2,1,0:T(8,128)(2,1)} %refs_2_.11), custom_call_target="tpu_custom_call" | custom-call | tf_op jit(solution)/shard_map/load_caches2/pallas_call | solution.py:134
  41.9 0.1 collective-permute-start.10
  42.0 1.9 %collective-permute-start.14 = (bf16[2,192,128]{2,1,0:T(8,128)(2,1)S(1)}, bf16[2,192,128]{2,1,0:T(8,128)(2,1)S(1)}, u32[]{:S(2)}, u32[]{:S(2)}) collective-permute-start(bf16[2,192,128]{2,1,0:T(8,128)(2,1)S(1)} %collective-permute-done.12.refs_3_), channel_id=1, source_target_pairs={{0,2},{2,0},{4,6},{6,4},{8,10},{10,8},{12,14},{14,12},{1,3},{3,1},... | collective-permute-start | bytes 294920 | tf_op jit(solution)/shard_map/ppermute | solution.py:532
  43.9 3.6 %attend1.1 = (f32[8,128]{1,0:T(8,128)S(1)}, bf16[1024,1024]{1,0:T(8,128)(2,1)S(1)}, bf16[1,384,128]{2,1,0:T(8,128)(2,1)S(1)}) custom-call(f32[8,128]{1,0:T(8,128)S(1)} %get-tuple-element.111.refs_0_, bf16[4096,1024]{1,0:T(8,128)(2,1)} %refs_1_.13, s32[3]{0:T(128)S(1)} %pad_add_fusion.refs_1_.refs_2_, s32[192]{0:T(256)S(1)} %copy-done.3, ...), custom_call_target="tpu_custom_call" | custom-call | flops 9228000256 | tf_op jit(solution)/shard_map/attend1/pallas_call | solution.py:134
  47.5 2.3 %collective-permute-start.11 = (bf16[1,384,128]{2,1,0:T(8,128)(2,1)S(1)}, bf16[1,384,128]{2,1,0:T(8,128)(2,1)S(1)}, u32[]{:S(2)}, u32[]{:S(2)}) collective-permute-start(bf16[1,384,128]{2,1,0:T(8,128)(2,1)S(1)} %get-tuple-element.123.refs_1_), channel_id=1, source_target_pairs={{0,8},{2,10},{4,12},{6,14},{8,0},{10,2},{12,4},{14,6},{1,9},{3,11}... | collective-permute-start | bytes 294920 | tf_op jit(solution)/shard_map/ppermute | solution.py:535
  49.8 2.9 %attend2.1 = (f32[8,128]{1,0:T(8,128)S(1)}, bf16[2048,1024]{1,0:T(8,128)(2,1)S(1)}, bf16[1,192,128]{2,1,0:T(8,128)(2,1)S(1)}) custom-call(f32[8,128]{1,0:T(8,128)S(1)} %get-tuple-element.117.refs_0_, bf16[4096,1024]{1,0:T(8,128)(2,1)} %refs_1_.13, s32[3]{0:T(128)S(1)} %pad_add_fusion.refs_1_.refs_2_, s32[192]{0:T(256)S(1)} %copy-done.3, ...), custom_call_target="tpu_custom_call" | custom-call | flops 1153500032 | tf_op jit(solution)/shard_map/attend2/pallas_call | solution.py:134
  52.7 0.7 collective-permute-start.15
  53.4 0.9 %collective-permute-done.11.refs_2_ = bf16[1,384,128]{2,1,0:T(8,128)(2,1)S(1)} collective-permute-done((bf16[1,384,128]{2,1,0:T(8,128)(2,1)S(1)}, bf16[1,384,128]{2,1,0:T(8,128)(2,1)S(1)}, u32[]{:S(2)}, u32[]{:S(2)}) %collective-permute-start.11) | collective-permute-done | bytes 98336 | tf_op jit(solution)/shard_map/ppermute | solution.py:535
  54.4 0.4 collective-permute-start.16
  54.8 0.9 %collective-permute-start.17 = (bf16[2,384,128]{2,1,0:T(8,128)(2,1)S(1)}, bf16[2,384,128]{2,1,0:T(8,128)(2,1)S(1)}, u32[]{:S(2)}, u32[]{:S(2)}) collective-permute-start(bf16[2,384,128]{2,1,0:T(8,128)(2,1)S(1)} %get-tuple-element.130.refs_2_), channel_id=1, source_target_pairs={{0,2},{2,0},{4,6},{6,4},{8,10},{10,8},{12,14},{14,12},{1,3},{3,1},... | collective-permute-start | bytes 589832 | tf_op jit(solution)/shard_map/ppermute | solution.py:532
  55.7 1.3 %output0.1 = (f32[8,128]{1,0:T(8,128)S(1)}, f32[192,1024]{1,0:T(8,128)S(1)}) custom-call(f32[8,128]{1,0:T(8,128)S(1)} %get-tuple-element.124.refs_0_, s32[3]{0:T(128)S(1)} %pad_add_fusion.refs_1_.refs_2_, bf16[2,192,128]{2,1,0:T(8,128)(2,1)S(1)} %get-tuple-element.125.refs_2_, bf16[2,192,128]{2,1,0:T(8,128)(2,1)S(1)} %collective-permute-done.12.refs_3_, ...), custom_call_target="tpu_custom_call" | custom-call | flops 4614000128 | tf_op jit(solution)/shard_map/output0/pallas_call | solution.py:134
  57.1 4.3 %collective-permute-done.16.refs_3_ = bf16[2,384,128]{2,1,0:T(8,128)(2,1)S(1)} collective-permute-done((bf16[2,384,128]{2,1,0:T(8,128)(2,1)S(1)}, bf16[2,384,128]{2,1,0:T(8,128)(2,1)S(1)}, u32[]{:S(2)}, u32[]{:S(2)}) %collective-permute-start.16) | collective-permute-done | bytes 196640 | tf_op jit(solution)/shard_map/ppermute | solution.py:535
  61.4 0.1 collective-permute-start.19
  61.5 2.1 %collective-permute-start.20 = (bf16[2,192,128]{2,1,0:T(8,128)(2,1)S(1)}, bf16[2,192,128]{2,1,0:T(8,128)(2,1)S(1)}, u32[]{:S(2)}, u32[]{:S(2)}) collective-permute-start(bf16[2,192,128]{2,1,0:T(8,128)(2,1)S(1)} %get-tuple-element.134.refs_2_), channel_id=1, source_target_pairs={{0,2},{2,0},{4,6},{6,4},{8,10},{10,8},{12,14},{14,12},{1,3},{3,1},... | collective-permute-start | bytes 294920 | tf_op jit(solution)/shard_map/ppermute | solution.py:532
  63.6 2.5 %collective-permute-done.19.refs_3_ = bf16[2,192,128]{2,1,0:T(8,128)(2,1)S(1)} collective-permute-done((bf16[2,192,128]{2,1,0:T(8,128)(2,1)S(1)}, bf16[2,192,128]{2,1,0:T(8,128)(2,1)S(1)}, u32[]{:S(2)}, u32[]{:S(2)}) %collective-permute-start.19) | collective-permute-done | bytes 98336 | tf_op jit(solution)/shard_map/ppermute | solution.py:535
  66.1 2.0 %collective-permute-start.21 = (bf16[2,192,128]{2,1,0:T(8,128)(2,1)S(1)}, bf16[2,192,128]{2,1,0:T(8,128)(2,1)S(1)}, u32[]{:S(2)}, u32[]{:S(2)}) collective-permute-start(bf16[2,192,128]{2,1,0:T(8,128)(2,1)S(1)} %collective-permute-done.19.refs_3_), channel_id=1, source_target_pairs={{0,2},{2,0},{4,6},{6,4},{8,10},{10,8},{12,14},{14,12},{1,3},{3,1},... | collective-permute-start | bytes 294920 | tf_op jit(solution)/shard_map/ppermute | solution.py:532
  68.1 1.8 %output1.1 = (f32[8,128]{1,0:T(8,128)S(1)}, f32[192,1024]{1,0:T(8,128)S(1)}) custom-call(f32[8,128]{1,0:T(8,128)S(1)} %get-tuple-element.129.refs_0_, s32[3]{0:T(128)S(1)} %pad_add_fusion.refs_1_.refs_2_, bf16[2,384,128]{2,1,0:T(8,128)(2,1)S(1)} %get-tuple-element.130.refs_2_, bf16[2,384,128]{2,1,0:T(8,128)(2,1)S(1)} %collective-permute-done.16.refs_3_, ...), custom_call_target="tpu_custom_call" | custom-call | tf_op jit(solution)/shard_map/output1/pallas_call | solution.py:134
  70.0 0.7 collective-permute-done.21.refs_5_
  70.7 1.8 %output2.1 = (f32[8,128]{1,0:T(8,128)}, f32[96,1024]{1,0:T(8,128)S(1)}, bf16[96,1024]{1,0:T(8,128)(2,1)S(1)}) custom-call(f32[8,128]{1,0:T(8,128)S(1)} %get-tuple-element.133.refs_0_, s32[3]{0:T(128)S(1)} %pad_add_fusion.refs_1_.refs_2_, bf16[2,192,128]{2,1,0:T(8,128)(2,1)S(1)} %get-tuple-element.134.refs_2_, ...), custom_call_target="tpu_custom_call" | custom-call | tf_op jit(solution)/shard_map/output2/pallas_call | solution.py:134
  72.5 1.4 %collective-permute-done.22 = bf16[96,1024]{1,0:T(8,128)(2,1)S(1)} collective-permute-done((bf16[96,1024]{1,0:T(8,128)(2,1)S(1)}, bf16[96,1024]{1,0:T(8,128)(2,1)S(1)}, u32[]{:S(2)}, u32[]{:S(2)}) %collective-permute-start.22) | collective-permute-done | bytes 196640 | tf_op jit(solution)/shard_map/ppermute | solution.py:676
  73.9 0.7 %add_convert_fusion = bf16[96,1024]{1,0:T(8,128)(2,1)} fusion(bf16[96,1024]{1,0:T(8,128)(2,1)S(1)} %collective-permute-done.22, f32[96,1024]{1,0:T(8,128)S(1)} %get-tuple-element.137, bf16[96,1024]{1,0:T(8,128)(2,1)S(1)} %copy-done), kind=kLoop, calls=%fused_computation | loop fusion | flops 491520 | bytes 983040 | tf_op jit(solution)/shard_map/convert_element_type | solution.py:677
  (41 shorter events, 0.2 us)
Async XLA Ops:
  0.0 3.1 %collective-permute-start = (bf16[96,1024]{1,0:T(8,128)(2,1)}, bf16[96,1024]{1,0:T(8,128)(2,1)S(1)}, u32[]{:S(2)}, u32[]{:S(2)}) collective-permute-start(bf16[96,1024]{1,0:T(8,128)(2,1)} %refs_2_.7), channel_id=1, source_target_pairs={{0,1},{1,0},{2,3},{3,2},{4,5},{5,4},{6,7},{7,6},{8,9},{9,8},{10,11... | collective-permute-start | bytes 589832 | tf_op jit(solution)/shard_map/ppermute | solution.py:505
  0.5 2.7 %copy-start = (bf16[96,1024]{1,0:T(8,128)(2,1)S(1)}, bf16[96,1024]{1,0:T(8,128)(2,1)}, u32[]{:S(2)}) copy-start(bf16[96,1024]{1,0:T(8,128)(2,1)} %refs_2_.7) | copy-start | bytes 589828
  0.5 2.7 %copy-start.2 = (s32[192]{0:T(256)S(1)}, s32[192]{0:T(256)}, u32[]{:S(2)}) copy-start(s32[192]{0:T(256)} %param.24) | copy-start | bytes 2308
  0.5 2.7 %copy-start.6 = (bf16[1024]{0:T(1024)(128)(2,1)S(1)}, bf16[1024]{0:T(1024)(128)(2,1)}, u32[]{:S(2)}) copy-start(bf16[1024]{0:T(1024)(128)(2,1)} %param.14) | copy-start | bytes 6148
  4.6 10.4 %collective-permute-start.1 = (bf16[4,272,128]{2,1,0:T(8,128)(2,1)S(1)}, bf16[4,272,128]{2,1,0:T(8,128)(2,1)S(1)}, u32[]{:S(2)}, u32[]{:S(2)}) collective-permute-start(bf16[4,272,128]{2,1,0:T(8,128)(2,1)S(1)} %get-tuple-element.89), channel_id=1, source_target_pairs={{0,2},{2,0},{4,6},{6,4},{8,10},{10,8},{12,14},{14,12},{1,3},{3,1},... | collective-permute-start | bytes 835592 | tf_op jit(solution)/shard_map/ppermute | solution.py:575
  12.0 13.5 %collective-permute-start.3 = (bf16[4,480,128]{2,1,0:T(8,128)(2,1)S(1)}, bf16[4,480,128]{2,1,0:T(8,128)(2,1)S(1)}, u32[]{:S(2)}, u32[]{:S(2)}) collective-permute-start(bf16[4,480,128]{2,1,0:T(8,128)(2,1)S(1)} %get-tuple-element.95), channel_id=1, source_target_pairs={{0,2},{2,0},{4,6},{6,4},{8,10},{10,8},{12,14},{14,12},{1,3},{3,1},... | collective-permute-start | bytes 1474568 | tf_op jit(solution)/shard_map/ppermute | solution.py:575
  15.0 2.2 %copy-start.3 = (s32[192]{0:T(256)S(1)}, s32[192]{0:T(256)}, u32[]{:S(2)}) copy-start(s32[192]{0:T(256)} %refs_3_.7) | copy-start | bytes 2308
  15.0 5.9 %collective-permute-start.2 = (bf16[2,272,128]{2,1,0:T(8,128)(2,1)S(1)}, bf16[2,272,128]{2,1,0:T(8,128)(2,1)S(1)}, u32[]{:S(2)}, u32[]{:S(2)}) collective-permute-start(bf16[2,272,128]{2,1,0:T(8,128)(2,1)S(1)} %get-tuple-element.92), channel_id=1, source_target_pairs={{0,4},{2,6},{4,0},{6,2},{8,12},{10,14},{12,8},{14,10},{1,5},{3,7},... | collective-permute-start | bytes 417800 | tf_op jit(solution)/shard_map/ppermute | solution.py:583
  19.2 8.0 %copy-start.1 = (bf16[4096]{0:T(1024)(128)(2,1)S(1)}, bf16[4096]{0:T(1024)(128)(2,1)}, u32[]{:S(2)}) copy-start(bf16[4096]{0:T(1024)(128)(2,1)} %param.18) | copy-start | bytes 24580
  19.2 8.0 %copy-start.4 = (bf16[512]{0:T(512)(128)(2,1)S(1)}, bf16[512]{0:T(512)(128)(2,1)}, u32[]{:S(2)}) copy-start(bf16[512]{0:T(512)(128)(2,1)} %param.19) | copy-start | bytes 3076
  19.2 8.0 %copy-start.5 = (bf16[512]{0:T(512)(128)(2,1)S(1)}, bf16[512]{0:T(512)(128)(2,1)}, u32[]{:S(2)}) copy-start(bf16[512]{0:T(512)(128)(2,1)} %param.20) | copy-start | bytes 3076
  21.0 6.2 %collective-permute-start.4 = (bf16[1,272,128]{2,1,0:T(8,128)(2,1)S(1)}, bf16[1,272,128]{2,1,0:T(8,128)(2,1)S(1)}, u32[]{:S(2)}, u32[]{:S(2)}) collective-permute-start(bf16[1,272,128]{2,1,0:T(8,128)(2,1)S(1)} %get-tuple-element.98), channel_id=1, source_target_pairs={{0,8},{2,10},{4,12},{6,14},{8,0},{10,2},{12,4},{14,6},{1,9},{3,11}... | collective-permute-start | bytes 208904 | tf_op jit(solution)/shard_map/ppermute | solution.py:592
  23.9 8.6 %collective-permute-start.5 = (bf16[4,240,128]{2,1,0:T(8,128)(2,1)S(1)}, bf16[4,240,128]{2,1,0:T(8,128)(2,1)S(1)}, u32[]{:S(2)}, u32[]{:S(2)}) collective-permute-start(bf16[4,240,128]{2,1,0:T(8,128)(2,1)S(1)} %get-tuple-element.103), channel_id=1, source_target_pairs={{0,2},{2,0},{4,6},{6,4},{8,10},{10,8},{12,14},{14,12},{1,3},{3,1},... | collective-permute-start | bytes 737288 | tf_op jit(solution)/shard_map/ppermute | solution.py:575
  25.6 7.8 %collective-permute-start.6 = (bf16[2,480,128]{2,1,0:T(8,128)(2,1)S(1)}, bf16[2,480,128]{2,1,0:T(8,128)(2,1)S(1)}, u32[]{:S(2)}, u32[]{:S(2)}) collective-permute-start(bf16[2,480,128]{2,1,0:T(8,128)(2,1)S(1)} %get-tuple-element.105), channel_id=1, source_target_pairs={{0,4},{2,6},{4,0},{6,2},{8,12},{10,14},{12,8},{14,10},{1,5},{3,7},... | collective-permute-start | bytes 737288 | tf_op jit(solution)/shard_map/ppermute | solution.py:583
  29.2 7.3 %collective-permute-start.7 = (bf16[1,192,128]{2,1,0:T(8,128)(2,1)S(1)}, bf16[1,192,128]{2,1,0:T(8,128)(2,1)S(1)}, u32[]{:S(2)}, u32[]{:S(2)}) collective-permute-start(bf16[1,192,128]{2,1,0:T(8,128)(2,1)S(1)} %get-tuple-element.107.refs_1_), channel_id=1, source_target_pairs={{0,8},{2,10},{4,12},{6,14},{8,0},{10,2},{12,4},{14,6},{1,9},{3,11}... | collective-permute-start | bytes 147464 | tf_op jit(solution)/shard_map/ppermute | solution.py:535
  32.5 9.3 %collective-permute-start.8 = (bf16[2,240,128]{2,1,0:T(8,128)(2,1)S(1)}, bf16[2,240,128]{2,1,0:T(8,128)(2,1)S(1)}, u32[]{:S(2)}, u32[]{:S(2)}) collective-permute-start(bf16[2,240,128]{2,1,0:T(8,128)(2,1)S(1)} %get-tuple-element.110), channel_id=1, source_target_pairs={{0,4},{2,6},{4,0},{6,2},{8,12},{10,14},{12,8},{14,10},{1,5},{3,7},... | collective-permute-start | bytes 368648 | tf_op jit(solution)/shard_map/ppermute | solution.py:583
  33.4 10.4 %collective-permute-start.9 = (bf16[1,480,128]{2,1,0:T(8,128)(2,1)S(1)}, bf16[1,480,128]{2,1,0:T(8,128)(2,1)S(1)}, u32[]{:S(2)}, u32[]{:S(2)}) collective-permute-start(bf16[1,480,128]{2,1,0:T(8,128)(2,1)S(1)} %get-tuple-element.113), channel_id=1, source_target_pairs={{0,8},{2,10},{4,12},{6,14},{8,0},{10,2},{12,4},{14,6},{1,9},{3,11}... | collective-permute-start | bytes 368648 | tf_op jit(solution)/shard_map/ppermute | solution.py:592
  36.5 5.5 %collective-permute-start.12 = (bf16[2,192,128]{2,1,0:T(8,128)(2,1)S(1)}, bf16[2,192,128]{2,1,0:T(8,128)(2,1)S(1)}, u32[]{:S(2)}, u32[]{:S(2)}) collective-permute-start(bf16[2,192,128]{2,1,0:T(8,128)(2,1)S(1)} %get-tuple-element.125.refs_2_), channel_id=1, source_target_pairs={{0,4},{2,6},{4,0},{6,2},{8,12},{10,14},{12,8},{14,10},{1,5},{3,7},... | collective-permute-start | bytes 294920 | tf_op jit(solution)/shard_map/ppermute | solution.py:535
  39.0 16.7 %collective-permute-start.13 = (bf16[2,192,128]{2,1,0:T(8,128)(2,1)S(1)}, bf16[2,192,128]{2,1,0:T(8,128)(2,1)S(1)}, u32[]{:S(2)}, u32[]{:S(2)}) collective-permute-start(bf16[2,192,128]{2,1,0:T(8,128)(2,1)S(1)} %get-tuple-element.125.refs_2_), channel_id=1, source_target_pairs={{0,2},{2,0},{4,6},{6,4},{8,10},{10,8},{12,14},{14,12},{1,3},{3,1},... | collective-permute-start | bytes 294920 | tf_op jit(solution)/shard_map/ppermute | solution.py:532
  41.9 7.9 %collective-permute-start.10 = (bf16[1,240,128]{2,1,0:T(8,128)(2,1)S(1)}, bf16[1,240,128]{2,1,0:T(8,128)(2,1)S(1)}, u32[]{:S(2)}, u32[]{:S(2)}) collective-permute-start(bf16[1,240,128]{2,1,0:T(8,128)(2,1)S(1)} %get-tuple-element.119), channel_id=1, source_target_pairs={{0,8},{2,10},{4,12},{6,14},{8,0},{10,2},{12,4},{14,6},{1,9},{3,11}... | collective-permute-start | bytes 184328 | tf_op jit(solution)/shard_map/ppermute | solution.py:592
  42.0 13.8 %collective-permute-start.14 = (bf16[2,192,128]{2,1,0:T(8,128)(2,1)S(1)}, bf16[2,192,128]{2,1,0:T(8,128)(2,1)S(1)}, u32[]{:S(2)}, u32[]{:S(2)}) collective-permute-start(bf16[2,192,128]{2,1,0:T(8,128)(2,1)S(1)} %collective-permute-done.12.refs_3_), channel_id=1, source_target_pairs={{0,2},{2,0},{4,6},{6,4},{8,10},{10,8},{12,14},{14,12},{1,3},{3,1},... | collective-permute-start | bytes 294920 | tf_op jit(solution)/shard_map/ppermute | solution.py:532
  47.5 6.9 %collective-permute-start.11 = (bf16[1,384,128]{2,1,0:T(8,128)(2,1)S(1)}, bf16[1,384,128]{2,1,0:T(8,128)(2,1)S(1)}, u32[]{:S(2)}, u32[]{:S(2)}) collective-permute-start(bf16[1,384,128]{2,1,0:T(8,128)(2,1)S(1)} %get-tuple-element.123.refs_1_), channel_id=1, source_target_pairs={{0,8},{2,10},{4,12},{6,14},{8,0},{10,2},{12,4},{14,6},{1,9},{3,11}... | collective-permute-start | bytes 294920 | tf_op jit(solution)/shard_map/ppermute | solution.py:535
  52.7 8.7 %collective-permute-start.15 = (bf16[1,192,128]{2,1,0:T(8,128)(2,1)S(1)}, bf16[1,192,128]{2,1,0:T(8,128)(2,1)S(1)}, u32[]{:S(2)}, u32[]{:S(2)}) collective-permute-start(bf16[1,192,128]{2,1,0:T(8,128)(2,1)S(1)} %get-tuple-element.128.refs_1_), channel_id=1, source_target_pairs={{0,8},{2,10},{4,12},{6,14},{8,0},{10,2},{12,4},{14,6},{1,9},{3,11}... | collective-permute-start | bytes 147464 | tf_op jit(solution)/shard_map/ppermute | solution.py:535
  54.4 7.0 %collective-permute-start.16 = (bf16[2,384,128]{2,1,0:T(8,128)(2,1)S(1)}, bf16[2,384,128]{2,1,0:T(8,128)(2,1)S(1)}, u32[]{:S(2)}, u32[]{:S(2)}) collective-permute-start(bf16[2,384,128]{2,1,0:T(8,128)(2,1)S(1)} %get-tuple-element.130.refs_2_), channel_id=1, source_target_pairs={{0,4},{2,6},{4,0},{6,2},{8,12},{10,14},{12,8},{14,10},{1,5},{3,7},... | collective-permute-start | bytes 589832 | tf_op jit(solution)/shard_map/ppermute | solution.py:535
  54.8 13.4 %collective-permute-start.17 = (bf16[2,384,128]{2,1,0:T(8,128)(2,1)S(1)}, bf16[2,384,128]{2,1,0:T(8,128)(2,1)S(1)}, u32[]{:S(2)}, u32[]{:S(2)}) collective-permute-start(bf16[2,384,128]{2,1,0:T(8,128)(2,1)S(1)} %get-tuple-element.130.refs_2_), channel_id=1, source_target_pairs={{0,2},{2,0},{4,6},{6,4},{8,10},{10,8},{12,14},{14,12},{1,3},{3,1},... | collective-permute-start | bytes 589832 | tf_op jit(solution)/shard_map/ppermute | solution.py:532
  61.4 6.7 %collective-permute-start.18 = (bf16[2,384,128]{2,1,0:T(8,128)(2,1)S(1)}, bf16[2,384,128]{2,1,0:T(8,128)(2,1)S(1)}, u32[]{:S(2)}, u32[]{:S(2)}) collective-permute-start(bf16[2,384,128]{2,1,0:T(8,128)(2,1)S(1)} %collective-permute-done.16.refs_3_), channel_id=1, source_target_pairs={{0,2},{2,0},{4,6},{6,4},{8,10},{10,8},{12,14},{14,12},{1,3},{3,1},... | collective-permute-start | bytes 589832 | tf_op jit(solution)/shard_map/ppermute | solution.py:532
  61.4 4.7 %collective-permute-start.19 = (bf16[2,192,128]{2,1,0:T(8,128)(2,1)S(1)}, bf16[2,192,128]{2,1,0:T(8,128)(2,1)S(1)}, u32[]{:S(2)}, u32[]{:S(2)}) collective-permute-start(bf16[2,192,128]{2,1,0:T(8,128)(2,1)S(1)} %get-tuple-element.134.refs_2_), channel_id=1, source_target_pairs={{0,4},{2,6},{4,0},{6,2},{8,12},{10,14},{12,8},{14,10},{1,5},{3,7},... | collective-permute-start | bytes 294920 | tf_op jit(solution)/shard_map/ppermute | solution.py:535
  61.5 8.5 %collective-permute-start.20 = (bf16[2,192,128]{2,1,0:T(8,128)(2,1)S(1)}, bf16[2,192,128]{2,1,0:T(8,128)(2,1)S(1)}, u32[]{:S(2)}, u32[]{:S(2)}) collective-permute-start(bf16[2,192,128]{2,1,0:T(8,128)(2,1)S(1)} %get-tuple-element.134.refs_2_), channel_id=1, source_target_pairs={{0,2},{2,0},{4,6},{6,4},{8,10},{10,8},{12,14},{14,12},{1,3},{3,1},... | collective-permute-start | bytes 294920 | tf_op jit(solution)/shard_map/ppermute | solution.py:532
  66.1 4.6 %collective-permute-start.21 = (bf16[2,192,128]{2,1,0:T(8,128)(2,1)S(1)}, bf16[2,192,128]{2,1,0:T(8,128)(2,1)S(1)}, u32[]{:S(2)}, u32[]{:S(2)}) collective-permute-start(bf16[2,192,128]{2,1,0:T(8,128)(2,1)S(1)} %collective-permute-done.19.refs_3_), channel_id=1, source_target_pairs={{0,2},{2,0},{4,6},{6,4},{8,10},{10,8},{12,14},{14,12},{1,3},{3,1},... | collective-permute-start | bytes 294920 | tf_op jit(solution)/shard_map/ppermute | solution.py:532
  72.5 1.4 %collective-permute-start.22 = (bf16[96,1024]{1,0:T(8,128)(2,1)S(1)}, bf16[96,1024]{1,0:T(8,128)(2,1)S(1)}, u32[]{:S(2)}, u32[]{:S(2)}) collective-permute-start(bf16[96,1024]{1,0:T(8,128)(2,1)S(1)} %get-tuple-element.138), channel_id=1, source_target_pairs={{0,1},{1,0},{2,3},{3,2},{4,5},{5,4},{6,7},{7,6},{8,9},{9,8},{10,11... | collective-permute-start | bytes 589832 | tf_op jit(solution)/shard_map/ppermute | solution.py:676

commit v9 on v7

--- a/solution.py
+++ b/solution.py
@@ -24,37 +24,32 @@
 MIB = 1024 * 1024
 SLOTS_AT_ONCE = {1: 24, 2: 8, 3: 8, 4: 4}
 PEAK_FLOP_PER_US = 1.1535e9
-COSTS = {'project0': 1.35, 'attend0': 2.1, 'join0_2': 0.1, 'join0': 0.1, 'output0': 8, 'project1': 1, 'add_near1_2': 2, 'attend1': 1, 'join1_2': 1, 'output1': 8, 'project2': 1.35, 'add_far2': 0.15, 'add_near2_2': 0.3, 'attend2': 2.1, 'join2_2': 8, 'output2': 1.28, 'join1_1': 2, 'join2_1': 4, 'add_far0': 2, 'join2': 4}
-GATHER = ("all_gather", "y halved", "y halved")
+COSTS = {'project0': 1.22, 'add_far0': 0.1, 'add_near0_2': 0.1, 'attend0': 1.9, 'join0_1': 0.1, 'join0': 0.1, 'output0': 1.4, 'project1': 1.8, 'add_far1': 0.1, 'add_near1_2': 0.1, 'attend1': 2.35, 'join1_1': 0.1, 'join1': 0.1, 'output1': 2, 'project2': 1.22, 'add_far2': 0.1, 'add_near2_2': 0.1, 'attend2': 1.9, 'join2': 0.1, 'output2': 4}
+Y_IN_HALVES = (True, True, True)
+GATHER = ('y halved', 'y halved', 'y halved')
 ORDER = (
-    ("caches", 0),
     ("weights", 0),
+    ("weights", 1),
     ("project", 0),
-    ("weights", 1),
     ("project", 1),
     ("far", 0),
-    ("out", 0),
-    ("caches", 1),
+    ("weights", 2),
+    ("far", 1),
     ("near", 0),
-    ("weights", 2),
     ("project", 2),
-    ("far", 1),
+    ("near", 1),
+    ("far", 2),
     ("attend", 0),
-    ("far", 2),
-    ("near", 1),
+    ("attend", 1),
+    ("near", 2),
     ("gather", 0),
-    ("caches", 2),
-    ("near", 2),
-    ("attend", 1),
+    ("gather", 1),
+    ("attend", 2),
+    ("forward", 1),
     ("forward", 0),
-    ("attend", 2),
-    ("gather", 1),
-    ("out", 2),
+    ("output", 0),
     ("gather", 2),
-    ("output", 0),
-    ("forward", 1),
     ("forward", 2),
-    ("out", 1),
     ("output", 1),
     ("output", 2),
 )
@@ -78,16 +73,13 @@
     return sorted(range(nz), key=lambda q: [(q & b) != 0 for b in strides(nz)])
 
 
-def slot_one_hot(place_ref, slot_of_row, nz, per, absolute=False):
+def slot_one_hot(place_ref, slot_of_row, nz, per):
     rows = slot_of_row.shape[1]
     base = lax.broadcasted_iota(jnp.int32, (per, rows), 0)
     blocks = []
     for h in range(2):
         for q in place_order(nz):
-            if absolute:
-                owner = len(blocks)
-            else:
-                owner = (place_ref[0] ^ q) * 2 + (place_ref[1] ^ h)
+            owner = (place_ref[0] ^ q) * 2 + (place_ref[1] ^ h)
             blocks.append(jnp.where(base + owner * per == slot_of_row, 1.0, 0.0).astype(F32))
     return jnp.concatenate(blocks, axis=0).astype(BF16)
 
@@ -107,7 +99,12 @@
     ]
 
 
-def call(kernel, name, token, scalars, arrays, out_shapes, scratch, vmem_mib, loads=()):
+def call(
+    kernel, name, token, scalars, arrays, out_shapes, scratch, vmem_mib, loads=(), resident=()
+):
+    arrays = list(arrays) + [
+        pltpu.with_memory_space_constraint(array, pltpu.VMEM) for array in resident
+    ]
     sources = [array for array, _ in loads]
     windows = [window for _, window in loads]
     loaded_shapes = [
@@ -154,11 +151,17 @@
     return outs[0], outs[1 : 1 + len(loads)], outs[1 + len(loads) :]
 
 
+def places_of(refs, per):
+    blocks = [(ref, z) for ref in refs for z in range(ref.shape[0])]
+    return [(i * per, ref, z) for i, (ref, z) in enumerate(blocks)]
+
+
 def project_kernel(*refs, nz, per, first, heads):
     place_ref = refs[0]
     if first:
         own_ref, other_ref, gain_ref, sor_ref, wq_ref, wk_ref, wv_ref = refs[1:8]
         *out_refs, slotted_ref, acc = refs[8:]
+        places = places_of(out_refs, per)
         one_hot = slot_one_hot(place_ref, sor_ref[...], nz, per)
         own, other = own_ref[...], other_ref[...]
         lower = place_ref[2] == 0
@@ -174,21 +177,20 @@
         low = squares - high
         lane = lax.broadcasted_iota(jnp.int32, (per, HEAD_SIZE), 1)
         lane_high = place_ref[1] * 2
-        for b, ref in enumerate(out_refs):
-            for z in range(nz):
-                at = (b * nz + z) * per
-                packed = jnp.where(
-                    lane == lane_high,
-                    high[at : at + per],
-                    jnp.where(lane == lane_high + 1, low[at : at + per], 0.0),
-                )
-                packed = jnp.concatenate(
-                    [packed, jnp.zeros((SQUARE_ROWS - per, HEAD_SIZE), F32)], axis=0
-                )
-                ref[z, heads * TILES * per :, :] = packed.astype(BF16)
+        for at, ref, z in places:
+            packed = jnp.where(
+                lane == lane_high,
+                high[at : at + per],
+                jnp.where(lane == lane_high + 1, low[at : at + per], 0.0),
+            )
+            packed = jnp.concatenate(
+                [packed, jnp.zeros((SQUARE_ROWS - per, HEAD_SIZE), F32)], axis=0
+            )
+            ref[z, heads * TILES * per :, :] = packed.astype(BF16)
     else:
         slotted_ref, wq_ref, wk_ref, wv_ref = refs[1:5]
         *out_refs, acc = refs[5:]
+        places = places_of(out_refs, per)
 
     columns = QUERIES_PER_KV * HEAD_SIZE
     slotted = slotted_ref[...]
@@ -202,17 +204,15 @@
             jnp.concatenate([wk_ref[:, narrow], wv_ref[:, narrow]], axis=1),
             preferred_element_type=F32,
         )
-        for b, ref in enumerate(out_refs):
-            for z in range(nz):
-                at = (b * nz + z) * per
-                block = jnp.concatenate(
-                    [
-                        acc[at : at + per, c * HEAD_SIZE : (c + 1) * HEAD_SIZE]
-                        for c in range(TILES)
-                    ],
-                    axis=0,
-                )
-                ref[z, g * TILES * per : (g + 1) * TILES * per, :] = block.astype(BF16)
+        for at, ref, z in places:
+            block = jnp.concatenate(
+                [
+                    acc[at : at + per, c * HEAD_SIZE : (c + 1) * HEAD_SIZE]
+                    for c in range(TILES)
+                ],
+                axis=0,
+            )
+            ref[z, g * TILES * per : (g + 1) * TILES * per, :] = block.astype(BF16)
 
 
 def project(token, place, inputs, weights, loads, *, chunk, heads, nz, per):
@@ -220,7 +220,8 @@
     rows = 2 * nz * per
     depth = weights[0].shape[0]
     block_rows = heads * TILES * per + (SQUARE_ROWS if first else 0)
-    out_shapes = [((nz, block_rows, HEAD_SIZE), BF16)] * 2
+    counts = [nz, nz // 2, nz // 2] if Y_IN_HALVES[chunk] else [nz, nz]
+    out_shapes = [((count, block_rows, HEAD_SIZE), BF16) for count in counts]
     return call(
         functools.partial(project_kernel, nz=nz, per=per, first=first, heads=heads),
         "project" + str(chunk),
@@ -310,6 +311,7 @@
             fresh[pl.ds(g * head_rows + c * per, per), :] = tile.astype(BF16).astype(F32)
 
     positions = k_ref.shape[1]
+    columns = slice(start_head * HEAD_SIZE, (start_head + heads) * HEAD_SIZE)
     qrows = heads * QUERIES_PER_KV
     lanes = group * qrows
     extra = 16
@@ -338,7 +340,7 @@
                 new_key.append(jnp.where(top_row, key, 0.0).astype(BF16))
         keys = jnp.concatenate(
             [
-                jnp.concatenate([k_ref[s] for s in slots], axis=1),
+                jnp.concatenate([k_ref[s, :, columns] for s in slots], axis=1),
                 jnp.concatenate(new_key, axis=1),
             ],
             axis=0,
@@ -359,7 +361,7 @@
             [jnp.where(row_slot == i, cache_weights, 0.0).astype(BF16) for i in range(group)],
             axis=1,
         )
-        values = v_ref[start : start + group].reshape(group * positions, heads * HEAD_SIZE)
+        values = v_ref[start : start + group, :, columns].reshape(group * positions, heads * HEAD_SIZE)
         mixed = jnp.dot(spread, values, preferred_element_type=F32)
         for i, s in enumerate(slots):
             for g in range(heads):
@@ -391,7 +393,7 @@
         "attend" + str(chunk),
         token,
         [place, lengths],
-        list(parts) + ([] if first else [scale]) + list(biases) + [cos, sin, keys, values],
+        list(parts) + ([] if first else [scale]) + list(biases) + [cos, sin],
         [((1, out_rows, HEAD_SIZE), BF16)] + ([((per, HEAD_SIZE), F32)] if first else []),
         [
             pltpu.VMEM((heads * TILES * per, HEAD_SIZE), F32),
@@ -399,61 +401,66 @@
         ],
         8,
         loads,
+        [keys, values],
     )
 
 
-def output_kernel(*refs, labels, nz, per, first, last, absolute):
+def output_kernel(*refs, labels, nz, per, first, last, start_depth):
     count = len(labels)
-    place_ref, block_refs, sor_ref, w_ref = refs[0], refs[1 : 1 + count], refs[1 + count], refs[2 + count]
-    rest = refs[3 + count :]
+    place_ref, block_refs, order_ref = refs[0], refs[1 : 1 + count], refs[1 + count]
+    rest = refs[2 + count :]
     if not first:
         acc_in_ref, rest = rest[0], rest[1:]
+    w_ref, rest = rest[0], rest[1:]
     if last:
         mine_ref, send_ref, stacked = rest
     else:
-        acc_out_ref, stacked = rest
+        acc_out_ref, *rest, stacked = rest
     tiles = block_refs[0].shape[1] // per
-
-    half = sor_ref.shape[1] // 2
-    slot_of_row = sor_ref[...]
-    swapped = jnp.concatenate([slot_of_row[:, half:], slot_of_row[:, :half]], axis=1)
-    slot_of_row = jnp.where(place_ref[2] == 0, slot_of_row, swapped)
-    one_hot = slot_one_hot(place_ref, slot_of_row, nz, per, absolute)
+    depth = tiles * HEAD_SIZE
+
+    if first:
+        slot_of_row = order_ref[...]
+        half = slot_of_row.shape[1] // 2
+        swapped = jnp.concatenate([slot_of_row[:, half:], slot_of_row[:, :half]], axis=1)
+        slot_of_row = jnp.where(place_ref[2] == 0, slot_of_row, swapped)
+        one_hot = slot_one_hot(place_ref, slot_of_row, nz, per).astype(F32).T.astype(BF16)
+        rest[0][...] = one_hot
+    else:
+        one_hot = order_ref[...]
     wide = {
         label: ref[z].astype(F32)
         for ref, own in zip(block_refs, labels)
         for z, label in enumerate(own)
     }
-    if absolute:
-        wide = [wide[owner] for owner in range(2 * nz)]
-    else:
-        wide = [wide[h, q] for h in range(2) for q in place_order(nz)]
+    wide = [wide[h, q] for h in range(2) for q in place_order(nz)]
     for c in range(tiles):
         stacked[:, c * HEAD_SIZE : (c + 1) * HEAD_SIZE] = jnp.concatenate(
             [block[c * per : (c + 1) * per] for block in wide], axis=0
         ).astype(BF16)
-    permuted = lax.dot_general(
-        one_hot, stacked[...], (((0,), (0,)), ((), ())), preferred_element_type=F32
-    ).astype(BF16)
-    stacked[...] = permuted
-    product = jnp.dot(stacked[...], w_ref[...], preferred_element_type=F32)
+    stacked[...] = jnp.dot(one_hot, stacked[...], preferred_element_type=F32).astype(BF16)
+    product = jnp.dot(
+        stacked[...], w_ref[start_depth : start_depth + depth, :], preferred_element_type=F32
+    )
     if not first:
         product = product + acc_in_ref[...]
     if last:
+        half = product.shape[0] // 2
         mine_ref[...] = product[:half]
         send_ref[...] = product[half:].astype(BF16)
     else:
         acc_out_ref[...] = product
 
 
-def output(token, place, blocks, labels, sor, w_out, acc, loads, *, chunk, chunks, nz, per):
+def output(token, place, blocks, labels, order, w_out, acc, loads, *, chunk, chunks, nz, per):
     first, last = chunk == 0, chunk == chunks - 1
     rows = 2 * nz * per
-    depth, width = w_out.shape
+    width = w_out.shape[1]
+    depth = CHUNK_HEADS[chunk] * QUERIES_PER_KV * HEAD_SIZE
     if last:
         out_shapes = [((rows // 2, width), F32), ((rows // 2, width), BF16)]
     else:
-        out_shapes = [((rows, width), F32)]
+        out_shapes = [((rows, width), F32)] + ([((rows, rows), BF16)] if first else [])
     return call(
         functools.partial(
             output_kernel,
@@ -462,16 +469,17 @@
             per=per,
             first=first,
             last=last,
-            absolute=GATHER[chunk] == "all_gather",
+            start_depth=sum(CHUNK_HEADS[:chunk]) * QUERIES_PER_KV * HEAD_SIZE,
         ),
         "output" + str(chunk),
         token,
         [place],
-        [*blocks, sor, w_out] + ([] if first else [acc]),
+        [*blocks, order] + ([] if first else [acc]),
         out_shapes,
         [pltpu.VMEM((rows, depth), BF16)],
         12,
         loads,
+        [w_out],
     )
 
 
@@ -524,6 +532,7 @@
     all_columns = pl.ds(0, w_out.shape[1])
     same_z = neighbour_pairs(nz)
     scale = acc = None
+    order = sor
     inputs = [hidden_rows, other, gain, sor]
     kept, swapped, reduced = {}, {}, {}
     loaded, gathered, waiting = {}, {}, {}
@@ -536,17 +545,10 @@
         return moved, [(h, q ^ stride) for h, q in labels]
 
     def windows_of(kind, c):
-        if kind == "weights":
-            return [
-                (array, (everything, head_window(c, n)))
-                for array, n in (
-                    (w_query, wide), (key_weight, HEAD_SIZE), (value_weight, HEAD_SIZE),
-                )
-            ]
-        if kind == "caches":
-            window = (pl.ds(0, per), pl.ds(0, positions), head_window(c, HEAD_SIZE))
-            return [(rotated_key_cache, window), (stored_value_cache, window)]
-        return [(w_out, (head_window(c, wide), all_columns))]
+        return [
+            (array, (everything, head_window(c, n)))
+            for array, n in ((w_query, wide), (key_weight, HEAD_SIZE), (value_weight, HEAD_SIZE))
+        ]
 
     def file_loaded(wanted, arrays):
         arrays = list(arrays)
@@ -571,20 +573,25 @@
         file_loaded(wanted, arrays)
         kept[c] = outs[0]
         if c == 0:
-            inputs = [outs[2]]
-        swapped[c] = lax.ppermute(outs[1], "gx", same_z)
+            inputs = [outs[-1]]
+        if Y_IN_HALVES[c]:
+            far = lax.ppermute(outs[2], "gx", same_z)
+            swapped[c] = (lax.ppermute(outs[1], "gx", same_z), 0), (far, 0)
+        else:
+            both = lax.ppermute(outs[1], "gx", same_z)
+            swapped[c] = (both, 0), (both, nz // 2)
         return token
 
     def do_far(token, c, wanted):
         half = nz // 2
         token, (total,) = add(
-            "add_far" + str(c), token, [kept[c], swapped[c]], [half, half], half, 1
+            "add_far" + str(c), token, [kept[c], swapped[c][1][0]], [half, swapped[c][1][1]], half, 1
         )
         reduced[c] = lax.ppermute(total, "gx", stride_pairs(nz, 1))
         return token
 
     def do_near(token, c, wanted):
-        terms, starts, count = [kept[c], swapped[c], reduced[c]], [0, 0, 0], nz // 2
+        terms, starts, count = [kept[c], swapped[c][0][0], reduced[c]], [0, 0, 0], nz // 2
         for stride in strides(nz)[1:]:
             token, (mine, sent) = add(
                 "add_near" + str(c) + "_" + str(stride), token, terms, starts, count, 2
@@ -597,24 +604,18 @@
     def do_attend(token, c, wanted):
         nonlocal scale
         token, arrays, outs = attend(
-            token, place, slot_valid_lengths, reduced[c], scale, biases, cos, sin, *loaded["caches", c],
+            token, place, slot_valid_lengths, reduced[c], scale, biases, cos, sin, rotated_key_cache, stored_value_cache,
             loads_of(wanted), chunk=c, heads=CHUNK_HEADS[c],
         )
         file_loaded(wanted, arrays)
         if c == 0:
             scale = outs[1]
-        if GATHER[c] == "all_gather":
-            whole = lax.all_gather(outs[0], "gx", axis=0, tiled=True)
-            gathered[c] = [(whole, list(range(2 * nz)))]
-            return token
         own = outs[0], [(0, 0)]
         first_move = over_y(*own) if GATHER[c] == "y first" else over_z(*own, strides(nz)[-1])
         waiting[c] = own, first_move
         return token
 
     def do_gather(token, c, wanted):
-        if GATHER[c] == "all_gather":
-            return token
         held, moved = waiting[c]
         for stride in reversed(strides(nz) if GATHER[c] == "y first" else strides(nz)[:-1]):
             if GATHER[c] == "y first" and stride == 1:
@@ -629,8 +630,6 @@
         return token
 
     def do_forward(token, c, wanted):
-        if GATHER[c] == "all_gather":
-            return token
         held, moved = waiting[c]
         if GATHER[c] == "y halved":
             gathered[c].append(over_y(*moved))
@@ -641,13 +640,18 @@
         return token
 
     def do_output(token, c, wanted):
-        nonlocal acc
-        token, arrays, acc = output(
-            token, place, [a for a, _ in gathered[c]], [own for _, own in gathered[c]], sor,
-            *loaded["out", c], acc if c == 0 else acc[0], loads_of(wanted),
+        nonlocal acc, order
+        token, arrays, outs = output(
+            token, place, [a for a, _ in gathered[c]], [own for _, own in gathered[c]], order,
+            w_out, acc, loads_of(wanted),
             chunk=c, chunks=chunks, nz=nz, per=per,
         )
         file_loaded(wanted, arrays)
+        acc = outs[0]
+        if c == 0:
+            order = outs[1]
+        if c == chunks - 1:
+            acc = outs
         return token
 
     token = jnp.zeros(TOKEN, F32)

time: 97.3 us -> 70 us (0.72)
  blocking collectives: 31.2 us -> 0 us
  starting transfers between devices: 24.1 us -> 38.1 us
  Pallas kernels: 30.2 us -> 21 us
  waiting for transfers between devices: 10.2 us -> 9.03 us
    all_gather x1 -> x0, blocking collectives: 31.2 us -> none  [do_attend(): whole = lax.all_gather(outs[0], 'gx', axis=0, tiled=True)]
    pallas_call x24 -> x20, Pallas kernels: 30.2 us -> 21 us  [call(): pl.pallas_call(body, in_specs=[vmem] + [pl.BlockSpec(memory_space=pltpu.H...]
    ppermute x4 -> x6, starting transfers between devices: 3.42 us -> 12.5 us  [over_z(): moved = lax.ppermute(blocks, 'gx', stride_pairs(nz, stride))]
    ppermute x3 -> x6, starting transfers between devices: 4.38 us -> 8.91 us  [the longest x3 5 us: do_project(): swapped[c] = ((lax.ppermute(outs[1], 'gx', same_z), 0), (far, 0))]
    ppermute x3, waiting for transfers between devices: 2.1 us -> 0.01 us  [do_far(): reduced[c] = lax.ppermute(total, 'gx', stride_pairs(nz, 1))]
    ppermute x4 -> x6, waiting for transfers between devices: 1.72 us -> 3.28 us  [over_z(): moved = lax.ppermute(blocks, 'gx', stride_pairs(nz, stride))]
    ppermute x3 -> x6, waiting for transfers between devices: 3.82 us -> 2.34 us  [the longest x3 1.28 us: do_project(): swapped[c] = ((lax.ppermute(outs[1], 'gx', same_z), 0), (far, 0))]
    ppermute x4 -> x6, starting transfers between devices: 5.91 us -> 5.76 us  [over_y(): return (lax.ppermute(blocks, 'gx', same_z), [(1 - h, q) for h, q in labels])]
  transfers between devices with their start and end apart: 19 -> 26, of which waited for: 7 -> 9; matrix products, arithmetic and copies ran while one was open for 0% -> 0% of each run, Pallas kernels for 28% -> 26%
where the time goes in v9:
time: 70 us; the launch traced here: 69.5 us
  starting transfers between devices  38.1 us (54%)
  Pallas kernels  21 us (30%)
  waiting for transfers between devices  9.03 us (13%)
  other arithmetic  1.04 us (1%)
    pallas_call x20, Pallas kernels, call(): pl.pallas_call(body, in_specs=[vmem] + [pl.BlockSpec(memory_space=pltpu.H...  21 us
    ppermute x6, starting transfers between devices, over_z(): moved = lax.ppermute(blocks, 'gx', stride_pairs(nz, stride))  12.5 us
    ppermute x6, starting transfers between devices, over_y(): return (lax.ppermute(blocks, 'gx', same_z), [(1 - h, q) for h, q in labels])  5.76 us
    ppermute x3, starting transfers between devices, do_near(): terms = [mine, lax.ppermute(sent, 'gx', stride_pairs(nz, stride))]  5.28 us
    ppermute x3, starting transfers between devices, do_far(): reduced[c] = lax.ppermute(total, 'gx', stride_pairs(nz, 1))  5.17 us
    ppermute x3, starting transfers between devices, do_project(): swapped[c] = ((lax.ppermute(outs[1], 'gx', same_z), 0), (far, 0))  5 us
    ppermute x3, starting transfers between devices, do_project(): far = lax.ppermute(outs[2], 'gx', same_z)  3.91 us
    ppermute x6, waiting for transfers between devices, over_z(): moved = lax.ppermute(blocks, 'gx', stride_pairs(nz, stride))  3.28 us
  transfers between devices with their start and end apart: 26, of which 9 were waited for; matrix products, arithmetic and copies ran while one was open for 0% of the time, Pallas kernels for 26%

profile of v9, /device:TPU:0, one launch (start us, length us, event | category | flops | bytes accessed | tf_op | source)
XLA Modules:
  0.0 69.5 jit_solution(8457730448953320017)
XLA Ops:
  0.0 0.5 collective-permute-start
  0.5 3.3 %load_weights0_weights1.1 = (f32[8,128]{1,0:T(8,128)S(1)}, bf16[1024,1024]{1,0:T(8,128)(2,1)S(1)}, bf16[1024,128]{1,0:T(8,128)(2,1)S(1)}, bf16[1024,128]{1,0:T(8...) custom-call(f32[8,128]{1,0:T(8,128)S(1)} %broadcast_in_dim.17.refs_0_, ...), custom_call_target="tpu_custom_call" | custom-call | tf_op jit(solution)/shard_map/load_weights0_weights1/pallas_call | solution.py:131
  3.8 0.1 pad_add_fusion.refs_1_
  3.9 1.4 %project0.1 = (f32[8,128]{1,0:T(8,128)S(1)}, bf16[4,272,128]{2,1,0:T(8,128)(2,1)S(1)}, bf16[2,272,128]{2,1,0:T(8,128)(2,1)S(1)}, bf16[2,272,128]{2,1,0:T(8,128)(2,1)S(1)}, bf16[192,1024]{1,0:T(8,128)(2,1)S(1)}) custom-call(f32[8,128]{1,0:T(8,128)S(1)} %get-tuple-element.64.refs_0_, s32[3]{0:T(128)S(1)} %pad_add_fusion.refs_1_, bf16[96,1024]{1,0:T(8,128)(2,1)S(1)} %copy-done, ...), custom_call_target="tpu_custom_call" | custom-call | flops 1407270016 | tf_op jit(solution)/shard_map/project0/pallas_call | solution.py:131
  5.3 2.6 %collective-permute-start.1 = (bf16[2,272,128]{2,1,0:T(8,128)(2,1)S(1)}, bf16[2,272,128]{2,1,0:T(8,128)(2,1)S(1)}, u32[]{:S(2)}, u32[]{:S(2)}) collective-permute-start(bf16[2,272,128]{2,1,0:T(8,128)(2,1)S(1)} %get-tuple-element.75), channel_id=1, source_target_pairs={{0,2},{2,0},{4,6},{6,4},{8,10},{10,8},{12,14},{14,12},{1,3},{3,1},... | collective-permute-start | bytes 417800 | tf_op jit(solution)/shard_map/ppermute | solution.py:578
  8.0 1.8 %project1.1 = (f32[8,128]{1,0:T(8,128)S(1)}, bf16[4,480,128]{2,1,0:T(8,128)(2,1)S(1)}, bf16[2,480,128]{2,1,0:T(8,128)(2,1)S(1)}, bf16[2,480,128]{2,1,0:T(8,128)(2,1)S(1)}) custom-call(f32[8,128]{1,0:T(8,128)S(1)} %get-tuple-element.68.refs_0_, s32[3]{0:T(128)S(1)} %pad_add_fusion.refs_1_, bf16[192,1024]{1,0:T(8,128)(2,1)S(1)} %get-tuple-element.69.refs_2_, ...), custom_call_target="tpu_custom_call" | custom-call | flops 2076300032 | tf_op jit(solution)/shard_map/project1/pallas_call | solution.py:131
  9.8 0.1 collective-permute-start.2
  9.8 2.0 %collective-permute-start.3 = (bf16[2,272,128]{2,1,0:T(8,128)(2,1)S(1)}, bf16[2,272,128]{2,1,0:T(8,128)(2,1)S(1)}, u32[]{:S(2)}, u32[]{:S(2)}) collective-permute-start(bf16[2,272,128]{2,1,0:T(8,128)(2,1)S(1)} %get-tuple-element.81), channel_id=1, source_target_pairs={{0,2},{2,0},{4,6},{6,4},{8,10},{10,8},{12,14},{14,12},{1,3},{3,1},... | collective-permute-start | bytes 417800 | tf_op jit(solution)/shard_map/ppermute | solution.py:579
  11.8 0.4 collective-permute-done.1.refs_2_
  12.3 1.9 %collective-permute-start.4 = (bf16[2,272,128]{2,1,0:T(8,128)(2,1)S(1)}, bf16[2,272,128]{2,1,0:T(8,128)(2,1)S(1)}, u32[]{:S(2)}, u32[]{:S(2)}) collective-permute-start(bf16[2,272,128]{2,1,0:T(8,128)(2,1)S(1)} %get-tuple-element.82), channel_id=1, source_target_pairs={{0,4},{2,6},{4,0},{6,2},{8,12},{10,14},{12,8},{14,10},{1,5},{3,7},... | collective-permute-start | bytes 417800 | tf_op jit(solution)/shard_map/ppermute | solution.py:590
  14.3 2.0 %collective-permute-start.5 = (bf16[2,480,128]{2,1,0:T(8,128)(2,1)S(1)}, bf16[2,480,128]{2,1,0:T(8,128)(2,1)S(1)}, u32[]{:S(2)}, u32[]{:S(2)}) collective-permute-start(bf16[2,480,128]{2,1,0:T(8,128)(2,1)S(1)} %get-tuple-element.88), channel_id=1, source_target_pairs={{0,2},{2,0},{4,6},{6,4},{8,10},{10,8},{12,14},{14,12},{1,3},{3,1},... | collective-permute-start | bytes 737288 | tf_op jit(solution)/shard_map/ppermute | solution.py:579
  16.3 1.7 %load_weights2.1 = (f32[8,128]{1,0:T(8,128)S(1)}, bf16[1024,1024]{1,0:T(8,128)(2,1)S(1)}, bf16[1024,128]{1,0:T(8,128)(2,1)S(1)}, bf16[1024,128]{1,0:T(8,128)(2,1)S(1)}) custom-call(f32[8,128]{1,0:T(8,128)S(1)} %get-tuple-element.76.refs_0_, bf16[1024,4096]{1,0:T(8,128)(2,1)} %refs_1_.3, bf16[1024,512]{1,0:T(8,128)(2,1)} %refs_2_.8, bf16[1024,512]{1,0:T(8,128)(2,1)} %refs_3_.3), custom_call_target="tpu_custom_call" | custom-call | tf_op jit(solution)/shard_map/load_weights2/pallas_call | solution.py:131
  18.0 0.7 collective-permute-done.2.refs_2_
  18.7 1.6 %collective-permute-start.6 = (bf16[2,480,128]{2,1,0:T(8,128)(2,1)S(1)}, bf16[2,480,128]{2,1,0:T(8,128)(2,1)S(1)}, u32[]{:S(2)}, u32[]{:S(2)}) collective-permute-start(bf16[2,480,128]{2,1,0:T(8,128)(2,1)S(1)} %get-tuple-element.89), channel_id=1, source_target_pairs={{0,4},{2,6},{4,0},{6,2},{8,12},{10,14},{12,8},{14,10},{1,5},{3,7},... | collective-permute-start | bytes 737288 | tf_op jit(solution)/shard_map/ppermute | solution.py:590
  20.3 1.3 %collective-permute-done.3.refs_2_ = bf16[2,272,128]{2,1,0:T(8,128)(2,1)S(1)} collective-permute-done((bf16[2,272,128]{2,1,0:T(8,128)(2,1)S(1)}, bf16[2,272,128]{2,1,0:T(8,128)(2,1)S(1)}, u32[]{:S(2)}, u32[]{:S(2)}) %collective-permute-start.3) | collective-permute-done | bytes 139296 | tf_op jit(solution)/shard_map/ppermute | solution.py:579
  21.7 1.2 %project2.1 = (f32[8,128]{1,0:T(8,128)S(1)}, bf16[4,240,128]{2,1,0:T(8,128)(2,1)S(1)}, bf16[2,240,128]{2,1,0:T(8,128)(2,1)S(1)}, bf16[2,240,128]{2,1,0:T(8,128)(2,1)S(1)}) custom-call(f32[8,128]{1,0:T(8,128)S(1)} %get-tuple-element.83.refs_0_, s32[3]{0:T(128)S(1)} %pad_add_fusion.refs_1_, bf16[192,1024]{1,0:T(8,128)(2,1)S(1)} %get-tuple-element.69.refs_2_, ...), custom_call_target="tpu_custom_call" | custom-call | flops 1407270016 | tf_op jit(solution)/shard_map/project2/pallas_call | solution.py:131
  23.0 1.2 %collective-permute-start.7 = (bf16[2,240,128]{2,1,0:T(8,128)(2,1)S(1)}, bf16[2,240,128]{2,1,0:T(8,128)(2,1)S(1)}, u32[]{:S(2)}, u32[]{:S(2)}) collective-permute-start(bf16[2,240,128]{2,1,0:T(8,128)(2,1)S(1)} %get-tuple-element.92), channel_id=1, source_target_pairs={{0,2},{2,0},{4,6},{6,4},{8,10},{10,8},{12,14},{14,12},{1,3},{3,1},... | collective-permute-start | bytes 368648 | tf_op jit(solution)/shard_map/ppermute | solution.py:578
  24.1 2.6 %collective-permute-start.8 = (bf16[1,272,128]{2,1,0:T(8,128)(2,1)S(1)}, bf16[1,272,128]{2,1,0:T(8,128)(2,1)S(1)}, u32[]{:S(2)}, u32[]{:S(2)}) collective-permute-start(bf16[1,272,128]{2,1,0:T(8,128)(2,1)S(1)} %get-tuple-element.95), channel_id=1, source_target_pairs={{0,8},{2,10},{4,12},{6,14},{8,0},{10,2},{12,4},{14,6},{1,9},{3,11}... | collective-permute-start | bytes 208904 | tf_op jit(solution)/shard_map/ppermute | solution.py:599
  26.7 0.1 fusion
  26.9 1.0 %collective-permute-start.10 = (bf16[2,240,128]{2,1,0:T(8,128)(2,1)S(1)}, bf16[2,240,128]{2,1,0:T(8,128)(2,1)S(1)}, u32[]{:S(2)}, u32[]{:S(2)}) collective-permute-start(bf16[2,240,128]{2,1,0:T(8,128)(2,1)S(1)} %get-tuple-element.101), channel_id=1, source_target_pairs={{0,2},{2,0},{4,6},{6,4},{8,10},{10,8},{12,14},{14,12},{1,3},{3,1},... | collective-permute-start | bytes 368648 | tf_op jit(solution)/shard_map/ppermute | solution.py:579
  27.9 0.1 add_near1_2.1
  28.0 1.7 %collective-permute-start.9 = (bf16[1,480,128]{2,1,0:T(8,128)(2,1)S(1)}, bf16[1,480,128]{2,1,0:T(8,128)(2,1)S(1)}, u32[]{:S(2)}, u32[]{:S(2)}) collective-permute-start(bf16[1,480,128]{2,1,0:T(8,128)(2,1)S(1)} %get-tuple-element.98), channel_id=1, source_target_pairs={{0,8},{2,10},{4,12},{6,14},{8,0},{10,2},{12,4},{14,6},{1,9},{3,11}... | collective-permute-start | bytes 368648 | tf_op jit(solution)/shard_map/ppermute | solution.py:599
  29.7 1.7 %collective-permute-start.11 = (bf16[2,240,128]{2,1,0:T(8,128)(2,1)S(1)}, bf16[2,240,128]{2,1,0:T(8,128)(2,1)S(1)}, u32[]{:S(2)}, u32[]{:S(2)}) collective-permute-start(bf16[2,240,128]{2,1,0:T(8,128)(2,1)S(1)} %get-tuple-element.102), channel_id=1, source_target_pairs={{0,4},{2,6},{4,0},{6,2},{8,12},{10,14},{12,8},{14,10},{1,5},{3,7},... | collective-permute-start | bytes 368648 | tf_op jit(solution)/shard_map/ppermute | solution.py:590
  31.4 2.0 %attend0.1 = (f32[8,128]{1,0:T(8,128)S(1)}, bf16[1,192,128]{2,1,0:T(8,128)(2,1)S(1)}, f32[24,128]{1,0:T(8,128)S(1)}) custom-call(f32[8,128]{1,0:T(8,128)S(1)} %get-tuple-element.93.refs_0_, s32[3]{0:T(128)S(1)} %pad_add_fusion.refs_1_, s32[192]{0:T(256)S(1)} %copy-done.6, bf16[1,272,128]{2,1,0:T(8,128)(2,1)S(1)} %get-tuple-element.94.refs_3_, ...), custom_call_target="tpu_custom_call" | custom-call | flops 2191650048 | tf_op jit(solution)/shard_map/attend0/pallas_call | solution.py:131
  33.4 2.5 %collective-permute-start.12 = (bf16[1,192,128]{2,1,0:T(8,128)(2,1)S(1)}, bf16[1,192,128]{2,1,0:T(8,128)(2,1)S(1)}, u32[]{:S(2)}, u32[]{:S(2)}) collective-permute-start(bf16[1,192,128]{2,1,0:T(8,128)(2,1)S(1)} %get-tuple-element.104.refs_1_), channel_id=1, source_target_pairs={{0,8},{2,10},{4,12},{6,14},{8,0},{10,2},{12,4},{14,6},{1,9},{3,11}... | collective-permute-start | bytes 147464 | tf_op jit(solution)/shard_map/ppermute | solution.py:544
  35.9 2.4 %attend1.1 = (f32[8,128]{1,0:T(8,128)S(1)}, bf16[1,384,128]{2,1,0:T(8,128)(2,1)S(1)}) custom-call(f32[8,128]{1,0:T(8,128)S(1)} %get-tuple-element.96.refs_0_, s32[3]{0:T(128)S(1)} %pad_add_fusion.refs_1_, s32[192]{0:T(256)S(1)} %copy-done.6, bf16[1,480,128]{2,1,0:T(8,128)(2,1)S(1)} %get-tuple-element.97.refs_3_, ...), custom_call_target="tpu_custom_call" | custom-call | flops 2710725120 | tf_op jit(solution)/shard_map/attend1/pallas_call | solution.py:131
  38.3 0.5 collective-permute-start.13
  38.9 4.3 %collective-permute-start.15 = (bf16[2,192,128]{2,1,0:T(8,128)(2,1)S(1)}, bf16[2,192,128]{2,1,0:T(8,128)(2,1)S(1)}, u32[]{:S(2)}, u32[]{:S(2)}) collective-permute-start(bf16[2,192,128]{2,1,0:T(8,128)(2,1)S(1)} %get-tuple-element.111.refs_2_), channel_id=1, source_target_pairs={{0,4},{2,6},{4,0},{6,2},{8,12},{10,14},{12,8},{14,10},{1,5},{3,7},... | collective-permute-start | bytes 294920 | tf_op jit(solution)/shard_map/ppermute | solution.py:544
  43.3 1.0 %collective-permute-start.14 = (bf16[1,240,128]{2,1,0:T(8,128)(2,1)S(1)}, bf16[1,240,128]{2,1,0:T(8,128)(2,1)S(1)}, u32[]{:S(2)}, u32[]{:S(2)}) collective-permute-start(bf16[1,240,128]{2,1,0:T(8,128)(2,1)S(1)} %get-tuple-element.109), channel_id=1, source_target_pairs={{0,8},{2,10},{4,12},{6,14},{8,0},{10,2},{12,4},{14,6},{1,9},{3,11}... | collective-permute-start | bytes 184328 | tf_op jit(solution)/shard_map/ppermute | solution.py:599
  44.3 0.8 %collective-permute-start.16 = (bf16[2,192,128]{2,1,0:T(8,128)(2,1)S(1)}, bf16[2,192,128]{2,1,0:T(8,128)(2,1)S(1)}, u32[]{:S(2)}, u32[]{:S(2)}) collective-permute-start(bf16[2,192,128]{2,1,0:T(8,128)(2,1)S(1)} %get-tuple-element.111.refs_2_), channel_id=1, source_target_pairs={{0,2},{2,0},{4,6},{6,4},{8,10},{10,8},{12,14},{14,12},{1,3},{3,1},... | collective-permute-start | bytes 294920 | tf_op jit(solution)/shard_map/ppermute | solution.py:541
  45.1 1.7 %collective-permute-start.19 = (bf16[2,384,128]{2,1,0:T(8,128)(2,1)S(1)}, bf16[2,384,128]{2,1,0:T(8,128)(2,1)S(1)}, u32[]{:S(2)}, u32[]{:S(2)}) collective-permute-start(bf16[2,384,128]{2,1,0:T(8,128)(2,1)S(1)} %get-tuple-element.115.refs_2_), channel_id=1, source_target_pairs={{0,4},{2,6},{4,0},{6,2},{8,12},{10,14},{12,8},{14,10},{1,5},{3,7},... | collective-permute-start | bytes 589832 | tf_op jit(solution)/shard_map/ppermute | solution.py:544
  46.8 0.7 collective-permute-start.20
  47.5 1.3 %collective-permute-start.17 = (bf16[2,192,128]{2,1,0:T(8,128)(2,1)S(1)}, bf16[2,192,128]{2,1,0:T(8,128)(2,1)S(1)}, u32[]{:S(2)}, u32[]{:S(2)}) collective-permute-start(bf16[2,192,128]{2,1,0:T(8,128)(2,1)S(1)} %collective-permute-done.15.refs_3_), channel_id=1, source_target_pairs={{0,2},{2,0},{4,6},{6,4},{8,10},{10,8},{12,14},{14,12},{1,3},{3,1},... | collective-permute-start | bytes 294920 | tf_op jit(solution)/shard_map/ppermute | solution.py:541
  48.8 0.1 collective-permute-done.14.refs_4_
  48.9 1.9 %attend2.1 = (f32[8,128]{1,0:T(8,128)S(1)}, bf16[1,192,128]{2,1,0:T(8,128)(2,1)S(1)}) custom-call(f32[8,128]{1,0:T(8,128)S(1)} %get-tuple-element.107.refs_0_, s32[3]{0:T(128)S(1)} %pad_add_fusion.refs_1_, s32[192]{0:T(256)S(1)} %copy-done.6, bf16[1,240,128]{2,1,0:T(8,128)(2,1)S(1)} %get-tuple-element.108.refs_3_, ...), custom_call_target="tpu_custom_call" | custom-call | flops 2191650048 | tf_op jit(solution)/shard_map/attend2/pallas_call | solution.py:131
  50.8 2.6 %collective-permute-start.18 = (bf16[1,192,128]{2,1,0:T(8,128)(2,1)S(1)}, bf16[1,192,128]{2,1,0:T(8,128)(2,1)S(1)}, u32[]{:S(2)}, u32[]{:S(2)}) collective-permute-start(bf16[1,192,128]{2,1,0:T(8,128)(2,1)S(1)} %get-tuple-element.113.refs_1_), channel_id=1, source_target_pairs={{0,8},{2,10},{4,12},{6,14},{8,0},{10,2},{12,4},{14,6},{1,9},{3,11}... | collective-permute-start | bytes 147464 | tf_op jit(solution)/shard_map/ppermute | solution.py:544
  53.4 1.2 %collective-permute-start.21 = (bf16[2,384,128]{2,1,0:T(8,128)(2,1)S(1)}, bf16[2,384,128]{2,1,0:T(8,128)(2,1)S(1)}, u32[]{:S(2)}, u32[]{:S(2)}) collective-permute-start(bf16[2,384,128]{2,1,0:T(8,128)(2,1)S(1)} %collective-permute-done.19.refs_3_), channel_id=1, source_target_pairs={{0,2},{2,0},{4,6},{6,4},{8,10},{10,8},{12,14},{14,12},{1,3},{3,1},... | collective-permute-start | bytes 589832 | tf_op jit(solution)/shard_map/ppermute | solution.py:541
  54.7 1.4 %output0.1 = (f32[8,128]{1,0:T(8,128)S(1)}, f32[192,1024]{1,0:T(8,128)S(1)}, bf16[192,192]{1,0:T(8,128)(2,1)S(1)}) custom-call(f32[8,128]{1,0:T(8,128)S(1)} %get-tuple-element.110.refs_0_, s32[3]{0:T(128)S(1)} %pad_add_fusion.refs_1_, bf16[2,192,128]{2,1,0:T(8,128)(2,1)S(1)} %get-tuple-element.111.refs_2_, ...), custom_call_target="tpu_custom_call" | custom-call | flops 1614899968 | tf_op jit(solution)/shard_map/output0/pallas_call | solution.py:131
  56.0 0.2 collective-permute-done.18.refs_2_
  56.2 0.8 %collective-permute-start.22 = (bf16[2,192,128]{2,1,0:T(8,128)(2,1)S(1)}, bf16[2,192,128]{2,1,0:T(8,128)(2,1)S(1)}, u32[]{:S(2)}, u32[]{:S(2)}) collective-permute-start(bf16[2,192,128]{2,1,0:T(8,128)(2,1)S(1)} %get-tuple-element.119.refs_2_), channel_id=1, source_target_pairs={{0,4},{2,6},{4,0},{6,2},{8,12},{10,14},{12,8},{14,10},{1,5},{3,7},... | collective-permute-start | bytes 294920 | tf_op jit(solution)/shard_map/ppermute | solution.py:544
  57.0 0.8 %collective-permute-start.23 = (bf16[2,192,128]{2,1,0:T(8,128)(2,1)S(1)}, bf16[2,192,128]{2,1,0:T(8,128)(2,1)S(1)}, u32[]{:S(2)}, u32[]{:S(2)}) collective-permute-start(bf16[2,192,128]{2,1,0:T(8,128)(2,1)S(1)} %get-tuple-element.119.refs_2_), channel_id=1, source_target_pairs={{0,2},{2,0},{4,6},{6,4},{8,10},{10,8},{12,14},{14,12},{1,3},{3,1},... | collective-permute-start | bytes 294920 | tf_op jit(solution)/shard_map/ppermute | solution.py:541
  57.9 3.0 %collective-permute-done.22.refs_3_ = bf16[2,192,128]{2,1,0:T(8,128)(2,1)S(1)} collective-permute-done((bf16[2,192,128]{2,1,0:T(8,128)(2,1)S(1)}, bf16[2,192,128]{2,1,0:T(8,128)(2,1)S(1)}, u32[]{:S(2)}, u32[]{:S(2)}) %collective-permute-start.22) | collective-permute-done | bytes 98336 | tf_op jit(solution)/shard_map/ppermute | solution.py:544
  60.9 0.9 %collective-permute-start.24 = (bf16[2,192,128]{2,1,0:T(8,128)(2,1)S(1)}, bf16[2,192,128]{2,1,0:T(8,128)(2,1)S(1)}, u32[]{:S(2)}, u32[]{:S(2)}) collective-permute-start(bf16[2,192,128]{2,1,0:T(8,128)(2,1)S(1)} %collective-permute-done.22.refs_3_), channel_id=1, source_target_pairs={{0,2},{2,0},{4,6},{6,4},{8,10},{10,8},{12,14},{14,12},{1,3},{3,1},... | collective-permute-start | bytes 294920 | tf_op jit(solution)/shard_map/ppermute | solution.py:541
  61.8 1.8 %output1.1 = (f32[8,128]{1,0:T(8,128)S(1)}, f32[192,1024]{1,0:T(8,128)S(1)}) custom-call(f32[8,128]{1,0:T(8,128)S(1)} %get-tuple-element.114.refs_0_, s32[3]{0:T(128)S(1)} %pad_add_fusion.refs_1_, bf16[2,384,128]{2,1,0:T(8,128)(2,1)S(1)} %get-tuple-element.115.refs_2_, bf16[2,384,128]{2,1,0:T(8,128)(2,1)S(1)} %collective-permute-done.19.refs_3_, ...), custom_call_target="tpu_custom_call" | custom-call | flops 2307000064 | tf_op jit(solution)/shard_map/output1/pallas_call | solution.py:131
  63.7 1.8 %collective-permute-done.24.refs_5_ = bf16[2,192,128]{2,1,0:T(8,128)(2,1)S(1)} collective-permute-done((bf16[2,192,128]{2,1,0:T(8,128)(2,1)S(1)}, bf16[2,192,128]{2,1,0:T(8,128)(2,1)S(1)}, u32[]{:S(2)}, u32[]{:S(2)}) %collective-permute-start.24) | collective-permute-done | bytes 98336 | tf_op jit(solution)/shard_map/ppermute | solution.py:541
  65.5 1.7 %output2.1 = (f32[8,128]{1,0:T(8,128)}, f32[96,1024]{1,0:T(8,128)S(1)}, bf16[96,1024]{1,0:T(8,128)(2,1)S(1)}) custom-call(f32[8,128]{1,0:T(8,128)S(1)} %get-tuple-element.118.refs_0_, s32[3]{0:T(128)S(1)} %pad_add_fusion.refs_1_, bf16[2,192,128]{2,1,0:T(8,128)(2,1)S(1)} %get-tuple-element.119.refs_2_, ...), custom_call_target="tpu_custom_call" | custom-call | flops 4614000128 | tf_op jit(solution)/shard_map/output2/pallas_call | solution.py:131
  67.3 1.4 %collective-permute-done.25 = bf16[96,1024]{1,0:T(8,128)(2,1)S(1)} collective-permute-done((bf16[96,1024]{1,0:T(8,128)(2,1)S(1)}, bf16[96,1024]{1,0:T(8,128)(2,1)S(1)}, u32[]{:S(2)}, u32[]{:S(2)}) %collective-permute-start.25) | collective-permute-done | bytes 196640 | tf_op jit(solution)/shard_map/ppermute | solution.py:680
  68.7 0.8 %add_convert_fusion = bf16[96,1024]{1,0:T(8,128)(2,1)} fusion(bf16[96,1024]{1,0:T(8,128)(2,1)S(1)} %collective-permute-done.25, f32[96,1024]{1,0:T(8,128)S(1)} %get-tuple-element.121, bf16[96,1024]{1,0:T(8,128)(2,1)S(1)} %copy-done), kind=kLoop, calls=%fused_computation | loop fusion | flops 491520 | bytes 983040 | tf_op jit(solution)/shard_map/convert_element_type | solution.py:681
  (53 shorter events, 0.5 us)
Async XLA Ops:
  0.0 3.9 %collective-permute-start = (bf16[96,1024]{1,0:T(8,128)(2,1)}, bf16[96,1024]{1,0:T(8,128)(2,1)S(1)}, u32[]{:S(2)}, u32[]{:S(2)}) collective-permute-start(bf16[96,1024]{1,0:T(8,128)(2,1)} %refs_2_.7), channel_id=1, source_target_pairs={{0,1},{1,0},{2,3},{3,2},{4,5},{5,4},{6,7},{7,6},{8,9},{9,8},{10,11... | collective-permute-start | bytes 589832 | tf_op jit(solution)/shard_map/ppermute | solution.py:513
  0.5 3.4 %copy-start = (bf16[96,1024]{1,0:T(8,128)(2,1)S(1)}, bf16[96,1024]{1,0:T(8,128)(2,1)}, u32[]{:S(2)}) copy-start(bf16[96,1024]{1,0:T(8,128)(2,1)} %refs_2_.7) | copy-start | bytes 589828
  0.5 3.4 %copy-start.1 = (s32[192]{0:T(256)S(1)}, s32[192]{0:T(256)}, u32[]{:S(2)}) copy-start(s32[192]{0:T(256)} %param.24) | copy-start | bytes 2308
  0.5 3.4 %copy-start.5 = (bf16[1024]{0:T(1024)(128)(2,1)S(1)}, bf16[1024]{0:T(1024)(128)(2,1)}, u32[]{:S(2)}) copy-start(bf16[1024]{0:T(1024)(128)(2,1)} %param.14) | copy-start | bytes 6148
  5.3 6.9 %collective-permute-start.1 = (bf16[2,272,128]{2,1,0:T(8,128)(2,1)S(1)}, bf16[2,272,128]{2,1,0:T(8,128)(2,1)S(1)}, u32[]{:S(2)}, u32[]{:S(2)}) collective-permute-start(bf16[2,272,128]{2,1,0:T(8,128)(2,1)S(1)} %get-tuple-element.75), channel_id=1, source_target_pairs={{0,2},{2,0},{4,6},{6,4},{8,10},{10,8},{12,14},{14,12},{1,3},{3,1},... | collective-permute-start | bytes 417800 | tf_op jit(solution)/shard_map/ppermute | solution.py:578
  8.0 6.2 %copy-start.6 = (s32[192]{0:T(256)S(1)}, s32[192]{0:T(256)}, u32[]{:S(2)}) copy-start(s32[192]{0:T(256)} %refs_2_.11) | copy-start | bytes 2308
  9.8 8.9 %collective-permute-start.2 = (bf16[2,480,128]{2,1,0:T(8,128)(2,1)S(1)}, bf16[2,480,128]{2,1,0:T(8,128)(2,1)S(1)}, u32[]{:S(2)}, u32[]{:S(2)}) collective-permute-start(bf16[2,480,128]{2,1,0:T(8,128)(2,1)S(1)} %get-tuple-element.79), channel_id=1, source_target_pairs={{0,2},{2,0},{4,6},{6,4},{8,10},{10,8},{12,14},{14,12},{1,3},{3,1},... | collective-permute-start | bytes 737288 | tf_op jit(solution)/shard_map/ppermute | solution.py:578
  9.8 11.8 %collective-permute-start.3 = (bf16[2,272,128]{2,1,0:T(8,128)(2,1)S(1)}, bf16[2,272,128]{2,1,0:T(8,128)(2,1)S(1)}, u32[]{:S(2)}, u32[]{:S(2)}) collective-permute-start(bf16[2,272,128]{2,1,0:T(8,128)(2,1)S(1)} %get-tuple-element.81), channel_id=1, source_target_pairs={{0,2},{2,0},{4,6},{6,4},{8,10},{10,8},{12,14},{14,12},{1,3},{3,1},... | collective-permute-start | bytes 417800 | tf_op jit(solution)/shard_map/ppermute | solution.py:579
  12.3 9.3 %collective-permute-start.4 = (bf16[2,272,128]{2,1,0:T(8,128)(2,1)S(1)}, bf16[2,272,128]{2,1,0:T(8,128)(2,1)S(1)}, u32[]{:S(2)}, u32[]{:S(2)}) collective-permute-start(bf16[2,272,128]{2,1,0:T(8,128)(2,1)S(1)} %get-tuple-element.82), channel_id=1, source_target_pairs={{0,4},{2,6},{4,0},{6,2},{8,12},{10,14},{12,8},{14,10},{1,5},{3,7},... | collective-permute-start | bytes 417800 | tf_op jit(solution)/shard_map/ppermute | solution.py:590
  14.3 13.6 %collective-permute-start.5 = (bf16[2,480,128]{2,1,0:T(8,128)(2,1)S(1)}, bf16[2,480,128]{2,1,0:T(8,128)(2,1)S(1)}, u32[]{:S(2)}, u32[]{:S(2)}) collective-permute-start(bf16[2,480,128]{2,1,0:T(8,128)(2,1)S(1)} %get-tuple-element.88), channel_id=1, source_target_pairs={{0,2},{2,0},{4,6},{6,4},{8,10},{10,8},{12,14},{14,12},{1,3},{3,1},... | collective-permute-start | bytes 737288 | tf_op jit(solution)/shard_map/ppermute | solution.py:579
  18.7 9.2 %collective-permute-start.6 = (bf16[2,480,128]{2,1,0:T(8,128)(2,1)S(1)}, bf16[2,480,128]{2,1,0:T(8,128)(2,1)S(1)}, u32[]{:S(2)}, u32[]{:S(2)}) collective-permute-start(bf16[2,480,128]{2,1,0:T(8,128)(2,1)S(1)} %get-tuple-element.89), channel_id=1, source_target_pairs={{0,4},{2,6},{4,0},{6,2},{8,12},{10,14},{12,8},{14,10},{1,5},{3,7},... | collective-permute-start | bytes 737288 | tf_op jit(solution)/shard_map/ppermute | solution.py:590
  21.7 9.7 %copy-start.2 = (bf16[24,128,512]{2,1,0:T(8,128)(2,1)S(1)}, bf16[24,128,512]{2,1,0:T(8,128)(2,1)}, u32[]{:S(2)}) copy-start(bf16[24,128,512]{2,1,0:T(8,128)(2,1)} %refs_11_.5) | copy-start | bytes 9437188
  21.7 9.7 %copy-start.3 = (bf16[24,128,512]{2,1,0:T(8,128)(2,1)S(1)}, bf16[24,128,512]{2,1,0:T(8,128)(2,1)}, u32[]{:S(2)}) copy-start(bf16[24,128,512]{2,1,0:T(8,128)(2,1)} %refs_12_.3) | copy-start | bytes 9437188
  21.7 9.7 %copy-start.4 = (bf16[4096]{0:T(1024)(128)(2,1)S(1)}, bf16[4096]{0:T(1024)(128)(2,1)}, u32[]{:S(2)}) copy-start(bf16[4096]{0:T(1024)(128)(2,1)} %param.18) | copy-start | bytes 24580
  21.7 9.7 %copy-start.7 = (bf16[512]{0:T(512)(128)(2,1)S(1)}, bf16[512]{0:T(512)(128)(2,1)}, u32[]{:S(2)}) copy-start(bf16[512]{0:T(512)(128)(2,1)} %param.19) | copy-start | bytes 3076
  21.7 9.7 %copy-start.8 = (bf16[512]{0:T(512)(128)(2,1)S(1)}, bf16[512]{0:T(512)(128)(2,1)}, u32[]{:S(2)}) copy-start(bf16[512]{0:T(512)(128)(2,1)} %param.20) | copy-start | bytes 3076
  23.0 6.7 %collective-permute-start.7 = (bf16[2,240,128]{2,1,0:T(8,128)(2,1)S(1)}, bf16[2,240,128]{2,1,0:T(8,128)(2,1)S(1)}, u32[]{:S(2)}, u32[]{:S(2)}) collective-permute-start(bf16[2,240,128]{2,1,0:T(8,128)(2,1)S(1)} %get-tuple-element.92), channel_id=1, source_target_pairs={{0,2},{2,0},{4,6},{6,4},{8,10},{10,8},{12,14},{14,12},{1,3},{3,1},... | collective-permute-start | bytes 368648 | tf_op jit(solution)/shard_map/ppermute | solution.py:578
  24.1 7.2 %collective-permute-start.8 = (bf16[1,272,128]{2,1,0:T(8,128)(2,1)S(1)}, bf16[1,272,128]{2,1,0:T(8,128)(2,1)S(1)}, u32[]{:S(2)}, u32[]{:S(2)}) collective-permute-start(bf16[1,272,128]{2,1,0:T(8,128)(2,1)S(1)} %get-tuple-element.95), channel_id=1, source_target_pairs={{0,8},{2,10},{4,12},{6,14},{8,0},{10,2},{12,4},{14,6},{1,9},{3,11}... | collective-permute-start | bytes 208904 | tf_op jit(solution)/shard_map/ppermute | solution.py:599
  26.9 12.0 %collective-permute-start.10 = (bf16[2,240,128]{2,1,0:T(8,128)(2,1)S(1)}, bf16[2,240,128]{2,1,0:T(8,128)(2,1)S(1)}, u32[]{:S(2)}, u32[]{:S(2)}) collective-permute-start(bf16[2,240,128]{2,1,0:T(8,128)(2,1)S(1)} %get-tuple-element.101), channel_id=1, source_target_pairs={{0,2},{2,0},{4,6},{6,4},{8,10},{10,8},{12,14},{14,12},{1,3},{3,1},... | collective-permute-start | bytes 368648 | tf_op jit(solution)/shard_map/ppermute | solution.py:579
  28.0 7.9 %collective-permute-start.9 = (bf16[1,480,128]{2,1,0:T(8,128)(2,1)S(1)}, bf16[1,480,128]{2,1,0:T(8,128)(2,1)S(1)}, u32[]{:S(2)}, u32[]{:S(2)}) collective-permute-start(bf16[1,480,128]{2,1,0:T(8,128)(2,1)S(1)} %get-tuple-element.98), channel_id=1, source_target_pairs={{0,8},{2,10},{4,12},{6,14},{8,0},{10,2},{12,4},{14,6},{1,9},{3,11}... | collective-permute-start | bytes 368648 | tf_op jit(solution)/shard_map/ppermute | solution.py:599
  29.7 9.2 %collective-permute-start.11 = (bf16[2,240,128]{2,1,0:T(8,128)(2,1)S(1)}, bf16[2,240,128]{2,1,0:T(8,128)(2,1)S(1)}, u32[]{:S(2)}, u32[]{:S(2)}) collective-permute-start(bf16[2,240,128]{2,1,0:T(8,128)(2,1)S(1)} %get-tuple-element.102), channel_id=1, source_target_pairs={{0,4},{2,6},{4,0},{6,2},{8,12},{10,14},{12,8},{14,10},{1,5},{3,7},... | collective-permute-start | bytes 368648 | tf_op jit(solution)/shard_map/ppermute | solution.py:590
  31.4 23.3 %slice-start = ((s8[8388608]{0:T(1024)(128)(4,1)}), s8[4194304]{0:T(1024)(128)(4,1)S(1)}, s32[]{:S(2)}) async-start(s8[8388608]{0:T(1024)(128)(4,1)} %bitcast.8), calls=%async_computation | async-start | bytes 8388608
  33.4 5.5 %collective-permute-start.12 = (bf16[1,192,128]{2,1,0:T(8,128)(2,1)S(1)}, bf16[1,192,128]{2,1,0:T(8,128)(2,1)S(1)}, u32[]{:S(2)}, u32[]{:S(2)}) collective-permute-start(bf16[1,192,128]{2,1,0:T(8,128)(2,1)S(1)} %get-tuple-element.104.refs_1_), channel_id=1, source_target_pairs={{0,8},{2,10},{4,12},{6,14},{8,0},{10,2},{12,4},{14,6},{1,9},{3,11}... | collective-permute-start | bytes 147464 | tf_op jit(solution)/shard_map/ppermute | solution.py:544
  35.9 18.7 %slice-start.1 = ((s8[8388608]{0:T(1024)(128)(4,1)}), s8[4194304]{0:T(1024)(128)(4,1)S(1)}, s32[]{:S(2)}) async-start(s8[8388608]{0:T(1024)(128)(4,1)} %bitcast.8), calls=%async_computation.1 | async-start | bytes 8388608
  38.3 6.8 %collective-permute-start.13 = (bf16[1,384,128]{2,1,0:T(8,128)(2,1)S(1)}, bf16[1,384,128]{2,1,0:T(8,128)(2,1)S(1)}, u32[]{:S(2)}, u32[]{:S(2)}) collective-permute-start(bf16[1,384,128]{2,1,0:T(8,128)(2,1)S(1)} %get-tuple-element.106.refs_1_), channel_id=1, source_target_pairs={{0,8},{2,10},{4,12},{6,14},{8,0},{10,2},{12,4},{14,6},{1,9},{3,11}... | collective-permute-start | bytes 294920 | tf_op jit(solution)/shard_map/ppermute | solution.py:544
  38.9 8.6 %collective-permute-start.15 = (bf16[2,192,128]{2,1,0:T(8,128)(2,1)S(1)}, bf16[2,192,128]{2,1,0:T(8,128)(2,1)S(1)}, u32[]{:S(2)}, u32[]{:S(2)}) collective-permute-start(bf16[2,192,128]{2,1,0:T(8,128)(2,1)S(1)} %get-tuple-element.111.refs_2_), channel_id=1, source_target_pairs={{0,4},{2,6},{4,0},{6,2},{8,12},{10,14},{12,8},{14,10},{1,5},{3,7},... | collective-permute-start | bytes 294920 | tf_op jit(solution)/shard_map/ppermute | solution.py:544
  43.3 5.7 %collective-permute-start.14 = (bf16[1,240,128]{2,1,0:T(8,128)(2,1)S(1)}, bf16[1,240,128]{2,1,0:T(8,128)(2,1)S(1)}, u32[]{:S(2)}, u32[]{:S(2)}) collective-permute-start(bf16[1,240,128]{2,1,0:T(8,128)(2,1)S(1)} %get-tuple-element.109), channel_id=1, source_target_pairs={{0,8},{2,10},{4,12},{6,14},{8,0},{10,2},{12,4},{14,6},{1,9},{3,11}... | collective-permute-start | bytes 184328 | tf_op jit(solution)/shard_map/ppermute | solution.py:599
  44.3 10.4 %collective-permute-start.16 = (bf16[2,192,128]{2,1,0:T(8,128)(2,1)S(1)}, bf16[2,192,128]{2,1,0:T(8,128)(2,1)S(1)}, u32[]{:S(2)}, u32[]{:S(2)}) collective-permute-start(bf16[2,192,128]{2,1,0:T(8,128)(2,1)S(1)} %get-tuple-element.111.refs_2_), channel_id=1, source_target_pairs={{0,2},{2,0},{4,6},{6,4},{8,10},{10,8},{12,14},{14,12},{1,3},{3,1},... | collective-permute-start | bytes 294920 | tf_op jit(solution)/shard_map/ppermute | solution.py:541
  45.1 8.3 %collective-permute-start.19 = (bf16[2,384,128]{2,1,0:T(8,128)(2,1)S(1)}, bf16[2,384,128]{2,1,0:T(8,128)(2,1)S(1)}, u32[]{:S(2)}, u32[]{:S(2)}) collective-permute-start(bf16[2,384,128]{2,1,0:T(8,128)(2,1)S(1)} %get-tuple-element.115.refs_2_), channel_id=1, source_target_pairs={{0,4},{2,6},{4,0},{6,2},{8,12},{10,14},{12,8},{14,10},{1,5},{3,7},... | collective-permute-start | bytes 589832 | tf_op jit(solution)/shard_map/ppermute | solution.py:544
  46.8 15.0 %collective-permute-start.20 = (bf16[2,384,128]{2,1,0:T(8,128)(2,1)S(1)}, bf16[2,384,128]{2,1,0:T(8,128)(2,1)S(1)}, u32[]{:S(2)}, u32[]{:S(2)}) collective-permute-start(bf16[2,384,128]{2,1,0:T(8,128)(2,1)S(1)} %get-tuple-element.115.refs_2_), channel_id=1, source_target_pairs={{0,2},{2,0},{4,6},{6,4},{8,10},{10,8},{12,14},{14,12},{1,3},{3,1},... | collective-permute-start | bytes 589832 | tf_op jit(solution)/shard_map/ppermute | solution.py:541
  47.5 7.1 %collective-permute-start.17 = (bf16[2,192,128]{2,1,0:T(8,128)(2,1)S(1)}, bf16[2,192,128]{2,1,0:T(8,128)(2,1)S(1)}, u32[]{:S(2)}, u32[]{:S(2)}) collective-permute-start(bf16[2,192,128]{2,1,0:T(8,128)(2,1)S(1)} %collective-permute-done.15.refs_3_), channel_id=1, source_target_pairs={{0,2},{2,0},{4,6},{6,4},{8,10},{10,8},{12,14},{14,12},{1,3},{3,1},... | collective-permute-start | bytes 294920 | tf_op jit(solution)/shard_map/ppermute | solution.py:541
  50.8 5.4 %collective-permute-start.18 = (bf16[1,192,128]{2,1,0:T(8,128)(2,1)S(1)}, bf16[1,192,128]{2,1,0:T(8,128)(2,1)S(1)}, u32[]{:S(2)}, u32[]{:S(2)}) collective-permute-start(bf16[1,192,128]{2,1,0:T(8,128)(2,1)S(1)} %get-tuple-element.113.refs_1_), channel_id=1, source_target_pairs={{0,8},{2,10},{4,12},{6,14},{8,0},{10,2},{12,4},{14,6},{1,9},{3,11}... | collective-permute-start | bytes 147464 | tf_op jit(solution)/shard_map/ppermute | solution.py:544
  53.4 8.4 %collective-permute-start.21 = (bf16[2,384,128]{2,1,0:T(8,128)(2,1)S(1)}, bf16[2,384,128]{2,1,0:T(8,128)(2,1)S(1)}, u32[]{:S(2)}, u32[]{:S(2)}) collective-permute-start(bf16[2,384,128]{2,1,0:T(8,128)(2,1)S(1)} %collective-permute-done.19.refs_3_), channel_id=1, source_target_pairs={{0,2},{2,0},{4,6},{6,4},{8,10},{10,8},{12,14},{14,12},{1,3},{3,1},... | collective-permute-start | bytes 589832 | tf_op jit(solution)/shard_map/ppermute | solution.py:541
  56.2 4.7 %collective-permute-start.22 = (bf16[2,192,128]{2,1,0:T(8,128)(2,1)S(1)}, bf16[2,192,128]{2,1,0:T(8,128)(2,1)S(1)}, u32[]{:S(2)}, u32[]{:S(2)}) collective-permute-start(bf16[2,192,128]{2,1,0:T(8,128)(2,1)S(1)} %get-tuple-element.119.refs_2_), channel_id=1, source_target_pairs={{0,4},{2,6},{4,0},{6,2},{8,12},{10,14},{12,8},{14,10},{1,5},{3,7},... | collective-permute-start | bytes 294920 | tf_op jit(solution)/shard_map/ppermute | solution.py:544
  57.0 6.6 %collective-permute-start.23 = (bf16[2,192,128]{2,1,0:T(8,128)(2,1)S(1)}, bf16[2,192,128]{2,1,0:T(8,128)(2,1)S(1)}, u32[]{:S(2)}, u32[]{:S(2)}) collective-permute-start(bf16[2,192,128]{2,1,0:T(8,128)(2,1)S(1)} %get-tuple-element.119.refs_2_), channel_id=1, source_target_pairs={{0,2},{2,0},{4,6},{6,4},{8,10},{10,8},{12,14},{14,12},{1,3},{3,1},... | collective-permute-start | bytes 294920 | tf_op jit(solution)/shard_map/ppermute | solution.py:541
  60.9 4.6 %collective-permute-start.24 = (bf16[2,192,128]{2,1,0:T(8,128)(2,1)S(1)}, bf16[2,192,128]{2,1,0:T(8,128)(2,1)S(1)}, u32[]{:S(2)}, u32[]{:S(2)}) collective-permute-start(bf16[2,192,128]{2,1,0:T(8,128)(2,1)S(1)} %collective-permute-done.22.refs_3_), channel_id=1, source_target_pairs={{0,2},{2,0},{4,6},{6,4},{8,10},{10,8},{12,14},{14,12},{1,3},{3,1},... | collective-permute-start | bytes 294920 | tf_op jit(solution)/shard_map/ppermute | solution.py:541
  67.3 1.4 %collective-permute-start.25 = (bf16[96,1024]{1,0:T(8,128)(2,1)S(1)}, bf16[96,1024]{1,0:T(8,128)(2,1)S(1)}, u32[]{:S(2)}, u32[]{:S(2)}) collective-permute-start(bf16[96,1024]{1,0:T(8,128)(2,1)S(1)} %get-tuple-element.122), channel_id=1, source_target_pairs={{0,1},{1,0},{2,3},{3,2},{4,5},{5,4},{6,7},{7,6},{8,9},{9,8},{10,11... | collective-permute-start | bytes 589832 | tf_op jit(solution)/shard_map/ppermute | solution.py:680

commit v10 on v9

--- a/solution.py
+++ b/solution.py
@@ -24,19 +24,17 @@
 MIB = 1024 * 1024
 SLOTS_AT_ONCE = {1: 24, 2: 8, 3: 8, 4: 4}
 PEAK_FLOP_PER_US = 1.1535e9
-COSTS = {'project0': 1.22, 'add_far0': 0.1, 'add_near0_2': 0.1, 'attend0': 1.9, 'join0_1': 0.1, 'join0': 0.1, 'output0': 1.4, 'project1': 1.8, 'add_far1': 0.1, 'add_near1_2': 0.1, 'attend1': 2.35, 'join1_1': 0.1, 'join1': 0.1, 'output1': 2, 'project2': 1.22, 'add_far2': 0.1, 'add_near2_2': 0.1, 'attend2': 1.9, 'join2': 0.1, 'output2': 4}
+COSTS = {'add_far0': 8, 'add_near0_2': 0.1, 'attend0': 2, 'output0': 1.4, 'project1': 1, 'add_far1': 1, 'attend1': 4, 'join1': 16, 'output1': 1, 'project2': 1, 'attend2': 4, 'join2': 16, 'join0': 2, 'join0_1': 0.3}
 Y_IN_HALVES = (True, True, True)
 GATHER = ('y halved', 'y halved', 'y halved')
 ORDER = (
     ("weights", 0),
-    ("weights", 1),
     ("project", 0),
     ("project", 1),
     ("far", 0),
-    ("weights", 2),
+    ("project", 2),
     ("far", 1),
     ("near", 0),
-    ("project", 2),
     ("near", 1),
     ("far", 2),
     ("attend", 0),
@@ -45,8 +43,8 @@
     ("gather", 0),
     ("gather", 1),
     ("attend", 2),
+    ("forward", 0),
     ("forward", 1),
-    ("forward", 0),
     ("output", 0),
     ("gather", 2),
     ("forward", 2),
@@ -156,7 +154,7 @@
     return [(i * per, ref, z) for i, (ref, z) in enumerate(blocks)]
 
 
-def project_kernel(*refs, nz, per, first, heads):
+def project_kernel(*refs, nz, per, first, heads, start_head):
     place_ref = refs[0]
     if first:
         own_ref, other_ref, gain_ref, sor_ref, wq_ref, wk_ref, wv_ref = refs[1:8]
@@ -195,10 +193,11 @@
     columns = QUERIES_PER_KV * HEAD_SIZE
     slotted = slotted_ref[...]
     for g in range(heads):
+        head = start_head + g
         acc[:, :columns] = jnp.dot(
-            slotted, wq_ref[:, g * columns : (g + 1) * columns], preferred_element_type=F32
-        )
-        narrow = slice(g * HEAD_SIZE, (g + 1) * HEAD_SIZE)
+            slotted, wq_ref[:, head * columns : (head + 1) * columns], preferred_element_type=F32
+        )
+        narrow = slice(head * HEAD_SIZE, (head + 1) * HEAD_SIZE)
         acc[:, columns:] = jnp.dot(
             slotted,
             jnp.concatenate([wk_ref[:, narrow], wv_ref[:, narrow]], axis=1),
@@ -223,15 +222,23 @@
     counts = [nz, nz // 2, nz // 2] if Y_IN_HALVES[chunk] else [nz, nz]
     out_shapes = [((count, block_rows, HEAD_SIZE), BF16) for count in counts]
     return call(
-        functools.partial(project_kernel, nz=nz, per=per, first=first, heads=heads),
+        functools.partial(
+            project_kernel,
+            nz=nz,
+            per=per,
+            first=first,
+            heads=heads,
+            start_head=sum(CHUNK_HEADS[:chunk]),
+        ),
         "project" + str(chunk),
         token,
         [place],
-        [*inputs, *weights],
+        [*inputs, *weights] if first else inputs,
         out_shapes + ([((rows, depth), BF16)] if first else []),
         [pltpu.VMEM((rows, TILES * HEAD_SIZE), F32)],
         12,
         loads,
+        () if first else weights,
     )
 
 
@@ -567,7 +574,9 @@
     def do_project(token, c, wanted):
         nonlocal inputs
         token, arrays, outs = project(
-            token, place, inputs, loaded["weights", c], loads_of(wanted),
+            token, place, inputs,
+            loaded["weights", 0] if c == 0 else [w_query, key_weight, value_weight],
+            loads_of(wanted),
             chunk=c, heads=CHUNK_HEADS[c], nz=nz, per=per,
         )
         file_loaded(wanted, arrays)

time: 70 us -> 72.1 us (1.030)
  waiting for transfers between devices: 9.03 us -> 16.1 us
  starting transfers between devices: 38.1 us -> 33.4 us
  local copies, waits for them, and re-layouts: 0.06 us -> 3.45 us
  Pallas kernels: 21 us -> 17.7 us
    unnamed x22 -> x28, local copies, waits for them, and re-layouts: 0.06 us -> 3.45 us
    pallas_call x20 -> x19, Pallas kernels: 21 us -> 17.7 us  [call(): pl.pallas_call(body, in_specs=[vmem] + [pl.BlockSpec(memory_space=pltpu.H...]
    ppermute x3, waiting for transfers between devices: 1.06 us -> 3.28 us  [do_project(): far = lax.ppermute(outs[2], 'gx', same_z)]
    ppermute x6, waiting for transfers between devices: 1.86 us -> 3.92 us  [over_y(): return (lax.ppermute(blocks, 'gx', same_z), [(1 - h, q) for h, q in labels])]
    ppermute x3, starting transfers between devices: 5 us -> 2.98 us  [do_project(): swapped[c] = ((lax.ppermute(outs[1], 'gx', same_z), 0), (far, 0))]
    ppermute x6, waiting for transfers between devices: 3.28 us -> 5.26 us  [over_z(): moved = lax.ppermute(blocks, 'gx', stride_pairs(nz, stride))]
    ppermute x6, starting transfers between devices: 5.76 us -> 4.26 us  [over_y(): return (lax.ppermute(blocks, 'gx', same_z), [(1 - h, q) for h, q in labels])]
    ppermute x6, starting transfers between devices: 12.5 us -> 11.4 us  [over_z(): moved = lax.ppermute(blocks, 'gx', stride_pairs(nz, stride))]
  transfers between devices with their start and end apart: 26 -> 26, of which waited for: 9 -> 8; matrix products, arithmetic and copies ran while one was open for 0% -> 0% of each run, Pallas kernels for 26% -> 20%
where the time goes in v10:
time: 72.1 us; the launch traced here: 72 us
  starting transfers between devices  33.4 us (46%)
  Pallas kernels  17.7 us (25%)
  waiting for transfers between devices  16.1 us (22%)
  local copies, waits for them, and re-layouts  3.45 us (5%)
  other arithmetic  1.04 us (1%)
    pallas_call x19, Pallas kernels, call(): pl.pallas_call(body, in_specs=[vmem] + [pl.BlockSpec(memory_space=pltpu.H...  17.7 us
    ppermute x6, starting transfers between devices, over_z(): moved = lax.ppermute(blocks, 'gx', stride_pairs(nz, stride))  11.4 us
    ppermute x3, starting transfers between devices, do_near(): terms = [mine, lax.ppermute(sent, 'gx', stride_pairs(nz, stride))]  5.71 us
    ppermute x3, starting transfers between devices, do_far(): reduced[c] = lax.ppermute(total, 'gx', stride_pairs(nz, 1))  5.35 us
    ppermute x6, waiting for transfers between devices, over_z(): moved = lax.ppermute(blocks, 'gx', stride_pairs(nz, stride))  5.26 us
    ppermute x6, starting transfers between devices, over_y(): return (lax.ppermute(blocks, 'gx', same_z), [(1 - h, q) for h, q in labels])  4.26 us
    ppermute x6, waiting for transfers between devices, over_y(): return (lax.ppermute(blocks, 'gx', same_z), [(1 - h, q) for h, q in labels])  3.92 us
    unnamed x28, local copies, waits for them, and re-layouts  3.45 us
  transfers between devices with their start and end apart: 26, of which 8 were waited for; matrix products, arithmetic and copies ran while one was open for 0% of the time, Pallas kernels for 20%

profile of v10, /device:TPU:0, one launch (start us, length us, event | category | flops | bytes accessed | tf_op | source)
XLA Modules:
  0.0 72.0 jit_solution(10103243281163228995)
XLA Ops:
  0.0 0.5 collective-permute-start
  0.5 1.7 %load_weights0.1 = (f32[8,128]{1,0:T(8,128)S(1)}, bf16[1024,1024]{1,0:T(8,128)(2,1)S(1)}, bf16[1024,128]{1,0:T(8,128)(2,1)S(1)}, bf16[1024,128]{1,0:T(8,128)(2,1)S(1)}) custom-call(f32[8,128]{1,0:T(8,128)S(1)} %broadcast_in_dim.17.refs_0_, bf16[1024,4096]{1,0:T(8,128)(2,1)} %refs_3_.5, bf16[1024,512]{1,0:T(8,128)(2,1)} %refs_4_.3, bf16[1024,512]{1,0:T(8,128)(2,1)} %refs_5_.3), custom_call_target="tpu_custom_call" | custom-call | tf_op jit(solution)/shard_map/load_weights0/pallas_call | solution.py:129
  2.2 0.1 pad_add_fusion.refs_1_
  2.3 1.5 %project0.1 = (f32[8,128]{1,0:T(8,128)S(1)}, bf16[4,272,128]{2,1,0:T(8,128)(2,1)S(1)}, bf16[2,272,128]{2,1,0:T(8,128)(2,1)S(1)}, bf16[2,272,128]{2,1,0:T(8,128)(2,1)S(1)}, bf16[192,1024]{1,0:T(8,128)(2,1)S(1)}) custom-call(f32[8,128]{1,0:T(8,128)S(1)} %get-tuple-element.57.refs_0_, s32[3]{0:T(128)S(1)} %pad_add_fusion.refs_1_, ...), custom_call_target="tpu_custom_call" | custom-call | tf_op jit(solution)/shard_map/project0/pallas_call | solution.py:129
  3.8 2.6 %collective-permute-start.1 = (bf16[2,272,128]{2,1,0:T(8,128)(2,1)S(1)}, bf16[2,272,128]{2,1,0:T(8,128)(2,1)S(1)}, u32[]{:S(2)}, u32[]{:S(2)}) collective-permute-start(bf16[2,272,128]{2,1,0:T(8,128)(2,1)S(1)} %get-tuple-element.65), channel_id=1, source_target_pairs={{0,2},{2,0},{4,6},{6,4},{8,10},{10,8},{12,14},{14,12},{1,3},{3,1},... | collective-permute-start | bytes 417800 | tf_op jit(solution)/shard_map/ppermute | solution.py:587
  6.5 3.4 %copy-done = bf16[1024,4096]{1,0:T(8,128)(2,1)S(1)} copy-done((bf16[1024,4096]{1,0:T(8,128)(2,1)S(1)}, bf16[1024,4096]{1,0:T(8,128)(2,1)}, u32[]{:S(2)}) %copy-start) | copy-done | bytes 8388632
  9.8 1.7 %project1.1 = (f32[8,128]{1,0:T(8,128)S(1)}, bf16[4,480,128]{2,1,0:T(8,128)(2,1)S(1)}, bf16[2,480,128]{2,1,0:T(8,128)(2,1)S(1)}, bf16[2,480,128]{2,1,0:T(8,128)(2,1)S(1)}) custom-call(f32[8,128]{1,0:T(8,128)S(1)} %get-tuple-element.61.refs_0_, s32[3]{0:T(128)S(1)} %pad_add_fusion.refs_1_, bf16[192,1024]{1,0:T(8,128)(2,1)S(1)} %get-tuple-element.62.refs_2_, ...), custom_call_target="tpu_custom_call" | custom-call | flops 1153500032 | tf_op jit(solution)/shard_map/project1/pallas_call | solution.py:129
  11.6 0.1 collective-permute-start.2
  11.7 2.0 %collective-permute-start.3 = (bf16[2,272,128]{2,1,0:T(8,128)(2,1)S(1)}, bf16[2,272,128]{2,1,0:T(8,128)(2,1)S(1)}, u32[]{:S(2)}, u32[]{:S(2)}) collective-permute-start(bf16[2,272,128]{2,1,0:T(8,128)(2,1)S(1)} %get-tuple-element.71), channel_id=1, source_target_pairs={{0,2},{2,0},{4,6},{6,4},{8,10},{10,8},{12,14},{14,12},{1,3},{3,1},... | collective-permute-start | bytes 417800 | tf_op jit(solution)/shard_map/ppermute | solution.py:588
  13.7 0.1 collective-permute-start.5
  13.8 2.1 %collective-permute-start.4 = (bf16[2,272,128]{2,1,0:T(8,128)(2,1)S(1)}, bf16[2,272,128]{2,1,0:T(8,128)(2,1)S(1)}, u32[]{:S(2)}, u32[]{:S(2)}) collective-permute-start(bf16[2,272,128]{2,1,0:T(8,128)(2,1)S(1)} %get-tuple-element.72), channel_id=1, source_target_pairs={{0,4},{2,6},{4,0},{6,2},{8,12},{10,14},{12,8},{14,10},{1,5},{3,7},... | collective-permute-start | bytes 417800 | tf_op jit(solution)/shard_map/ppermute | solution.py:599
  15.8 1.2 %project2.1 = (f32[8,128]{1,0:T(8,128)S(1)}, bf16[4,240,128]{2,1,0:T(8,128)(2,1)S(1)}, bf16[2,240,128]{2,1,0:T(8,128)(2,1)S(1)}, bf16[2,240,128]{2,1,0:T(8,128)(2,1)S(1)}) custom-call(f32[8,128]{1,0:T(8,128)S(1)} %get-tuple-element.66.refs_0_, s32[3]{0:T(128)S(1)} %pad_add_fusion.refs_1_, bf16[192,1024]{1,0:T(8,128)(2,1)S(1)} %get-tuple-element.62.refs_2_, ...), custom_call_target="tpu_custom_call" | custom-call | flops 1153500032 | tf_op jit(solution)/shard_map/project2/pallas_call | solution.py:129
  17.1 3.3 %collective-permute-done.2.refs_2_ = bf16[2,480,128]{2,1,0:T(8,128)(2,1)S(1)} collective-permute-done((bf16[2,480,128]{2,1,0:T(8,128)(2,1)S(1)}, bf16[2,480,128]{2,1,0:T(8,128)(2,1)S(1)}, u32[]{:S(2)}, u32[]{:S(2)}) %collective-permute-start.2) | collective-permute-done | bytes 245792 | tf_op jit(solution)/shard_map/ppermute | solution.py:587
  20.5 1.6 %collective-permute-start.6 = (bf16[2,480,128]{2,1,0:T(8,128)(2,1)S(1)}, bf16[2,480,128]{2,1,0:T(8,128)(2,1)S(1)}, u32[]{:S(2)}, u32[]{:S(2)}) collective-permute-start(bf16[2,480,128]{2,1,0:T(8,128)(2,1)S(1)} %get-tuple-element.75), channel_id=1, source_target_pairs={{0,4},{2,6},{4,0},{6,2},{8,12},{10,14},{12,8},{14,10},{1,5},{3,7},... | collective-permute-start | bytes 737288 | tf_op jit(solution)/shard_map/ppermute | solution.py:599
  22.1 0.1 dynamic-slice_convert_fusion
  22.2 0.5 collective-permute-start.7
  22.7 0.7 collective-permute-done.3.refs_2_
  23.5 2.7 %collective-permute-start.8 = (bf16[1,272,128]{2,1,0:T(8,128)(2,1)S(1)}, bf16[1,272,128]{2,1,0:T(8,128)(2,1)S(1)}, u32[]{:S(2)}, u32[]{:S(2)}) collective-permute-start(bf16[1,272,128]{2,1,0:T(8,128)(2,1)S(1)} %get-tuple-element.81), channel_id=1, source_target_pairs={{0,8},{2,10},{4,12},{6,14},{8,0},{10,2},{12,4},{14,6},{1,9},{3,11}... | collective-permute-start | bytes 208904 | tf_op jit(solution)/shard_map/ppermute | solution.py:608
  26.1 0.1 fusion
  26.3 0.9 %collective-permute-start.10 = (bf16[2,240,128]{2,1,0:T(8,128)(2,1)S(1)}, bf16[2,240,128]{2,1,0:T(8,128)(2,1)S(1)}, u32[]{:S(2)}, u32[]{:S(2)}) collective-permute-start(bf16[2,240,128]{2,1,0:T(8,128)(2,1)S(1)} %get-tuple-element.87), channel_id=1, source_target_pairs={{0,2},{2,0},{4,6},{6,4},{8,10},{10,8},{12,14},{14,12},{1,3},{3,1},... | collective-permute-start | bytes 368648 | tf_op jit(solution)/shard_map/ppermute | solution.py:588
  27.1 1.5 %collective-permute-done.5.refs_2_ = bf16[2,480,128]{2,1,0:T(8,128)(2,1)S(1)} collective-permute-done((bf16[2,480,128]{2,1,0:T(8,128)(2,1)S(1)}, bf16[2,480,128]{2,1,0:T(8,128)(2,1)S(1)}, u32[]{:S(2)}, u32[]{:S(2)}) %collective-permute-start.5) | collective-permute-done | bytes 245792 | tf_op jit(solution)/shard_map/ppermute | solution.py:588
  28.7 0.1 add_near1_2.1
  28.8 2.7 %collective-permute-start.9 = (bf16[1,480,128]{2,1,0:T(8,128)(2,1)S(1)}, bf16[1,480,128]{2,1,0:T(8,128)(2,1)S(1)}, u32[]{:S(2)}, u32[]{:S(2)}) collective-permute-start(bf16[1,480,128]{2,1,0:T(8,128)(2,1)S(1)} %get-tuple-element.84), channel_id=1, source_target_pairs={{0,8},{2,10},{4,12},{6,14},{8,0},{10,2},{12,4},{14,6},{1,9},{3,11}... | collective-permute-start | bytes 368648 | tf_op jit(solution)/shard_map/ppermute | solution.py:608
  31.5 1.6 %collective-permute-start.11 = (bf16[2,240,128]{2,1,0:T(8,128)(2,1)S(1)}, bf16[2,240,128]{2,1,0:T(8,128)(2,1)S(1)}, u32[]{:S(2)}, u32[]{:S(2)}) collective-permute-start(bf16[2,240,128]{2,1,0:T(8,128)(2,1)S(1)} %get-tuple-element.88), channel_id=1, source_target_pairs={{0,4},{2,6},{4,0},{6,2},{8,12},{10,14},{12,8},{14,10},{1,5},{3,7},... | collective-permute-start | bytes 368648 | tf_op jit(solution)/shard_map/ppermute | solution.py:599
  33.2 2.0 %attend0.1 = (f32[8,128]{1,0:T(8,128)S(1)}, bf16[1,192,128]{2,1,0:T(8,128)(2,1)S(1)}, f32[24,128]{1,0:T(8,128)S(1)}) custom-call(f32[8,128]{1,0:T(8,128)S(1)} %get-tuple-element.79.refs_0_, s32[3]{0:T(128)S(1)} %pad_add_fusion.refs_1_, s32[192]{0:T(256)S(1)} %copy-done.9, bf16[1,272,128]{2,1,0:T(8,128)(2,1)S(1)} %get-tuple-element.80.refs_3_, ...), custom_call_target="tpu_custom_call" | custom-call | flops 2307000064 | tf_op jit(solution)/shard_map/attend0/pallas_call | solution.py:129
  35.1 2.5 %collective-permute-start.12 = (bf16[1,192,128]{2,1,0:T(8,128)(2,1)S(1)}, bf16[1,192,128]{2,1,0:T(8,128)(2,1)S(1)}, u32[]{:S(2)}, u32[]{:S(2)}) collective-permute-start(bf16[1,192,128]{2,1,0:T(8,128)(2,1)S(1)} %get-tuple-element.90.refs_1_), channel_id=1, source_target_pairs={{0,8},{2,10},{4,12},{6,14},{8,0},{10,2},{12,4},{14,6},{1,9},{3,11}... | collective-permute-start | bytes 147464 | tf_op jit(solution)/shard_map/ppermute | solution.py:551
  37.7 2.4 %attend1.1 = (f32[8,128]{1,0:T(8,128)S(1)}, bf16[1,384,128]{2,1,0:T(8,128)(2,1)S(1)}) custom-call(f32[8,128]{1,0:T(8,128)S(1)} %get-tuple-element.82.refs_0_, s32[3]{0:T(128)S(1)} %pad_add_fusion.refs_1_, s32[192]{0:T(256)S(1)} %copy-done.9, bf16[1,480,128]{2,1,0:T(8,128)(2,1)S(1)} %get-tuple-element.83.refs_3_, ...), custom_call_target="tpu_custom_call" | custom-call | flops 4614000128 | tf_op jit(solution)/shard_map/attend1/pallas_call | solution.py:129
  40.1 0.5 collective-permute-start.13
  40.7 2.6 %collective-permute-start.15 = (bf16[2,192,128]{2,1,0:T(8,128)(2,1)S(1)}, bf16[2,192,128]{2,1,0:T(8,128)(2,1)S(1)}, u32[]{:S(2)}, u32[]{:S(2)}) collective-permute-start(bf16[2,192,128]{2,1,0:T(8,128)(2,1)S(1)} %get-tuple-element.97.refs_2_), channel_id=1, source_target_pairs={{0,4},{2,6},{4,0},{6,2},{8,12},{10,14},{12,8},{14,10},{1,5},{3,7},... | collective-permute-start | bytes 294920 | tf_op jit(solution)/shard_map/ppermute | solution.py:551
  43.3 0.4 collective-permute-start.14
  43.7 0.5 collective-permute-start.16
  44.2 3.2 %collective-permute-done.13.refs_2_ = bf16[1,384,128]{2,1,0:T(8,128)(2,1)S(1)} collective-permute-done((bf16[1,384,128]{2,1,0:T(8,128)(2,1)S(1)}, bf16[1,384,128]{2,1,0:T(8,128)(2,1)S(1)}, u32[]{:S(2)}, u32[]{:S(2)}) %collective-permute-start.13) | collective-permute-done | bytes 98336 | tf_op jit(solution)/shard_map/ppermute | solution.py:551
  47.5 0.6 collective-permute-start.20
  48.1 1.5 %collective-permute-start.17 = (bf16[2,192,128]{2,1,0:T(8,128)(2,1)S(1)}, bf16[2,192,128]{2,1,0:T(8,128)(2,1)S(1)}, u32[]{:S(2)}, u32[]{:S(2)}) collective-permute-start(bf16[2,192,128]{2,1,0:T(8,128)(2,1)S(1)} %collective-permute-done.15.refs_3_), channel_id=1, source_target_pairs={{0,2},{2,0},{4,6},{6,4},{8,10},{10,8},{12,14},{14,12},{1,3},{3,1},... | collective-permute-start | bytes 294920 | tf_op jit(solution)/shard_map/ppermute | solution.py:548
  49.6 1.9 %attend2.1 = (f32[8,128]{1,0:T(8,128)S(1)}, bf16[1,192,128]{2,1,0:T(8,128)(2,1)S(1)}) custom-call(f32[8,128]{1,0:T(8,128)S(1)} %get-tuple-element.93.refs_0_, s32[3]{0:T(128)S(1)} %pad_add_fusion.refs_1_, s32[192]{0:T(256)S(1)} %copy-done.9, bf16[1,240,128]{2,1,0:T(8,128)(2,1)S(1)} %get-tuple-element.94.refs_3_, ...), custom_call_target="tpu_custom_call" | custom-call | flops 4614000128 | tf_op jit(solution)/shard_map/attend2/pallas_call | solution.py:129
  51.5 2.3 %collective-permute-start.18 = (bf16[1,192,128]{2,1,0:T(8,128)(2,1)S(1)}, bf16[1,192,128]{2,1,0:T(8,128)(2,1)S(1)}, u32[]{:S(2)}, u32[]{:S(2)}) collective-permute-start(bf16[1,192,128]{2,1,0:T(8,128)(2,1)S(1)} %get-tuple-element.99.refs_1_), channel_id=1, source_target_pairs={{0,8},{2,10},{4,12},{6,14},{8,0},{10,2},{12,4},{14,6},{1,9},{3,11}... | collective-permute-start | bytes 147464 | tf_op jit(solution)/shard_map/ppermute | solution.py:551
  53.8 0.5 collective-permute-start.21
  54.3 1.7 %collective-permute-done.17.refs_5_ = bf16[2,192,128]{2,1,0:T(8,128)(2,1)S(1)} collective-permute-done((bf16[2,192,128]{2,1,0:T(8,128)(2,1)S(1)}, bf16[2,192,128]{2,1,0:T(8,128)(2,1)S(1)}, u32[]{:S(2)}, u32[]{:S(2)}) %collective-permute-start.17) | collective-permute-done | bytes 98336 | tf_op jit(solution)/shard_map/ppermute | solution.py:548
  56.1 1.4 %output0.1 = (f32[8,128]{1,0:T(8,128)S(1)}, f32[192,1024]{1,0:T(8,128)S(1)}, bf16[192,192]{1,0:T(8,128)(2,1)S(1)}) custom-call(f32[8,128]{1,0:T(8,128)S(1)} %get-tuple-element.96.refs_0_, s32[3]{0:T(128)S(1)} %pad_add_fusion.refs_1_, bf16[2,192,128]{2,1,0:T(8,128)(2,1)S(1)} %get-tuple-element.97.refs_2_, ...), custom_call_target="tpu_custom_call" | custom-call | flops 1614899968 | tf_op jit(solution)/shard_map/output0/pallas_call | solution.py:129
  57.5 3.3 %collective-permute-start.22 = (bf16[2,192,128]{2,1,0:T(8,128)(2,1)S(1)}, bf16[2,192,128]{2,1,0:T(8,128)(2,1)S(1)}, u32[]{:S(2)}, u32[]{:S(2)}) collective-permute-start(bf16[2,192,128]{2,1,0:T(8,128)(2,1)S(1)} %get-tuple-element.105.refs_2_), channel_id=1, source_target_pairs={{0,4},{2,6},{4,0},{6,2},{8,12},{10,14},{12,8},{14,10},{1,5},{3,7},... | collective-permute-start | bytes 294920 | tf_op jit(solution)/shard_map/ppermute | solution.py:551
  60.8 0.6 collective-permute-start.23
  61.4 2.0 %collective-permute-done.22.refs_3_ = bf16[2,192,128]{2,1,0:T(8,128)(2,1)S(1)} collective-permute-done((bf16[2,192,128]{2,1,0:T(8,128)(2,1)S(1)}, bf16[2,192,128]{2,1,0:T(8,128)(2,1)S(1)}, u32[]{:S(2)}, u32[]{:S(2)}) %collective-permute-start.22) | collective-permute-done | bytes 98336 | tf_op jit(solution)/shard_map/ppermute | solution.py:551
  63.4 0.6 collective-permute-start.24
  64.0 1.8 %output1.1 = (f32[8,128]{1,0:T(8,128)S(1)}, f32[192,1024]{1,0:T(8,128)S(1)}) custom-call(f32[8,128]{1,0:T(8,128)S(1)} %get-tuple-element.100.refs_0_, s32[3]{0:T(128)S(1)} %pad_add_fusion.refs_1_, bf16[2,384,128]{2,1,0:T(8,128)(2,1)S(1)} %get-tuple-element.101.refs_2_, bf16[2,384,128]{2,1,0:T(8,128)(2,1)S(1)} %collective-permute-done.19.refs_3_, ...), custom_call_target="tpu_custom_call" | custom-call | flops 1153500032 | tf_op jit(solution)/shard_map/output1/pallas_call | solution.py:129
  65.8 2.2 %collective-permute-done.24.refs_5_ = bf16[2,192,128]{2,1,0:T(8,128)(2,1)S(1)} collective-permute-done((bf16[2,192,128]{2,1,0:T(8,128)(2,1)S(1)}, bf16[2,192,128]{2,1,0:T(8,128)(2,1)S(1)}, u32[]{:S(2)}, u32[]{:S(2)}) %collective-permute-start.24) | collective-permute-done | bytes 98336 | tf_op jit(solution)/shard_map/ppermute | solution.py:548
  68.0 1.7 %output2.1 = (f32[8,128]{1,0:T(8,128)}, f32[96,1024]{1,0:T(8,128)S(1)}, bf16[96,1024]{1,0:T(8,128)(2,1)S(1)}) custom-call(f32[8,128]{1,0:T(8,128)S(1)} %get-tuple-element.104.refs_0_, s32[3]{0:T(128)S(1)} %pad_add_fusion.refs_1_, bf16[2,192,128]{2,1,0:T(8,128)(2,1)S(1)} %get-tuple-element.105.refs_2_, ...), custom_call_target="tpu_custom_call" | custom-call | tf_op jit(solution)/shard_map/output2/pallas_call | solution.py:129
  69.8 1.4 %collective-permute-done.25 = bf16[96,1024]{1,0:T(8,128)(2,1)S(1)} collective-permute-done((bf16[96,1024]{1,0:T(8,128)(2,1)S(1)}, bf16[96,1024]{1,0:T(8,128)(2,1)S(1)}, u32[]{:S(2)}, u32[]{:S(2)}) %collective-permute-start.25) | collective-permute-done | bytes 196640 | tf_op jit(solution)/shard_map/ppermute | solution.py:689
  71.2 0.8 %add_convert_fusion = bf16[96,1024]{1,0:T(8,128)(2,1)} fusion(bf16[96,1024]{1,0:T(8,128)(2,1)S(1)} %collective-permute-done.25, f32[96,1024]{1,0:T(8,128)S(1)} %get-tuple-element.107, bf16[96,1024]{1,0:T(8,128)(2,1)S(1)} %copy-done.3), kind=kLoop, calls=%fused_computation | loop fusion | flops 491520 | bytes 983040 | tf_op jit(solution)/shard_map/convert_element_type | solution.py:690
  (58 shorter events, 0.5 us)
Async XLA Ops:
  0.0 2.3 %collective-permute-start = (bf16[96,1024]{1,0:T(8,128)(2,1)}, bf16[96,1024]{1,0:T(8,128)(2,1)S(1)}, u32[]{:S(2)}, u32[]{:S(2)}) collective-permute-start(bf16[96,1024]{1,0:T(8,128)(2,1)} %refs_2_.6), channel_id=1, source_target_pairs={{0,1},{1,0},{2,3},{3,2},{4,5},{5,4},{6,7},{7,6},{8,9},{9,8},{10,11... | collective-permute-start | bytes 589832 | tf_op jit(solution)/shard_map/ppermute | solution.py:520
  0.5 1.9 %copy-start.3 = (bf16[96,1024]{1,0:T(8,128)(2,1)S(1)}, bf16[96,1024]{1,0:T(8,128)(2,1)}, u32[]{:S(2)}) copy-start(bf16[96,1024]{1,0:T(8,128)(2,1)} %refs_2_.6) | copy-start | bytes 589828
  0.5 1.9 %copy-start.4 = (s32[192]{0:T(256)S(1)}, s32[192]{0:T(256)}, u32[]{:S(2)}) copy-start(s32[192]{0:T(256)} %param.24) | copy-start | bytes 2308
  0.5 1.9 %copy-start.5 = (bf16[1024]{0:T(1024)(128)(2,1)S(1)}, bf16[1024]{0:T(1024)(128)(2,1)}, u32[]{:S(2)}) copy-start(bf16[1024]{0:T(1024)(128)(2,1)} %param.14) | copy-start | bytes 6148
  2.2 4.2 %copy-start.1 = (bf16[1024,512]{1,0:T(8,128)(2,1)S(1)}, bf16[1024,512]{1,0:T(8,128)(2,1)}, u32[]{:S(2)}) copy-start(bf16[1024,512]{1,0:T(8,128)(2,1)} %refs_4_.3) | copy-start | bytes 3145732
  2.2 4.2 %copy-start.2 = (bf16[1024,512]{1,0:T(8,128)(2,1)S(1)}, bf16[1024,512]{1,0:T(8,128)(2,1)}, u32[]{:S(2)}) copy-start(bf16[1024,512]{1,0:T(8,128)(2,1)} %refs_5_.3) | copy-start | bytes 3145732
  3.8 9.9 %collective-permute-start.1 = (bf16[2,272,128]{2,1,0:T(8,128)(2,1)S(1)}, bf16[2,272,128]{2,1,0:T(8,128)(2,1)S(1)}, u32[]{:S(2)}, u32[]{:S(2)}) collective-permute-start(bf16[2,272,128]{2,1,0:T(8,128)(2,1)S(1)} %get-tuple-element.65), channel_id=1, source_target_pairs={{0,2},{2,0},{4,6},{6,4},{8,10},{10,8},{12,14},{14,12},{1,3},{3,1},... | collective-permute-start | bytes 417800 | tf_op jit(solution)/shard_map/ppermute | solution.py:587
  6.4 3.4 %copy-start = (bf16[1024,4096]{1,0:T(8,128)(2,1)S(1)}, bf16[1024,4096]{1,0:T(8,128)(2,1)}, u32[]{:S(2)}) copy-start(bf16[1024,4096]{1,0:T(8,128)(2,1)} %refs_3_.5) | copy-start | bytes 25165828
  11.6 8.9 %collective-permute-start.2 = (bf16[2,480,128]{2,1,0:T(8,128)(2,1)S(1)}, bf16[2,480,128]{2,1,0:T(8,128)(2,1)S(1)}, u32[]{:S(2)}, u32[]{:S(2)}) collective-permute-start(bf16[2,480,128]{2,1,0:T(8,128)(2,1)S(1)} %get-tuple-element.69), channel_id=1, source_target_pairs={{0,2},{2,0},{4,6},{6,4},{8,10},{10,8},{12,14},{14,12},{1,3},{3,1},... | collective-permute-start | bytes 737288 | tf_op jit(solution)/shard_map/ppermute | solution.py:587
  11.7 11.8 %collective-permute-start.3 = (bf16[2,272,128]{2,1,0:T(8,128)(2,1)S(1)}, bf16[2,272,128]{2,1,0:T(8,128)(2,1)S(1)}, u32[]{:S(2)}, u32[]{:S(2)}) collective-permute-start(bf16[2,272,128]{2,1,0:T(8,128)(2,1)S(1)} %get-tuple-element.71), channel_id=1, source_target_pairs={{0,2},{2,0},{4,6},{6,4},{8,10},{10,8},{12,14},{14,12},{1,3},{3,1},... | collective-permute-start | bytes 417800 | tf_op jit(solution)/shard_map/ppermute | solution.py:588
  13.7 15.0 %collective-permute-start.5 = (bf16[2,480,128]{2,1,0:T(8,128)(2,1)S(1)}, bf16[2,480,128]{2,1,0:T(8,128)(2,1)S(1)}, u32[]{:S(2)}, u32[]{:S(2)}) collective-permute-start(bf16[2,480,128]{2,1,0:T(8,128)(2,1)S(1)} %get-tuple-element.74), channel_id=1, source_target_pairs={{0,2},{2,0},{4,6},{6,4},{8,10},{10,8},{12,14},{14,12},{1,3},{3,1},... | collective-permute-start | bytes 737288 | tf_op jit(solution)/shard_map/ppermute | solution.py:588
  13.8 9.6 %collective-permute-start.4 = (bf16[2,272,128]{2,1,0:T(8,128)(2,1)S(1)}, bf16[2,272,128]{2,1,0:T(8,128)(2,1)S(1)}, u32[]{:S(2)}, u32[]{:S(2)}) collective-permute-start(bf16[2,272,128]{2,1,0:T(8,128)(2,1)S(1)} %get-tuple-element.72), channel_id=1, source_target_pairs={{0,4},{2,6},{4,0},{6,2},{8,12},{10,14},{12,8},{14,10},{1,5},{3,7},... | collective-permute-start | bytes 417800 | tf_op jit(solution)/shard_map/ppermute | solution.py:599
  15.8 17.3 %copy-start.7 = (bf16[24,128,512]{2,1,0:T(8,128)(2,1)S(1)}, bf16[24,128,512]{2,1,0:T(8,128)(2,1)}, u32[]{:S(2)}) copy-start(bf16[24,128,512]{2,1,0:T(8,128)(2,1)} %refs_12_.3) | copy-start | bytes 9437188
  17.1 5.0 %copy-start.9 = (s32[192]{0:T(256)S(1)}, s32[192]{0:T(256)}, u32[]{:S(2)}) copy-start(s32[192]{0:T(256)} %refs_2_.9) | copy-start | bytes 2308
  17.1 16.0 %copy-start.6 = (bf16[24,128,512]{2,1,0:T(8,128)(2,1)S(1)}, bf16[24,128,512]{2,1,0:T(8,128)(2,1)}, u32[]{:S(2)}) copy-start(bf16[24,128,512]{2,1,0:T(8,128)(2,1)} %refs_11_.5) | copy-start | bytes 9437188
  17.1 16.0 %copy-start.8 = (bf16[4096]{0:T(1024)(128)(2,1)S(1)}, bf16[4096]{0:T(1024)(128)(2,1)}, u32[]{:S(2)}) copy-start(bf16[4096]{0:T(1024)(128)(2,1)} %param.18) | copy-start | bytes 24580
  17.1 16.0 %copy-start.10 = (bf16[512]{0:T(512)(128)(2,1)S(1)}, bf16[512]{0:T(512)(128)(2,1)}, u32[]{:S(2)}) copy-start(bf16[512]{0:T(512)(128)(2,1)} %param.19) | copy-start | bytes 3076
  17.1 16.0 %copy-start.11 = (bf16[512]{0:T(512)(128)(2,1)S(1)}, bf16[512]{0:T(512)(128)(2,1)}, u32[]{:S(2)}) copy-start(bf16[512]{0:T(512)(128)(2,1)} %param.20) | copy-start | bytes 3076
  20.5 8.2 %collective-permute-start.6 = (bf16[2,480,128]{2,1,0:T(8,128)(2,1)S(1)}, bf16[2,480,128]{2,1,0:T(8,128)(2,1)S(1)}, u32[]{:S(2)}, u32[]{:S(2)}) collective-permute-start(bf16[2,480,128]{2,1,0:T(8,128)(2,1)S(1)} %get-tuple-element.75), channel_id=1, source_target_pairs={{0,4},{2,6},{4,0},{6,2},{8,12},{10,14},{12,8},{14,10},{1,5},{3,7},... | collective-permute-start | bytes 737288 | tf_op jit(solution)/shard_map/ppermute | solution.py:599
  22.2 9.2 %collective-permute-start.7 = (bf16[2,240,128]{2,1,0:T(8,128)(2,1)S(1)}, bf16[2,240,128]{2,1,0:T(8,128)(2,1)S(1)}, u32[]{:S(2)}, u32[]{:S(2)}) collective-permute-start(bf16[2,240,128]{2,1,0:T(8,128)(2,1)S(1)} %get-tuple-element.78), channel_id=1, source_target_pairs={{0,2},{2,0},{4,6},{6,4},{8,10},{10,8},{12,14},{14,12},{1,3},{3,1},... | collective-permute-start | bytes 368648 | tf_op jit(solution)/shard_map/ppermute | solution.py:587
  23.5 9.6 %collective-permute-start.8 = (bf16[1,272,128]{2,1,0:T(8,128)(2,1)S(1)}, bf16[1,272,128]{2,1,0:T(8,128)(2,1)S(1)}, u32[]{:S(2)}, u32[]{:S(2)}) collective-permute-start(bf16[1,272,128]{2,1,0:T(8,128)(2,1)S(1)} %get-tuple-element.81), channel_id=1, source_target_pairs={{0,8},{2,10},{4,12},{6,14},{8,0},{10,2},{12,4},{14,6},{1,9},{3,11}... | collective-permute-start | bytes 208904 | tf_op jit(solution)/shard_map/ppermute | solution.py:608
  26.3 14.3 %collective-permute-start.10 = (bf16[2,240,128]{2,1,0:T(8,128)(2,1)S(1)}, bf16[2,240,128]{2,1,0:T(8,128)(2,1)S(1)}, u32[]{:S(2)}, u32[]{:S(2)}) collective-permute-start(bf16[2,240,128]{2,1,0:T(8,128)(2,1)S(1)} %get-tuple-element.87), channel_id=1, source_target_pairs={{0,2},{2,0},{4,6},{6,4},{8,10},{10,8},{12,14},{14,12},{1,3},{3,1},... | collective-permute-start | bytes 368648 | tf_op jit(solution)/shard_map/ppermute | solution.py:588
  28.8 8.9 %collective-permute-start.9 = (bf16[1,480,128]{2,1,0:T(8,128)(2,1)S(1)}, bf16[1,480,128]{2,1,0:T(8,128)(2,1)S(1)}, u32[]{:S(2)}, u32[]{:S(2)}) collective-permute-start(bf16[1,480,128]{2,1,0:T(8,128)(2,1)S(1)} %get-tuple-element.84), channel_id=1, source_target_pairs={{0,8},{2,10},{4,12},{6,14},{8,0},{10,2},{12,4},{14,6},{1,9},{3,11}... | collective-permute-start | bytes 368648 | tf_op jit(solution)/shard_map/ppermute | solution.py:608
  31.5 9.1 %collective-permute-start.11 = (bf16[2,240,128]{2,1,0:T(8,128)(2,1)S(1)}, bf16[2,240,128]{2,1,0:T(8,128)(2,1)S(1)}, u32[]{:S(2)}, u32[]{:S(2)}) collective-permute-start(bf16[2,240,128]{2,1,0:T(8,128)(2,1)S(1)} %get-tuple-element.88), channel_id=1, source_target_pairs={{0,4},{2,6},{4,0},{6,2},{8,12},{10,14},{12,8},{14,10},{1,5},{3,7},... | collective-permute-start | bytes 368648 | tf_op jit(solution)/shard_map/ppermute | solution.py:599
  35.1 5.5 %collective-permute-start.12 = (bf16[1,192,128]{2,1,0:T(8,128)(2,1)S(1)}, bf16[1,192,128]{2,1,0:T(8,128)(2,1)S(1)}, u32[]{:S(2)}, u32[]{:S(2)}) collective-permute-start(bf16[1,192,128]{2,1,0:T(8,128)(2,1)S(1)} %get-tuple-element.90.refs_1_), channel_id=1, source_target_pairs={{0,8},{2,10},{4,12},{6,14},{8,0},{10,2},{12,4},{14,6},{1,9},{3,11}... | collective-permute-start | bytes 147464 | tf_op jit(solution)/shard_map/ppermute | solution.py:551
  40.1 7.4 %collective-permute-start.13 = (bf16[1,384,128]{2,1,0:T(8,128)(2,1)S(1)}, bf16[1,384,128]{2,1,0:T(8,128)(2,1)S(1)}, u32[]{:S(2)}, u32[]{:S(2)}) collective-permute-start(bf16[1,384,128]{2,1,0:T(8,128)(2,1)S(1)} %get-tuple-element.92.refs_1_), channel_id=1, source_target_pairs={{0,8},{2,10},{4,12},{6,14},{8,0},{10,2},{12,4},{14,6},{1,9},{3,11}... | collective-permute-start | bytes 294920 | tf_op jit(solution)/shard_map/ppermute | solution.py:551
  40.7 15.4 %slice-start = ((s8[8388608]{0:T(1024)(128)(4,1)}), s8[4194304]{0:T(1024)(128)(4,1)S(1)}, s32[]{:S(2)}) async-start(s8[8388608]{0:T(1024)(128)(4,1)} %bitcast.8), calls=%async_computation | async-start | bytes 8388608
  40.7 7.4 %collective-permute-start.15 = (bf16[2,192,128]{2,1,0:T(8,128)(2,1)S(1)}, bf16[2,192,128]{2,1,0:T(8,128)(2,1)S(1)}, u32[]{:S(2)}, u32[]{:S(2)}) collective-permute-start(bf16[2,192,128]{2,1,0:T(8,128)(2,1)S(1)} %get-tuple-element.97.refs_2_), channel_id=1, source_target_pairs={{0,4},{2,6},{4,0},{6,2},{8,12},{10,14},{12,8},{14,10},{1,5},{3,7},... | collective-permute-start | bytes 294920 | tf_op jit(solution)/shard_map/ppermute | solution.py:551
  43.3 6.3 %collective-permute-start.14 = (bf16[1,240,128]{2,1,0:T(8,128)(2,1)S(1)}, bf16[1,240,128]{2,1,0:T(8,128)(2,1)S(1)}, u32[]{:S(2)}, u32[]{:S(2)}) collective-permute-start(bf16[1,240,128]{2,1,0:T(8,128)(2,1)S(1)} %get-tuple-element.95), channel_id=1, source_target_pairs={{0,8},{2,10},{4,12},{6,14},{8,0},{10,2},{12,4},{14,6},{1,9},{3,11}... | collective-permute-start | bytes 184328 | tf_op jit(solution)/shard_map/ppermute | solution.py:608
  43.7 10.7 %collective-permute-start.16 = (bf16[2,192,128]{2,1,0:T(8,128)(2,1)S(1)}, bf16[2,192,128]{2,1,0:T(8,128)(2,1)S(1)}, u32[]{:S(2)}, u32[]{:S(2)}) collective-permute-start(bf16[2,192,128]{2,1,0:T(8,128)(2,1)S(1)} %get-tuple-element.97.refs_2_), channel_id=1, source_target_pairs={{0,2},{2,0},{4,6},{6,4},{8,10},{10,8},{12,14},{14,12},{1,3},{3,1},... | collective-permute-start | bytes 294920 | tf_op jit(solution)/shard_map/ppermute | solution.py:548
  47.4 6.4 %collective-permute-start.19 = (bf16[2,384,128]{2,1,0:T(8,128)(2,1)S(1)}, bf16[2,384,128]{2,1,0:T(8,128)(2,1)S(1)}, u32[]{:S(2)}, u32[]{:S(2)}) collective-permute-start(bf16[2,384,128]{2,1,0:T(8,128)(2,1)S(1)} %get-tuple-element.101.refs_2_), channel_id=1, source_target_pairs={{0,4},{2,6},{4,0},{6,2},{8,12},{10,14},{12,8},{14,10},{1,5},{3,7},... | collective-permute-start | bytes 589832 | tf_op jit(solution)/shard_map/ppermute | solution.py:551
  47.5 16.5 %collective-permute-start.20 = (bf16[2,384,128]{2,1,0:T(8,128)(2,1)S(1)}, bf16[2,384,128]{2,1,0:T(8,128)(2,1)S(1)}, u32[]{:S(2)}, u32[]{:S(2)}) collective-permute-start(bf16[2,384,128]{2,1,0:T(8,128)(2,1)S(1)} %get-tuple-element.101.refs_2_), channel_id=1, source_target_pairs={{0,2},{2,0},{4,6},{6,4},{8,10},{10,8},{12,14},{14,12},{1,3},{3,1},... | collective-permute-start | bytes 589832 | tf_op jit(solution)/shard_map/ppermute | solution.py:548
  48.1 8.0 %collective-permute-start.17 = (bf16[2,192,128]{2,1,0:T(8,128)(2,1)S(1)}, bf16[2,192,128]{2,1,0:T(8,128)(2,1)S(1)}, u32[]{:S(2)}, u32[]{:S(2)}) collective-permute-start(bf16[2,192,128]{2,1,0:T(8,128)(2,1)S(1)} %collective-permute-done.15.refs_3_), channel_id=1, source_target_pairs={{0,2},{2,0},{4,6},{6,4},{8,10},{10,8},{12,14},{14,12},{1,3},{3,1},... | collective-permute-start | bytes 294920 | tf_op jit(solution)/shard_map/ppermute | solution.py:548
  49.6 6.5 %slice-start.1 = ((s8[8388608]{0:T(1024)(128)(4,1)}), s8[4194304]{0:T(1024)(128)(4,1)S(1)}, s32[]{:S(2)}) async-start(s8[8388608]{0:T(1024)(128)(4,1)} %bitcast.8), calls=%async_computation.1 | async-start | bytes 8388608
  51.5 6.0 %collective-permute-start.18 = (bf16[1,192,128]{2,1,0:T(8,128)(2,1)S(1)}, bf16[1,192,128]{2,1,0:T(8,128)(2,1)S(1)}, u32[]{:S(2)}, u32[]{:S(2)}) collective-permute-start(bf16[1,192,128]{2,1,0:T(8,128)(2,1)S(1)} %get-tuple-element.99.refs_1_), channel_id=1, source_target_pairs={{0,8},{2,10},{4,12},{6,14},{8,0},{10,2},{12,4},{14,6},{1,9},{3,11}... | collective-permute-start | bytes 147464 | tf_op jit(solution)/shard_map/ppermute | solution.py:551
  53.8 10.2 %collective-permute-start.21 = (bf16[2,384,128]{2,1,0:T(8,128)(2,1)S(1)}, bf16[2,384,128]{2,1,0:T(8,128)(2,1)S(1)}, u32[]{:S(2)}, u32[]{:S(2)}) collective-permute-start(bf16[2,384,128]{2,1,0:T(8,128)(2,1)S(1)} %collective-permute-done.19.refs_3_), channel_id=1, source_target_pairs={{0,2},{2,0},{4,6},{6,4},{8,10},{10,8},{12,14},{14,12},{1,3},{3,1},... | collective-permute-start | bytes 589832 | tf_op jit(solution)/shard_map/ppermute | solution.py:548
  57.5 5.9 %collective-permute-start.22 = (bf16[2,192,128]{2,1,0:T(8,128)(2,1)S(1)}, bf16[2,192,128]{2,1,0:T(8,128)(2,1)S(1)}, u32[]{:S(2)}, u32[]{:S(2)}) collective-permute-start(bf16[2,192,128]{2,1,0:T(8,128)(2,1)S(1)} %get-tuple-element.105.refs_2_), channel_id=1, source_target_pairs={{0,4},{2,6},{4,0},{6,2},{8,12},{10,14},{12,8},{14,10},{1,5},{3,7},... | collective-permute-start | bytes 294920 | tf_op jit(solution)/shard_map/ppermute | solution.py:551
  60.8 5.0 %collective-permute-start.23 = (bf16[2,192,128]{2,1,0:T(8,128)(2,1)S(1)}, bf16[2,192,128]{2,1,0:T(8,128)(2,1)S(1)}, u32[]{:S(2)}, u32[]{:S(2)}) collective-permute-start(bf16[2,192,128]{2,1,0:T(8,128)(2,1)S(1)} %get-tuple-element.105.refs_2_), channel_id=1, source_target_pairs={{0,2},{2,0},{4,6},{6,4},{8,10},{10,8},{12,14},{14,12},{1,3},{3,1},... | collective-permute-start | bytes 294920 | tf_op jit(solution)/shard_map/ppermute | solution.py:548
  63.4 4.6 %collective-permute-start.24 = (bf16[2,192,128]{2,1,0:T(8,128)(2,1)S(1)}, bf16[2,192,128]{2,1,0:T(8,128)(2,1)S(1)}, u32[]{:S(2)}, u32[]{:S(2)}) collective-permute-start(bf16[2,192,128]{2,1,0:T(8,128)(2,1)S(1)} %collective-permute-done.22.refs_3_), channel_id=1, source_target_pairs={{0,2},{2,0},{4,6},{6,4},{8,10},{10,8},{12,14},{14,12},{1,3},{3,1},... | collective-permute-start | bytes 294920 | tf_op jit(solution)/shard_map/ppermute | solution.py:548
  69.8 1.4 %collective-permute-start.25 = (bf16[96,1024]{1,0:T(8,128)(2,1)S(1)}, bf16[96,1024]{1,0:T(8,128)(2,1)S(1)}, u32[]{:S(2)}, u32[]{:S(2)}) collective-permute-start(bf16[96,1024]{1,0:T(8,128)(2,1)S(1)} %get-tuple-element.108), channel_id=1, source_target_pairs={{0,1},{1,0},{2,3},{3,2},{4,5},{5,4},{6,7},{7,6},{8,9},{9,8},{10,11... | collective-permute-start | bytes 589832 | tf_op jit(solution)/shard_map/ppermute | solution.py:689

commit v11 on v9

--- a/solution.py
+++ b/solution.py
@@ -22,7 +22,7 @@
 F32 = jnp.float32
 BF16 = jnp.bfloat16
 MIB = 1024 * 1024
-SLOTS_AT_ONCE = {1: 24, 2: 8, 3: 8, 4: 4}
+SLOTS_AT_ONCE = {1: 8, 2: 8, 3: 8, 4: 4}
 PEAK_FLOP_PER_US = 1.1535e9
 COSTS = {'project0': 1.22, 'add_far0': 0.1, 'add_near0_2': 0.1, 'attend0': 1.9, 'join0_1': 0.1, 'join0': 0.1, 'output0': 1.4, 'project1': 1.8, 'add_far1': 0.1, 'add_near1_2': 0.1, 'attend1': 2.35, 'join1_1': 0.1, 'join1': 0.1, 'output1': 2, 'project2': 1.22, 'add_far2': 0.1, 'add_near2_2': 0.1, 'attend2': 1.9, 'join2': 0.1, 'output2': 4}
 Y_IN_HALVES = (True, True, True)
@@ -315,11 +315,17 @@
     qrows = heads * QUERIES_PER_KV
     lanes = group * qrows
     extra = 16
-    lane_block = lax.broadcasted_iota(jnp.int32, (HEAD_SIZE, lanes), 1) // QUERIES_PER_KV
+    tile = min(lanes, HEAD_SIZE)
+    tile_pairs = tile // QUERIES_PER_KV
+    tiles = lanes // tile if lanes % tile == 0 else -(-lanes // tile)
+    widths = [min(tile, lanes - t * tile) for t in range(tiles)]
+    lane_pairs = [
+        lax.broadcasted_iota(jnp.int32, (HEAD_SIZE, width), 1) // QUERIES_PER_KV
+        for width in widths
+    ]
     top_row = lax.broadcasted_iota(jnp.int32, (extra, HEAD_SIZE), 0) == 0
     lane_slot = lax.broadcasted_iota(jnp.int32, (1, lanes), 1) // qrows
     row = lax.broadcasted_iota(jnp.int32, (positions + extra, lanes), 0)
-    row_slot = lax.broadcasted_iota(jnp.int32, (lanes, positions), 0) // qrows
     base = (place_ref[0] * 2 + place_ref[1]) * per
     for start in range(0, per, group):
         slots = range(start, start + group)
@@ -335,7 +341,13 @@
         query, new_key = [], []
         for i, s in enumerate(slots):
             for g in range(heads):
-                query.append(jnp.where(lane_block == i * heads + g, turned, 0.0).astype(BF16))
+                pair = i * heads + g
+                at, own = divmod(pair, tile_pairs)
+                pieces = [jnp.zeros((HEAD_SIZE, width), BF16) for width in widths]
+                pieces[at] = jnp.where(
+                    lane_pairs[at] == own, turned[:, at * tile : at * tile + widths[at]], 0.0
+                ).astype(BF16)
+                query.append(jnp.concatenate(pieces, axis=1))
                 key = fresh[pl.ds(g * head_rows + QUERIES_PER_KV * per + s, 1), :]
                 new_key.append(jnp.where(top_row, key, 0.0).astype(BF16))
         keys = jnp.concatenate(
@@ -357,10 +369,21 @@
         weights = exps * (1.0 / jnp.sum(exps, axis=0, keepdims=True))
         cache_weights = weights[:positions].T
         own_weights = weights[positions : positions + 8].T[:, 0:1].astype(BF16).astype(F32)
-        spread = jnp.concatenate(
-            [jnp.where(row_slot == i, cache_weights, 0.0).astype(BF16) for i in range(group)],
-            axis=1,
-        )
+        spread = []
+        for i in range(group):
+            lo, hi = i * qrows, (i + 1) * qrows
+            low, high = lo // 16 * 16, -(-hi // 16) * 16
+            rows = [
+                jnp.zeros((lo - low, positions), F32),
+                cache_weights[lo:hi],
+                jnp.zeros((high - hi, positions), F32),
+            ]
+            rows = jnp.concatenate([r for r in rows if r.shape[0]], axis=0).astype(BF16)
+            blocks = [
+                jnp.zeros((low, positions), BF16), rows, jnp.zeros((lanes - high, positions), BF16),
+            ]
+            spread.append(jnp.concatenate([r for r in blocks if r.shape[0]], axis=0))
+        spread = jnp.concatenate(spread, axis=1)
         values = v_ref[start : start + group, :, columns].reshape(group * positions, heads * HEAD_SIZE)
         mixed = jnp.dot(spread, values, preferred_element_type=F32)
         for i, s in enumerate(slots):
@@ -504,7 +527,7 @@
     assert size % 2 == 0 and nz & (nz - 1) == 0 and nz > 2
     per = rotated_key_cache.shape[0]
     kv_heads = key_weight.shape[1] // HEAD_SIZE
-    assert sum(CHUNK_HEADS) == kv_heads and per == SLOTS_AT_ONCE[1]
+    assert sum(CHUNK_HEADS) == kv_heads and per % SLOTS_AT_ONCE[1] == 0
     chunks = len(CHUNK_HEADS)
     gx = lax.axis_index("gx")
     gy = lax.axis_index("gy")

time: 70 us -> 70.1 us (level)
  transfers between devices with their start and end apart: 26 -> 26, of which waited for: 9 -> 8; matrix products, arithmetic and copies ran while one was open for 0% -> 0% of each run, Pallas kernels for 26% -> 26%
where the time goes in v11:
time: 70.1 us; the launch traced here: 69.7 us
  starting transfers between devices  37.8 us (54%)
  Pallas kernels  21.3 us (30%)
  waiting for transfers between devices  9.28 us (13%)
  other arithmetic  1.04 us (1%)
    pallas_call x20, Pallas kernels, call(): pl.pallas_call(body, in_specs=[vmem] + [pl.BlockSpec(memory_space=pltpu.H...  21.3 us
    ppermute x6, starting transfers between devices, over_z(): moved = lax.ppermute(blocks, 'gx', stride_pairs(nz, stride))  12.6 us
    ppermute x3, starting transfers between devices, do_near(): terms = [mine, lax.ppermute(sent, 'gx', stride_pairs(nz, stride))]  5.41 us
    ppermute x6, starting transfers between devices, over_y(): return (lax.ppermute(blocks, 'gx', same_z), [(1 - h, q) for h, q in labels])  5.3 us
    ppermute x3, starting transfers between devices, do_far(): reduced[c] = lax.ppermute(total, 'gx', stride_pairs(nz, 1))  5.17 us
    ppermute x3, starting transfers between devices, do_project(): swapped[c] = ((lax.ppermute(outs[1], 'gx', same_z), 0), (far, 0))  5 us
    ppermute x3, starting transfers between devices, do_project(): far = lax.ppermute(outs[2], 'gx', same_z)  3.91 us
    ppermute x6, waiting for transfers between devices, over_z(): moved = lax.ppermute(blocks, 'gx', stride_pairs(nz, stride))  3.24 us
  transfers between devices with their start and end apart: 26, of which 8 were waited for; matrix products, arithmetic and copies ran while one was open for 0% of the time, Pallas kernels for 26%

profile of v11, /device:TPU:0, one launch (start us, length us, event | category | flops | bytes accessed | tf_op | source)
XLA Modules:
  0.0 69.7 jit_solution(342886609880612234)
XLA Ops:
  0.0 0.5 collective-permute-start
  0.5 3.3 %load_weights0_weights1.1 = (f32[8,128]{1,0:T(8,128)S(1)}, bf16[1024,1024]{1,0:T(8,128)(2,1)S(1)}, bf16[1024,128]{1,0:T(8,128)(2,1)S(1)}, bf16[1024,128]{1,0:T(8...) custom-call(f32[8,128]{1,0:T(8,128)S(1)} %broadcast_in_dim.17.refs_0_, ...), custom_call_target="tpu_custom_call" | custom-call | tf_op jit(solution)/shard_map/load_weights0_weights1/pallas_call | solution.py:131
  3.8 0.1 pad_add_fusion.refs_1_
  3.9 1.4 %project0.1 = (f32[8,128]{1,0:T(8,128)S(1)}, bf16[4,272,128]{2,1,0:T(8,128)(2,1)S(1)}, bf16[2,272,128]{2,1,0:T(8,128)(2,1)S(1)}, bf16[2,272,128]{2,1,0:T(8,128)(2,1)S(1)}, bf16[192,1024]{1,0:T(8,128)(2,1)S(1)}) custom-call(f32[8,128]{1,0:T(8,128)S(1)} %get-tuple-element.64.refs_0_, s32[3]{0:T(128)S(1)} %pad_add_fusion.refs_1_, bf16[96,1024]{1,0:T(8,128)(2,1)S(1)} %copy-done, ...), custom_call_target="tpu_custom_call" | custom-call | flops 1407270016 | tf_op jit(solution)/shard_map/project0/pallas_call | solution.py:131
  5.3 2.6 %collective-permute-start.1 = (bf16[2,272,128]{2,1,0:T(8,128)(2,1)S(1)}, bf16[2,272,128]{2,1,0:T(8,128)(2,1)S(1)}, u32[]{:S(2)}, u32[]{:S(2)}) collective-permute-start(bf16[2,272,128]{2,1,0:T(8,128)(2,1)S(1)} %get-tuple-element.75), channel_id=1, source_target_pairs={{0,2},{2,0},{4,6},{6,4},{8,10},{10,8},{12,14},{14,12},{1,3},{3,1},... | collective-permute-start | bytes 417800 | tf_op jit(solution)/shard_map/ppermute | solution.py:601
  8.0 1.8 %project1.1 = (f32[8,128]{1,0:T(8,128)S(1)}, bf16[4,480,128]{2,1,0:T(8,128)(2,1)S(1)}, bf16[2,480,128]{2,1,0:T(8,128)(2,1)S(1)}, bf16[2,480,128]{2,1,0:T(8,128)(2,1)S(1)}) custom-call(f32[8,128]{1,0:T(8,128)S(1)} %get-tuple-element.68.refs_0_, s32[3]{0:T(128)S(1)} %pad_add_fusion.refs_1_, bf16[192,1024]{1,0:T(8,128)(2,1)S(1)} %get-tuple-element.69.refs_2_, ...), custom_call_target="tpu_custom_call" | custom-call | flops 2076300032 | tf_op jit(solution)/shard_map/project1/pallas_call | solution.py:131
  9.8 0.1 collective-permute-start.2
  9.8 2.0 %collective-permute-start.3 = (bf16[2,272,128]{2,1,0:T(8,128)(2,1)S(1)}, bf16[2,272,128]{2,1,0:T(8,128)(2,1)S(1)}, u32[]{:S(2)}, u32[]{:S(2)}) collective-permute-start(bf16[2,272,128]{2,1,0:T(8,128)(2,1)S(1)} %get-tuple-element.81), channel_id=1, source_target_pairs={{0,2},{2,0},{4,6},{6,4},{8,10},{10,8},{12,14},{14,12},{1,3},{3,1},... | collective-permute-start | bytes 417800 | tf_op jit(solution)/shard_map/ppermute | solution.py:602
  11.8 0.4 collective-permute-done.1.refs_2_
  12.3 1.9 %collective-permute-start.4 = (bf16[2,272,128]{2,1,0:T(8,128)(2,1)S(1)}, bf16[2,272,128]{2,1,0:T(8,128)(2,1)S(1)}, u32[]{:S(2)}, u32[]{:S(2)}) collective-permute-start(bf16[2,272,128]{2,1,0:T(8,128)(2,1)S(1)} %get-tuple-element.82), channel_id=1, source_target_pairs={{0,4},{2,6},{4,0},{6,2},{8,12},{10,14},{12,8},{14,10},{1,5},{3,7},... | collective-permute-start | bytes 417800 | tf_op jit(solution)/shard_map/ppermute | solution.py:613
  14.2 0.1 dynamic-slice_convert_fusion
  14.3 2.0 %collective-permute-start.5 = (bf16[2,480,128]{2,1,0:T(8,128)(2,1)S(1)}, bf16[2,480,128]{2,1,0:T(8,128)(2,1)S(1)}, u32[]{:S(2)}, u32[]{:S(2)}) collective-permute-start(bf16[2,480,128]{2,1,0:T(8,128)(2,1)S(1)} %get-tuple-element.88), channel_id=1, source_target_pairs={{0,2},{2,0},{4,6},{6,4},{8,10},{10,8},{12,14},{14,12},{1,3},{3,1},... | collective-permute-start | bytes 737288 | tf_op jit(solution)/shard_map/ppermute | solution.py:602
  16.3 1.7 %load_weights2.1 = (f32[8,128]{1,0:T(8,128)S(1)}, bf16[1024,1024]{1,0:T(8,128)(2,1)S(1)}, bf16[1024,128]{1,0:T(8,128)(2,1)S(1)}, bf16[1024,128]{1,0:T(8,128)(2,1)S(1)}) custom-call(f32[8,128]{1,0:T(8,128)S(1)} %get-tuple-element.76.refs_0_, bf16[1024,4096]{1,0:T(8,128)(2,1)} %refs_1_.3, bf16[1024,512]{1,0:T(8,128)(2,1)} %refs_2_.8, bf16[1024,512]{1,0:T(8,128)(2,1)} %refs_3_.3), custom_call_target="tpu_custom_call" | custom-call | tf_op jit(solution)/shard_map/load_weights2/pallas_call | solution.py:131
  18.0 0.7 collective-permute-done.2.refs_2_
  18.7 1.6 %collective-permute-start.6 = (bf16[2,480,128]{2,1,0:T(8,128)(2,1)S(1)}, bf16[2,480,128]{2,1,0:T(8,128)(2,1)S(1)}, u32[]{:S(2)}, u32[]{:S(2)}) collective-permute-start(bf16[2,480,128]{2,1,0:T(8,128)(2,1)S(1)} %get-tuple-element.89), channel_id=1, source_target_pairs={{0,4},{2,6},{4,0},{6,2},{8,12},{10,14},{12,8},{14,10},{1,5},{3,7},... | collective-permute-start | bytes 737288 | tf_op jit(solution)/shard_map/ppermute | solution.py:613
  20.3 1.3 %collective-permute-done.3.refs_2_ = bf16[2,272,128]{2,1,0:T(8,128)(2,1)S(1)} collective-permute-done((bf16[2,272,128]{2,1,0:T(8,128)(2,1)S(1)}, bf16[2,272,128]{2,1,0:T(8,128)(2,1)S(1)}, u32[]{:S(2)}, u32[]{:S(2)}) %collective-permute-start.3) | collective-permute-done | bytes 139296 | tf_op jit(solution)/shard_map/ppermute | solution.py:602
  21.7 1.2 %project2.1 = (f32[8,128]{1,0:T(8,128)S(1)}, bf16[4,240,128]{2,1,0:T(8,128)(2,1)S(1)}, bf16[2,240,128]{2,1,0:T(8,128)(2,1)S(1)}, bf16[2,240,128]{2,1,0:T(8,128)(2,1)S(1)}) custom-call(f32[8,128]{1,0:T(8,128)S(1)} %get-tuple-element.83.refs_0_, s32[3]{0:T(128)S(1)} %pad_add_fusion.refs_1_, bf16[192,1024]{1,0:T(8,128)(2,1)S(1)} %get-tuple-element.69.refs_2_, ...), custom_call_target="tpu_custom_call" | custom-call | flops 1407270016 | tf_op jit(solution)/shard_map/project2/pallas_call | solution.py:131
  23.0 1.2 %collective-permute-start.7 = (bf16[2,240,128]{2,1,0:T(8,128)(2,1)S(1)}, bf16[2,240,128]{2,1,0:T(8,128)(2,1)S(1)}, u32[]{:S(2)}, u32[]{:S(2)}) collective-permute-start(bf16[2,240,128]{2,1,0:T(8,128)(2,1)S(1)} %get-tuple-element.92), channel_id=1, source_target_pairs={{0,2},{2,0},{4,6},{6,4},{8,10},{10,8},{12,14},{14,12},{1,3},{3,1},... | collective-permute-start | bytes 368648 | tf_op jit(solution)/shard_map/ppermute | solution.py:601
  24.1 2.6 %collective-permute-start.8 = (bf16[1,272,128]{2,1,0:T(8,128)(2,1)S(1)}, bf16[1,272,128]{2,1,0:T(8,128)(2,1)S(1)}, u32[]{:S(2)}, u32[]{:S(2)}) collective-permute-start(bf16[1,272,128]{2,1,0:T(8,128)(2,1)S(1)} %get-tuple-element.95), channel_id=1, source_target_pairs={{0,8},{2,10},{4,12},{6,14},{8,0},{10,2},{12,4},{14,6},{1,9},{3,11}... | collective-permute-start | bytes 208904 | tf_op jit(solution)/shard_map/ppermute | solution.py:622
  26.7 0.1 fusion
  26.9 1.0 %collective-permute-start.10 = (bf16[2,240,128]{2,1,0:T(8,128)(2,1)S(1)}, bf16[2,240,128]{2,1,0:T(8,128)(2,1)S(1)}, u32[]{:S(2)}, u32[]{:S(2)}) collective-permute-start(bf16[2,240,128]{2,1,0:T(8,128)(2,1)S(1)} %get-tuple-element.101), channel_id=1, source_target_pairs={{0,2},{2,0},{4,6},{6,4},{8,10},{10,8},{12,14},{14,12},{1,3},{3,1},... | collective-permute-start | bytes 368648 | tf_op jit(solution)/shard_map/ppermute | solution.py:602
  27.9 0.1 add_near1_2.1
  28.0 1.7 %collective-permute-start.9 = (bf16[1,480,128]{2,1,0:T(8,128)(2,1)S(1)}, bf16[1,480,128]{2,1,0:T(8,128)(2,1)S(1)}, u32[]{:S(2)}, u32[]{:S(2)}) collective-permute-start(bf16[1,480,128]{2,1,0:T(8,128)(2,1)S(1)} %get-tuple-element.98), channel_id=1, source_target_pairs={{0,8},{2,10},{4,12},{6,14},{8,0},{10,2},{12,4},{14,6},{1,9},{3,11}... | collective-permute-start | bytes 368648 | tf_op jit(solution)/shard_map/ppermute | solution.py:622
  29.7 1.7 %collective-permute-start.11 = (bf16[2,240,128]{2,1,0:T(8,128)(2,1)S(1)}, bf16[2,240,128]{2,1,0:T(8,128)(2,1)S(1)}, u32[]{:S(2)}, u32[]{:S(2)}) collective-permute-start(bf16[2,240,128]{2,1,0:T(8,128)(2,1)S(1)} %get-tuple-element.102), channel_id=1, source_target_pairs={{0,4},{2,6},{4,0},{6,2},{8,12},{10,14},{12,8},{14,10},{1,5},{3,7},... | collective-permute-start | bytes 368648 | tf_op jit(solution)/shard_map/ppermute | solution.py:613
  31.4 2.1 %attend0.1 = (f32[8,128]{1,0:T(8,128)S(1)}, bf16[1,192,128]{2,1,0:T(8,128)(2,1)S(1)}, f32[24,128]{1,0:T(8,128)S(1)}) custom-call(f32[8,128]{1,0:T(8,128)S(1)} %get-tuple-element.93.refs_0_, s32[3]{0:T(128)S(1)} %pad_add_fusion.refs_1_, s32[192]{0:T(256)S(1)} %copy-done.6, bf16[1,272,128]{2,1,0:T(8,128)(2,1)S(1)} %get-tuple-element.94.refs_3_, ...), custom_call_target="tpu_custom_call" | custom-call | flops 2191650048 | tf_op jit(solution)/shard_map/attend0/pallas_call | solution.py:131
  33.5 2.5 %collective-permute-start.12 = (bf16[1,192,128]{2,1,0:T(8,128)(2,1)S(1)}, bf16[1,192,128]{2,1,0:T(8,128)(2,1)S(1)}, u32[]{:S(2)}, u32[]{:S(2)}) collective-permute-start(bf16[1,192,128]{2,1,0:T(8,128)(2,1)S(1)} %get-tuple-element.104.refs_1_), channel_id=1, source_target_pairs={{0,8},{2,10},{4,12},{6,14},{8,0},{10,2},{12,4},{14,6},{1,9},{3,11}... | collective-permute-start | bytes 147464 | tf_op jit(solution)/shard_map/ppermute | solution.py:567
  36.0 2.4 %attend1.1 = (f32[8,128]{1,0:T(8,128)S(1)}, bf16[1,384,128]{2,1,0:T(8,128)(2,1)S(1)}) custom-call(f32[8,128]{1,0:T(8,128)S(1)} %get-tuple-element.96.refs_0_, s32[3]{0:T(128)S(1)} %pad_add_fusion.refs_1_, s32[192]{0:T(256)S(1)} %copy-done.6, bf16[1,480,128]{2,1,0:T(8,128)(2,1)S(1)} %get-tuple-element.97.refs_3_, ...), custom_call_target="tpu_custom_call" | custom-call | flops 2710725120 | tf_op jit(solution)/shard_map/attend1/pallas_call | solution.py:131
  38.4 0.5 collective-permute-start.13
  39.0 4.2 %collective-permute-start.15 = (bf16[2,192,128]{2,1,0:T(8,128)(2,1)S(1)}, bf16[2,192,128]{2,1,0:T(8,128)(2,1)S(1)}, u32[]{:S(2)}, u32[]{:S(2)}) collective-permute-start(bf16[2,192,128]{2,1,0:T(8,128)(2,1)S(1)} %get-tuple-element.111.refs_2_), channel_id=1, source_target_pairs={{0,4},{2,6},{4,0},{6,2},{8,12},{10,14},{12,8},{14,10},{1,5},{3,7},... | collective-permute-start | bytes 294920 | tf_op jit(solution)/shard_map/ppermute | solution.py:567
  43.3 1.1 %collective-permute-start.14 = (bf16[1,240,128]{2,1,0:T(8,128)(2,1)S(1)}, bf16[1,240,128]{2,1,0:T(8,128)(2,1)S(1)}, u32[]{:S(2)}, u32[]{:S(2)}) collective-permute-start(bf16[1,240,128]{2,1,0:T(8,128)(2,1)S(1)} %get-tuple-element.109), channel_id=1, source_target_pairs={{0,8},{2,10},{4,12},{6,14},{8,0},{10,2},{12,4},{14,6},{1,9},{3,11}... | collective-permute-start | bytes 184328 | tf_op jit(solution)/shard_map/ppermute | solution.py:622
  44.4 0.8 %collective-permute-start.16 = (bf16[2,192,128]{2,1,0:T(8,128)(2,1)S(1)}, bf16[2,192,128]{2,1,0:T(8,128)(2,1)S(1)}, u32[]{:S(2)}, u32[]{:S(2)}) collective-permute-start(bf16[2,192,128]{2,1,0:T(8,128)(2,1)S(1)} %get-tuple-element.111.refs_2_), channel_id=1, source_target_pairs={{0,2},{2,0},{4,6},{6,4},{8,10},{10,8},{12,14},{14,12},{1,3},{3,1},... | collective-permute-start | bytes 294920 | tf_op jit(solution)/shard_map/ppermute | solution.py:564
  45.2 1.7 %collective-permute-start.19 = (bf16[2,384,128]{2,1,0:T(8,128)(2,1)S(1)}, bf16[2,384,128]{2,1,0:T(8,128)(2,1)S(1)}, u32[]{:S(2)}, u32[]{:S(2)}) collective-permute-start(bf16[2,384,128]{2,1,0:T(8,128)(2,1)S(1)} %get-tuple-element.115.refs_2_), channel_id=1, source_target_pairs={{0,4},{2,6},{4,0},{6,2},{8,12},{10,14},{12,8},{14,10},{1,5},{3,7},... | collective-permute-start | bytes 589832 | tf_op jit(solution)/shard_map/ppermute | solution.py:567
  46.9 0.6 collective-permute-start.20
  47.5 1.4 %collective-permute-start.17 = (bf16[2,192,128]{2,1,0:T(8,128)(2,1)S(1)}, bf16[2,192,128]{2,1,0:T(8,128)(2,1)S(1)}, u32[]{:S(2)}, u32[]{:S(2)}) collective-permute-start(bf16[2,192,128]{2,1,0:T(8,128)(2,1)S(1)} %collective-permute-done.15.refs_3_), channel_id=1, source_target_pairs={{0,2},{2,0},{4,6},{6,4},{8,10},{10,8},{12,14},{14,12},{1,3},{3,1},... | collective-permute-start | bytes 294920 | tf_op jit(solution)/shard_map/ppermute | solution.py:564
  49.0 2.0 %attend2.1 = (f32[8,128]{1,0:T(8,128)S(1)}, bf16[1,192,128]{2,1,0:T(8,128)(2,1)S(1)}) custom-call(f32[8,128]{1,0:T(8,128)S(1)} %get-tuple-element.107.refs_0_, s32[3]{0:T(128)S(1)} %pad_add_fusion.refs_1_, s32[192]{0:T(256)S(1)} %copy-done.6, bf16[1,240,128]{2,1,0:T(8,128)(2,1)S(1)} %get-tuple-element.108.refs_3_, ...), custom_call_target="tpu_custom_call" | custom-call | flops 2191650048 | tf_op jit(solution)/shard_map/attend2/pallas_call | solution.py:131
  51.0 2.6 %collective-permute-start.18 = (bf16[1,192,128]{2,1,0:T(8,128)(2,1)S(1)}, bf16[1,192,128]{2,1,0:T(8,128)(2,1)S(1)}, u32[]{:S(2)}, u32[]{:S(2)}) collective-permute-start(bf16[1,192,128]{2,1,0:T(8,128)(2,1)S(1)} %get-tuple-element.113.refs_1_), channel_id=1, source_target_pairs={{0,8},{2,10},{4,12},{6,14},{8,0},{10,2},{12,4},{14,6},{1,9},{3,11}... | collective-permute-start | bytes 147464 | tf_op jit(solution)/shard_map/ppermute | solution.py:567
  53.6 1.1 %collective-permute-start.21 = (bf16[2,384,128]{2,1,0:T(8,128)(2,1)S(1)}, bf16[2,384,128]{2,1,0:T(8,128)(2,1)S(1)}, u32[]{:S(2)}, u32[]{:S(2)}) collective-permute-start(bf16[2,384,128]{2,1,0:T(8,128)(2,1)S(1)} %collective-permute-done.19.refs_3_), channel_id=1, source_target_pairs={{0,2},{2,0},{4,6},{6,4},{8,10},{10,8},{12,14},{14,12},{1,3},{3,1},... | collective-permute-start | bytes 589832 | tf_op jit(solution)/shard_map/ppermute | solution.py:564
  54.8 1.4 %output0.1 = (f32[8,128]{1,0:T(8,128)S(1)}, f32[192,1024]{1,0:T(8,128)S(1)}, bf16[192,192]{1,0:T(8,128)(2,1)S(1)}) custom-call(f32[8,128]{1,0:T(8,128)S(1)} %get-tuple-element.110.refs_0_, s32[3]{0:T(128)S(1)} %pad_add_fusion.refs_1_, bf16[2,192,128]{2,1,0:T(8,128)(2,1)S(1)} %get-tuple-element.111.refs_2_, ...), custom_call_target="tpu_custom_call" | custom-call | flops 1614899968 | tf_op jit(solution)/shard_map/output0/pallas_call | solution.py:131
  56.2 0.3 collective-permute-done.18.refs_2_
  56.5 1.0 %collective-permute-start.22 = (bf16[2,192,128]{2,1,0:T(8,128)(2,1)S(1)}, bf16[2,192,128]{2,1,0:T(8,128)(2,1)S(1)}, u32[]{:S(2)}, u32[]{:S(2)}) collective-permute-start(bf16[2,192,128]{2,1,0:T(8,128)(2,1)S(1)} %get-tuple-element.119.refs_2_), channel_id=1, source_target_pairs={{0,4},{2,6},{4,0},{6,2},{8,12},{10,14},{12,8},{14,10},{1,5},{3,7},... | collective-permute-start | bytes 294920 | tf_op jit(solution)/shard_map/ppermute | solution.py:567
  57.5 0.7 %collective-permute-start.23 = (bf16[2,192,128]{2,1,0:T(8,128)(2,1)S(1)}, bf16[2,192,128]{2,1,0:T(8,128)(2,1)S(1)}, u32[]{:S(2)}, u32[]{:S(2)}) collective-permute-start(bf16[2,192,128]{2,1,0:T(8,128)(2,1)S(1)} %get-tuple-element.119.refs_2_), channel_id=1, source_target_pairs={{0,2},{2,0},{4,6},{6,4},{8,10},{10,8},{12,14},{14,12},{1,3},{3,1},... | collective-permute-start | bytes 294920 | tf_op jit(solution)/shard_map/ppermute | solution.py:564
  58.3 2.9 %collective-permute-done.22.refs_3_ = bf16[2,192,128]{2,1,0:T(8,128)(2,1)S(1)} collective-permute-done((bf16[2,192,128]{2,1,0:T(8,128)(2,1)S(1)}, bf16[2,192,128]{2,1,0:T(8,128)(2,1)S(1)}, u32[]{:S(2)}, u32[]{:S(2)}) %collective-permute-start.22) | collective-permute-done | bytes 98336 | tf_op jit(solution)/shard_map/ppermute | solution.py:567
  61.2 0.6 collective-permute-start.24
  61.8 1.8 %output1.1 = (f32[8,128]{1,0:T(8,128)S(1)}, f32[192,1024]{1,0:T(8,128)S(1)}) custom-call(f32[8,128]{1,0:T(8,128)S(1)} %get-tuple-element.114.refs_0_, s32[3]{0:T(128)S(1)} %pad_add_fusion.refs_1_, bf16[2,384,128]{2,1,0:T(8,128)(2,1)S(1)} %get-tuple-element.115.refs_2_, bf16[2,384,128]{2,1,0:T(8,128)(2,1)S(1)} %collective-permute-done.19.refs_3_, ...), custom_call_target="tpu_custom_call" | custom-call | flops 2307000064 | tf_op jit(solution)/shard_map/output1/pallas_call | solution.py:131
  63.6 2.2 %collective-permute-done.24.refs_5_ = bf16[2,192,128]{2,1,0:T(8,128)(2,1)S(1)} collective-permute-done((bf16[2,192,128]{2,1,0:T(8,128)(2,1)S(1)}, bf16[2,192,128]{2,1,0:T(8,128)(2,1)S(1)}, u32[]{:S(2)}, u32[]{:S(2)}) %collective-permute-start.24) | collective-permute-done | bytes 98336 | tf_op jit(solution)/shard_map/ppermute | solution.py:564
  65.8 1.7 %output2.1 = (f32[8,128]{1,0:T(8,128)}, f32[96,1024]{1,0:T(8,128)S(1)}, bf16[96,1024]{1,0:T(8,128)(2,1)S(1)}) custom-call(f32[8,128]{1,0:T(8,128)S(1)} %get-tuple-element.118.refs_0_, s32[3]{0:T(128)S(1)} %pad_add_fusion.refs_1_, bf16[2,192,128]{2,1,0:T(8,128)(2,1)S(1)} %get-tuple-element.119.refs_2_, ...), custom_call_target="tpu_custom_call" | custom-call | flops 4614000128 | tf_op jit(solution)/shard_map/output2/pallas_call | solution.py:131
  67.5 1.4 %collective-permute-done.25 = bf16[96,1024]{1,0:T(8,128)(2,1)S(1)} collective-permute-done((bf16[96,1024]{1,0:T(8,128)(2,1)S(1)}, bf16[96,1024]{1,0:T(8,128)(2,1)S(1)}, u32[]{:S(2)}, u32[]{:S(2)}) %collective-permute-start.25) | collective-permute-done | bytes 196640 | tf_op jit(solution)/shard_map/ppermute | solution.py:703
  69.0 0.8 %add_convert_fusion = bf16[96,1024]{1,0:T(8,128)(2,1)} fusion(bf16[96,1024]{1,0:T(8,128)(2,1)S(1)} %collective-permute-done.25, f32[96,1024]{1,0:T(8,128)S(1)} %get-tuple-element.121, bf16[96,1024]{1,0:T(8,128)(2,1)S(1)} %copy-done), kind=kLoop, calls=%fused_computation | loop fusion | flops 491520 | bytes 983040 | tf_op jit(solution)/shard_map/convert_element_type | solution.py:704
  (53 shorter events, 0.4 us)
Async XLA Ops:
  0.0 3.9 %collective-permute-start = (bf16[96,1024]{1,0:T(8,128)(2,1)}, bf16[96,1024]{1,0:T(8,128)(2,1)S(1)}, u32[]{:S(2)}, u32[]{:S(2)}) collective-permute-start(bf16[96,1024]{1,0:T(8,128)(2,1)} %refs_2_.7), channel_id=1, source_target_pairs={{0,1},{1,0},{2,3},{3,2},{4,5},{5,4},{6,7},{7,6},{8,9},{9,8},{10,11... | collective-permute-start | bytes 589832 | tf_op jit(solution)/shard_map/ppermute | solution.py:536
  0.5 3.4 %copy-start = (bf16[96,1024]{1,0:T(8,128)(2,1)S(1)}, bf16[96,1024]{1,0:T(8,128)(2,1)}, u32[]{:S(2)}) copy-start(bf16[96,1024]{1,0:T(8,128)(2,1)} %refs_2_.7) | copy-start | bytes 589828
  0.5 3.4 %copy-start.1 = (s32[192]{0:T(256)S(1)}, s32[192]{0:T(256)}, u32[]{:S(2)}) copy-start(s32[192]{0:T(256)} %param.24) | copy-start | bytes 2308
  0.5 3.4 %copy-start.5 = (bf16[1024]{0:T(1024)(128)(2,1)S(1)}, bf16[1024]{0:T(1024)(128)(2,1)}, u32[]{:S(2)}) copy-start(bf16[1024]{0:T(1024)(128)(2,1)} %param.14) | copy-start | bytes 6148
  5.3 6.9 %collective-permute-start.1 = (bf16[2,272,128]{2,1,0:T(8,128)(2,1)S(1)}, bf16[2,272,128]{2,1,0:T(8,128)(2,1)S(1)}, u32[]{:S(2)}, u32[]{:S(2)}) collective-permute-start(bf16[2,272,128]{2,1,0:T(8,128)(2,1)S(1)} %get-tuple-element.75), channel_id=1, source_target_pairs={{0,2},{2,0},{4,6},{6,4},{8,10},{10,8},{12,14},{14,12},{1,3},{3,1},... | collective-permute-start | bytes 417800 | tf_op jit(solution)/shard_map/ppermute | solution.py:601
  8.0 6.2 %copy-start.6 = (s32[192]{0:T(256)S(1)}, s32[192]{0:T(256)}, u32[]{:S(2)}) copy-start(s32[192]{0:T(256)} %refs_2_.11) | copy-start | bytes 2308
  9.8 8.9 %collective-permute-start.2 = (bf16[2,480,128]{2,1,0:T(8,128)(2,1)S(1)}, bf16[2,480,128]{2,1,0:T(8,128)(2,1)S(1)}, u32[]{:S(2)}, u32[]{:S(2)}) collective-permute-start(bf16[2,480,128]{2,1,0:T(8,128)(2,1)S(1)} %get-tuple-element.79), channel_id=1, source_target_pairs={{0,2},{2,0},{4,6},{6,4},{8,10},{10,8},{12,14},{14,12},{1,3},{3,1},... | collective-permute-start | bytes 737288 | tf_op jit(solution)/shard_map/ppermute | solution.py:601
  9.8 11.8 %collective-permute-start.3 = (bf16[2,272,128]{2,1,0:T(8,128)(2,1)S(1)}, bf16[2,272,128]{2,1,0:T(8,128)(2,1)S(1)}, u32[]{:S(2)}, u32[]{:S(2)}) collective-permute-start(bf16[2,272,128]{2,1,0:T(8,128)(2,1)S(1)} %get-tuple-element.81), channel_id=1, source_target_pairs={{0,2},{2,0},{4,6},{6,4},{8,10},{10,8},{12,14},{14,12},{1,3},{3,1},... | collective-permute-start | bytes 417800 | tf_op jit(solution)/shard_map/ppermute | solution.py:602
  12.3 9.3 %collective-permute-start.4 = (bf16[2,272,128]{2,1,0:T(8,128)(2,1)S(1)}, bf16[2,272,128]{2,1,0:T(8,128)(2,1)S(1)}, u32[]{:S(2)}, u32[]{:S(2)}) collective-permute-start(bf16[2,272,128]{2,1,0:T(8,128)(2,1)S(1)} %get-tuple-element.82), channel_id=1, source_target_pairs={{0,4},{2,6},{4,0},{6,2},{8,12},{10,14},{12,8},{14,10},{1,5},{3,7},... | collective-permute-start | bytes 417800 | tf_op jit(solution)/shard_map/ppermute | solution.py:613
  14.3 13.6 %collective-permute-start.5 = (bf16[2,480,128]{2,1,0:T(8,128)(2,1)S(1)}, bf16[2,480,128]{2,1,0:T(8,128)(2,1)S(1)}, u32[]{:S(2)}, u32[]{:S(2)}) collective-permute-start(bf16[2,480,128]{2,1,0:T(8,128)(2,1)S(1)} %get-tuple-element.88), channel_id=1, source_target_pairs={{0,2},{2,0},{4,6},{6,4},{8,10},{10,8},{12,14},{14,12},{1,3},{3,1},... | collective-permute-start | bytes 737288 | tf_op jit(solution)/shard_map/ppermute | solution.py:602
  18.7 9.2 %collective-permute-start.6 = (bf16[2,480,128]{2,1,0:T(8,128)(2,1)S(1)}, bf16[2,480,128]{2,1,0:T(8,128)(2,1)S(1)}, u32[]{:S(2)}, u32[]{:S(2)}) collective-permute-start(bf16[2,480,128]{2,1,0:T(8,128)(2,1)S(1)} %get-tuple-element.89), channel_id=1, source_target_pairs={{0,4},{2,6},{4,0},{6,2},{8,12},{10,14},{12,8},{14,10},{1,5},{3,7},... | collective-permute-start | bytes 737288 | tf_op jit(solution)/shard_map/ppermute | solution.py:613
  21.7 9.7 %copy-start.2 = (bf16[24,128,512]{2,1,0:T(8,128)(2,1)S(1)}, bf16[24,128,512]{2,1,0:T(8,128)(2,1)}, u32[]{:S(2)}) copy-start(bf16[24,128,512]{2,1,0:T(8,128)(2,1)} %refs_11_.5) | copy-start | bytes 9437188
  21.7 9.7 %copy-start.3 = (bf16[24,128,512]{2,1,0:T(8,128)(2,1)S(1)}, bf16[24,128,512]{2,1,0:T(8,128)(2,1)}, u32[]{:S(2)}) copy-start(bf16[24,128,512]{2,1,0:T(8,128)(2,1)} %refs_12_.3) | copy-start | bytes 9437188
  21.7 9.7 %copy-start.4 = (bf16[4096]{0:T(1024)(128)(2,1)S(1)}, bf16[4096]{0:T(1024)(128)(2,1)}, u32[]{:S(2)}) copy-start(bf16[4096]{0:T(1024)(128)(2,1)} %param.18) | copy-start | bytes 24580
  21.7 9.7 %copy-start.7 = (bf16[512]{0:T(512)(128)(2,1)S(1)}, bf16[512]{0:T(512)(128)(2,1)}, u32[]{:S(2)}) copy-start(bf16[512]{0:T(512)(128)(2,1)} %param.19) | copy-start | bytes 3076
  21.7 9.7 %copy-start.8 = (bf16[512]{0:T(512)(128)(2,1)S(1)}, bf16[512]{0:T(512)(128)(2,1)}, u32[]{:S(2)}) copy-start(bf16[512]{0:T(512)(128)(2,1)} %param.20) | copy-start | bytes 3076
  23.0 6.7 %collective-permute-start.7 = (bf16[2,240,128]{2,1,0:T(8,128)(2,1)S(1)}, bf16[2,240,128]{2,1,0:T(8,128)(2,1)S(1)}, u32[]{:S(2)}, u32[]{:S(2)}) collective-permute-start(bf16[2,240,128]{2,1,0:T(8,128)(2,1)S(1)} %get-tuple-element.92), channel_id=1, source_target_pairs={{0,2},{2,0},{4,6},{6,4},{8,10},{10,8},{12,14},{14,12},{1,3},{3,1},... | collective-permute-start | bytes 368648 | tf_op jit(solution)/shard_map/ppermute | solution.py:601
  24.1 7.2 %collective-permute-start.8 = (bf16[1,272,128]{2,1,0:T(8,128)(2,1)S(1)}, bf16[1,272,128]{2,1,0:T(8,128)(2,1)S(1)}, u32[]{:S(2)}, u32[]{:S(2)}) collective-permute-start(bf16[1,272,128]{2,1,0:T(8,128)(2,1)S(1)} %get-tuple-element.95), channel_id=1, source_target_pairs={{0,8},{2,10},{4,12},{6,14},{8,0},{10,2},{12,4},{14,6},{1,9},{3,11}... | collective-permute-start | bytes 208904 | tf_op jit(solution)/shard_map/ppermute | solution.py:622
  26.9 12.1 %collective-permute-start.10 = (bf16[2,240,128]{2,1,0:T(8,128)(2,1)S(1)}, bf16[2,240,128]{2,1,0:T(8,128)(2,1)S(1)}, u32[]{:S(2)}, u32[]{:S(2)}) collective-permute-start(bf16[2,240,128]{2,1,0:T(8,128)(2,1)S(1)} %get-tuple-element.101), channel_id=1, source_target_pairs={{0,2},{2,0},{4,6},{6,4},{8,10},{10,8},{12,14},{14,12},{1,3},{3,1},... | collective-permute-start | bytes 368648 | tf_op jit(solution)/shard_map/ppermute | solution.py:602
  28.0 8.1 %collective-permute-start.9 = (bf16[1,480,128]{2,1,0:T(8,128)(2,1)S(1)}, bf16[1,480,128]{2,1,0:T(8,128)(2,1)S(1)}, u32[]{:S(2)}, u32[]{:S(2)}) collective-permute-start(bf16[1,480,128]{2,1,0:T(8,128)(2,1)S(1)} %get-tuple-element.98), channel_id=1, source_target_pairs={{0,8},{2,10},{4,12},{6,14},{8,0},{10,2},{12,4},{14,6},{1,9},{3,11}... | collective-permute-start | bytes 368648 | tf_op jit(solution)/shard_map/ppermute | solution.py:622
  29.7 9.3 %collective-permute-start.11 = (bf16[2,240,128]{2,1,0:T(8,128)(2,1)S(1)}, bf16[2,240,128]{2,1,0:T(8,128)(2,1)S(1)}, u32[]{:S(2)}, u32[]{:S(2)}) collective-permute-start(bf16[2,240,128]{2,1,0:T(8,128)(2,1)S(1)} %get-tuple-element.102), channel_id=1, source_target_pairs={{0,4},{2,6},{4,0},{6,2},{8,12},{10,14},{12,8},{14,10},{1,5},{3,7},... | collective-permute-start | bytes 368648 | tf_op jit(solution)/shard_map/ppermute | solution.py:613
  31.4 23.4 %slice-start = ((s8[8388608]{0:T(1024)(128)(4,1)}), s8[4194304]{0:T(1024)(128)(4,1)S(1)}, s32[]{:S(2)}) async-start(s8[8388608]{0:T(1024)(128)(4,1)} %bitcast.8), calls=%async_computation | async-start | bytes 8388608
  33.5 5.5 %collective-permute-start.12 = (bf16[1,192,128]{2,1,0:T(8,128)(2,1)S(1)}, bf16[1,192,128]{2,1,0:T(8,128)(2,1)S(1)}, u32[]{:S(2)}, u32[]{:S(2)}) collective-permute-start(bf16[1,192,128]{2,1,0:T(8,128)(2,1)S(1)} %get-tuple-element.104.refs_1_), channel_id=1, source_target_pairs={{0,8},{2,10},{4,12},{6,14},{8,0},{10,2},{12,4},{14,6},{1,9},{3,11}... | collective-permute-start | bytes 147464 | tf_op jit(solution)/shard_map/ppermute | solution.py:567
  36.0 18.8 %slice-start.1 = ((s8[8388608]{0:T(1024)(128)(4,1)}), s8[4194304]{0:T(1024)(128)(4,1)S(1)}, s32[]{:S(2)}) async-start(s8[8388608]{0:T(1024)(128)(4,1)} %bitcast.8), calls=%async_computation.1 | async-start | bytes 8388608
  38.4 6.8 %collective-permute-start.13 = (bf16[1,384,128]{2,1,0:T(8,128)(2,1)S(1)}, bf16[1,384,128]{2,1,0:T(8,128)(2,1)S(1)}, u32[]{:S(2)}, u32[]{:S(2)}) collective-permute-start(bf16[1,384,128]{2,1,0:T(8,128)(2,1)S(1)} %get-tuple-element.106.refs_1_), channel_id=1, source_target_pairs={{0,8},{2,10},{4,12},{6,14},{8,0},{10,2},{12,4},{14,6},{1,9},{3,11}... | collective-permute-start | bytes 294920 | tf_op jit(solution)/shard_map/ppermute | solution.py:567
  39.0 8.5 %collective-permute-start.15 = (bf16[2,192,128]{2,1,0:T(8,128)(2,1)S(1)}, bf16[2,192,128]{2,1,0:T(8,128)(2,1)S(1)}, u32[]{:S(2)}, u32[]{:S(2)}) collective-permute-start(bf16[2,192,128]{2,1,0:T(8,128)(2,1)S(1)} %get-tuple-element.111.refs_2_), channel_id=1, source_target_pairs={{0,4},{2,6},{4,0},{6,2},{8,12},{10,14},{12,8},{14,10},{1,5},{3,7},... | collective-permute-start | bytes 294920 | tf_op jit(solution)/shard_map/ppermute | solution.py:567
  43.3 5.8 %collective-permute-start.14 = (bf16[1,240,128]{2,1,0:T(8,128)(2,1)S(1)}, bf16[1,240,128]{2,1,0:T(8,128)(2,1)S(1)}, u32[]{:S(2)}, u32[]{:S(2)}) collective-permute-start(bf16[1,240,128]{2,1,0:T(8,128)(2,1)S(1)} %get-tuple-element.109), channel_id=1, source_target_pairs={{0,8},{2,10},{4,12},{6,14},{8,0},{10,2},{12,4},{14,6},{1,9},{3,11}... | collective-permute-start | bytes 184328 | tf_op jit(solution)/shard_map/ppermute | solution.py:622
  44.4 10.4 %collective-permute-start.16 = (bf16[2,192,128]{2,1,0:T(8,128)(2,1)S(1)}, bf16[2,192,128]{2,1,0:T(8,128)(2,1)S(1)}, u32[]{:S(2)}, u32[]{:S(2)}) collective-permute-start(bf16[2,192,128]{2,1,0:T(8,128)(2,1)S(1)} %get-tuple-element.111.refs_2_), channel_id=1, source_target_pairs={{0,2},{2,0},{4,6},{6,4},{8,10},{10,8},{12,14},{14,12},{1,3},{3,1},... | collective-permute-start | bytes 294920 | tf_op jit(solution)/shard_map/ppermute | solution.py:564
  45.2 8.4 %collective-permute-start.19 = (bf16[2,384,128]{2,1,0:T(8,128)(2,1)S(1)}, bf16[2,384,128]{2,1,0:T(8,128)(2,1)S(1)}, u32[]{:S(2)}, u32[]{:S(2)}) collective-permute-start(bf16[2,384,128]{2,1,0:T(8,128)(2,1)S(1)} %get-tuple-element.115.refs_2_), channel_id=1, source_target_pairs={{0,4},{2,6},{4,0},{6,2},{8,12},{10,14},{12,8},{14,10},{1,5},{3,7},... | collective-permute-start | bytes 589832 | tf_op jit(solution)/shard_map/ppermute | solution.py:567
  46.9 14.8 %collective-permute-start.20 = (bf16[2,384,128]{2,1,0:T(8,128)(2,1)S(1)}, bf16[2,384,128]{2,1,0:T(8,128)(2,1)S(1)}, u32[]{:S(2)}, u32[]{:S(2)}) collective-permute-start(bf16[2,384,128]{2,1,0:T(8,128)(2,1)S(1)} %get-tuple-element.115.refs_2_), channel_id=1, source_target_pairs={{0,2},{2,0},{4,6},{6,4},{8,10},{10,8},{12,14},{14,12},{1,3},{3,1},... | collective-permute-start | bytes 589832 | tf_op jit(solution)/shard_map/ppermute | solution.py:564
  47.5 7.2 %collective-permute-start.17 = (bf16[2,192,128]{2,1,0:T(8,128)(2,1)S(1)}, bf16[2,192,128]{2,1,0:T(8,128)(2,1)S(1)}, u32[]{:S(2)}, u32[]{:S(2)}) collective-permute-start(bf16[2,192,128]{2,1,0:T(8,128)(2,1)S(1)} %collective-permute-done.15.refs_3_), channel_id=1, source_target_pairs={{0,2},{2,0},{4,6},{6,4},{8,10},{10,8},{12,14},{14,12},{1,3},{3,1},... | collective-permute-start | bytes 294920 | tf_op jit(solution)/shard_map/ppermute | solution.py:564
  51.0 5.5 %collective-permute-start.18 = (bf16[1,192,128]{2,1,0:T(8,128)(2,1)S(1)}, bf16[1,192,128]{2,1,0:T(8,128)(2,1)S(1)}, u32[]{:S(2)}, u32[]{:S(2)}) collective-permute-start(bf16[1,192,128]{2,1,0:T(8,128)(2,1)S(1)} %get-tuple-element.113.refs_1_), channel_id=1, source_target_pairs={{0,8},{2,10},{4,12},{6,14},{8,0},{10,2},{12,4},{14,6},{1,9},{3,11}... | collective-permute-start | bytes 147464 | tf_op jit(solution)/shard_map/ppermute | solution.py:567
  53.6 8.1 %collective-permute-start.21 = (bf16[2,384,128]{2,1,0:T(8,128)(2,1)S(1)}, bf16[2,384,128]{2,1,0:T(8,128)(2,1)S(1)}, u32[]{:S(2)}, u32[]{:S(2)}) collective-permute-start(bf16[2,384,128]{2,1,0:T(8,128)(2,1)S(1)} %collective-permute-done.19.refs_3_), channel_id=1, source_target_pairs={{0,2},{2,0},{4,6},{6,4},{8,10},{10,8},{12,14},{14,12},{1,3},{3,1},... | collective-permute-start | bytes 589832 | tf_op jit(solution)/shard_map/ppermute | solution.py:564
  56.5 4.7 %collective-permute-start.22 = (bf16[2,192,128]{2,1,0:T(8,128)(2,1)S(1)}, bf16[2,192,128]{2,1,0:T(8,128)(2,1)S(1)}, u32[]{:S(2)}, u32[]{:S(2)}) collective-permute-start(bf16[2,192,128]{2,1,0:T(8,128)(2,1)S(1)} %get-tuple-element.119.refs_2_), channel_id=1, source_target_pairs={{0,4},{2,6},{4,0},{6,2},{8,12},{10,14},{12,8},{14,10},{1,5},{3,7},... | collective-permute-start | bytes 294920 | tf_op jit(solution)/shard_map/ppermute | solution.py:567
  57.5 6.1 %collective-permute-start.23 = (bf16[2,192,128]{2,1,0:T(8,128)(2,1)S(1)}, bf16[2,192,128]{2,1,0:T(8,128)(2,1)S(1)}, u32[]{:S(2)}, u32[]{:S(2)}) collective-permute-start(bf16[2,192,128]{2,1,0:T(8,128)(2,1)S(1)} %get-tuple-element.119.refs_2_), channel_id=1, source_target_pairs={{0,2},{2,0},{4,6},{6,4},{8,10},{10,8},{12,14},{14,12},{1,3},{3,1},... | collective-permute-start | bytes 294920 | tf_op jit(solution)/shard_map/ppermute | solution.py:564
  61.2 4.6 %collective-permute-start.24 = (bf16[2,192,128]{2,1,0:T(8,128)(2,1)S(1)}, bf16[2,192,128]{2,1,0:T(8,128)(2,1)S(1)}, u32[]{:S(2)}, u32[]{:S(2)}) collective-permute-start(bf16[2,192,128]{2,1,0:T(8,128)(2,1)S(1)} %collective-permute-done.22.refs_3_), channel_id=1, source_target_pairs={{0,2},{2,0},{4,6},{6,4},{8,10},{10,8},{12,14},{14,12},{1,3},{3,1},... | collective-permute-start | bytes 294920 | tf_op jit(solution)/shard_map/ppermute | solution.py:564
  67.5 1.4 %collective-permute-start.25 = (bf16[96,1024]{1,0:T(8,128)(2,1)S(1)}, bf16[96,1024]{1,0:T(8,128)(2,1)S(1)}, u32[]{:S(2)}, u32[]{:S(2)}) collective-permute-start(bf16[96,1024]{1,0:T(8,128)(2,1)S(1)} %get-tuple-element.122), channel_id=1, source_target_pairs={{0,1},{1,0},{2,3},{3,2},{4,5},{5,4},{6,7},{7,6},{8,9},{9,8},{10,11... | collective-permute-start | bytes 589832 | tf_op jit(solution)/shard_map/ppermute | solution.py:703

commit v12 on v11

--- a/solution.py
+++ b/solution.py
@@ -22,9 +22,9 @@
 F32 = jnp.float32
 BF16 = jnp.bfloat16
 MIB = 1024 * 1024
-SLOTS_AT_ONCE = {1: 8, 2: 8, 3: 8, 4: 4}
+SLOTS_AT_ONCE = {1: 24, 2: 8, 3: 8, 4: 4}
 PEAK_FLOP_PER_US = 1.1535e9
-COSTS = {'project0': 1.22, 'add_far0': 0.1, 'add_near0_2': 0.1, 'attend0': 1.9, 'join0_1': 0.1, 'join0': 0.1, 'output0': 1.4, 'project1': 1.8, 'add_far1': 0.1, 'add_near1_2': 0.1, 'attend1': 2.35, 'join1_1': 0.1, 'join1': 0.1, 'output1': 2, 'project2': 1.22, 'add_far2': 0.1, 'add_near2_2': 0.1, 'attend2': 1.9, 'join2': 0.1, 'output2': 4}
+COSTS = {'attend0': 2, 'output0': 16, 'project1': 1, 'join1': 4, 'output1': 4, 'project2': 1, 'attend2': 4, 'join2': 8, 'join0_1': 4, 'add_near2_2': 1, 'join1_1': 0.3, 'project0': 16, 'output2': 16}
 Y_IN_HALVES = (True, True, True)
 GATHER = ('y halved', 'y halved', 'y halved')
 ORDER = (
@@ -32,11 +32,11 @@
     ("weights", 1),
     ("project", 0),
     ("project", 1),
+    ("weights", 2),
     ("far", 0),
-    ("weights", 2),
     ("far", 1),
+    ("project", 2),
     ("near", 0),
-    ("project", 2),
     ("near", 1),
     ("far", 2),
     ("attend", 0),
@@ -44,9 +44,9 @@
     ("near", 2),
     ("gather", 0),
     ("gather", 1),
+    ("forward", 0),
     ("attend", 2),
     ("forward", 1),
-    ("forward", 0),
     ("output", 0),
     ("gather", 2),
     ("forward", 2),
@@ -176,7 +176,7 @@
         high = squares.astype(BF16).astype(F32)
         low = squares - high
         lane = lax.broadcasted_iota(jnp.int32, (per, HEAD_SIZE), 1)
-        lane_high = place_ref[1] * 2
+        lane_high = (place_ref[0] * 2 + place_ref[1]) * 2
         for at, ref, z in places:
             packed = jnp.where(
                 lane == lane_high,
@@ -436,7 +436,7 @@
         acc_in_ref, rest = rest[0], rest[1:]
     w_ref, rest = rest[0], rest[1:]
     if last:
-        mine_ref, send_ref, stacked = rest
+        send_ref, stacked = rest
     else:
         acc_out_ref, *rest, stacked = rest
     tiles = block_refs[0].shape[1] // per
@@ -461,18 +461,33 @@
         stacked[:, c * HEAD_SIZE : (c + 1) * HEAD_SIZE] = jnp.concatenate(
             [block[c * per : (c + 1) * per] for block in wide], axis=0
         ).astype(BF16)
-    stacked[...] = jnp.dot(one_hot, stacked[...], preferred_element_type=F32).astype(BF16)
+    if last:
+        half = one_hot.shape[0] // 2
+        one_hot, acc = one_hot[half:], acc_in_ref[half:]
+    permuted = jnp.dot(one_hot, stacked[...], preferred_element_type=F32).astype(BF16)
     product = jnp.dot(
-        stacked[...], w_ref[start_depth : start_depth + depth, :], preferred_element_type=F32
-    )
-    if not first:
-        product = product + acc_in_ref[...]
+        permuted, w_ref[start_depth : start_depth + depth, :], preferred_element_type=F32
+    )
     if last:
-        half = product.shape[0] // 2
-        mine_ref[...] = product[:half]
-        send_ref[...] = product[half:].astype(BF16)
+        send_ref[...] = (product + acc).astype(BF16)
+    elif first:
+        acc_out_ref[...] = product
     else:
-        acc_out_ref[...] = product
+        acc_out_ref[...] = product + acc_in_ref[...]
+
+
+def own_output_kernel(
+    stacked_ref, order_ref, acc_ref, hidden_ref, w_ref, mine_ref, *, start_depth
+):
+    half = mine_ref.shape[0]
+    depth = stacked_ref.shape[1]
+    permuted = jnp.dot(order_ref[:half], stacked_ref[...], preferred_element_type=F32)
+    product = jnp.dot(
+        permuted.astype(BF16),
+        w_ref[start_depth : start_depth + depth, :],
+        preferred_element_type=F32,
+    )
+    mine_ref[...] = hidden_ref[...].astype(F32) + (product + acc_ref[:half])
 
 
 def output(token, place, blocks, labels, order, w_out, acc, loads, *, chunk, chunks, nz, per):
@@ -481,7 +496,7 @@
     width = w_out.shape[1]
     depth = CHUNK_HEADS[chunk] * QUERIES_PER_KV * HEAD_SIZE
     if last:
-        out_shapes = [((rows // 2, width), F32), ((rows // 2, width), BF16)]
+        out_shapes = [((rows // 2, width), BF16), ((rows, depth), BF16)]
     else:
         out_shapes = [((rows, width), F32)] + ([((rows, rows), BF16)] if first else [])
     return call(
@@ -499,11 +514,28 @@
         [place],
         [*blocks, order] + ([] if first else [acc]),
         out_shapes,
-        [pltpu.VMEM((rows, depth), BF16)],
+        [] if last else [pltpu.VMEM((rows, depth), BF16)],
         12,
         loads,
         [w_out],
     )
+
+
+def own_output(token, stacked, order, acc, hidden, w_out, *, chunk):
+    start = sum(CHUNK_HEADS[:chunk]) * QUERIES_PER_KV * HEAD_SIZE
+    token, _, (mine,) = call(
+        functools.partial(own_output_kernel, start_depth=start),
+        "own_output",
+        token,
+        [],
+        [stacked, order, acc, hidden],
+        [(hidden.shape, F32)],
+        [],
+        12,
+        (),
+        [w_out],
+    )
+    return token, mine
 
 
 def on_device(
@@ -670,11 +702,14 @@
             chunk=c, chunks=chunks, nz=nz, per=per,
         )
         file_loaded(wanted, arrays)
+        if c == chunks - 1:
+            send, stacked = outs
+            token, mine = own_output(token, stacked, order, acc, hidden_rows, w_out, chunk=c)
+            acc = mine, send
+            return token
         acc = outs[0]
         if c == 0:
             order = outs[1]
-        if c == chunks - 1:
-            acc = outs
         return token
 
     token = jnp.zeros(TOKEN, F32)
@@ -701,7 +736,7 @@
         wanted = []
     mine, send = acc
     received = lax.ppermute(send, "gy", [(0, 1), (1, 0)])
-    return (hidden_rows.astype(F32) + mine + received.astype(F32)).astype(BF16)
+    return (mine + received.astype(F32)).astype(BF16)
 
 
 def solution(mesh):

time: 70.1 us -> 68.7 us (0.980)
  waiting for transfers between devices: 9.28 us -> 6.47 us
  starting transfers between devices: 37.8 us -> 39.2 us
    ppermute x6, starting transfers between devices: 5.3 us -> 9.5 us  [over_y(): return (lax.ppermute(blocks, 'gx', same_z), [(1 - h, q) for h, q in labels])]
    ppermute x6, starting transfers between devices: 12.6 us -> 10.8 us  [over_z(): moved = lax.ppermute(blocks, 'gx', stride_pairs(nz, stride))]
    ppermute x6, waiting for transfers between devices: 2.2 us -> 0.74 us  [over_y(): return (lax.ppermute(blocks, 'gx', same_z), [(1 - h, q) for h, q in labels])]
    ppermute x3, waiting for transfers between devices: 1.06 us -> 2.41 us  [do_project(): far = lax.ppermute(outs[2], 'gx', same_z)]
    ppermute x3, starting transfers between devices: 5 us -> 3.86 us  [do_project(): swapped[c] = ((lax.ppermute(outs[1], 'gx', same_z), 0), (far, 0))]
    ppermute x1, waiting for transfers between devices: 1.44 us -> 0.37 us  [on_device(): received = lax.ppermute(send, 'gy', [(0, 1), (1, 0)])]
    ppermute x3, waiting for transfers between devices: 1.28 us -> 0.26 us  [do_project(): swapped[c] = ((lax.ppermute(outs[1], 'gx', same_z), 0), (far, 0))]
    pallas_call x20 -> x21, Pallas kernels: 21.3 us -> 21.4 us  [call(): pl.pallas_call(body, in_specs=[vmem] + [pl.BlockSpec(memory_space=pltpu.H...]
  transfers between devices with their start and end apart: 26 -> 26, of which waited for: 8 -> 6; matrix products, arithmetic and copies ran while one was open for 0% -> 0% of each run, Pallas kernels for 26% -> 27%
where the time goes in v12:
time: 68.7 us; the launch traced here: 68.5 us
  starting transfers between devices  39.2 us (57%)
  Pallas kernels  21.4 us (31%)
  waiting for transfers between devices  6.47 us (9%)
  other arithmetic  1.02 us (1%)
    pallas_call x21, Pallas kernels, call(): pl.pallas_call(body, in_specs=[vmem] + [pl.BlockSpec(memory_space=pltpu.H...  21.4 us
    ppermute x6, starting transfers between devices, over_z(): moved = lax.ppermute(blocks, 'gx', stride_pairs(nz, stride))  10.8 us
    ppermute x6, starting transfers between devices, over_y(): return (lax.ppermute(blocks, 'gx', same_z), [(1 - h, q) for h, q in labels])  9.5 us
    ppermute x3, starting transfers between devices, do_near(): terms = [mine, lax.ppermute(sent, 'gx', stride_pairs(nz, stride))]  5.73 us
    ppermute x3, starting transfers between devices, do_far(): reduced[c] = lax.ppermute(total, 'gx', stride_pairs(nz, 1))  4.92 us
    ppermute x3, starting transfers between devices, do_project(): far = lax.ppermute(outs[2], 'gx', same_z)  3.89 us
    ppermute x3, starting transfers between devices, do_project(): swapped[c] = ((lax.ppermute(outs[1], 'gx', same_z), 0), (far, 0))  3.86 us
    ppermute x6, waiting for transfers between devices, over_z(): moved = lax.ppermute(blocks, 'gx', stride_pairs(nz, stride))  2.67 us
  transfers between devices with their start and end apart: 26, of which 6 were waited for; matrix products, arithmetic and copies ran while one was open for 0% of the time, Pallas kernels for 27%

profile of v12, /device:TPU:0, one launch (start us, length us, event | category | flops | bytes accessed | tf_op | source)
XLA Modules:
  0.0 68.5 jit_solution(7652595196375415647)
XLA Ops:
  0.0 0.5 collective-permute-start
  0.5 3.3 %load_weights0_weights1.1 = (f32[8,128]{1,0:T(8,128)S(1)}, bf16[1024,1024]{1,0:T(8,128)(2,1)S(1)}, bf16[1024,128]{1,0:T(8,128)(2,1)S(1)}, bf16[1024,128]{1,0:T(8...) custom-call(f32[8,128]{1,0:T(8,128)S(1)} %broadcast_in_dim.17.refs_0_, ...), custom_call_target="tpu_custom_call" | custom-call | tf_op jit(solution)/shard_map/load_weights0_weights1/pallas_call | solution.py:131
  3.8 0.1 pad_add_fusion.refs_1_
  3.9 1.4 %project0.1 = (f32[8,128]{1,0:T(8,128)S(1)}, bf16[4,272,128]{2,1,0:T(8,128)(2,1)S(1)}, bf16[2,272,128]{2,1,0:T(8,128)(2,1)S(1)}, bf16[2,272,128]{2,1,0:T(8,128)(2,1)S(1)}, bf16[192,1024]{1,0:T(8,128)(2,1)S(1)}) custom-call(f32[8,128]{1,0:T(8,128)S(1)} %get-tuple-element.66.refs_0_, s32[3]{0:T(128)S(1)} %pad_add_fusion.refs_1_, ...), custom_call_target="tpu_custom_call" | custom-call | flops 18456000512 | tf_op jit(solution)/shard_map/project0/pallas_call | solution.py:131
  5.3 2.6 %collective-permute-start.1 = (bf16[2,272,128]{2,1,0:T(8,128)(2,1)S(1)}, bf16[2,272,128]{2,1,0:T(8,128)(2,1)S(1)}, u32[]{:S(2)}, u32[]{:S(2)}) collective-permute-start(bf16[2,272,128]{2,1,0:T(8,128)(2,1)S(1)} %get-tuple-element.78), channel_id=1, source_target_pairs={{0,2},{2,0},{4,6},{6,4},{8,10},{10,8},{12,14},{14,12},{1,3},{3,1},... | collective-permute-start | bytes 417800 | tf_op jit(solution)/shard_map/ppermute | solution.py:633
  8.0 1.8 %project1.1 = (f32[8,128]{1,0:T(8,128)S(1)}, bf16[4,480,128]{2,1,0:T(8,128)(2,1)S(1)}, bf16[2,480,128]{2,1,0:T(8,128)(2,1)S(1)}, bf16[2,480,128]{2,1,0:T(8,128)(2,1)S(1)}) custom-call(f32[8,128]{1,0:T(8,128)S(1)} %get-tuple-element.70.refs_0_, s32[3]{0:T(128)S(1)} %pad_add_fusion.refs_1_, bf16[192,1024]{1,0:T(8,128)(2,1)S(1)} %get-tuple-element.71.refs_2_, ...), custom_call_target="tpu_custom_call" | custom-call | flops 1153500032 | tf_op jit(solution)/shard_map/project1/pallas_call | solution.py:131
  9.8 0.1 collective-permute-start.2
  9.9 1.7 %load_weights2.1 = (f32[8,128]{1,0:T(8,128)S(1)}, bf16[1024,1024]{1,0:T(8,128)(2,1)S(1)}, bf16[1024,128]{1,0:T(8,128)(2,1)S(1)}, bf16[1024,128]{1,0:T(8,128)(2,1)S(1)}) custom-call(f32[8,128]{1,0:T(8,128)S(1)} %get-tuple-element.75.refs_0_, bf16[1024,4096]{1,0:T(8,128)(2,1)} %refs_1_.3, bf16[1024,512]{1,0:T(8,128)(2,1)} %refs_2_.8, bf16[1024,512]{1,0:T(8,128)(2,1)} %refs_3_.3), custom_call_target="tpu_custom_call" | custom-call | tf_op jit(solution)/shard_map/load_weights2/pallas_call | solution.py:131
  11.6 2.1 %collective-permute-start.3 = (bf16[2,272,128]{2,1,0:T(8,128)(2,1)S(1)}, bf16[2,272,128]{2,1,0:T(8,128)(2,1)S(1)}, u32[]{:S(2)}, u32[]{:S(2)}) collective-permute-start(bf16[2,272,128]{2,1,0:T(8,128)(2,1)S(1)} %get-tuple-element.87), channel_id=1, source_target_pairs={{0,2},{2,0},{4,6},{6,4},{8,10},{10,8},{12,14},{14,12},{1,3},{3,1},... | collective-permute-start | bytes 417800 | tf_op jit(solution)/shard_map/ppermute | solution.py:634
  13.7 1.6 %collective-permute-start.4 = (bf16[2,272,128]{2,1,0:T(8,128)(2,1)S(1)}, bf16[2,272,128]{2,1,0:T(8,128)(2,1)S(1)}, u32[]{:S(2)}, u32[]{:S(2)}) collective-permute-start(bf16[2,272,128]{2,1,0:T(8,128)(2,1)S(1)} %get-tuple-element.88), channel_id=1, source_target_pairs={{0,4},{2,6},{4,0},{6,2},{8,12},{10,14},{12,8},{14,10},{1,5},{3,7},... | collective-permute-start | bytes 417800 | tf_op jit(solution)/shard_map/ppermute | solution.py:645
  15.3 0.1 dynamic-slice_convert_fusion
  15.4 0.8 %collective-permute-start.5 = (bf16[2,480,128]{2,1,0:T(8,128)(2,1)S(1)}, bf16[2,480,128]{2,1,0:T(8,128)(2,1)S(1)}, u32[]{:S(2)}, u32[]{:S(2)}) collective-permute-start(bf16[2,480,128]{2,1,0:T(8,128)(2,1)S(1)} %get-tuple-element.90), channel_id=1, source_target_pairs={{0,2},{2,0},{4,6},{6,4},{8,10},{10,8},{12,14},{14,12},{1,3},{3,1},... | collective-permute-start | bytes 737288 | tf_op jit(solution)/shard_map/ppermute | solution.py:634
  16.2 2.4 %collective-permute-done.2.refs_2_ = bf16[2,480,128]{2,1,0:T(8,128)(2,1)S(1)} collective-permute-done((bf16[2,480,128]{2,1,0:T(8,128)(2,1)S(1)}, bf16[2,480,128]{2,1,0:T(8,128)(2,1)S(1)}, u32[]{:S(2)}, u32[]{:S(2)}) %collective-permute-start.2) | collective-permute-done | bytes 245792 | tf_op jit(solution)/shard_map/ppermute | solution.py:633
  18.7 1.6 %collective-permute-start.6 = (bf16[2,480,128]{2,1,0:T(8,128)(2,1)S(1)}, bf16[2,480,128]{2,1,0:T(8,128)(2,1)S(1)}, u32[]{:S(2)}, u32[]{:S(2)}) collective-permute-start(bf16[2,480,128]{2,1,0:T(8,128)(2,1)S(1)} %get-tuple-element.91), channel_id=1, source_target_pairs={{0,4},{2,6},{4,0},{6,2},{8,12},{10,14},{12,8},{14,10},{1,5},{3,7},... | collective-permute-start | bytes 737288 | tf_op jit(solution)/shard_map/ppermute | solution.py:645
  20.4 1.2 %project2.1 = (f32[8,128]{1,0:T(8,128)S(1)}, bf16[4,240,128]{2,1,0:T(8,128)(2,1)S(1)}, bf16[2,240,128]{2,1,0:T(8,128)(2,1)S(1)}, bf16[2,240,128]{2,1,0:T(8,128)(2,1)S(1)}) custom-call(f32[8,128]{1,0:T(8,128)S(1)} %get-tuple-element.82.refs_0_, s32[3]{0:T(128)S(1)} %pad_add_fusion.refs_1_, bf16[192,1024]{1,0:T(8,128)(2,1)S(1)} %get-tuple-element.71.refs_2_, ...), custom_call_target="tpu_custom_call" | custom-call | flops 1153500032 | tf_op jit(solution)/shard_map/project2/pallas_call | solution.py:131
  21.6 1.2 %collective-permute-start.7 = (bf16[2,240,128]{2,1,0:T(8,128)(2,1)S(1)}, bf16[2,240,128]{2,1,0:T(8,128)(2,1)S(1)}, u32[]{:S(2)}, u32[]{:S(2)}) collective-permute-start(bf16[2,240,128]{2,1,0:T(8,128)(2,1)S(1)} %get-tuple-element.94), channel_id=1, source_target_pairs={{0,2},{2,0},{4,6},{6,4},{8,10},{10,8},{12,14},{14,12},{1,3},{3,1},... | collective-permute-start | bytes 368648 | tf_op jit(solution)/shard_map/ppermute | solution.py:633
  22.9 2.7 %collective-permute-start.8 = (bf16[1,272,128]{2,1,0:T(8,128)(2,1)S(1)}, bf16[1,272,128]{2,1,0:T(8,128)(2,1)S(1)}, u32[]{:S(2)}, u32[]{:S(2)}) collective-permute-start(bf16[1,272,128]{2,1,0:T(8,128)(2,1)S(1)} %get-tuple-element.97), channel_id=1, source_target_pairs={{0,8},{2,10},{4,12},{6,14},{8,0},{10,2},{12,4},{14,6},{1,9},{3,11}... | collective-permute-start | bytes 208904 | tf_op jit(solution)/shard_map/ppermute | solution.py:654
  25.5 0.1 fusion
  25.6 1.0 %collective-permute-start.10 = (bf16[2,240,128]{2,1,0:T(8,128)(2,1)S(1)}, bf16[2,240,128]{2,1,0:T(8,128)(2,1)S(1)}, u32[]{:S(2)}, u32[]{:S(2)}) collective-permute-start(bf16[2,240,128]{2,1,0:T(8,128)(2,1)S(1)} %get-tuple-element.103), channel_id=1, source_target_pairs={{0,2},{2,0},{4,6},{6,4},{8,10},{10,8},{12,14},{14,12},{1,3},{3,1},... | collective-permute-start | bytes 368648 | tf_op jit(solution)/shard_map/ppermute | solution.py:634
  26.6 0.3 collective-permute-done.5.refs_2_
  26.9 0.1 add_near1_2.1
  27.0 2.6 %collective-permute-start.9 = (bf16[1,480,128]{2,1,0:T(8,128)(2,1)S(1)}, bf16[1,480,128]{2,1,0:T(8,128)(2,1)S(1)}, u32[]{:S(2)}, u32[]{:S(2)}) collective-permute-start(bf16[1,480,128]{2,1,0:T(8,128)(2,1)S(1)} %get-tuple-element.100), channel_id=1, source_target_pairs={{0,8},{2,10},{4,12},{6,14},{8,0},{10,2},{12,4},{14,6},{1,9},{3,11}... | collective-permute-start | bytes 368648 | tf_op jit(solution)/shard_map/ppermute | solution.py:654
  29.7 1.6 %collective-permute-start.11 = (bf16[2,240,128]{2,1,0:T(8,128)(2,1)S(1)}, bf16[2,240,128]{2,1,0:T(8,128)(2,1)S(1)}, u32[]{:S(2)}, u32[]{:S(2)}) collective-permute-start(bf16[2,240,128]{2,1,0:T(8,128)(2,1)S(1)} %get-tuple-element.104), channel_id=1, source_target_pairs={{0,4},{2,6},{4,0},{6,2},{8,12},{10,14},{12,8},{14,10},{1,5},{3,7},... | collective-permute-start | bytes 368648 | tf_op jit(solution)/shard_map/ppermute | solution.py:645
  31.3 1.9 %attend0.1 = (f32[8,128]{1,0:T(8,128)S(1)}, bf16[1,192,128]{2,1,0:T(8,128)(2,1)S(1)}, f32[24,128]{1,0:T(8,128)S(1)}) custom-call(f32[8,128]{1,0:T(8,128)S(1)} %get-tuple-element.95.refs_0_, s32[3]{0:T(128)S(1)} %pad_add_fusion.refs_1_, s32[192]{0:T(256)S(1)} %copy-done.4, bf16[1,272,128]{2,1,0:T(8,128)(2,1)S(1)} %get-tuple-element.96.refs_3_, ...), custom_call_target="tpu_custom_call" | custom-call | flops 2307000064 | tf_op jit(solution)/shard_map/attend0/pallas_call | solution.py:131
  33.3 2.5 %collective-permute-start.12 = (bf16[1,192,128]{2,1,0:T(8,128)(2,1)S(1)}, bf16[1,192,128]{2,1,0:T(8,128)(2,1)S(1)}, u32[]{:S(2)}, u32[]{:S(2)}) collective-permute-start(bf16[1,192,128]{2,1,0:T(8,128)(2,1)S(1)} %get-tuple-element.106.refs_1_), channel_id=1, source_target_pairs={{0,8},{2,10},{4,12},{6,14},{8,0},{10,2},{12,4},{14,6},{1,9},{3,11}... | collective-permute-start | bytes 147464 | tf_op jit(solution)/shard_map/ppermute | solution.py:599
  35.8 2.4 %attend1.1 = (f32[8,128]{1,0:T(8,128)S(1)}, bf16[1,384,128]{2,1,0:T(8,128)(2,1)S(1)}) custom-call(f32[8,128]{1,0:T(8,128)S(1)} %get-tuple-element.98.refs_0_, s32[3]{0:T(128)S(1)} %pad_add_fusion.refs_1_, s32[192]{0:T(256)S(1)} %copy-done.4, bf16[1,480,128]{2,1,0:T(8,128)(2,1)S(1)} %get-tuple-element.99.refs_3_, ...), custom_call_target="tpu_custom_call" | custom-call | tf_op jit(solution)/shard_map/attend1/pallas_call | solution.py:131
  38.2 0.5 collective-permute-start.13
  38.9 2.6 %collective-permute-start.15 = (bf16[2,192,128]{2,1,0:T(8,128)(2,1)S(1)}, bf16[2,192,128]{2,1,0:T(8,128)(2,1)S(1)}, u32[]{:S(2)}, u32[]{:S(2)}) collective-permute-start(bf16[2,192,128]{2,1,0:T(8,128)(2,1)S(1)} %get-tuple-element.113.refs_2_), channel_id=1, source_target_pairs={{0,4},{2,6},{4,0},{6,2},{8,12},{10,14},{12,8},{14,10},{1,5},{3,7},... | collective-permute-start | bytes 294920 | tf_op jit(solution)/shard_map/ppermute | solution.py:599
  41.4 0.4 collective-permute-start.14
  41.8 1.4 %collective-permute-start.16 = (bf16[2,192,128]{2,1,0:T(8,128)(2,1)S(1)}, bf16[2,192,128]{2,1,0:T(8,128)(2,1)S(1)}, u32[]{:S(2)}, u32[]{:S(2)}) collective-permute-start(bf16[2,192,128]{2,1,0:T(8,128)(2,1)S(1)} %get-tuple-element.113.refs_2_), channel_id=1, source_target_pairs={{0,2},{2,0},{4,6},{6,4},{8,10},{10,8},{12,14},{14,12},{1,3},{3,1},... | collective-permute-start | bytes 294920 | tf_op jit(solution)/shard_map/ppermute | solution.py:596
  43.2 2.1 %collective-permute-done.13.refs_2_ = bf16[1,384,128]{2,1,0:T(8,128)(2,1)S(1)} collective-permute-done((bf16[1,384,128]{2,1,0:T(8,128)(2,1)S(1)}, bf16[1,384,128]{2,1,0:T(8,128)(2,1)S(1)}, u32[]{:S(2)}, u32[]{:S(2)}) %collective-permute-start.13) | collective-permute-done | bytes 98336 | tf_op jit(solution)/shard_map/ppermute | solution.py:599
  45.3 0.1 collective-permute-start.19
  45.4 1.9 %collective-permute-start.20 = (bf16[2,384,128]{2,1,0:T(8,128)(2,1)S(1)}, bf16[2,384,128]{2,1,0:T(8,128)(2,1)S(1)}, u32[]{:S(2)}, u32[]{:S(2)}) collective-permute-start(bf16[2,384,128]{2,1,0:T(8,128)(2,1)S(1)} %get-tuple-element.117.refs_2_), channel_id=1, source_target_pairs={{0,2},{2,0},{4,6},{6,4},{8,10},{10,8},{12,14},{14,12},{1,3},{3,1},... | collective-permute-start | bytes 589832 | tf_op jit(solution)/shard_map/ppermute | solution.py:596
  47.3 0.1 collective-permute-start.17
  47.5 1.8 %attend2.1 = (f32[8,128]{1,0:T(8,128)S(1)}, bf16[1,192,128]{2,1,0:T(8,128)(2,1)S(1)}) custom-call(f32[8,128]{1,0:T(8,128)S(1)} %get-tuple-element.109.refs_0_, s32[3]{0:T(128)S(1)} %pad_add_fusion.refs_1_, s32[192]{0:T(256)S(1)} %copy-done.4, bf16[1,240,128]{2,1,0:T(8,128)(2,1)S(1)} %get-tuple-element.110.refs_3_, ...), custom_call_target="tpu_custom_call" | custom-call | flops 4614000128 | tf_op jit(solution)/shard_map/attend2/pallas_call | solution.py:131
  49.3 2.6 %collective-permute-start.18 = (bf16[1,192,128]{2,1,0:T(8,128)(2,1)S(1)}, bf16[1,192,128]{2,1,0:T(8,128)(2,1)S(1)}, u32[]{:S(2)}, u32[]{:S(2)}) collective-permute-start(bf16[1,192,128]{2,1,0:T(8,128)(2,1)S(1)} %get-tuple-element.115.refs_1_), channel_id=1, source_target_pairs={{0,8},{2,10},{4,12},{6,14},{8,0},{10,2},{12,4},{14,6},{1,9},{3,11}... | collective-permute-start | bytes 147464 | tf_op jit(solution)/shard_map/ppermute | solution.py:599
  52.0 2.0 %collective-permute-start.21 = (bf16[2,384,128]{2,1,0:T(8,128)(2,1)S(1)}, bf16[2,384,128]{2,1,0:T(8,128)(2,1)S(1)}, u32[]{:S(2)}, u32[]{:S(2)}) collective-permute-start(bf16[2,384,128]{2,1,0:T(8,128)(2,1)S(1)} %collective-permute-done.19.refs_3_), channel_id=1, source_target_pairs={{0,2},{2,0},{4,6},{6,4},{8,10},{10,8},{12,14},{14,12},{1,3},{3,1},... | collective-permute-start | bytes 589832 | tf_op jit(solution)/shard_map/ppermute | solution.py:596
  54.0 1.4 %output0.1 = (f32[8,128]{1,0:T(8,128)S(1)}, f32[192,1024]{1,0:T(8,128)S(1)}, bf16[192,192]{1,0:T(8,128)(2,1)S(1)}) custom-call(f32[8,128]{1,0:T(8,128)S(1)} %get-tuple-element.112.refs_0_, s32[3]{0:T(128)S(1)} %pad_add_fusion.refs_1_, bf16[2,192,128]{2,1,0:T(8,128)(2,1)S(1)} %get-tuple-element.113.refs_2_, ...), custom_call_target="tpu_custom_call" | custom-call | flops 18456000512 | tf_op jit(solution)/shard_map/output0/pallas_call | solution.py:131
  55.4 2.5 %collective-permute-start.22 = (bf16[2,192,128]{2,1,0:T(8,128)(2,1)S(1)}, bf16[2,192,128]{2,1,0:T(8,128)(2,1)S(1)}, u32[]{:S(2)}, u32[]{:S(2)}) collective-permute-start(bf16[2,192,128]{2,1,0:T(8,128)(2,1)S(1)} %get-tuple-element.121.refs_2_), channel_id=1, source_target_pairs={{0,4},{2,6},{4,0},{6,2},{8,12},{10,14},{12,8},{14,10},{1,5},{3,7},... | collective-permute-start | bytes 294920 | tf_op jit(solution)/shard_map/ppermute | solution.py:599
  57.9 2.0 %collective-permute-start.23 = (bf16[2,192,128]{2,1,0:T(8,128)(2,1)S(1)}, bf16[2,192,128]{2,1,0:T(8,128)(2,1)S(1)}, u32[]{:S(2)}, u32[]{:S(2)}) collective-permute-start(bf16[2,192,128]{2,1,0:T(8,128)(2,1)S(1)} %get-tuple-element.121.refs_2_), channel_id=1, source_target_pairs={{0,2},{2,0},{4,6},{6,4},{8,10},{10,8},{12,14},{14,12},{1,3},{3,1},... | collective-permute-start | bytes 294920 | tf_op jit(solution)/shard_map/ppermute | solution.py:596
  60.0 0.6 collective-permute-done.22.refs_3_
  60.5 2.0 %collective-permute-start.24 = (bf16[2,192,128]{2,1,0:T(8,128)(2,1)S(1)}, bf16[2,192,128]{2,1,0:T(8,128)(2,1)S(1)}, u32[]{:S(2)}, u32[]{:S(2)}) collective-permute-start(bf16[2,192,128]{2,1,0:T(8,128)(2,1)S(1)} %collective-permute-done.22.refs_3_), channel_id=1, source_target_pairs={{0,2},{2,0},{4,6},{6,4},{8,10},{10,8},{12,14},{14,12},{1,3},{3,1},... | collective-permute-start | bytes 294920 | tf_op jit(solution)/shard_map/ppermute | solution.py:596
  62.6 1.8 %output1.1 = (f32[8,128]{1,0:T(8,128)S(1)}, f32[192,1024]{1,0:T(8,128)S(1)}) custom-call(f32[8,128]{1,0:T(8,128)S(1)} %get-tuple-element.116.refs_0_, s32[3]{0:T(128)S(1)} %pad_add_fusion.refs_1_, bf16[2,384,128]{2,1,0:T(8,128)(2,1)S(1)} %get-tuple-element.117.refs_2_, bf16[2,384,128]{2,1,0:T(8,128)(2,1)S(1)} %collective-permute-done.19.refs_3_, ...), custom_call_target="tpu_custom_call" | custom-call | flops 4614000128 | tf_op jit(solution)/shard_map/output1/pallas_call | solution.py:131
  64.4 0.7 %collective-permute-done.24.refs_5_ = bf16[2,192,128]{2,1,0:T(8,128)(2,1)S(1)} collective-permute-done((bf16[2,192,128]{2,1,0:T(8,128)(2,1)S(1)}, bf16[2,192,128]{2,1,0:T(8,128)(2,1)S(1)}, u32[]{:S(2)}, u32[]{:S(2)}) %collective-permute-start.24) | collective-permute-done | bytes 98336 | tf_op jit(solution)/shard_map/ppermute | solution.py:596
  65.1 1.2 %output2.1 = (f32[8,128]{1,0:T(8,128)S(1)}, bf16[96,1024]{1,0:T(8,128)(2,1)S(1)}, bf16[192,1024]{1,0:T(8,128)(2,1)S(1)}) custom-call(f32[8,128]{1,0:T(8,128)S(1)} %get-tuple-element.120.refs_0_, s32[3]{0:T(128)S(1)} %pad_add_fusion.refs_1_, bf16[2,192,128]{2,1,0:T(8,128)(2,1)S(1)} %get-tuple-element.121.refs_2_, ...), custom_call_target="tpu_custom_call" | custom-call | flops 18456000512 | tf_op jit(solution)/shard_map/output2/pallas_call | solution.py:131
  66.4 1.1 %own_output.1 = (f32[8,128]{1,0:T(8,128)}, f32[96,1024]{1,0:T(8,128)S(1)}) custom-call(f32[8,128]{1,0:T(8,128)S(1)} %get-tuple-element.123.refs_0_, bf16[192,1024]{1,0:T(8,128)(2,1)S(1)} %get-tuple-element.124.refs_1_, bf16[192,192]{1,0:T(8,128)(2,1)S(1)} %get-tuple-element.118.refs_6_.refs_2_, f32[192,1024]{1,0:T(8,128)S(1)} %get-tuple-element.122.refs_7_.refs_3_, ...), custom_call_target="tpu_custom_call" | custom-call | tf_op jit(solution)/shard_map/own_output/pallas_call | solution.py:131
  67.4 0.4 collective-permute-done.25
  67.8 0.7 %add_convert_fusion = bf16[96,1024]{1,0:T(8,128)(2,1)} fusion(f32[96,1024]{1,0:T(8,128)S(1)} %get-tuple-element.125, bf16[96,1024]{1,0:T(8,128)(2,1)S(1)} %collective-permute-done.25), kind=kLoop, calls=%fused_computation | loop fusion | flops 294912 | bytes 786432 | tf_op jit(solution)/shard_map/convert_element_type | solution.py:739
  (54 shorter events, 0.5 us)
Async XLA Ops:
  0.0 3.9 %collective-permute-start = (bf16[96,1024]{1,0:T(8,128)(2,1)}, bf16[96,1024]{1,0:T(8,128)(2,1)S(1)}, u32[]{:S(2)}, u32[]{:S(2)}) collective-permute-start(bf16[96,1024]{1,0:T(8,128)(2,1)} %refs_4_.3), channel_id=1, source_target_pairs={{0,1},{1,0},{2,3},{3,2},{4,5},{5,4},{6,7},{7,6},{8,9},{9,8},{10,11... | collective-permute-start | bytes 589832 | tf_op jit(solution)/shard_map/ppermute | solution.py:568
  0.5 3.4 %copy-start.2 = (bf16[96,1024]{1,0:T(8,128)(2,1)S(1)}, bf16[96,1024]{1,0:T(8,128)(2,1)}, u32[]{:S(2)}) copy-start(bf16[96,1024]{1,0:T(8,128)(2,1)} %refs_4_.3) | copy-start | bytes 589828
  0.5 3.4 %copy-start.7 = (bf16[1024]{0:T(1024)(128)(2,1)S(1)}, bf16[1024]{0:T(1024)(128)(2,1)}, u32[]{:S(2)}) copy-start(bf16[1024]{0:T(1024)(128)(2,1)} %param.14) | copy-start | bytes 6148
  0.5 3.4 %copy-start.8 = (s32[192]{0:T(256)S(1)}, s32[192]{0:T(256)}, u32[]{:S(2)}) copy-start(s32[192]{0:T(256)} %param.24) | copy-start | bytes 2308
  5.3 8.3 %collective-permute-start.1 = (bf16[2,272,128]{2,1,0:T(8,128)(2,1)S(1)}, bf16[2,272,128]{2,1,0:T(8,128)(2,1)S(1)}, u32[]{:S(2)}, u32[]{:S(2)}) collective-permute-start(bf16[2,272,128]{2,1,0:T(8,128)(2,1)S(1)} %get-tuple-element.78), channel_id=1, source_target_pairs={{0,2},{2,0},{4,6},{6,4},{8,10},{10,8},{12,14},{14,12},{1,3},{3,1},... | collective-permute-start | bytes 417800 | tf_op jit(solution)/shard_map/ppermute | solution.py:633
  9.8 8.9 %collective-permute-start.2 = (bf16[2,480,128]{2,1,0:T(8,128)(2,1)S(1)}, bf16[2,480,128]{2,1,0:T(8,128)(2,1)S(1)}, u32[]{:S(2)}, u32[]{:S(2)}) collective-permute-start(bf16[2,480,128]{2,1,0:T(8,128)(2,1)S(1)} %get-tuple-element.81), channel_id=1, source_target_pairs={{0,2},{2,0},{4,6},{6,4},{8,10},{10,8},{12,14},{14,12},{1,3},{3,1},... | collective-permute-start | bytes 737288 | tf_op jit(solution)/shard_map/ppermute | solution.py:633
  9.9 5.5 %copy-start.4 = (s32[192]{0:T(256)S(1)}, s32[192]{0:T(256)}, u32[]{:S(2)}) copy-start(s32[192]{0:T(256)} %refs_2_.11) | copy-start | bytes 2308
  11.6 11.2 %collective-permute-start.3 = (bf16[2,272,128]{2,1,0:T(8,128)(2,1)S(1)}, bf16[2,272,128]{2,1,0:T(8,128)(2,1)S(1)}, u32[]{:S(2)}, u32[]{:S(2)}) collective-permute-start(bf16[2,272,128]{2,1,0:T(8,128)(2,1)S(1)} %get-tuple-element.87), channel_id=1, source_target_pairs={{0,2},{2,0},{4,6},{6,4},{8,10},{10,8},{12,14},{14,12},{1,3},{3,1},... | collective-permute-start | bytes 417800 | tf_op jit(solution)/shard_map/ppermute | solution.py:634
  13.7 9.1 %collective-permute-start.4 = (bf16[2,272,128]{2,1,0:T(8,128)(2,1)S(1)}, bf16[2,272,128]{2,1,0:T(8,128)(2,1)S(1)}, u32[]{:S(2)}, u32[]{:S(2)}) collective-permute-start(bf16[2,272,128]{2,1,0:T(8,128)(2,1)S(1)} %get-tuple-element.88), channel_id=1, source_target_pairs={{0,4},{2,6},{4,0},{6,2},{8,12},{10,14},{12,8},{14,10},{1,5},{3,7},... | collective-permute-start | bytes 417800 | tf_op jit(solution)/shard_map/ppermute | solution.py:645
  15.4 11.5 %collective-permute-start.5 = (bf16[2,480,128]{2,1,0:T(8,128)(2,1)S(1)}, bf16[2,480,128]{2,1,0:T(8,128)(2,1)S(1)}, u32[]{:S(2)}, u32[]{:S(2)}) collective-permute-start(bf16[2,480,128]{2,1,0:T(8,128)(2,1)S(1)} %get-tuple-element.90), channel_id=1, source_target_pairs={{0,2},{2,0},{4,6},{6,4},{8,10},{10,8},{12,14},{14,12},{1,3},{3,1},... | collective-permute-start | bytes 737288 | tf_op jit(solution)/shard_map/ppermute | solution.py:634
  18.6 12.7 %copy-start.1 = (bf16[24,128,512]{2,1,0:T(8,128)(2,1)S(1)}, bf16[24,128,512]{2,1,0:T(8,128)(2,1)}, u32[]{:S(2)}) copy-start(bf16[24,128,512]{2,1,0:T(8,128)(2,1)} %refs_12_.3) | copy-start | bytes 9437188
  18.7 12.6 %copy-start = (bf16[24,128,512]{2,1,0:T(8,128)(2,1)S(1)}, bf16[24,128,512]{2,1,0:T(8,128)(2,1)}, u32[]{:S(2)}) copy-start(bf16[24,128,512]{2,1,0:T(8,128)(2,1)} %refs_11_.5) | copy-start | bytes 9437188
  18.7 12.6 %copy-start.3 = (bf16[4096]{0:T(1024)(128)(2,1)S(1)}, bf16[4096]{0:T(1024)(128)(2,1)}, u32[]{:S(2)}) copy-start(bf16[4096]{0:T(1024)(128)(2,1)} %param.18) | copy-start | bytes 24580
  18.7 12.6 %copy-start.5 = (bf16[512]{0:T(512)(128)(2,1)S(1)}, bf16[512]{0:T(512)(128)(2,1)}, u32[]{:S(2)}) copy-start(bf16[512]{0:T(512)(128)(2,1)} %param.19) | copy-start | bytes 3076
  18.7 12.6 %copy-start.6 = (bf16[512]{0:T(512)(128)(2,1)S(1)}, bf16[512]{0:T(512)(128)(2,1)}, u32[]{:S(2)}) copy-start(bf16[512]{0:T(512)(128)(2,1)} %param.20) | copy-start | bytes 3076
  18.7 8.1 %collective-permute-start.6 = (bf16[2,480,128]{2,1,0:T(8,128)(2,1)S(1)}, bf16[2,480,128]{2,1,0:T(8,128)(2,1)S(1)}, u32[]{:S(2)}, u32[]{:S(2)}) collective-permute-start(bf16[2,480,128]{2,1,0:T(8,128)(2,1)S(1)} %get-tuple-element.91), channel_id=1, source_target_pairs={{0,4},{2,6},{4,0},{6,2},{8,12},{10,14},{12,8},{14,10},{1,5},{3,7},... | collective-permute-start | bytes 737288 | tf_op jit(solution)/shard_map/ppermute | solution.py:645
  21.6 8.0 %collective-permute-start.7 = (bf16[2,240,128]{2,1,0:T(8,128)(2,1)S(1)}, bf16[2,240,128]{2,1,0:T(8,128)(2,1)S(1)}, u32[]{:S(2)}, u32[]{:S(2)}) collective-permute-start(bf16[2,240,128]{2,1,0:T(8,128)(2,1)S(1)} %get-tuple-element.94), channel_id=1, source_target_pairs={{0,2},{2,0},{4,6},{6,4},{8,10},{10,8},{12,14},{14,12},{1,3},{3,1},... | collective-permute-start | bytes 368648 | tf_op jit(solution)/shard_map/ppermute | solution.py:633
  22.9 8.4 %collective-permute-start.8 = (bf16[1,272,128]{2,1,0:T(8,128)(2,1)S(1)}, bf16[1,272,128]{2,1,0:T(8,128)(2,1)S(1)}, u32[]{:S(2)}, u32[]{:S(2)}) collective-permute-start(bf16[1,272,128]{2,1,0:T(8,128)(2,1)S(1)} %get-tuple-element.97), channel_id=1, source_target_pairs={{0,8},{2,10},{4,12},{6,14},{8,0},{10,2},{12,4},{14,6},{1,9},{3,11}... | collective-permute-start | bytes 208904 | tf_op jit(solution)/shard_map/ppermute | solution.py:654
  25.6 13.1 %collective-permute-start.10 = (bf16[2,240,128]{2,1,0:T(8,128)(2,1)S(1)}, bf16[2,240,128]{2,1,0:T(8,128)(2,1)S(1)}, u32[]{:S(2)}, u32[]{:S(2)}) collective-permute-start(bf16[2,240,128]{2,1,0:T(8,128)(2,1)S(1)} %get-tuple-element.103), channel_id=1, source_target_pairs={{0,2},{2,0},{4,6},{6,4},{8,10},{10,8},{12,14},{14,12},{1,3},{3,1},... | collective-permute-start | bytes 368648 | tf_op jit(solution)/shard_map/ppermute | solution.py:634
  27.0 8.9 %collective-permute-start.9 = (bf16[1,480,128]{2,1,0:T(8,128)(2,1)S(1)}, bf16[1,480,128]{2,1,0:T(8,128)(2,1)S(1)}, u32[]{:S(2)}, u32[]{:S(2)}) collective-permute-start(bf16[1,480,128]{2,1,0:T(8,128)(2,1)S(1)} %get-tuple-element.100), channel_id=1, source_target_pairs={{0,8},{2,10},{4,12},{6,14},{8,0},{10,2},{12,4},{14,6},{1,9},{3,11}... | collective-permute-start | bytes 368648 | tf_op jit(solution)/shard_map/ppermute | solution.py:654
  29.7 9.1 %collective-permute-start.11 = (bf16[2,240,128]{2,1,0:T(8,128)(2,1)S(1)}, bf16[2,240,128]{2,1,0:T(8,128)(2,1)S(1)}, u32[]{:S(2)}, u32[]{:S(2)}) collective-permute-start(bf16[2,240,128]{2,1,0:T(8,128)(2,1)S(1)} %get-tuple-element.104), channel_id=1, source_target_pairs={{0,4},{2,6},{4,0},{6,2},{8,12},{10,14},{12,8},{14,10},{1,5},{3,7},... | collective-permute-start | bytes 368648 | tf_op jit(solution)/shard_map/ppermute | solution.py:645
  33.3 5.5 %collective-permute-start.12 = (bf16[1,192,128]{2,1,0:T(8,128)(2,1)S(1)}, bf16[1,192,128]{2,1,0:T(8,128)(2,1)S(1)}, u32[]{:S(2)}, u32[]{:S(2)}) collective-permute-start(bf16[1,192,128]{2,1,0:T(8,128)(2,1)S(1)} %get-tuple-element.106.refs_1_), channel_id=1, source_target_pairs={{0,8},{2,10},{4,12},{6,14},{8,0},{10,2},{12,4},{14,6},{1,9},{3,11}... | collective-permute-start | bytes 147464 | tf_op jit(solution)/shard_map/ppermute | solution.py:599
  38.2 7.1 %collective-permute-start.13 = (bf16[1,384,128]{2,1,0:T(8,128)(2,1)S(1)}, bf16[1,384,128]{2,1,0:T(8,128)(2,1)S(1)}, u32[]{:S(2)}, u32[]{:S(2)}) collective-permute-start(bf16[1,384,128]{2,1,0:T(8,128)(2,1)S(1)} %get-tuple-element.108.refs_1_), channel_id=1, source_target_pairs={{0,8},{2,10},{4,12},{6,14},{8,0},{10,2},{12,4},{14,6},{1,9},{3,11}... | collective-permute-start | bytes 294920 | tf_op jit(solution)/shard_map/ppermute | solution.py:599
  38.8 15.1 %slice-start = ((s8[8388608]{0:T(1024)(128)(4,1)}), s8[4194304]{0:T(1024)(128)(4,1)S(1)}, s32[]{:S(2)}) async-start(s8[8388608]{0:T(1024)(128)(4,1)} %bitcast.8), calls=%async_computation | async-start | bytes 8388608
  38.9 8.5 %collective-permute-start.15 = (bf16[2,192,128]{2,1,0:T(8,128)(2,1)S(1)}, bf16[2,192,128]{2,1,0:T(8,128)(2,1)S(1)}, u32[]{:S(2)}, u32[]{:S(2)}) collective-permute-start(bf16[2,192,128]{2,1,0:T(8,128)(2,1)S(1)} %get-tuple-element.113.refs_2_), channel_id=1, source_target_pairs={{0,4},{2,6},{4,0},{6,2},{8,12},{10,14},{12,8},{14,10},{1,5},{3,7},... | collective-permute-start | bytes 294920 | tf_op jit(solution)/shard_map/ppermute | solution.py:599
  41.4 6.1 %collective-permute-start.14 = (bf16[1,240,128]{2,1,0:T(8,128)(2,1)S(1)}, bf16[1,240,128]{2,1,0:T(8,128)(2,1)S(1)}, u32[]{:S(2)}, u32[]{:S(2)}) collective-permute-start(bf16[1,240,128]{2,1,0:T(8,128)(2,1)S(1)} %get-tuple-element.111), channel_id=1, source_target_pairs={{0,8},{2,10},{4,12},{6,14},{8,0},{10,2},{12,4},{14,6},{1,9},{3,11}... | collective-permute-start | bytes 184328 | tf_op jit(solution)/shard_map/ppermute | solution.py:654
  41.8 12.1 %collective-permute-start.16 = (bf16[2,192,128]{2,1,0:T(8,128)(2,1)S(1)}, bf16[2,192,128]{2,1,0:T(8,128)(2,1)S(1)}, u32[]{:S(2)}, u32[]{:S(2)}) collective-permute-start(bf16[2,192,128]{2,1,0:T(8,128)(2,1)S(1)} %get-tuple-element.113.refs_2_), channel_id=1, source_target_pairs={{0,2},{2,0},{4,6},{6,4},{8,10},{10,8},{12,14},{14,12},{1,3},{3,1},... | collective-permute-start | bytes 294920 | tf_op jit(solution)/shard_map/ppermute | solution.py:596
  45.3 8.7 %slice-start.1 = ((s8[8388608]{0:T(1024)(128)(4,1)}), s8[4194304]{0:T(1024)(128)(4,1)S(1)}, s32[]{:S(2)}) async-start(s8[8388608]{0:T(1024)(128)(4,1)} %bitcast.8), calls=%async_computation.1 | async-start | bytes 8388608
  45.3 6.6 %collective-permute-start.19 = (bf16[2,384,128]{2,1,0:T(8,128)(2,1)S(1)}, bf16[2,384,128]{2,1,0:T(8,128)(2,1)S(1)}, u32[]{:S(2)}, u32[]{:S(2)}) collective-permute-start(bf16[2,384,128]{2,1,0:T(8,128)(2,1)S(1)} %get-tuple-element.117.refs_2_), channel_id=1, source_target_pairs={{0,4},{2,6},{4,0},{6,2},{8,12},{10,14},{12,8},{14,10},{1,5},{3,7},... | collective-permute-start | bytes 589832 | tf_op jit(solution)/shard_map/ppermute | solution.py:599
  45.4 17.2 %collective-permute-start.20 = (bf16[2,384,128]{2,1,0:T(8,128)(2,1)S(1)}, bf16[2,384,128]{2,1,0:T(8,128)(2,1)S(1)}, u32[]{:S(2)}, u32[]{:S(2)}) collective-permute-start(bf16[2,384,128]{2,1,0:T(8,128)(2,1)S(1)} %get-tuple-element.117.refs_2_), channel_id=1, source_target_pairs={{0,2},{2,0},{4,6},{6,4},{8,10},{10,8},{12,14},{14,12},{1,3},{3,1},... | collective-permute-start | bytes 589832 | tf_op jit(solution)/shard_map/ppermute | solution.py:596
  47.3 6.6 %collective-permute-start.17 = (bf16[2,192,128]{2,1,0:T(8,128)(2,1)S(1)}, bf16[2,192,128]{2,1,0:T(8,128)(2,1)S(1)}, u32[]{:S(2)}, u32[]{:S(2)}) collective-permute-start(bf16[2,192,128]{2,1,0:T(8,128)(2,1)S(1)} %collective-permute-done.15.refs_3_), channel_id=1, source_target_pairs={{0,2},{2,0},{4,6},{6,4},{8,10},{10,8},{12,14},{14,12},{1,3},{3,1},... | collective-permute-start | bytes 294920 | tf_op jit(solution)/shard_map/ppermute | solution.py:596
  49.3 6.0 %collective-permute-start.18 = (bf16[1,192,128]{2,1,0:T(8,128)(2,1)S(1)}, bf16[1,192,128]{2,1,0:T(8,128)(2,1)S(1)}, u32[]{:S(2)}, u32[]{:S(2)}) collective-permute-start(bf16[1,192,128]{2,1,0:T(8,128)(2,1)S(1)} %get-tuple-element.115.refs_1_), channel_id=1, source_target_pairs={{0,8},{2,10},{4,12},{6,14},{8,0},{10,2},{12,4},{14,6},{1,9},{3,11}... | collective-permute-start | bytes 147464 | tf_op jit(solution)/shard_map/ppermute | solution.py:599
  52.0 10.6 %collective-permute-start.21 = (bf16[2,384,128]{2,1,0:T(8,128)(2,1)S(1)}, bf16[2,384,128]{2,1,0:T(8,128)(2,1)S(1)}, u32[]{:S(2)}, u32[]{:S(2)}) collective-permute-start(bf16[2,384,128]{2,1,0:T(8,128)(2,1)S(1)} %collective-permute-done.19.refs_3_), channel_id=1, source_target_pairs={{0,2},{2,0},{4,6},{6,4},{8,10},{10,8},{12,14},{14,12},{1,3},{3,1},... | collective-permute-start | bytes 589832 | tf_op jit(solution)/shard_map/ppermute | solution.py:596
  55.4 5.1 %collective-permute-start.22 = (bf16[2,192,128]{2,1,0:T(8,128)(2,1)S(1)}, bf16[2,192,128]{2,1,0:T(8,128)(2,1)S(1)}, u32[]{:S(2)}, u32[]{:S(2)}) collective-permute-start(bf16[2,192,128]{2,1,0:T(8,128)(2,1)S(1)} %get-tuple-element.121.refs_2_), channel_id=1, source_target_pairs={{0,4},{2,6},{4,0},{6,2},{8,12},{10,14},{12,8},{14,10},{1,5},{3,7},... | collective-permute-start | bytes 294920 | tf_op jit(solution)/shard_map/ppermute | solution.py:599
  57.9 6.5 %collective-permute-start.23 = (bf16[2,192,128]{2,1,0:T(8,128)(2,1)S(1)}, bf16[2,192,128]{2,1,0:T(8,128)(2,1)S(1)}, u32[]{:S(2)}, u32[]{:S(2)}) collective-permute-start(bf16[2,192,128]{2,1,0:T(8,128)(2,1)S(1)} %get-tuple-element.121.refs_2_), channel_id=1, source_target_pairs={{0,2},{2,0},{4,6},{6,4},{8,10},{10,8},{12,14},{14,12},{1,3},{3,1},... | collective-permute-start | bytes 294920 | tf_op jit(solution)/shard_map/ppermute | solution.py:596
  60.5 4.6 %collective-permute-start.24 = (bf16[2,192,128]{2,1,0:T(8,128)(2,1)S(1)}, bf16[2,192,128]{2,1,0:T(8,128)(2,1)S(1)}, u32[]{:S(2)}, u32[]{:S(2)}) collective-permute-start(bf16[2,192,128]{2,1,0:T(8,128)(2,1)S(1)} %collective-permute-done.22.refs_3_), channel_id=1, source_target_pairs={{0,2},{2,0},{4,6},{6,4},{8,10},{10,8},{12,14},{14,12},{1,3},{3,1},... | collective-permute-start | bytes 294920 | tf_op jit(solution)/shard_map/ppermute | solution.py:596
  66.3 1.5 %collective-permute-start.25 = (bf16[96,1024]{1,0:T(8,128)(2,1)S(1)}, bf16[96,1024]{1,0:T(8,128)(2,1)S(1)}, u32[]{:S(2)}, u32[]{:S(2)}) collective-permute-start(bf16[96,1024]{1,0:T(8,128)(2,1)S(1)} %get-tuple-element.126), channel_id=1, source_target_pairs={{0,1},{1,0},{2,3},{3,2},{4,5},{5,4},{6,7},{7,6},{8,9},{9,8},{10,11... | collective-permute-start | bytes 589832 | tf_op jit(solution)/shard_map/ppermute | solution.py:738
